TPU v7x, 32 devices: a whole 2x2x4 slice. The times are simulated.
32 devices in a mesh: dp: 8 (over z, x), feat: 4 (over y, core).
Axes of the slice: x: 2, y: 2, z: 4, core: 2. Of those that a mesh axis runs over, the one named last changes fastest.
Arguments:
- tokens: bfloat16 [4096, 1024], P('dp'), may hold values from -6 to 6
- gain_one: float32 [1024], replicated, may hold values from 0.5 to 1.5
- w_query: bfloat16 [1024, 256], replicated, may hold values from -0.1875 to 0.1875
- w_key: bfloat16 [1024, 256], replicated, may hold values from -0.1875 to 0.1875
- w_value: bfloat16 [1024, 1024], replicated, may hold values from -0.1875 to 0.1875
- w_out: bfloat16 [1024, 1024], replicated, may hold values from -1.5 to 1.5
- gain_two: float32 [1024], replicated, may hold values from 0.5 to 1.5
- w_gate: bfloat16 [1024, 2752], P(None, 'feat'), may hold values from -0.1875 to 0.1875
- w_up: bfloat16 [1024, 2752], P(None, 'feat'), may hold values from -0.1875 to 0.1875
- w_down: bfloat16 [2752, 1024], P('feat'), may hold values from -0.109375 to 0.109375
- lengths: int32 [8, 4], P('dp'), may hold values from 0 to 512, as said below
- cotangent: bfloat16 [4096, 1024], P('dp'), may hold values from -6 to 6
Outputs:
- output: bfloat16 [4096, 1024], P('dp')
- grad_input: bfloat16 [4096, 1024], P('dp')
- grad_gain_one: float32 [1024], P('dp')
- grad_w_query: float32 [1024, 256], P('dp')
- grad_w_key: float32 [1024, 256], P('dp')
- grad_w_value: float32 [1024, 1024], P('dp')
- grad_w_out: float32 [1024, 1024], P('feat', 'dp')
- grad_gain_two: float32 [1024], P('dp')
- grad_w_gate: float32 [1024, 2752], P('dp', 'feat')
- grad_w_up: float32 [1024, 2752], P('dp', 'feat')
- grad_w_down: float32 [2752, 1024], P('feat', 'dp')
Inputs may be any that keep to these rules, and one draw needn't show every extreme that they name: `lengths`: row p lists the sequences packed from slot 0 of dp position p, in order; a row sums to at most 512, zeros are empty slots, and the slots after the sum are padding. One dp position holds a single sequence of 512 tokens.
All inputs are finite; a program needn't handle non-finite values.
Results may differ from a plain program's by a relative error of at most 0.023.
Values may be sent and summed in bfloat16 or wider, within the bound.
No kernel may reach another device: no remote copies, remote signals or barrier semaphores. Data moves between devices by JAX's collectives and lax.ppermute only.
A program may use at most 192 MiB of HBM per device.

v0:
```python
import math

import jax
import jax.numpy as jnp
from jax import lax
from jax.sharding import PartitionSpec as P

HEADS = 16
QK = 16
VD = 64
BLOCK = 512


EPSILON = 1e-05


def rms_factor(values):
    return lax.rsqrt(jnp.mean(values * values, axis=-1, keepdims=True) + EPSILON)


def norm_back(values, factor, gain_row, incoming):
    weighted = incoming * gain_row
    gain_grad = jnp.sum(incoming * values * factor, axis=0)
    value_grad = factor * weighted - values * factor * factor * factor * jnp.mean(
        weighted * values, axis=-1, keepdims=True
    )
    return (gain_grad, value_grad)


def split_parts(array):
    if array.dtype == jnp.bfloat16:
        return (array,)
    leading = array.astype(jnp.bfloat16)
    remainder = (array - leading.astype(jnp.float32)).astype(jnp.bfloat16)
    return (leading, remainder)


def exact_einsum(form, first, second):
    first_parts = split_parts(first)
    second_parts = split_parts(second)
    total = None
    for left_rank, left_part in enumerate(first_parts):
        for right_rank, right_part in enumerate(second_parts):
            if left_rank + right_rank < 2:
                term = jnp.einsum(form, left_part, right_part, preferred_element_type=jnp.float32)
                total = term if total is None else total + term
    return total


def feature_slice(projected, first_feature, slice_width, padded):
    row_count = projected.shape[0]
    split_heads = projected.reshape(row_count, -1, QK)
    heads_count = split_heads.shape[1]
    ones_part = jnp.ones((row_count, heads_count, 1), jnp.float32)
    linear = split_heads * QK ** (-0.25)
    square = (split_heads[:, :, :, None] * split_heads[:, :, None, :]).reshape(
        row_count, heads_count, QK * QK
    ) / math.sqrt(2.0 * QK)
    zeros_part = jnp.zeros((row_count, heads_count, padded - 1 - QK - QK * QK), jnp.float32)
    whole_map = jnp.concatenate([ones_part, linear, square, zeros_part], axis=2)
    return lax.dynamic_slice_in_dim(whole_map, first_feature, slice_width, 2)


def block_allowed(seg_block):
    places = jnp.arange(seg_block.shape[0], dtype=jnp.int32)
    return (places[:, None] >= places[None, :]) & (seg_block[:, None] == seg_block[None, :])


def segment_states(key_side, value_side, extra_side, seg_blocks, reverse):
    heads_count = key_side.shape[2]
    feature_count = key_side.shape[3]
    column_count = value_side.shape[3]

    def advance(carry_data, block_data):
        carried_state, carried_total, marker = carry_data
        key_block, value_block, extra_block, seg_block = block_data
        edge_segment = seg_block[0] if reverse else seg_block[-1]
        keep_state = (edge_segment == marker).astype(jnp.float32)
        chosen = seg_block == edge_segment
        key_selected = jnp.where(chosen[:, None, None], key_block, jnp.zeros_like(key_block))
        state_next = keep_state * carried_state + exact_einsum(
            "jhf,jhc->hfc", key_selected, value_block
        )
        total_next = keep_state * carried_total + exact_einsum(
            "jhf,jh->hf", key_selected, extra_block
        )
        return ((state_next, total_next, edge_segment), (carried_state, carried_total, marker))

    initial = (
        jnp.zeros((heads_count, feature_count, column_count), jnp.float32),
        jnp.zeros((heads_count, feature_count), jnp.float32),
        jnp.int32(-1),
    )
    _, entering = lax.scan(
        advance, initial, (key_side, value_side, extra_side, seg_blocks), reverse=reverse
    )
    return entering


def forward_block(inputs):
    query_block, key_block, value_block, seg_block, carried_state, carried_total, marker = inputs
    allowed = block_allowed(seg_block)
    scores = jnp.einsum("ihf,jhf->hij", query_block, key_block, preferred_element_type=jnp.float32)
    scores = jnp.where(allowed[None], scores, 0.0)
    numerator = exact_einsum("hij,jhc->ihc", scores, value_block)
    denominator = jnp.sum(scores, axis=2).T
    carried = (seg_block == marker).astype(jnp.float32)
    numerator = numerator + carried[:, None, None] * exact_einsum(
        "ihf,hfc->ihc", query_block, carried_state
    )
    denominator = denominator + carried[:, None] * exact_einsum(
        "ihf,hf->ih", query_block, carried_total
    )
    return (numerator, denominator)


def backward_block(inputs):
    (
        query_block,
        key_block,
        value_block,
        seg_block,
        grad_numer,
        grad_denom,
        carried_state,
        carried_total,
        marker,
        later_state,
        later_total,
        later_marker,
    ) = inputs
    allowed = block_allowed(seg_block)
    scores = jnp.einsum("ihf,jhf->hij", query_block, key_block, preferred_element_type=jnp.float32)
    scores = jnp.where(allowed[None], scores, 0.0)
    grad_scores = exact_einsum("ihc,jhc->hij", grad_numer, value_block) + grad_denom.T[:, :, None]
    grad_scores = jnp.where(allowed[None], grad_scores, 0.0)
    grad_query = exact_einsum("hij,jhf->ihf", grad_scores, key_block)
    grad_key = exact_einsum("hij,ihf->jhf", grad_scores, query_block)
    grad_value = exact_einsum("hij,ihc->jhc", scores, grad_numer)
    forward_on = (seg_block == marker).astype(jnp.float32)[:, None, None]
    grad_query = grad_query + forward_on * (
        exact_einsum("ihc,hfc->ihf", grad_numer, carried_state)
        + grad_denom[:, :, None] * carried_total[None]
    )
    later_on = (seg_block == later_marker).astype(jnp.float32)[:, None, None]
    grad_key = grad_key + later_on * (
        exact_einsum("jhc,hfc->jhf", value_block, later_state) + later_total[None]
    )
    grad_value = grad_value + later_on * exact_einsum("jhf,hfc->jhc", key_block, later_state)
    return (grad_query, grad_key, grad_value)


def local(
    tokens,
    gain_one,
    w_query,
    w_key,
    w_value,
    w_out,
    gain_two,
    w_gate,
    w_up,
    w_down,
    lengths,
    cotangent,
):
    token_count = tokens.shape[0]
    feat_count = lax.axis_size("feat")
    feat_index = lax.axis_index("feat")
    padded = (1 + QK + QK * QK + feat_count - 1) // feat_count * feat_count
    slice_width = padded // feat_count
    head_share = HEADS // feat_count
    column_share = head_share * VD
    block_count = token_count // BLOCK
    places = jnp.arange(token_count, dtype=jnp.int32)
    bounds = jnp.cumsum(lengths[0])
    segments = jnp.sum((places[:, None] >= bounds[None, :]).astype(jnp.int32), axis=1)
    live_rows = (places < bounds[-1]).astype(jnp.float32)[:, None]

    def blocked(array):
        return array.reshape((block_count, BLOCK) + array.shape[1:])

    first_feature = feat_index * slice_width

    def make_features(projected):
        return feature_slice(projected, first_feature, slice_width, padded)

    inputs = tokens.astype(jnp.float32)
    scale_one = rms_factor(inputs)
    normed = (inputs * scale_one * gain_one).astype(jnp.bfloat16)
    queries = jnp.dot(normed, w_query, preferred_element_type=jnp.float32)
    key_rows = jnp.dot(normed, w_key, preferred_element_type=jnp.float32)
    values = jnp.dot(normed, w_value, preferred_element_type=jnp.float32).astype(jnp.bfloat16)
    query_feats = make_features(queries).astype(jnp.bfloat16)
    key_feats = make_features(key_rows).astype(jnp.bfloat16)
    value_heads = values.reshape(token_count, -1, VD)
    heads_here = value_heads.shape[1]
    seg_blocks = segments.reshape(block_count, BLOCK)
    query_blocks = blocked(query_feats)
    key_blocks = blocked(key_feats)
    value_blocks = blocked(value_heads)
    ones_extra = jnp.ones((block_count, BLOCK, heads_here), jnp.bfloat16)
    states, totals, markers = segment_states(
        key_blocks, value_blocks, ones_extra, seg_blocks, False
    )
    numerator, denominator = lax.map(
        forward_block, (query_blocks, key_blocks, value_blocks, seg_blocks, states, totals, markers)
    )
    numerator = numerator.reshape(token_count, heads_here * VD)
    denominator = denominator.reshape(token_count, heads_here)
    own_numer, own_denom = (
        lax.psum_scatter(numerator, "feat", scatter_dimension=1, tiled=True),
        lax.psum_scatter(denominator, "feat", scatter_dimension=1, tiled=True),
    )
    context_exact = own_numer.reshape(token_count, head_share, VD) / own_denom[:, :, None]
    context_low = context_exact.reshape(token_count, column_share).astype(jnp.bfloat16)
    out_rows = lax.dynamic_slice_in_dim(w_out, feat_index * column_share, column_share, 0)
    mixed_rows = jnp.dot(
        lax.all_gather(context_low, "feat", axis=1, tiled=True),
        w_out,
        preferred_element_type=jnp.float32,
    )
    residual = inputs + live_rows * mixed_rows
    scale_two = rms_factor(residual)
    normed_two = (residual * scale_two * gain_two).astype(jnp.bfloat16)
    gate_values = jnp.dot(normed_two, w_gate, preferred_element_type=jnp.float32)
    up_values = jnp.dot(normed_two, w_up, preferred_element_type=jnp.float32)
    gate_sigmoid = jax.nn.sigmoid(gate_values)
    activated = gate_values * gate_sigmoid
    inner_rows = (activated * up_values).astype(jnp.bfloat16)
    feed_rows = lax.psum(
        jnp.dot(inner_rows, w_down, preferred_element_type=jnp.float32).astype(jnp.bfloat16), "feat"
    ).astype(jnp.float32)
    output = (residual + live_rows * feed_rows).astype(jnp.bfloat16)
    grad_output = cotangent.astype(jnp.float32)
    grad_feed = (grad_output * live_rows).astype(jnp.bfloat16)
    grad_wdown = jnp.einsum("tf,td->fd", inner_rows, grad_feed, preferred_element_type=jnp.float32)
    grad_inner = jnp.dot(grad_feed, w_down.T, preferred_element_type=jnp.float32)
    grad_gate = (
        grad_inner * up_values * gate_sigmoid * (1.0 + gate_values * (1.0 - gate_sigmoid))
    ).astype(jnp.bfloat16)
    grad_upper = (grad_inner * activated).astype(jnp.bfloat16)
    grad_wgate = jnp.einsum("td,tf->df", normed_two, grad_gate, preferred_element_type=jnp.float32)
    grad_wup = jnp.einsum("td,tf->df", normed_two, grad_upper, preferred_element_type=jnp.float32)
    grad_normed_part = jnp.dot(grad_gate, w_gate.T, preferred_element_type=jnp.float32) + jnp.dot(
        grad_upper, w_up.T, preferred_element_type=jnp.float32
    )
    grad_normed_two = lax.psum(grad_normed_part.astype(jnp.bfloat16), "feat").astype(jnp.float32)
    grad_gain_second, grad_resid_norm = norm_back(residual, scale_two, gain_two, grad_normed_two)
    grad_residual = grad_output + grad_resid_norm
    grad_mixed = (live_rows * grad_residual).astype(jnp.bfloat16)
    grad_wout = jnp.einsum("tc,td->cd", context_low, grad_mixed, preferred_element_type=jnp.float32)
    grad_context = jnp.dot(grad_mixed, out_rows.T, preferred_element_type=jnp.float32).astype(
        jnp.bfloat16
    )
    grad_context_heads = grad_context.astype(jnp.float32).reshape(token_count, head_share, VD)
    grad_own_numer = grad_context_heads / own_denom[:, :, None]
    grad_own_denom = -jnp.sum(grad_context_heads * context_exact, axis=2) / own_denom
    grad_numer, grad_denom = (
        lax.all_gather(
            grad_own_numer.reshape(token_count, column_share).astype(jnp.bfloat16),
            "feat",
            axis=1,
            tiled=True,
        ).astype(jnp.float32),
        lax.all_gather(grad_own_denom.astype(jnp.bfloat16), "feat", axis=1, tiled=True).astype(
            grad_own_denom.dtype
        ),
    )
    grad_numer_blocks = blocked(grad_numer.reshape(token_count, heads_here, VD))
    grad_denom_blocks = blocked(grad_denom)
    later_states, later_totals, later_markers = segment_states(
        query_blocks, grad_numer_blocks, grad_denom_blocks, seg_blocks, True
    )
    grad_qfeat, grad_kfeat, grad_vpart = lax.map(
        backward_block,
        (
            query_blocks,
            key_blocks,
            value_blocks,
            seg_blocks,
            grad_numer_blocks,
            grad_denom_blocks,
            states,
            totals,
            markers,
            later_states,
            later_totals,
            later_markers,
        ),
    )
    _, query_pull = jax.vjp(make_features, queries)
    _, key_pull = jax.vjp(make_features, key_rows)
    grad_query_part = query_pull(grad_qfeat.reshape(token_count, heads_here, slice_width))[0]
    grad_key_part = key_pull(grad_kfeat.reshape(token_count, heads_here, slice_width))[0]
    grad_value_part = grad_vpart.reshape(token_count, heads_here * VD)
    summed_query, summed_key, summed_value = (
        lax.psum(grad_query_part.astype(jnp.bfloat16), "feat").astype(jnp.float32),
        lax.psum(grad_key_part.astype(jnp.bfloat16), "feat").astype(jnp.float32),
        lax.psum(grad_value_part.astype(jnp.bfloat16), "feat").astype(jnp.float32),
    )
    grad_queries = summed_query.astype(jnp.bfloat16)
    grad_keys = summed_key.astype(jnp.bfloat16)
    grad_values = summed_value.astype(jnp.bfloat16)
    grad_wquery = jnp.einsum("td,tk->dk", normed, grad_queries, preferred_element_type=jnp.float32)
    grad_wkey = jnp.einsum("td,tk->dk", normed, grad_keys, preferred_element_type=jnp.float32)
    grad_wvalue = jnp.einsum("td,tk->dk", normed, grad_values, preferred_element_type=jnp.float32)
    grad_normed = (
        jnp.dot(grad_queries, w_query.T, preferred_element_type=jnp.float32)
        + jnp.dot(grad_keys, w_key.T, preferred_element_type=jnp.float32)
        + jnp.dot(grad_values, w_value.T, preferred_element_type=jnp.float32)
    )
    grad_gain_first, grad_input_norm = norm_back(inputs, scale_one, gain_one, grad_normed)
    grad_input = (grad_residual + grad_input_norm).astype(jnp.bfloat16)
    summed_all = (
        lax.psum_scatter(
            grad_wquery.astype(jnp.bfloat16), "dp", scatter_dimension=0, tiled=True
        ).astype(jnp.float32),
        lax.psum_scatter(
            grad_wkey.astype(jnp.bfloat16), "dp", scatter_dimension=0, tiled=True
        ).astype(jnp.float32),
        lax.psum_scatter(
            grad_wvalue.astype(jnp.bfloat16), "dp", scatter_dimension=0, tiled=True
        ).astype(jnp.float32),
        lax.psum_scatter(
            grad_wout.astype(jnp.bfloat16), "dp", scatter_dimension=1, tiled=True
        ).astype(jnp.float32),
        lax.psum_scatter(
            grad_gain_first.astype(jnp.bfloat16), "dp", scatter_dimension=0, tiled=True
        ).astype(jnp.float32),
        lax.psum_scatter(
            grad_wgate.astype(jnp.bfloat16), "dp", scatter_dimension=0, tiled=True
        ).astype(jnp.float32),
        lax.psum_scatter(
            grad_wup.astype(jnp.bfloat16), "dp", scatter_dimension=0, tiled=True
        ).astype(jnp.float32),
        lax.psum_scatter(
            grad_wdown.astype(jnp.bfloat16), "dp", scatter_dimension=1, tiled=True
        ).astype(jnp.float32),
        lax.psum_scatter(
            grad_gain_second.astype(jnp.bfloat16), "dp", scatter_dimension=0, tiled=True
        ).astype(jnp.float32),
    )
    (
        sum_query,
        sum_key,
        sum_value,
        sum_out,
        sum_gain_first,
        sum_gate,
        sum_up,
        sum_down,
        sum_gain_second,
    ) = summed_all
    return (
        output,
        grad_input,
        sum_gain_first,
        sum_query,
        sum_key,
        sum_value,
        sum_out,
        sum_gain_second,
        sum_gate,
        sum_up,
        sum_down,
    )


def solution(mesh):
    in_specs = (
        P("dp", None),
        P(),
        P(),
        P(),
        P(),
        P(),
        P(),
        P(None, "feat"),
        P(None, "feat"),
        P("feat", None),
        P("dp", None),
        P("dp", None),
    )
    out_specs = (
        P("dp", None),
        P("dp", None),
        P("dp"),
        P("dp", None),
        P("dp", None),
        P("dp", None),
        P("feat", "dp"),
        P("dp"),
        P("dp", "feat"),
        P("dp", "feat"),
        P("feat", "dp"),
    )
    return jax.shard_map(local, mesh=mesh, in_specs=in_specs, out_specs=out_specs, check_vma=False)
```

profile of v0, /device:TPU:0, one launch (start us, length us, event | category | flops | bytes accessed | tf_op | source)
XLA Modules:
  0.0 863.4 jit_solution(9750265666757219043)
XLA Ops:
  9.1 3.5 convolution_convert_fusion.5
  18.6 3.2 multiply_multiply_fusion
  27.7 3.1 select_reduce_fusion
  32.4 4.1 copy-done.1
  36.5 2.5 fusion.36
  44.5 14.1 %all-reduce = f32[512,16]{0,1:T(8,128)} all-reduce(f32[512,16]{0,1:T(8,128)} %fusion.55), channel_id=3, replica_groups=mesh['dp'=8,'feat'=4] {'feat'}, use_global_device_ids=true, to_apply=%region_5.6.clone | all-reduce | flops 8192 | bytes 65536
  59.3 15.9 %reduce-scatter.17.cloned.1.call-done = f32[512,256]{0,1:T(8,128)} async-done(((f32[512,1024]{0,1:T(8,128)}), f32[512,256]{0,1:T(8,128)}) %reduce-scatter.17.cloned.1.call-update) | async-done | bytes 524304 | tf_op jit(solution)/shard_map/reduce_scatter | solution.py:212
  78.3 15.9 %all-gather.4.cloned.1.call-done = bf16[512,1024]{0,1:T(8,128)(2,1)} async-done(((bf16[512,256]{0,1:T(8,128)(2,1)}), bf16[512,1024]{0,1:T(8,128)(2,1)}) %all-gather.4.cloned.1.call-update) | async-done | bytes 1048592 | tf_op jit(solution)/shard_map/all_gather | solution.py:219
  94.2 3.6 multiply_reduce_fusion.4
  103.3 2.5 multiply_convert_fusion.2
  109.0 36.2 %all-reduce.8.cloned.1.call-done = bf16[512,1024]{1,0:T(8,128)(2,1)} async-done(((bf16[512,1024]{1,0:T(8,128)(2,1)}), bf16[512,1024]{1,0:T(8,128)(2,1)}) %all-reduce.8.cloned.1.call-update) | async-done | bytes 1048592 | tf_op jit(solution)/shard_map/psum | solution.py:248
  145.2 3.3 fusion.24
  151.9 2.5 fusion.39
  154.5 3.6 convolution_convert_fusion.4
  159.0 6.0 all-gather
  167.7 4.0 all-gather.6.cloned.1.call-done
  171.6 10.2 %fusion.35 = f32[16,64,512]{2,1,0:T(8,128)} fusion(bf16[512,16,64]{0,2,1:T(8,128)(2,1)} %bitcast.118, f32[16,512,512]{1,2,0:T(8,128)} %copy-done.1, pred[512,512]{0,1:T(8,128)(4,1)S(1)} %fusion.31), kind=kOutput, calls=%fused_computation.87 | convolution fusion | flops 557842432 | bytes 20185088 | tf_op jit(solution)/shard_map/while/body/eval_jaxpr/hij,ihc->jhc/dot_general | solution.py:45
  181.9 9.8 %fusion.33 = f32[16,64,512]{2,1,0:T(8,128)} fusion(bf16[512,16,64]{0,2,1:T(8,128)(2,1)S(1)} %bitcast.119, f32[16,512,512]{1,2,0:T(8,128)} %copy-done.1, pred[512,512]{0,1:T(8,128)(4,1)S(1)} %fusion.31), kind=kOutput, calls=%fused_computation.85 | convolution fusion | flops 541065216 | bytes 20185088 | tf_op jit(solution)/shard_map/while/body/eval_jaxpr/hij,ihc->jhc/dot_general | solution.py:45
  191.6 9.7 %fusion.32 = f32[16,64,512]{2,1,0:T(8,128)} fusion(f32[16,512,512]{1,2,0:T(8,128)} %copy-done.1, pred[512,512]{0,1:T(8,128)(4,1)S(1)} %fusion.31, bf16[512,16,64]{0,2,1:T(8,128)(2,1)S(1)} %bitcast.120), kind=kOutput, calls=%fused_computation.84 | convolution fusion | flops 542638080 | bytes 20185088 | tf_op jit(solution)/shard_map/while/body/eval_jaxpr/hij,ihc->jhc/dot_general | solution.py:45
  203.3 8.1 fusion.90
  211.4 11.0 %add_select_fusion = f32[16,512,512]{1,2,0:T(8,128)} fusion(f32[16,512,512]{1,2,0:T(8,128)} %fusion.90, bf16[512,16,64]{0,2,1:T(8,128)(2,1)S(1)} %bitcast.128, f32[16,512]{1,0:T(8,128)S(1)} %copy-done.37, pred[512,512]{0,1:T(8,128)(4,1)S(1)} %fusion.31, bf16[512,16,64]{0,2,1:T(8,128)(2,1)S(1)} %bitcast.123), kind=kOutput, calls=%fused_computation.1 | convolution fusion | flops 551026688 | bytes 35946496 | tf_op jit(solution)/shard_map/while/body/eval_jaxpr/ihc,jhc->hij/dot_general | solution.py:45
  222.5 9.0 %fusion.64 = f32[16,69,512]{2,1,0:T(8,128)} fusion(bf16[512,16,69]{0,2,1:T(8,128)(2,1)S(1)} %copy-done.13, f32[16,512,512]{1,2,0:T(8,128)} %add_select_fusion), kind=kOutput, calls=%fused_computation.136 | convolution fusion | flops 583008256 | bytes 20168704 | tf_op jit(solution)/shard_map/while/body/eval_jaxpr/hij,jhf->ihf/dot_general | solution.py:45
  231.5 2.4 copy-done.2
  233.9 3.0 fusion.67
  236.8 9.9 %fusion.62 = f32[16,69,512]{2,1,0:T(8,128)} fusion(bf16[512,16,69]{0,2,1:T(8,128)(2,1)S(1)} %get-tuple-element.138, f32[16,512,512]{1,2,0:T(8,128)} %add_select_fusion), kind=kOutput, calls=%fused_computation.134 | convolution fusion | flops 583008256 | bytes 20168704 | tf_op jit(solution)/shard_map/while/body/eval_jaxpr/hij,ihf->jhf/dot_general | solution.py:45
  246.7 14.8 %fusion.66 = f32[16,69,512]{2,1,0:T(8,128)} fusion(bf16[512,16,69]{0,2,1:T(8,128)(2,1)S(1)} %get-tuple-element.138, f32[16,512,512]{1,2,0:T(8,128)} %add_select_fusion), kind=kOutput, calls=%fused_computation.138 | convolution fusion | flops 595591168 | bytes 20168704 | tf_op jit(solution)/shard_map/while/body/eval_jaxpr/hij,ihf->jhf/dot_general | solution.py:45
  263.7 4.8 broadcast.179.clone
  268.5 11.4 %dynamic_update_slice.34 = f32[512,16,276]{0,2,1:T(8,128)} dynamic-update-slice(f32[512,16,276]{0,2,1:T(8,128)} %broadcast.179.clone, f32[512,16,69]{0,2,1:T(8,128)} %fusion.13, s32[]{:T(128)} %constant.122.clone.1, s32[]{:T(128)} %constant.122.clone.1, s32[]{:T(128)S(6)} %select_n.25) | dynamic-update-slice | bytes 4521988 | tf_op jit(solution)/shard_map/transpose(jvp())/dynamic_update_slice | solution.py:61
  279.9 4.8 slice_multiply_fusion.1
  286.0 5.7 multiply_reduce_fusion.2
  293.7 4.7 broadcast.179.clone.1
  298.4 11.4 %dynamic_update_slice.35 = f32[512,16,276]{0,2,1:T(8,128)} dynamic-update-slice(f32[512,16,276]{0,2,1:T(8,128)} %broadcast.179.clone.1, f32[512,16,69]{0,2,1:T(8,128)} %add_bitcast_fusion, s32[]{:T(128)} %constant.122.clone.1, s32[]{:T(128)} %constant.122.clone.1, s32[]{:T(128)S(6)} %select_n.25) | dynamic-update-slice | bytes 4521988 | tf_op jit(solution)/shard_map/transpose(jvp())/dynamic_update_slice | solution.py:61
  309.8 4.8 slice_multiply_fusion
  315.9 5.5 multiply_reduce_fusion
  338.8 3.6 convolution_convert_fusion.3
  342.4 2.7 copy.94
  345.1 42.0 %all-reduce.10.cloned.1.call-done = (bf16[512,1024]{1,0:T(8,128)(2,1)}, bf16[512,1024]{0,1:T(8,128)(2,1)}, bf16[512,256]{0,1:T(8,128)(2,1)}, bf16[512,256]{0,1:T(8,128)(2,1)}) async-done(((bf16[512,1024]{1,0:T(8,128)(2,1)}, bf16[512,1024]{0,1:T(8,128)(2,1)}, bf16[512,256]{0,1:T(8,128)(2,1)}, bf16[512,256]{0,1:T(8,128)(2,1)}), (bf16[512,1024]{1,0:T(8,128)(2,1)}, bf16[512,1024]{0,1:T(8,128)(2,1)}, ...) | async-done | bytes 2621456 | tf_op jit(solution)/shard_map/psum | solution.py:231
  387.1 2.4 convolution_convert_fusion.8
  391.2 4.0 convolution_convert_fusion
  397.1 55.2 %reduce-scatter.25.cloned.1.call-done = bf16[128,256]{1,0:T(8,128)(2,1)} async-done(((bf16[1024,256]{1,0:T(8,128)(2,1)}), bf16[128,256]{1,0:T(8,128)(2,1)}) %reduce-scatter.25.cloned.1.call-update) | async-done | bytes 65552
  453.9 66.0 %reduce-scatter.27.cloned.1.call-done = bf16[128,688]{1,0:T(8,128)(2,1)} async-done(((bf16[1024,688]{1,0:T(8,128)(2,1)}), bf16[128,688]{1,0:T(8,128)(2,1)}) %reduce-scatter.27.cloned.1.call-update) | async-done | bytes 176144
  521.8 65.4 %reduce-scatter.29.cloned.1.call-done = bf16[128,688]{1,0:T(8,128)(2,1)} async-done(((bf16[1024,688]{1,0:T(8,128)(2,1)}), bf16[128,688]{1,0:T(8,128)(2,1)}) %reduce-scatter.29.cloned.1.call-update) | async-done | bytes 176144
  589.1 65.8 %reduce-scatter.31.cloned.1.call-done = bf16[128,688]{1,0:T(8,128)(2,1)} async-done(((bf16[1024,688]{1,0:T(8,128)(2,1)}), bf16[128,688]{1,0:T(8,128)(2,1)}) %reduce-scatter.31.cloned.1.call-update) | async-done | bytes 176144
  662.0 19.3 %all-reduce.3 = (bf16[1024]{0:T(1024)(128)(2,1)S(1)}, bf16[1024]{0:T(1024)(128)(2,1)S(1)}) all-reduce(bf16[1024]{0:T(1024)(128)(2,1)S(1)} %get-tuple-element.111, bf16[1024]{0:T(1024)(128)(2,1)S(1)} %copy-done.48), channel_id=4, replica_groups=mesh['dp'=8,'feat'=4] {'dp'}, use_global_device_ids=true, to_apply=%region_20.21.clone | all-reduce | flops 2048 | bytes 8192
  682.0 5.3 fusion.19
  687.3 32.2 %reduce-scatter.19.cloned.1.call-done = bf16[128,256]{1,0:T(8,128)(2,1)} async-done(((bf16[1024,256]{1,0:T(8,128)(2,1)}), bf16[128,256]{1,0:T(8,128)(2,1)}) %reduce-scatter.19.cloned.1.call-update) | async-done | bytes 65552 | tf_op jit(solution)/shard_map/reduce_scatter | solution.py:316
  721.0 63.2 %reduce-scatter.21.cloned.1.call-done = bf16[128,256]{1,0:T(8,128)(2,1)} async-done(((bf16[1024,256]{1,0:T(8,128)(2,1)}), bf16[128,256]{1,0:T(8,128)(2,1)}) %reduce-scatter.21.cloned.1.call-update) | async-done | bytes 65552 | tf_op jit(solution)/shard_map/reduce_scatter | solution.py:319
  785.7 68.6 %reduce-scatter.23.cloned.1.call-done = bf16[128,1024]{1,0:T(8,128)(2,1)} async-done(((bf16[1024,1024]{1,0:T(8,128)(2,1)}), bf16[128,1024]{1,0:T(8,128)(2,1)}) %reduce-scatter.23.cloned.1.call-update) | async-done | bytes 262160 | tf_op jit(solution)/shard_map/reduce_scatter | solution.py:322
  (208 shorter events, 86.0 us)
Async XLA Ops:
  7.2 68.0 %reduce-scatter.17.cloned.1.call-start = ((), (), s32[]{:S(2)}) async-start(), calls=%async_computation.8 | async-start | bytes 2621440 | tf_op jit(solution)/shard_map/reduce_scatter | solution.py:212
  9.1 12.9 %copy-start.44 = (f32[512]{0:T(512)}, f32[512]{0:T(512)S(1)}, u32[]{:S(2)}) copy-start(f32[512]{0:T(512)S(1)} %add_rsqrt_fusion.1) | copy-start | bytes 6148
  12.6 2.9 copy-start.16
  12.6 2.9 copy-start.46
  15.1 6.7 copy-start.49
  27.7 3.1 copy-start.12
  27.7 3.1 copy-start.8
  30.8 5.8 copy-start.1
  40.9 36.2 %copy-start.50 = (s32[4,1]{0,1:T(1,128)S(1)}, s32[4,1]{0,1:T(1,128)}, u32[]{:S(2)}) copy-start(s32[4,1]{0,1:T(1,128)} %copy-done.49) | copy-start | bytes 52
  40.9 53.3 %all-gather.4.cloned.1.call-start = ((), (), s32[]{:S(2)}) async-start(), calls=%async_computation.9 | async-start | bytes 1310720 | tf_op jit(solution)/shard_map/all_gather | solution.py:219
  77.0 68.2 %all-reduce.8.cloned.1.call-start = ((), (), s32[]{:S(2)}) async-start(), calls=%async_computation.10 | async-start | bytes 2097152 | tf_op jit(solution)/shard_map/psum | solution.py:248
  94.2 3.7 copy-start.42
  97.8 3.1 copy-start.5
  108.9 62.7 %all-gather.6.cloned.1.call-start = ((), (), s32[]{:S(2)}) async-start(), calls=%async_computation.11 | async-start | bytes 1310720 | tf_op jit(solution)/shard_map/all_gather | solution.py:260
  145.2 3.3 copy-start.6
  145.2 3.3 copy-start.30
  154.4 232.7 %all-reduce.10.cloned.1.call-start = ((), (), s32[]{:S(2)}) async-start(), calls=%async_computation.19 | async-start | bytes 5242880 | tf_op jit(solution)/shard_map/psum | solution.py:231
  154.4 3.6 copy-start.32
  154.5 3.6 copy-start.33
  171.6 10.2 %copy-start.7 = (bf16[512,1024]{0,1:T(8,128)(2,1)S(1)}, bf16[512,1024]{0,1:T(8,128)(2,1)}, u32[]{:S(2)}) copy-start(bf16[512,1024]{0,1:T(8,128)(2,1)} %all-gather.6.cloned.1.call-done) | copy-start | bytes 3145732
  203.3 8.1 copy-start.37
  211.4 11.0 %copy-start.13 = (bf16[512,16,69]{0,2,1:T(8,128)(2,1)S(1)}, bf16[512,16,69]{0,2,1:T(8,128)(2,1)}, u32[]{:S(2)}) copy-start(bf16[512,16,69]{0,2,1:T(8,128)(2,1)} %copy-done.12) | copy-start | bytes 3391492
  222.5 11.4 %copy-start.2 = (f32[16,512,512]{1,2,0:T(8,128)S(1)}, f32[16,512,512]{1,2,0:T(8,128)}, u32[]{:S(2)}) copy-start(f32[16,512,512]{1,2,0:T(8,128)} %add_select_fusion) | copy-start | bytes 50331652
  246.7 14.8 %copy-start.20 = (f32[16,69,512]{2,1,0:T(8,128)S(1)}, f32[16,69,512]{2,1,0:T(8,128)}, u32[]{:S(2)}) copy-start(f32[16,69,512]{2,1,0:T(8,128)} %fusion.64) | copy-start | bytes 6782980
  246.7 14.8 %copy-start.21 = (f32[16,69,512]{2,1,0:T(8,128)S(1)}, f32[16,69,512]{2,1,0:T(8,128)}, u32[]{:S(2)}) copy-start(f32[16,69,512]{2,1,0:T(8,128)} %fusion.67) | copy-start | bytes 6782980
  246.7 14.8 %copy-start.22 = (f32[16,69,512]{2,1,0:T(8,128)S(1)}, f32[16,69,512]{2,1,0:T(8,128)}, u32[]{:S(2)}) copy-start(f32[16,69,512]{2,1,0:T(8,128)} %fusion.37) | copy-start | bytes 6782980
  246.7 14.8 %copy-start.41 = (f32[512,16]{0,1:T(8,128)S(1)}, f32[512,16]{0,1:T(8,128)}, u32[]{:S(2)}) copy-start(f32[512,16]{0,1:T(8,128)} %multiply_bitcast_fusion) | copy-start | bytes 98308
  279.9 6.1 copy-start.4
  279.9 6.1 copy-start.29
  286.0 5.7 copy-start.10
  286.0 5.7 copy-start.18
  286.0 5.7 copy-start.19
  309.8 6.1 copy-start.3
  309.8 6.1 copy-start.27
  315.9 8.7 %copy-start.24 = (f32[16,64,512]{2,1,0:T(8,128)S(1)}, f32[16,64,512]{2,1,0:T(8,128)}, u32[]{:S(2)}) copy-start(f32[16,64,512]{2,1,0:T(8,128)} %fusion.33) | copy-start | bytes 6291460
  315.9 8.7 %copy-start.25 = (f32[16,64,512]{2,1,0:T(8,128)S(1)}, f32[16,64,512]{2,1,0:T(8,128)}, u32[]{:S(2)}) copy-start(f32[16,64,512]{2,1,0:T(8,128)} %fusion.32) | copy-start | bytes 6291460
  321.5 3.2 copy-start.14
  321.5 3.1 copy-start.23
  326.4 125.9 %reduce-scatter.25.cloned.1.call-start = ((), (), s32[]{:S(2)}) async-start(), calls=%async_computation.15 | async-start | bytes 589824
  330.5 189.5 %reduce-scatter.27.cloned.1.call-start = ((), (), s32[]{:S(2)}) async-start(), calls=%async_computation.16 | async-start | bytes 1769472
  334.5 252.7 %reduce-scatter.29.cloned.1.call-start = ((), (), s32[]{:S(2)}) async-start(), calls=%async_computation.17 | async-start | bytes 1769472
  338.5 316.4 %reduce-scatter.31.cloned.1.call-start = ((), (), s32[]{:S(2)}) async-start(), calls=%async_computation.18 | async-start | bytes 1769472
  342.4 44.8 %copy-start.17 = (bf16[512,1024]{1,0:T(8,128)(2,1)S(1)}, bf16[512,1024]{1,0:T(8,128)(2,1)}, u32[]{:S(2)}) copy-start(bf16[512,1024]{1,0:T(8,128)(2,1)} %param.12) | copy-start | bytes 3145732
  342.4 44.8 %copy-start.45 = (f32[512]{0:T(512)S(1)}, f32[512]{0:T(512)}, u32[]{:S(2)}) copy-start(f32[512]{0:T(512)} %copy-done.44) | copy-start | bytes 6148
  342.4 44.8 %copy-start.47 = (f32[1024]{0:T(1024)S(1)}, f32[1024]{0:T(1024)}, u32[]{:S(2)}) copy-start(f32[1024]{0:T(1024)} %param.13) | copy-start | bytes 12292
  345.1 374.4 %reduce-scatter.19.cloned.1.call-start = ((), (), s32[]{:S(2)}) async-start(), calls=%async_computation.12 | async-start | bytes 589824 | tf_op jit(solution)/shard_map/reduce_scatter | solution.py:316
  389.6 394.6 %reduce-scatter.21.cloned.1.call-start = ((), (), s32[]{:S(2)}) async-start(), calls=%async_computation.13 | async-start | bytes 589824 | tf_op jit(solution)/shard_map/reduce_scatter | solution.py:319
  391.1 463.2 %reduce-scatter.23.cloned.1.call-start = ((), (), s32[]{:S(2)}) async-start(), calls=%async_computation.14 | async-start | bytes 2359296 | tf_op jit(solution)/shard_map/reduce_scatter | solution.py:322
  (24 other events, 37.1 us)
Sparse Core Ops, SparseCore 0:
  41.0 34.1 reduce-scatter.16
  77.4 16.7 all-gather.3
  109.0 36.0 all-reduce.7
  154.5 17.0 all-gather.5
  326.5 60.5 all-reduce.9
  390.3 61.9 reduce-scatter.24
  456.1 63.7 reduce-scatter.26
  523.4 63.8 reduce-scatter.28
  591.0 63.8 reduce-scatter.30
  658.7 60.7 reduce-scatter.18
  723.2 60.9 reduce-scatter.20
  787.6 66.7 reduce-scatter.22
where the time goes:
time: 875 us; the launch traced here: 863 us
  waiting for transfers between devices  531 us (61%)
  matrix products  151 us (17%)
  local copies, waits for them, and re-layouts  67.7 us (8%)
  other arithmetic  57.5 us (7%)
  blocking collectives  39.5 us (5%)
  between operations  16.5 us (2%)
    unnamed x16, waiting for transfers between devices  253 us
    dot_general x17, matrix products, exact_einsum(): jnp.einsum(form, left_part, right_part, preferred_element_type=jnp.float32)  99.6 us
    reduce_scatter x1, waiting for transfers between devices, local(): lax.psum_scatter(grad_wvalue.astype(jnp.bfloat16), 'dp', scatter_dimensio...  68.6 us
    reduce_scatter x1, waiting for transfers between devices, local(): lax.psum_scatter(grad_wkey.astype(jnp.bfloat16), 'dp', scatter_dimension=...  63.2 us
    psum x1, waiting for transfers between devices, local(): lax.psum(jnp.dot(inner_rows, w_down, preferred_element_type=jnp.float32)....  42 us
    psum x1, waiting for transfers between devices, local(): lax.psum(grad_normed_part.astype(jnp.bfloat16), 'feat').astype(jnp.float32)  36.2 us
    unnamed x2, blocking collectives  33.4 us
    reduce_scatter x1, waiting for transfers between devices, local(): lax.psum_scatter(grad_wquery.astype(jnp.bfloat16), 'dp', scatter_dimensio...  32.2 us
  transfers between devices with their start and end apart: 12, of which 12 were waited for; matrix products, arithmetic and copies ran while one was open for 7% of the time, Pallas kernels for 0%

commit v1 on v0

--- a/solution.py
+++ b/solution.py
@@ -173,7 +173,8 @@
     column_share = head_share * VD
     block_count = token_count // BLOCK
     places = jnp.arange(token_count, dtype=jnp.int32)
-    bounds = jnp.cumsum(lengths[0])
+    slots = jnp.arange(lengths.shape[1])
+    bounds = jnp.sum(jnp.where(slots[None, :] <= slots[:, None], lengths[0][None, :], 0), axis=1)
     segments = jnp.sum((places[:, None] >= bounds[None, :]).astype(jnp.int32), axis=1)
     live_rows = (places < bounds[-1]).astype(jnp.float32)[:, None]
 

time: 875 us -> 875 us (level)
  no operation moved by 1% of the time
where the time goes in v1:
time: 875 us; the launch traced here: 863 us
  waiting for transfers between devices  531 us (61%)
  matrix products  151 us (17%)
  local copies, waits for them, and re-layouts  67.8 us (8%)
  other arithmetic  57.4 us (7%)
  blocking collectives  39.5 us (5%)
  between operations  16.5 us (2%)
    unnamed x16, waiting for transfers between devices  253 us
    dot_general x17, matrix products, exact_einsum(): jnp.einsum(form, left_part, right_part, preferred_element_type=jnp.float32)  99.6 us
    reduce_scatter x1, waiting for transfers between devices, local(): lax.psum_scatter(grad_wvalue.astype(jnp.bfloat16), 'dp', scatter_dimensio...  68.6 us
    reduce_scatter x1, waiting for transfers between devices, local(): lax.psum_scatter(grad_wkey.astype(jnp.bfloat16), 'dp', scatter_dimension=...  63.2 us
    psum x1, waiting for transfers between devices, local(): lax.psum(jnp.dot(inner_rows, w_down, preferred_element_type=jnp.float32)....  42 us
    psum x1, waiting for transfers between devices, local(): lax.psum(grad_normed_part.astype(jnp.bfloat16), 'feat').astype(jnp.float32)  36.2 us
    unnamed x2, blocking collectives  33.4 us
    reduce_scatter x1, waiting for transfers between devices, local(): lax.psum_scatter(grad_wquery.astype(jnp.bfloat16), 'dp', scatter_dimensio...  32.2 us
  transfers between devices with their start and end apart: 12, of which 12 were waited for; matrix products, arithmetic and copies ran while one was open for 7% of the time, Pallas kernels for 0%

profile of v1, /device:TPU:0, one launch (start us, length us, event | category | flops | bytes accessed | tf_op | source)
XLA Modules:
  0.0 863.3 jit_solution(11175286774580664384)
XLA Ops:
  9.1 3.5 convolution_convert_fusion.5
  18.6 3.2 multiply_multiply_fusion
  27.6 3.1 select_reduce_fusion
  32.4 4.1 copy-done.1
  36.5 2.5 fusion.36
  44.4 14.1 %all-reduce = f32[512,16]{0,1:T(8,128)} all-reduce(f32[512,16]{0,1:T(8,128)} %fusion.55), channel_id=3, replica_groups=mesh['dp'=8,'feat'=4] {'feat'}, use_global_device_ids=true, to_apply=%region_5.6.clone | all-reduce | flops 8192 | bytes 65536
  59.2 15.9 %reduce-scatter.17.cloned.1.call-done = f32[512,256]{0,1:T(8,128)} async-done(((f32[512,1024]{0,1:T(8,128)}), f32[512,256]{0,1:T(8,128)}) %reduce-scatter.17.cloned.1.call-update) | async-done | bytes 524304 | tf_op jit(solution)/shard_map/reduce_scatter | solution.py:213
  78.2 15.9 %all-gather.4.cloned.1.call-done = bf16[512,1024]{0,1:T(8,128)(2,1)} async-done(((bf16[512,256]{0,1:T(8,128)(2,1)}), bf16[512,1024]{0,1:T(8,128)(2,1)}) %all-gather.4.cloned.1.call-update) | async-done | bytes 1048592 | tf_op jit(solution)/shard_map/all_gather | solution.py:220
  94.1 3.6 multiply_reduce_fusion.4
  103.2 2.5 multiply_convert_fusion.2
  108.9 36.2 %all-reduce.8.cloned.1.call-done = bf16[512,1024]{1,0:T(8,128)(2,1)} async-done(((bf16[512,1024]{1,0:T(8,128)(2,1)}), bf16[512,1024]{1,0:T(8,128)(2,1)}) %all-reduce.8.cloned.1.call-update) | async-done | bytes 1048592 | tf_op jit(solution)/shard_map/psum | solution.py:249
  145.1 3.3 fusion.24
  151.8 2.5 fusion.39
  154.4 3.6 convolution_convert_fusion.4
  158.9 6.0 all-gather
  167.6 4.0 all-gather.6.cloned.1.call-done
  171.6 10.2 %fusion.35 = f32[16,64,512]{2,1,0:T(8,128)} fusion(bf16[512,16,64]{0,2,1:T(8,128)(2,1)} %bitcast.117, f32[16,512,512]{1,2,0:T(8,128)} %copy-done.1, pred[512,512]{0,1:T(8,128)(4,1)S(1)} %fusion.31), kind=kOutput, calls=%fused_computation.87 | convolution fusion | flops 557842432 | bytes 20185088 | tf_op jit(solution)/shard_map/while/body/eval_jaxpr/hij,ihc->jhc/dot_general | solution.py:45
  181.8 9.8 %fusion.33 = f32[16,64,512]{2,1,0:T(8,128)} fusion(bf16[512,16,64]{0,2,1:T(8,128)(2,1)S(1)} %bitcast.118, f32[16,512,512]{1,2,0:T(8,128)} %copy-done.1, pred[512,512]{0,1:T(8,128)(4,1)S(1)} %fusion.31), kind=kOutput, calls=%fused_computation.85 | convolution fusion | flops 541065216 | bytes 20185088 | tf_op jit(solution)/shard_map/while/body/eval_jaxpr/hij,ihc->jhc/dot_general | solution.py:45
  191.6 9.7 %fusion.32 = f32[16,64,512]{2,1,0:T(8,128)} fusion(f32[16,512,512]{1,2,0:T(8,128)} %copy-done.1, pred[512,512]{0,1:T(8,128)(4,1)S(1)} %fusion.31, bf16[512,16,64]{0,2,1:T(8,128)(2,1)S(1)} %bitcast.119), kind=kOutput, calls=%fused_computation.84 | convolution fusion | flops 542638080 | bytes 20185088 | tf_op jit(solution)/shard_map/while/body/eval_jaxpr/hij,ihc->jhc/dot_general | solution.py:45
  203.2 8.1 fusion.90
  211.3 11.0 %add_select_fusion = f32[16,512,512]{1,2,0:T(8,128)} fusion(f32[16,512,512]{1,2,0:T(8,128)} %fusion.90, bf16[512,16,64]{0,2,1:T(8,128)(2,1)S(1)} %bitcast.127, f32[16,512]{1,0:T(8,128)S(1)} %copy-done.37, pred[512,512]{0,1:T(8,128)(4,1)S(1)} %fusion.31, bf16[512,16,64]{0,2,1:T(8,128)(2,1)S(1)} %bitcast.122), kind=kOutput, calls=%fused_computation.1 | convolution fusion | flops 551026688 | bytes 35946496 | tf_op jit(solution)/shard_map/while/body/eval_jaxpr/ihc,jhc->hij/dot_general | solution.py:45
  222.4 9.0 %fusion.64 = f32[16,69,512]{2,1,0:T(8,128)} fusion(bf16[512,16,69]{0,2,1:T(8,128)(2,1)S(1)} %copy-done.13, f32[16,512,512]{1,2,0:T(8,128)} %add_select_fusion), kind=kOutput, calls=%fused_computation.138 | convolution fusion | flops 583008256 | bytes 20168704 | tf_op jit(solution)/shard_map/while/body/eval_jaxpr/hij,jhf->ihf/dot_general | solution.py:45
  231.4 2.4 copy-done.2
  233.8 3.0 fusion.67
  236.7 9.9 %fusion.62 = f32[16,69,512]{2,1,0:T(8,128)} fusion(bf16[512,16,69]{0,2,1:T(8,128)(2,1)S(1)} %get-tuple-element.138, f32[16,512,512]{1,2,0:T(8,128)} %add_select_fusion), kind=kOutput, calls=%fused_computation.136 | convolution fusion | flops 583008256 | bytes 20168704 | tf_op jit(solution)/shard_map/while/body/eval_jaxpr/hij,ihf->jhf/dot_general | solution.py:45
  246.6 14.8 %fusion.66 = f32[16,69,512]{2,1,0:T(8,128)} fusion(bf16[512,16,69]{0,2,1:T(8,128)(2,1)S(1)} %get-tuple-element.138, f32[16,512,512]{1,2,0:T(8,128)} %add_select_fusion), kind=kOutput, calls=%fused_computation.140 | convolution fusion | flops 595591168 | bytes 20168704 | tf_op jit(solution)/shard_map/while/body/eval_jaxpr/hij,ihf->jhf/dot_general | solution.py:45
  263.6 4.8 broadcast.180.clone
  268.4 11.4 %dynamic_update_slice.34 = f32[512,16,276]{0,2,1:T(8,128)} dynamic-update-slice(f32[512,16,276]{0,2,1:T(8,128)} %broadcast.180.clone, f32[512,16,69]{0,2,1:T(8,128)} %fusion.13, s32[]{:T(128)} %constant.119.clone.1, s32[]{:T(128)} %constant.119.clone.1, s32[]{:T(128)S(6)} %select_n.30) | dynamic-update-slice | bytes 4521988 | tf_op jit(solution)/shard_map/transpose(jvp())/dynamic_update_slice | solution.py:61
  279.8 4.8 slice_multiply_fusion.1
  285.9 5.7 multiply_reduce_fusion.2
  293.6 4.7 broadcast.180.clone.1
  298.3 11.4 %dynamic_update_slice.35 = f32[512,16,276]{0,2,1:T(8,128)} dynamic-update-slice(f32[512,16,276]{0,2,1:T(8,128)} %broadcast.180.clone.1, f32[512,16,69]{0,2,1:T(8,128)} %add_bitcast_fusion, s32[]{:T(128)} %constant.119.clone.1, s32[]{:T(128)} %constant.119.clone.1, s32[]{:T(128)S(6)} %select_n.30) | dynamic-update-slice | bytes 4521988 | tf_op jit(solution)/shard_map/transpose(jvp())/dynamic_update_slice | solution.py:61
  309.7 4.8 slice_multiply_fusion
  315.9 5.5 multiply_reduce_fusion
  338.7 3.6 convolution_convert_fusion.3
  342.3 2.7 copy.94
  345.0 42.0 %all-reduce.10.cloned.1.call-done = (bf16[512,1024]{1,0:T(8,128)(2,1)}, bf16[512,1024]{0,1:T(8,128)(2,1)}, bf16[512,256]{0,1:T(8,128)(2,1)}, bf16[512,256]{0,1:T(8,128)(2,1)}) async-done(((bf16[512,1024]{1,0:T(8,128)(2,1)}, bf16[512,1024]{0,1:T(8,128)(2,1)}, bf16[512,256]{0,1:T(8,128)(2,1)}, bf16[512,256]{0,1:T(8,128)(2,1)}), (bf16[512,1024]{1,0:T(8,128)(2,1)}, bf16[512,1024]{0,1:T(8,128)(2,1)}, ...) | async-done | bytes 2621456 | tf_op jit(solution)/shard_map/psum | solution.py:232
  387.0 2.4 convolution_convert_fusion.8
  391.1 4.0 convolution_convert_fusion
  397.0 55.2 %reduce-scatter.25.cloned.1.call-done = bf16[128,256]{1,0:T(8,128)(2,1)} async-done(((bf16[1024,256]{1,0:T(8,128)(2,1)}), bf16[128,256]{1,0:T(8,128)(2,1)}) %reduce-scatter.25.cloned.1.call-update) | async-done | bytes 65552
  453.8 66.0 %reduce-scatter.27.cloned.1.call-done = bf16[128,688]{1,0:T(8,128)(2,1)} async-done(((bf16[1024,688]{1,0:T(8,128)(2,1)}), bf16[128,688]{1,0:T(8,128)(2,1)}) %reduce-scatter.27.cloned.1.call-update) | async-done | bytes 176144
  521.7 65.4 %reduce-scatter.29.cloned.1.call-done = bf16[128,688]{1,0:T(8,128)(2,1)} async-done(((bf16[1024,688]{1,0:T(8,128)(2,1)}), bf16[128,688]{1,0:T(8,128)(2,1)}) %reduce-scatter.29.cloned.1.call-update) | async-done | bytes 176144
  589.0 65.8 %reduce-scatter.31.cloned.1.call-done = bf16[128,688]{1,0:T(8,128)(2,1)} async-done(((bf16[1024,688]{1,0:T(8,128)(2,1)}), bf16[128,688]{1,0:T(8,128)(2,1)}) %reduce-scatter.31.cloned.1.call-update) | async-done | bytes 176144
  661.9 19.3 %all-reduce.3 = (bf16[1024]{0:T(1024)(128)(2,1)S(1)}, bf16[1024]{0:T(1024)(128)(2,1)S(1)}) all-reduce(bf16[1024]{0:T(1024)(128)(2,1)S(1)} %get-tuple-element.111, bf16[1024]{0:T(1024)(128)(2,1)S(1)} %copy-done.48), channel_id=4, replica_groups=mesh['dp'=8,'feat'=4] {'dp'}, use_global_device_ids=true, to_apply=%region_20.21.clone | all-reduce | flops 2048 | bytes 8192
  681.9 5.3 fusion.19
  687.2 32.2 %reduce-scatter.19.cloned.1.call-done = bf16[128,256]{1,0:T(8,128)(2,1)} async-done(((bf16[1024,256]{1,0:T(8,128)(2,1)}), bf16[128,256]{1,0:T(8,128)(2,1)}) %reduce-scatter.19.cloned.1.call-update) | async-done | bytes 65552 | tf_op jit(solution)/shard_map/reduce_scatter | solution.py:317
  720.9 63.2 %reduce-scatter.21.cloned.1.call-done = bf16[128,256]{1,0:T(8,128)(2,1)} async-done(((bf16[1024,256]{1,0:T(8,128)(2,1)}), bf16[128,256]{1,0:T(8,128)(2,1)}) %reduce-scatter.21.cloned.1.call-update) | async-done | bytes 65552 | tf_op jit(solution)/shard_map/reduce_scatter | solution.py:320
  785.6 68.6 %reduce-scatter.23.cloned.1.call-done = bf16[128,1024]{1,0:T(8,128)(2,1)} async-done(((bf16[1024,1024]{1,0:T(8,128)(2,1)}), bf16[128,1024]{1,0:T(8,128)(2,1)}) %reduce-scatter.23.cloned.1.call-update) | async-done | bytes 262160 | tf_op jit(solution)/shard_map/reduce_scatter | solution.py:323
  (208 shorter events, 86.0 us)
Async XLA Ops:
  7.2 67.9 %reduce-scatter.17.cloned.1.call-start = ((), (), s32[]{:S(2)}) async-start(), calls=%async_computation.8 | async-start | bytes 2621440 | tf_op jit(solution)/shard_map/reduce_scatter | solution.py:213
  9.1 12.8 %copy-start.44 = (f32[512]{0:T(512)}, f32[512]{0:T(512)S(1)}, u32[]{:S(2)}) copy-start(f32[512]{0:T(512)S(1)} %add_rsqrt_fusion.1) | copy-start | bytes 6148
  12.6 2.8 copy-start.16
  12.6 2.8 copy-start.46
  15.1 6.7 copy-start.49
  27.6 3.1 copy-start.12
  27.6 3.1 copy-start.8
  30.7 5.8 copy-start.1
  40.8 36.2 %copy-start.50 = (s32[4]{0:T(128)S(1)}, s32[4]{0:T(128)}, u32[]{:S(2)}) copy-start(s32[4]{0:T(128)} %copy-done.49) | copy-start | bytes 52
  40.9 53.2 %all-gather.4.cloned.1.call-start = ((), (), s32[]{:S(2)}) async-start(), calls=%async_computation.9 | async-start | bytes 1310720 | tf_op jit(solution)/shard_map/all_gather | solution.py:220
  76.9 68.2 %all-reduce.8.cloned.1.call-start = ((), (), s32[]{:S(2)}) async-start(), calls=%async_computation.10 | async-start | bytes 2097152 | tf_op jit(solution)/shard_map/psum | solution.py:249
  94.1 3.7 copy-start.42
  97.7 3.1 copy-start.5
  108.8 62.7 %all-gather.6.cloned.1.call-start = ((), (), s32[]{:S(2)}) async-start(), calls=%async_computation.11 | async-start | bytes 1310720 | tf_op jit(solution)/shard_map/all_gather | solution.py:261
  145.1 3.3 copy-start.6
  145.1 3.3 copy-start.30
  154.3 232.7 %all-reduce.10.cloned.1.call-start = ((), (), s32[]{:S(2)}) async-start(), calls=%async_computation.19 | async-start | bytes 5242880 | tf_op jit(solution)/shard_map/psum | solution.py:232
  154.4 3.6 copy-start.32
  154.4 3.6 copy-start.33
  171.6 10.2 %copy-start.7 = (bf16[512,1024]{0,1:T(8,128)(2,1)S(1)}, bf16[512,1024]{0,1:T(8,128)(2,1)}, u32[]{:S(2)}) copy-start(bf16[512,1024]{0,1:T(8,128)(2,1)} %all-gather.6.cloned.1.call-done) | copy-start | bytes 3145732
  203.2 8.1 copy-start.37
  211.3 11.0 %copy-start.13 = (bf16[512,16,69]{0,2,1:T(8,128)(2,1)S(1)}, bf16[512,16,69]{0,2,1:T(8,128)(2,1)}, u32[]{:S(2)}) copy-start(bf16[512,16,69]{0,2,1:T(8,128)(2,1)} %copy-done.12) | copy-start | bytes 3391492
  222.4 11.4 %copy-start.2 = (f32[16,512,512]{1,2,0:T(8,128)S(1)}, f32[16,512,512]{1,2,0:T(8,128)}, u32[]{:S(2)}) copy-start(f32[16,512,512]{1,2,0:T(8,128)} %add_select_fusion) | copy-start | bytes 50331652
  246.6 14.8 %copy-start.20 = (f32[16,69,512]{2,1,0:T(8,128)S(1)}, f32[16,69,512]{2,1,0:T(8,128)}, u32[]{:S(2)}) copy-start(f32[16,69,512]{2,1,0:T(8,128)} %fusion.64) | copy-start | bytes 6782980
  246.6 14.8 %copy-start.21 = (f32[16,69,512]{2,1,0:T(8,128)S(1)}, f32[16,69,512]{2,1,0:T(8,128)}, u32[]{:S(2)}) copy-start(f32[16,69,512]{2,1,0:T(8,128)} %fusion.67) | copy-start | bytes 6782980
  246.6 14.8 %copy-start.22 = (f32[16,69,512]{2,1,0:T(8,128)S(1)}, f32[16,69,512]{2,1,0:T(8,128)}, u32[]{:S(2)}) copy-start(f32[16,69,512]{2,1,0:T(8,128)} %fusion.37) | copy-start | bytes 6782980
  246.6 14.8 %copy-start.41 = (f32[512,16]{0,1:T(8,128)S(1)}, f32[512,16]{0,1:T(8,128)}, u32[]{:S(2)}) copy-start(f32[512,16]{0,1:T(8,128)} %multiply_bitcast_fusion) | copy-start | bytes 98308
  279.8 6.1 copy-start.4
  279.8 6.1 copy-start.29
  285.9 5.7 copy-start.10
  285.9 5.7 copy-start.18
  285.9 5.7 copy-start.19
  309.7 6.1 copy-start.3
  309.7 6.1 copy-start.27
  315.9 8.7 %copy-start.24 = (f32[16,64,512]{2,1,0:T(8,128)S(1)}, f32[16,64,512]{2,1,0:T(8,128)}, u32[]{:S(2)}) copy-start(f32[16,64,512]{2,1,0:T(8,128)} %fusion.33) | copy-start | bytes 6291460
  315.9 8.7 %copy-start.25 = (f32[16,64,512]{2,1,0:T(8,128)S(1)}, f32[16,64,512]{2,1,0:T(8,128)}, u32[]{:S(2)}) copy-start(f32[16,64,512]{2,1,0:T(8,128)} %fusion.32) | copy-start | bytes 6291460
  321.4 3.2 copy-start.14
  321.4 3.1 copy-start.23
  326.3 125.9 %reduce-scatter.25.cloned.1.call-start = ((), (), s32[]{:S(2)}) async-start(), calls=%async_computation.15 | async-start | bytes 589824
  330.4 189.5 %reduce-scatter.27.cloned.1.call-start = ((), (), s32[]{:S(2)}) async-start(), calls=%async_computation.16 | async-start | bytes 1769472
  334.4 252.7 %reduce-scatter.29.cloned.1.call-start = ((), (), s32[]{:S(2)}) async-start(), calls=%async_computation.17 | async-start | bytes 1769472
  338.4 316.4 %reduce-scatter.31.cloned.1.call-start = ((), (), s32[]{:S(2)}) async-start(), calls=%async_computation.18 | async-start | bytes 1769472
  342.3 44.8 %copy-start.17 = (bf16[512,1024]{1,0:T(8,128)(2,1)S(1)}, bf16[512,1024]{1,0:T(8,128)(2,1)}, u32[]{:S(2)}) copy-start(bf16[512,1024]{1,0:T(8,128)(2,1)} %param.12) | copy-start | bytes 3145732
  342.3 44.8 %copy-start.45 = (f32[512]{0:T(512)S(1)}, f32[512]{0:T(512)}, u32[]{:S(2)}) copy-start(f32[512]{0:T(512)} %copy-done.44) | copy-start | bytes 6148
  342.3 44.8 %copy-start.47 = (f32[1024]{0:T(1024)S(1)}, f32[1024]{0:T(1024)}, u32[]{:S(2)}) copy-start(f32[1024]{0:T(1024)} %param.13) | copy-start | bytes 12292
  345.0 374.4 %reduce-scatter.19.cloned.1.call-start = ((), (), s32[]{:S(2)}) async-start(), calls=%async_computation.12 | async-start | bytes 589824 | tf_op jit(solution)/shard_map/reduce_scatter | solution.py:317
  389.5 394.6 %reduce-scatter.21.cloned.1.call-start = ((), (), s32[]{:S(2)}) async-start(), calls=%async_computation.13 | async-start | bytes 589824 | tf_op jit(solution)/shard_map/reduce_scatter | solution.py:320
  391.0 463.2 %reduce-scatter.23.cloned.1.call-start = ((), (), s32[]{:S(2)}) async-start(), calls=%async_computation.14 | async-start | bytes 2359296 | tf_op jit(solution)/shard_map/reduce_scatter | solution.py:323
  (24 other events, 37.1 us)
Sparse Core Ops, SparseCore 0:
  41.0 34.0 reduce-scatter.16
  77.3 16.7 all-gather.3
  109.0 36.1 all-reduce.7
  154.4 17.0 all-gather.5
  326.5 60.5 all-reduce.9
  390.2 61.9 reduce-scatter.24
  456.0 63.7 reduce-scatter.26
  523.3 63.8 reduce-scatter.28
  590.9 63.8 reduce-scatter.30
  658.6 60.7 reduce-scatter.18
  723.1 60.9 reduce-scatter.20
  787.5 66.7 reduce-scatter.22

commit v2 on v0

v2 whole, which is shorter than its diff:
```python
import functools

import jax
import jax.numpy as jnp
from jax import lax
from jax.experimental import pallas as pl
from jax.experimental.pallas import tpu as pltpu
from jax.sharding import PartitionSpec as P

HEADS = 16
QK = 16
VD = 64
EPSILON = 1e-05
F32 = jnp.float32
BF16 = jnp.bfloat16
VMEM_LIMIT = 48 * 1024 * 1024


def dot(a, b):
    return lax.dot_general(a, b, (((1,), (0,)), ((), ())), preferred_element_type=F32)


def dot_nt(a, b):
    return lax.dot_general(a, b, (((1,), (1,)), ((), ())), preferred_element_type=F32)


def dot_tn(a, b):
    return lax.dot_general(a, b, (((0,), (0,)), ((), ())), preferred_element_type=F32)


def lane_mask(shape, width, head):
    return lax.broadcasted_iota(jnp.int32, shape, 1) // width == head


def only_head(array, width, head):
    return jnp.where(lane_mask(array.shape, width, head), array, jnp.zeros_like(array))


def absolute_order(blocks, place):
    blocks = list(blocks)
    mask = 1
    while mask < len(blocks):
        flip = (place & mask) != 0
        blocks = [jnp.where(flip, blocks[j ^ mask], blocks[j]) for j in range(len(blocks))]
        mask *= 2
    return blocks


def attend_kernel(tok, gain, weights, start, n_out, r_out, q_out, k_out, v_out, ctx_out, exact_out, den_out):
    rows = tok.shape[0]
    hq, hv = q_out.shape[1], v_out.shape[1]
    block = rows // 2
    x = tok[...].astype(F32)
    r = lax.rsqrt(jnp.mean(x * x, axis=1, keepdims=True) + EPSILON)
    n = (x * r * gain[...]).astype(BF16)
    n_out[...] = n
    r_out[...] = r
    projected = dot(n, weights[...])
    v = projected[:, :hv].astype(BF16)
    q = (projected[:, hv : hv + hq] * QK**-0.5).astype(BF16)
    k = projected[:, hv + hq :].astype(BF16)
    v_out[...] = v
    q_out[...] = q
    k_out[...] = k
    for part in range(2):
        low, high = part * block, (part + 1) * block
        row = lax.broadcasted_iota(jnp.int32, (block, high), 0) + low
        col = lax.broadcasted_iota(jnp.int32, (block, high), 1)
        allowed = (col <= row) & (col >= start[low:high, :])
        number = jnp.zeros((block, hv), F32)
        total = jnp.zeros((block, hv), F32)
        for head in range(hq // QK):
            t = dot_nt(only_head(q[low:high], QK, head), k[:high]) + 1.0
            p = jnp.where(allowed, t * t + 1.0, 0.0).astype(BF16)
            number = number + dot(p, only_head(v[:high], VD, head))
            ones = jnp.where(lane_mask((high, hv), VD, head), 1.0, 0.0).astype(BF16)
            total = total + dot(p, ones)
        exact = number / total
        exact_out[low:high, :] = exact
        ctx_out[low:high, :] = exact.astype(BF16)
        den_out[low:high, :] = total


def feed_kernel(place, *refs, share):
    ctx = refs[:share]
    tok, live, gain, w_out, w_gate, w_up, w_down, gfeed = refs[share : share + 8]
    res_out, r_out, n_out, inner_out, gg_out, gu_out, back_out = refs[share + 8 :]
    context = jnp.concatenate(absolute_order([c[...] for c in ctx], place[0]), axis=1)
    mixed = dot(context, w_out[...])
    residual = tok[...].astype(F32) + live[...] * mixed
    res_out[...] = residual
    r = lax.rsqrt(jnp.mean(residual * residual, axis=1, keepdims=True) + EPSILON)
    r_out[...] = r
    n = (residual * r * gain[...]).astype(BF16)
    n_out[...] = n
    gate = dot(n, w_gate[...])
    up = dot(n, w_up[...])
    ginner = dot_nt(gfeed[...], w_down[...])
    sig = jax.nn.sigmoid(gate)
    act = gate * sig
    inner_out[...] = (act * up).astype(BF16)
    ggate = (ginner * up * sig * (1.0 + gate * (1.0 - sig))).astype(BF16)
    gup = (ginner * act).astype(BF16)
    gg_out[...] = ggate
    gu_out[...] = gup
    back_out[...] = (dot_nt(ggate, w_gate[...]) + dot_nt(gup, w_up[...])).astype(BF16)


def back_kernel(
    place, own, other, res, r2, cot, live, gain, w_own, start_row, q_in, k_in, v_in, exact_in, den_in,
    gr_out, gm_out, g_out, gain_out, gctx,
):
    rows = res.shape[0]
    hq, hv = q_in.shape[1], v_in.shape[1]
    half = rows // 2
    core = place[0] & 1
    gain_sum = jnp.zeros_like(gain_out)
    for which, source in ((core, own), (1 - core, other)):
        here = pl.ds(pl.multiple_of(which * half, half), half)
        e = source[...].astype(F32)
        residual, r = res[here, :], r2[here, :]
        weighted = e * gain[...]
        gain_sum = gain_sum + jnp.sum(e * residual * r, axis=0, keepdims=True)
        scale = r * r * r * jnp.mean(weighted * residual, axis=1, keepdims=True)
        grad = cot[here, :].astype(F32) + r * weighted - residual * scale
        gr_out[here, :] = grad
        gm = (live[here, :] * grad).astype(BF16)
        gm_out[here, :] = gm
        gctx[here, :] = dot_nt(gm, w_own[...]).astype(BF16)
    gain_out[...] = gain_sum
    number = gctx[...].astype(F32) / den_in[...]
    gn = number.astype(BF16)
    product = number * exact_in[...]
    leading = product.astype(BF16)
    remainder = (product - leading.astype(F32)).astype(BF16)
    select = (
        lax.broadcasted_iota(jnp.int32, (16, hv), 1) // VD == lax.broadcasted_iota(jnp.int32, (16, hv), 0)
    )
    select = jnp.where(select, 1.0, 0.0).astype(BF16)
    shift = dot_nt(select, leading) + dot_nt(select, remainder)
    q, k, v = q_in[...], k_in[...], v_in[...]
    gq = [jnp.zeros((half, hq), F32) for _ in range(2)]
    for part in range(2):
        low, high = part * half, (part + 1) * half
        row = lax.broadcasted_iota(jnp.int32, (half, rows - low), 0) + low
        col = lax.broadcasted_iota(jnp.int32, (half, rows - low), 1) + low
        allowed = (row <= col) & (row >= start_row[:, low:])
        gk = jnp.zeros((half, hq), F32)
        gv = jnp.zeros((half, hv), F32)
        for head in range(hq // QK):
            q_head = only_head(q[low:], QK, head)
            g_head = only_head(gn[low:], VD, head)
            t = dot_nt(k[low:high], q_head) + 1.0
            p = jnp.where(allowed, t * t + 1.0, 0.0).astype(BF16)
            g = dot_nt(v[low:high], g_head) - shift[head : head + 1, low:]
            ds = jnp.where(allowed, g * t, 0.0).astype(BF16)
            gv = gv + dot(p, g_head)
            gk = gk + dot(ds, q_head)
            k_head = only_head(k[low:high], QK, head)
            for second in range(part, 2):
                piece = ds[:, second * half - low : (second + 1) * half - low]
                gq[second] = gq[second] + dot_tn(piece, k_head)
        g_out[low:high, :hv] = gv.astype(BF16)
        g_out[low:high, hv + hq :] = (gk * 2.0).astype(BF16)
    for part in range(2):
        g_out[part * half : (part + 1) * half, hv : hv + hq] = (gq[part] * (2.0 * QK**-0.5)).astype(BF16)


def input_kernel(place, *refs, share, hv, hq):
    grads = refs[:share]
    gr, tok, r1, gain, w_query, w_key, w_value, out = refs[share:]
    blocks = absolute_order([g[...] for g in grads], place[0])
    values = jnp.concatenate([b[:, :hv] for b in blocks], axis=1)
    queries = jnp.concatenate([b[:, hv : hv + hq] for b in blocks], axis=1)
    keys = jnp.concatenate([b[:, hv + hq :] for b in blocks], axis=1)
    e = dot_nt(queries, w_query[...]) + dot_nt(keys, w_key[...]) + dot_nt(values, w_value[...])
    x, r = tok[...].astype(F32), r1[...]
    weighted = e * gain[...]
    scale = r * r * r * jnp.mean(weighted * x, axis=1, keepdims=True)
    out[...] = (gr[...] + r * weighted - x * scale).astype(BF16)


def whole(array):
    return pl.BlockSpec(array.shape, lambda *_: (0,) * len(array.shape))


def by_rows(array, block):
    return pl.BlockSpec((block,) + array.shape[1:], lambda i, *_: (i, 0))


def shape_of(rows, columns, kind):
    return jax.ShapeDtypeStruct((rows, columns), kind)


def params():
    return pltpu.CompilerParams(vmem_limit_bytes=VMEM_LIMIT)


def cost(flops, moved):
    return pl.CostEstimate(flops=flops, bytes_accessed=moved, transcendentals=0)


def local(
    tokens, gain_one, w_query, w_key, w_value, w_out, gain_two, w_gate, w_up, w_down, lengths, cotangent
):
    rows, width = tokens.shape
    share, groups = lax.axis_size("feat"), lax.axis_size("dp")
    feat, group = lax.axis_index("feat"), lax.axis_index("dp")
    hq, hv = w_query.shape[1] // share, w_value.shape[1] // share
    hidden = w_gate.shape[1]
    chunk = width // groups
    place = feat.astype(jnp.int32).reshape(1)
    half = rows // 2

    def swap(array, axis, mask):
        count = share if axis == "feat" else groups
        return lax.ppermute(array, axis, [(i, i ^ mask) for i in range(count)])

    def masks_of(count):
        found, mask = [], 1
        while mask < count:
            found.append(mask)
            mask *= 2
        return found

    feat_masks = masks_of(share)[::-1]
    dp_masks = masks_of(groups)

    def gather_feat(own):
        held = {0: own}
        for mask in feat_masks:
            for j in list(held):
                held[j ^ mask] = swap(held[j], "feat", mask)
        return [held[j] for j in range(share)]

    def sum_feat(part):
        core = feat & 1
        away = lax.dynamic_slice_in_dim(part, (1 - core) * half, half, 0)
        own = lax.dynamic_slice_in_dim(part, core * half, half, 0)
        total = (own.astype(F32) + swap(away, "feat", 1).astype(F32)).astype(BF16)
        for mask in feat_masks[:-1]:
            total = (total.astype(F32) + swap(total, "feat", mask).astype(F32)).astype(BF16)
        return total

    def bit_of(mask):
        return (group & mask) // mask

    def bit_axes(array, masks):
        lead = array.shape[:-1]
        return array.reshape(lead + (2,) * len(masks) + (array.shape[-1] // 2 ** len(masks),))

    def side(array, axis, bit):
        return lax.dynamic_index_in_dim(array, bit, axis, keepdims=False)

    def columns_side(array, mask, away):
        order = dp_masks[::-1]
        bits = bit_axes(array, order)
        bit = bit_of(mask)
        picked = side(bits, 1 + order.index(mask), 1 - bit if away else bit)
        return picked.reshape(array.shape[0], -1)

    def finish(total, masks, hops, lead):
        for mask in hops:
            axis = lead + masks.index(mask)
            bit = bit_of(mask)
            sent = side(total, axis, 1 - bit).astype(BF16)
            total = side(total, axis, bit) + swap(sent, "dp", mask).astype(F32)
            masks = [m for m in masks if m != mask]
        return total

    def sum_rows(left_away, left_keep, right, hops):
        sent = swap(dot_tn(left_away, right).astype(BF16), "dp", hops[0])
        total = dot_tn(left_keep, right) + sent.astype(F32)
        masks = [m for m in dp_masks[::-1] if m != hops[0]]
        total = total.reshape((2,) * len(masks) + (chunk, right.shape[1]))
        return finish(total, masks, hops[1:], 0)

    def sum_columns(left, right_away, right_keep, hops):
        sent = swap(dot_tn(left, right_away).astype(BF16), "dp", hops[0])
        total = dot_tn(left, right_keep) + sent.astype(F32)
        masks = [m for m in dp_masks[::-1] if m != hops[0]]
        total = total.reshape((left.shape[1],) + (2,) * len(masks) + (chunk,))
        return finish(total, masks, hops[1:], 1)

    x_first = dp_masks
    z_first = dp_masks[1:] + dp_masks[:1]

    places = jnp.arange(rows, dtype=jnp.int32)
    slots = jnp.arange(lengths.shape[1], dtype=jnp.int32)
    bounds = jnp.sum(jnp.where(slots[None, :] <= slots[:, None], lengths[0][None, :], 0), axis=1)
    passed = places[:, None] >= bounds[None, :]
    start = jnp.max(jnp.where(passed, bounds[None, :], 0), axis=1)
    live = (places < bounds[-1]).astype(F32)[:, None]

    gain_a, gain_b = gain_one[None, :], gain_two[None, :]

    def own_columns(array, count):
        return lax.dynamic_slice_in_dim(array, feat * count, count, 1)

    w_own = jnp.concatenate(
        [own_columns(w_value, hv), own_columns(w_query, hq), own_columns(w_key, hq)], axis=1
    )
    pack = hv + 2 * hq
    heads = hq // QK
    normed, r_one, q, k, v, ctx, exact, den = pl.pallas_call(
        attend_kernel,
        out_shape=[
            shape_of(rows, width, BF16),
            shape_of(rows, 1, F32),
            shape_of(rows, hq, BF16),
            shape_of(rows, hq, BF16),
            shape_of(rows, hv, BF16),
            shape_of(rows, hv, BF16),
            shape_of(rows, hv, F32),
            shape_of(rows, hv, F32),
        ],
        compiler_params=params(),
        cost_estimate=cost(2 * rows * width * pack + heads * 6 * rows * rows * 256, 4 * rows * width),
        name="attend",
    )(tokens, gain_a, w_own, start[:, None])

    ctx_all = gather_feat(ctx)
    grad_feed = (cotangent.astype(F32) * live).astype(BF16)

    feed_in = [*ctx_all, tokens, live, gain_b, w_out, w_gate, w_up, w_down, grad_feed]
    specs = [by_rows(a, half) for a in ctx_all + [tokens, live]]
    specs += [whole(a) for a in (gain_b, w_out, w_gate, w_up, w_down)] + [by_rows(grad_feed, half)]
    feed_shapes = [
        shape_of(rows, width, F32),
        shape_of(rows, 1, F32),
        shape_of(rows, width, BF16),
        shape_of(rows, hidden, BF16),
        shape_of(rows, hidden, BF16),
        shape_of(rows, hidden, BF16),
        shape_of(rows, width, BF16),
    ]
    residual, r_two, normed_two, inner, grad_gate, grad_up, back_part = pl.pallas_call(
        functools.partial(feed_kernel, share=share),
        grid_spec=pltpu.PrefetchScalarGridSpec(
            num_scalar_prefetch=1,
            grid=(2,),
            in_specs=specs,
            out_specs=[by_rows(s, half) for s in feed_shapes],
        ),
        out_shape=feed_shapes,
        compiler_params=params(),
        cost_estimate=cost(2 * rows * width * (width + 5 * hidden), 16 * width * width),
        name="feed",
    )(place, *feed_in)

    back_own = sum_feat(back_part)
    back_other = swap(back_own, "feat", 1)

    feed_part = dot(inner, w_down).astype(BF16)
    feed_own = sum_feat(feed_part)
    core_start = (feat & 1) * half
    own_rows = lambda array: lax.dynamic_slice_in_dim(array, core_start, half, 0)
    out_own = (own_rows(residual) + own_rows(live) * feed_own.astype(F32)).astype(BF16)
    out_other = swap(out_own, "feat", 1)
    output = jnp.concatenate(absolute_order([out_own, out_other], feat & 1), axis=0)

    n_away, n_keep = columns_side(normed_two, x_first[0], True), columns_side(normed_two, x_first[0], False)
    f_away, f_keep = columns_side(grad_feed, x_first[0], True), columns_side(grad_feed, x_first[0], False)
    sum_down = sum_columns(inner, f_away, f_keep, x_first)
    sum_gate = sum_rows(n_away, n_keep, grad_gate, x_first)
    sum_up = sum_rows(n_away, n_keep, grad_up, x_first)

    w_out_own = lax.dynamic_slice_in_dim(w_out, feat * hv, hv, 0)
    vmem = pl.BlockSpec(memory_space=pltpu.VMEM)
    grad_res, grad_mixed, grads, gain_part = pl.pallas_call(
        back_kernel,
        in_specs=[pl.BlockSpec(memory_space=pltpu.SMEM)] + [vmem] * 14,
        out_shape=[
            shape_of(rows, width, F32),
            shape_of(rows, width, BF16),
            shape_of(rows, pack, BF16),
            shape_of(1, width, F32),
        ],
        scratch_shapes=[pltpu.VMEM((rows, hv), BF16)],
        compiler_params=params(),
        cost_estimate=cost(2 * rows * width * hv + heads * 10 * rows * rows * 256, 12 * rows * width),
        name="back",
    )(
        place, back_own, back_other, residual, r_two, cotangent, live, gain_b, w_out_own, start[None, :],
        q, k, v, exact, den,
    )

    m_away, m_keep = columns_side(grad_mixed, z_first[0], True), columns_side(grad_mixed, z_first[0], False)
    sum_out = sum_columns(ctx, m_away, m_keep, z_first)
    gain_bits = gain_part.reshape((2,) * len(dp_masks) + (chunk,))
    masks = dp_masks[::-1]
    sum_gain_two = gain_bits
    left = list(masks)
    for mask in z_first:
        axis = left.index(mask)
        sent = side(sum_gain_two, axis, 1 - bit_of(mask))
        sum_gain_two = side(sum_gain_two, axis, bit_of(mask)) + swap(sent, "dp", mask)
        left.remove(mask)

    own_away, own_keep = columns_side(normed, x_first[0], True), columns_side(normed, x_first[0], False)
    sum_own = sum_rows(own_away, own_keep, grads, x_first).astype(BF16)

    grads_all = gather_feat(grads)
    in_args = [*grads_all, grad_res, tokens, r_one, gain_a, w_query, w_key, w_value]
    in_specs = [by_rows(a, half) for a in grads_all + [grad_res, tokens, r_one]]
    in_specs += [whole(a) for a in (gain_a, w_query, w_key, w_value)]
    grad_input = pl.pallas_call(
        functools.partial(input_kernel, share=share, hv=hv, hq=hq),
        grid_spec=pltpu.PrefetchScalarGridSpec(
            num_scalar_prefetch=1,
            grid=(2,),
            in_specs=in_specs,
            out_specs=by_rows(shape_of(rows, width, BF16), half),
        ),
        out_shape=shape_of(rows, width, BF16),
        compiler_params=params(),
        cost_estimate=cost(2 * rows * width * pack * share, 12 * rows * width),
        name="grad_input",
    )(place, *in_args)

    sums = absolute_order(gather_feat(sum_own), feat)
    sum_value = jnp.concatenate([s[:, :hv] for s in sums], axis=1).astype(F32)
    sum_query = jnp.concatenate([s[:, hv : hv + hq] for s in sums], axis=1).astype(F32)
    sum_key = jnp.concatenate([s[:, hv + hq :] for s in sums], axis=1).astype(F32)

    def own_chunk(array):
        return lax.dynamic_slice_in_dim(array, group * chunk, chunk, 0)

    sum_gain_one = sum(
        jnp.sum(own_chunk(w).astype(F32) * s, axis=1)
        for w, s in ((w_query, sum_query), (w_key, sum_key), (w_value, sum_value))
    ) / own_chunk(gain_one)

    return (
        output,
        grad_input,
        sum_gain_one,
        sum_query,
        sum_key,
        sum_value,
        sum_out,
        sum_gain_two,
        sum_gate,
        sum_up,
        sum_down,
    )


def solution(mesh):
    in_specs = (
        P("dp", None),
        P(),
        P(),
        P(),
        P(),
        P(),
        P(),
        P(None, "feat"),
        P(None, "feat"),
        P("feat", None),
        P("dp", None),
        P("dp", None),
    )
    out_specs = (
        P("dp", None),
        P("dp", None),
        P("dp"),
        P("dp", None),
        P("dp", None),
        P("dp", None),
        P("feat", "dp"),
        P("dp"),
        P("dp", "feat"),
        P("dp", "feat"),
        P("feat", "dp"),
    )
    return jax.shard_map(local, mesh=mesh, in_specs=in_specs, out_specs=out_specs, check_vma=False)
```

time: 875 us -> 233 us (0.27)
  waiting for transfers between devices: 531 us -> 37.4 us
  matrix products: 151 us -> 22.9 us
  blocking collectives: 39.5 us -> 0 us
  other arithmetic: 57.5 us -> 22.3 us
  starting transfers between devices: 0.96 us -> 31.3 us
  Pallas kernels: 0 us -> 25.5 us
  local copies, waits for them, and re-layouts: 67.7 us -> 87.6 us
  between operations: 16.5 us -> 1.63 us
    unnamed x16 -> x0, waiting for transfers between devices: 253 us -> none
    reduce_scatter x4 -> x0, waiting for transfers between devices: 180 us -> none  [the longest x1 68.6 us: local(): lax.psum_scatter(grad_wvalue.astype(jnp.bfloat16), 'dp', scatter_dimensio...]
    dot_general x39 -> x11, matrix products: 151 us -> 22.9 us  [the longest x10 20.9 us: dot_tn(): lax.dot_general(a, b, (((0,), (0,)), ((), ())), preferred_element_type=F32)]
    psum x2 -> x0, waiting for transfers between devices: 78.2 us -> none  [the longest x1 42 us: local(): lax.psum(jnp.dot(inner_rows, w_down, preferred_element_type=jnp.float32)....]
    ppermute x0 -> x33, waiting for transfers between devices: none -> 37.4 us  [swap(): return lax.ppermute(array, axis, [(i, i ^ mask) for i in range(count)])]
    unnamed x2 -> x0, blocking collectives: 33.4 us -> none
    ppermute x0 -> x33, starting transfers between devices: none -> 31.3 us  [swap(): return lax.ppermute(array, axis, [(i, i ^ mask) for i in range(count)])]
    dynamic_slice x2 -> x17, local copies, waits for them, and re-layouts: 0.16 us -> 28 us  [the longest x12 21.7 us: side(): return lax.dynamic_index_in_dim(array, bit, axis, keepdims=False)]
  transfers between devices with their start and end apart: 12 -> 33, of which waited for: 12 -> 10; matrix products, arithmetic and copies ran while one was open for 7% -> 49% of each run, Pallas kernels for 0% -> 5%
where the time goes in v2:
time: 233 us; the launch traced here: 229 us
  local copies, waits for them, and re-layouts  87.6 us (38%)
  waiting for transfers between devices  37.4 us (16%)
  starting transfers between devices  31.3 us (13%)
  Pallas kernels  25.5 us (11%)
  matrix products  22.9 us (10%)
  other arithmetic  22.3 us (10%)
    ppermute x33, waiting for transfers between devices, swap(): return lax.ppermute(array, axis, [(i, i ^ mask) for i in range(count)])  37.4 us
    unnamed x114, local copies, waits for them, and re-layouts  36 us
    ppermute x33, starting transfers between devices, swap(): return lax.ppermute(array, axis, [(i, i ^ mask) for i in range(count)])  31.3 us
    dynamic_slice x12, local copies, waits for them, and re-layouts, side(): return lax.dynamic_index_in_dim(array, bit, axis, keepdims=False)  21.7 us
    dot_general x10, matrix products, dot_tn(): lax.dot_general(a, b, (((0,), (0,)), ((), ())), preferred_element_type=F32)  20.9 us
    pallas_call x1, Pallas kernels, local(): pl.pallas_call(functools.partial(feed_kernel, share=share), grid_spec=plt...  11.2 us
    reshape x4, local copies, waits for them, and re-layouts, bit_axes(): array.reshape(lead + (2,) * len(masks) + (array.shape[-1] // 2 ** len(mas...  9.13 us
    pallas_call x1, Pallas kernels, local(): pl.pallas_call(back_kernel, in_specs=[pl.BlockSpec(memory_space=pltpu.SME...  6.4 us
  transfers between devices with their start and end apart: 33, of which 10 were waited for; matrix products, arithmetic and copies ran while one was open for 49% of the time, Pallas kernels for 5%

profile of v2, /device:TPU:0, one launch (start us, length us, event | category | flops | bytes accessed | tf_op | source)
XLA Modules:
  0.0 228.6 jit_solution(6539420106183479351)
XLA Ops:
  4.1 2.9 %attend.1 = (bf16[512,1024]{1,0:T(8,128)(2,1)S(1)}, f32[512,1]{1,0:T(8,128)S(1)}, bf16[512,64]{1,0:T(8,128)(2,1)S(1)}, bf16[512,64]{1,0:T(8,128)(2,1)S(1)}, bf16...) custom-call(bf16[512,1024]{1,0:T(8,128)(2,1)S(1)} %copy-done.3, ...), custom_call_target="tpu_custom_call" | custom-call | flops 2013265920 | bytes 2097152 | tf_op jit(solution)/shard_map/attend/pallas_call | solution.py:305
  10.7 3.0 %collective-permute-start.1 = (bf16[512,256]{1,0:T(8,128)(2,1)S(1)}, bf16[512,256]{1,0:T(8,128)(2,1)S(1)}, u32[]{:S(2)}, u32[]{:S(2)}) collective-permute-start(bf16[512,256]{1,0:T(8,128)(2,1)S(1)} %get-tuple-element.30.refs_0_), channel_id=1, source_target_pairs={{0,2},{1,3},{2,0},{3,1},{4,6},{5,7},{6,4},{7,5},{8,10},{9,11},{10,... | collective-permute-start | bytes 786440 | tf_op jit(solution)/shard_map/ppermute | solution.py:217
  16.1 3.1 %reshape.130 = bf16[512,2,2,2,128]{4,3,2,1,0:T(2,128)(2,1)} reshape(bf16[512,1024]{1,0:T(8,128)(2,1)} %multiply_convert_fusion.refs_11_) | data formatting | bytes 2097152 | tf_op jit(solution)/shard_map/reshape | solution.py:250
  20.7 4.8 %constant_dynamic-slice_fusion.2 = (bf16[512,2,2,1,128]{4,3,2,1,0:T(2,128)(2,1)}, bf16[512,2,2,1,128]{4,3,2,1,0:T(2,128)(2,1)S(1)}) fusion(bf16[512,2,2,2,128]{4,3,2,1,0:T(2,128)(2,1)} %reshape.130, s32[]{:T(128)S(6)} %select_n.184, s32[]{:T(128)S(6)} %select_n.183), kind=kLoop, calls=%fused_computation.70 | loop fusion | bytes 2097160 | tf_op jit(solution)/shard_map/jit(dynamic_index_in_dim)/dynamic_slice | solution.py:253
  26.0 3.5 %constant_dynamic-slice_fusion.20 = (bf16[512,2,2,1,128]{4,3,2,1,0:T(2,128)(2,1)}, bf16[512,2,2,1,128]{4,3,2,1,0:T(2,128)(2,1)}) fusion(bf16[512,2,2,2,128]{4,3,2,1,0:T(2,128)(2,1)S(1)} %copy-done.36, s32[]{:T(128)S(6)} %select_n.184, s32[]{:T(128)S(6)} %select_n.183), kind=kLoop, calls=%fused_computation.88 | loop fusion | bytes 2097160 | tf_op jit(solution)/shard_map/jit(dynamic_index_in_dim)/dynamic_slice | solution.py:253
  29.5 2.6 %copy.53.refs_8_ = bf16[1024,688]{1,0:T(8,128)(2,1)} copy(bf16[1024,688]{0,1:T(8,128)(2,1)} %param.19) | data formatting | bytes 2818048 | tf_op args[7]
  32.1 2.6 %copy.54.refs_9_ = bf16[1024,688]{1,0:T(8,128)(2,1)} copy(bf16[1024,688]{0,1:T(8,128)(2,1)} %param.20) | data formatting | bytes 2818048 | tf_op args[8]
  34.7 3.5 %copy.79 = bf16[512,2,2,1,128]{0,4,2,1,3:T(8,128)(2,1)} copy(bf16[512,2,2,1,128]{4,3,2,1,0:T(2,128)(2,1)} %get-tuple-element.55) | data formatting | bytes 1048576
  38.2 2.3 copy.78
  40.5 3.6 %copy.71 = bf16[512,2,2,1,128]{0,4,2,1,3:T(8,128)(2,1)} copy(bf16[512,2,2,1,128]{4,3,2,1,0:T(2,128)(2,1)} %get-tuple-element.61) | data formatting | bytes 1048576
  44.0 2.3 copy.70
  47.1 2.0 constant_dynamic-slice_fusion.22.w_own
  54.3 11.2 %feed.1 = (f32[512,1024]{1,0:T(8,128)}, f32[512,1]{1,0:T(8,128)S(1)}, bf16[512,1024]{1,0:T(8,128)(2,1)S(1)}, bf16[512,688]{1,0:T(8,128)(2,1)S(1)}, bf16[512,688]...) custom-call(s32[1]{0:T(128)} %bitcast.place, bf16[512,256]{1,0:T(8,128)(2,1)S(1)} %copy-done.11, ...), custom_call_target="tpu_custom_call" | custom-call | flops 4680843264 | bytes 16777216 | tf_op jit(solution)/shard_map/feed/pallas_call | solution.py:337
  65.5 2.0 convolution_convert_fusion
  70.5 2.7 %reshape.125 = bf16[512,2,2,2,128]{4,3,2,1,0:T(2,128)(2,1)} reshape(bf16[512,1024]{1,0:T(8,128)(2,1)} %copy-done.7) | data formatting | bytes 2097152 | tf_op jit(solution)/shard_map/reshape | solution.py:250
  73.3 5.1 %constant_dynamic-slice_fusion.8 = (bf16[512,2,2,1,128]{4,3,2,1,0:T(2,128)(2,1)}, bf16[512,2,2,1,128]{4,3,2,1,0:T(2,128)(2,1)}) fusion(bf16[512,2,2,2,128]{4,3,2,1,0:T(2,128)(2,1)} %reshape.125, s32[]{:T(128)S(6)} %select_n.184, s32[]{:T(128)S(6)} %select_n.183), kind=kLoop, calls=%fused_computation.76 | loop fusion | bytes 2097160 | tf_op jit(solution)/shard_map/jit(dynamic_index_in_dim)/dynamic_slice | solution.py:253
  78.4 3.5 %copy.75 = bf16[512,2,2,1,128]{0,4,2,1,3:T(8,128)(2,1)} copy(bf16[512,2,2,1,128]{4,3,2,1,0:T(2,128)(2,1)} %get-tuple-element.57) | data formatting | bytes 1048576
  81.9 1.9 constant_dynamic-slice_fusion.23
  83.8 2.5 %convolution_convert_fusion.2 = bf16[512,688]{0,1:T(8,128)(2,1)} fusion(bf16[512,512]{0,1:T(8,128)(2,1)} %bitcast.119, bf16[512,688]{1,0:T(8,128)(2,1)S(1)} %get-tuple-element.48), kind=kOutput, calls=%fused_computation.6 | convolution fusion | flops 361062400 | bytes 1933312 | tf_op jit(solution)/shard_map/dot_general | solution.py:28
  86.8 3.5 %copy.74 = bf16[512,2,2,1,128]{0,4,2,1,3:T(8,128)(2,1)} copy(bf16[512,2,2,1,128]{4,3,2,1,0:T(2,128)(2,1)} %get-tuple-element.58) | data formatting | bytes 1048576
  91.8 2.6 %convolution_convert_fusion.3 = bf16[512,688]{0,1:T(8,128)(2,1)} fusion(bf16[512,512]{0,1:T(8,128)(2,1)} %bitcast.120, bf16[512,688]{1,0:T(8,128)(2,1)S(1)} %get-tuple-element.47), kind=kOutput, calls=%fused_computation.7 | convolution fusion | flops 361062400 | bytes 1933312 | tf_op jit(solution)/shard_map/dot_general | solution.py:28
  95.8 2.0 add_convert_fusion.1
  100.9 2.8 %convolution_add_fusion = f32[688,512]{1,0:T(8,128)} fusion(bf16[512,688]{1,0:T(8,128)(2,1)S(1)} %get-tuple-element.32, bf16[512,512]{0,1:T(8,128)(2,1)S(1)} %bitcast.125, bf16[688,512]{1,0:T(8,128)(2,1)} %collective-permute-done.30), kind=kOutput, calls=%fused_computation.2 | convolution fusion | flops 361414656 | bytes 3342336 | tf_op jit(solution)/shard_map/dot_general | solution.py:28
  103.7 3.0 %reshape.133 = f32[688,2,2,128]{3,2,1,0:T(2,128)} reshape(f32[688,512]{1,0:T(8,128)} %convolution_add_fusion) | data formatting | bytes 2818048 | tf_op jit(solution)/shard_map/reshape | solution.py:282
  106.7 2.0 constant_dynamic-slice_fusion
  111.1 2.8 %convolution_add_fusion.1 = f32[512,688]{0,1:T(8,128)} fusion(bf16[512,512]{0,1:T(8,128)(2,1)S(1)} %bitcast.117, bf16[512,688]{1,0:T(8,128)(2,1)S(1)} %get-tuple-element.48, bf16[512,688]{0,1:T(8,128)(2,1)} %collective-permute-done.27), kind=kOutput, calls=%fused_computation.3 | convolution fusion | flops 361414656 | bytes 3342336 | tf_op jit(solution)/shard_map/dot_general | solution.py:28
  113.9 2.2 reshape.129
  118.0 1.9 collective-permute-done.24
  119.9 2.8 %convolution_add_fusion.2 = f32[512,688]{0,1:T(8,128)} fusion(bf16[512,512]{0,1:T(8,128)(2,1)S(1)} %bitcast.118, bf16[512,688]{1,0:T(8,128)(2,1)S(1)} %get-tuple-element.47, bf16[512,688]{0,1:T(8,128)(2,1)} %collective-permute-done.24), kind=kOutput, calls=%fused_computation.4 | convolution fusion | flops 361414656 | bytes 3342336 | tf_op jit(solution)/shard_map/dot_general | solution.py:28
  122.7 3.3 %reshape.128 = f32[2,2,128,688]{2,1,0,3:T(2,128)} reshape(f32[512,688]{0,1:T(8,128)} %convolution_add_fusion.2) | data formatting | bytes 2818048 | tf_op jit(solution)/shard_map/reshape | solution.py:275
  132.4 2.2 add_convert_fusion.2
  136.2 2.7 %collective-permute-start.32 = (bf16[688,128]{1,0:T(8,128)(2,1)S(1)}, bf16[688,128]{1,0:T(8,128)(2,1)S(1)}, u32[]{:S(2)}, u32[]{:S(2)}) collective-permute-start(bf16[688,128]{1,0:T(8,128)(2,1)S(1)} %fusion.8), channel_id=1, source_target_pairs={{0,16},{4,20},{8,24},{12,28},{16,0},{20,4},{24,8},{28,12},{1,17},{... | collective-permute-start | bytes 528392 | tf_op jit(solution)/shard_map/ppermute | solution.py:217
  140.5 2.7 %collective-permute-start.26 = (bf16[128,688]{0,1:T(8,128)(2,1)S(1)}, bf16[128,688]{0,1:T(8,128)(2,1)S(1)}, u32[]{:S(2)}, u32[]{:S(2)}) collective-permute-start(bf16[128,688]{0,1:T(8,128)(2,1)S(1)} %fusion.6), channel_id=1, source_target_pairs={{0,16},{4,20},{8,24},{12,28},{16,0},{20,4},{24,8},{28,12},{1,17},{... | collective-permute-start | bytes 528392 | tf_op jit(solution)/shard_map/ppermute | solution.py:217
  143.2 12.0 %collective-permute-done.32 = bf16[688,128]{1,0:T(8,128)(2,1)S(1)} collective-permute-done((bf16[688,128]{1,0:T(8,128)(2,1)S(1)}, bf16[688,128]{1,0:T(8,128)(2,1)S(1)}, u32[]{:S(2)}, u32[]{:S(2)}) %collective-permute-start.32) | collective-permute-done | bytes 176160 | tf_op jit(solution)/shard_map/ppermute | solution.py:217
  155.9 3.0 %collective-permute-done.29 = bf16[128,688]{0,1:T(8,128)(2,1)S(1)} collective-permute-done((bf16[128,688]{0,1:T(8,128)(2,1)S(1)}, bf16[128,688]{0,1:T(8,128)(2,1)S(1)}, u32[]{:S(2)}, u32[]{:S(2)}) %collective-permute-start.29) | collective-permute-done | bytes 176160 | tf_op jit(solution)/shard_map/ppermute | solution.py:217
  159.7 2.7 %collective-permute-done.26 = bf16[128,688]{0,1:T(8,128)(2,1)S(1)} collective-permute-done((bf16[128,688]{0,1:T(8,128)(2,1)S(1)}, bf16[128,688]{0,1:T(8,128)(2,1)S(1)}, u32[]{:S(2)}, u32[]{:S(2)}) %collective-permute-start.26) | collective-permute-done | bytes 176160 | tf_op jit(solution)/shard_map/ppermute | solution.py:217
  163.2 6.4 %back.1 = (f32[512,1024]{1,0:T(8,128)}, bf16[512,1024]{1,0:T(8,128)(2,1)S(1)}, bf16[512,384]{1,0:T(8,128)(2,1)S(1)}, f32[1,1024]{1,0:T(1,128)S(1)}) custom-call(s32[1]{0:T(128)} %bitcast.place, bf16[256,1024]{1,0:T(8,128)(2,1)S(1)} %add_convert_fusion.own, bf16[256,1024]{1,0:T(8,128)(2,1)S(1)} %collective-permute-done.8.other, ...), custom_call_target="tpu_custom_call" | custom-call | flops 2952790016 | bytes 6291456 | tf_op jit(solution)/shard_map/back/pallas_call | solution.py:370
  172.0 3.0 %constant_dynamic-slice_fusion.18 = (bf16[512,2,1,2,128]{4,3,2,1,0:T(2,128)(2,1)}, bf16[512,2,1,2,128]{4,3,2,1,0:T(2,128)(2,1)}) fusion(bf16[512,2,2,2,128]{4,3,2,1,0:T(2,128)(2,1)} %reshape.120, s32[]{:T(128)S(6)} %select_n.187, s32[]{:T(128)S(6)} %select_n.186), kind=kLoop, calls=%fused_computation.86 | loop fusion | bytes 2097160 | tf_op jit(solution)/shard_map/jit(dynamic_index_in_dim)/dynamic_slice | solution.py:253
  174.9 2.1 reshape.122
  177.0 2.1 convolution_convert_fusion.5
  179.1 2.0 collective-permute-start.18
  185.3 2.0 collective-permute-done.22
  191.2 2.4 %collective-permute-done.23 = f32[128]{0:T(128)S(1)} collective-permute-done((f32[128]{0:T(128)S(1)}, f32[128]{0:T(128)S(1)}, u32[]{:S(2)}, u32[]{:S(2)}) %collective-permute-start.23) | collective-permute-done | bytes 544 | tf_op jit(solution)/shard_map/ppermute | solution.py:217
  201.7 3.4 %collective-permute-done.19 = bf16[256,2,128]{2,0,1:T(8,128)(2,1)S(1)} collective-permute-done((bf16[256,2,128]{2,0,1:T(8,128)(2,1)S(1)}, bf16[256,2,128]{2,0,1:T(8,128)(2,1)S(1)}, u32[]{:S(2)}, u32[]{:S(2)}) %collective-permute-start.19) | collective-permute-done | bytes 131104 | tf_op jit(solution)/shard_map/ppermute | solution.py:217
  205.1 2.7 %collective-permute-done.13 = bf16[2,128,384]{2,1,0:T(8,128)(2,1)S(1)} collective-permute-done((bf16[2,128,384]{2,1,0:T(8,128)(2,1)S(1)}, bf16[2,128,384]{2,1,0:T(8,128)(2,1)S(1)}, u32[]{:S(2)}, u32[]{:S(2)}) %collective-permute-start.13) | collective-permute-done | bytes 196640 | tf_op jit(solution)/shard_map/ppermute | solution.py:217
  209.2 4.9 %collective-permute-done.14 = bf16[128,384]{1,0:T(8,128)(2,1)S(1)} collective-permute-done((bf16[128,384]{1,0:T(8,128)(2,1)S(1)}, bf16[128,384]{1,0:T(8,128)(2,1)S(1)}, u32[]{:S(2)}, u32[]{:S(2)}) %collective-permute-start.14) | collective-permute-done | bytes 98336 | tf_op jit(solution)/shard_map/ppermute | solution.py:217
  216.5 2.4 %collective-permute-done.15 = bf16[128,384]{1,0:T(8,128)(2,1)S(1)} collective-permute-done((bf16[128,384]{1,0:T(8,128)(2,1)S(1)}, bf16[128,384]{1,0:T(8,128)(2,1)S(1)}, u32[]{:S(2)}, u32[]{:S(2)}) %collective-permute-start.15) | collective-permute-done | bytes 98336 | tf_op jit(solution)/shard_map/ppermute | solution.py:217
  218.9 5.1 %grad_input.1 = bf16[512,1024]{1,0:T(8,128)(2,1)} custom-call(s32[1]{0:T(128)} %bitcast.place, bf16[512,384]{1,0:T(8,128)(2,1)S(1)} %get-tuple-element.40.refs_0_, bf16[512,384]{1,0:T(8,128)(2,1)S(1)} %collective-permute-done.9.refs_1_, bf16[512,384]{1,0:T(8,128)(2,1)S(1)} %collective-permute-done.10.refs_2_, ...), custom_call_target="tpu_custom_call" | custom-call | flops 1610612736 | bytes 6291456 | tf_op jit(solution)/shard_map/grad_input/pallas_call | solution.py:407
  (224 shorter events, 69.7 us)
Async XLA Ops:
  4.1 10.8 %copy-start.5 = (bf16[512,1024]{1,0:T(8,128)(2,1)S(1)}, bf16[512,1024]{1,0:T(8,128)(2,1)}, u32[]{:S(2)}) copy-start(bf16[512,1024]{1,0:T(8,128)(2,1)} %cot.1) | copy-start | bytes 3145732
  10.7 8.5 %copy-start.10 = (bf16[512,256]{1,0:T(8,128)(2,1)}, bf16[512,256]{1,0:T(8,128)(2,1)S(1)}, u32[]{:S(2)}) copy-start(bf16[512,256]{1,0:T(8,128)(2,1)S(1)} %get-tuple-element.30.refs_0_) | copy-start | bytes 786436
  10.7 14.8 %collective-permute-start.1 = (bf16[512,256]{1,0:T(8,128)(2,1)S(1)}, bf16[512,256]{1,0:T(8,128)(2,1)S(1)}, u32[]{:S(2)}, u32[]{:S(2)}) collective-permute-start(bf16[512,256]{1,0:T(8,128)(2,1)S(1)} %get-tuple-element.30.refs_0_), channel_id=1, source_target_pairs={{0,2},{1,3},{2,0},{3,1},{4,6},{5,7},{6,4},{7,5},{8,10},{9,11},{10,... | collective-permute-start | bytes 786440 | tf_op jit(solution)/shard_map/ppermute | solution.py:217
  13.6 35.4 %collective-permute-start = (bf16[512,256]{1,0:T(8,128)(2,1)S(1)}, bf16[512,256]{1,0:T(8,128)(2,1)S(1)}, u32[]{:S(2)}, u32[]{:S(2)}) collective-permute-start(bf16[512,256]{1,0:T(8,128)(2,1)S(1)} %get-tuple-element.30.refs_0_), channel_id=1, source_target_pairs={{0,1},{1,0},{2,3},{3,2},{4,5},{5,4},{6,7},{7,6},{8,9},{9,8},{10,11... | collective-permute-start | bytes 786440 | tf_op jit(solution)/shard_map/ppermute | solution.py:217
  25.5 24.2 %collective-permute-start.2 = (bf16[512,256]{1,0:T(8,128)(2,1)S(1)}, bf16[512,256]{1,0:T(8,128)(2,1)S(1)}, u32[]{:S(2)}, u32[]{:S(2)}) collective-permute-start(bf16[512,256]{1,0:T(8,128)(2,1)S(1)} %collective-permute-done.1.refs_2_), channel_id=1, source_target_pairs={{0,1},{1,0},{2,3},{3,2},{4,5},{5,4},{6,7},{7,6},{8,9},{9,8},{10,11... | collective-permute-start | bytes 786440 | tf_op jit(solution)/shard_map/ppermute | solution.py:217
  47.1 18.4 %copy-start.16 = (f32[512,1]{1,0:T(8,128)}, f32[512,1]{1,0:T(8,128)S(1)}, u32[]{:S(2)}) copy-start(f32[512,1]{1,0:T(8,128)S(1)} %fusion.3.refs_5_.live) | copy-start | bytes 6148
  54.3 11.2 %copy-start.50 = (bf16[688,1024]{1,0:T(8,128)(2,1)S(1)}, bf16[688,1024]{1,0:T(8,128)(2,1)}, u32[]{:S(2)}) copy-start(bf16[688,1024]{1,0:T(8,128)(2,1)} %refs_10_.2) | copy-start | bytes 4227076
  69.0 31.9 %collective-permute-start.30 = (bf16[688,512]{1,0:T(8,128)(2,1)}, bf16[688,512]{1,0:T(8,128)(2,1)}, u32[]{:S(2)}, u32[]{:S(2)}) collective-permute-start(bf16[688,512]{1,0:T(8,128)(2,1)} %convolution_convert_fusion.1), channel_id=1, source_target_pairs={{0,4},{4,0},{8,12},{12,8},{16,20},{20,16},{24,28},{28,24},{1,5},{5... | collective-permute-start | bytes 2113544 | tf_op jit(solution)/shard_map/ppermute | solution.py:217
  83.7 12.1 %collective-permute-start.6 = (bf16[256,1024]{1,0:T(8,128)(2,1)}, bf16[256,1024]{1,0:T(8,128)(2,1)}, u32[]{:S(2)}, u32[]{:S(2)}) collective-permute-start(bf16[256,1024]{1,0:T(8,128)(2,1)} %constant_dynamic-slice_fusion.23), channel_id=1, source_target_pairs={{0,1},{1,0},{2,3},{3,2},{4,5},{5,4},{6,7},{7,6},{8,9},{9,8},{10,11... | collective-permute-start | bytes 1572872 | tf_op jit(solution)/shard_map/ppermute | solution.py:217
  86.3 24.9 %collective-permute-start.27 = (bf16[512,688]{0,1:T(8,128)(2,1)}, bf16[512,688]{0,1:T(8,128)(2,1)}, u32[]{:S(2)}, u32[]{:S(2)}) collective-permute-start(bf16[512,688]{0,1:T(8,128)(2,1)} %convolution_convert_fusion.2), channel_id=1, source_target_pairs={{0,4},{4,0},{8,12},{12,8},{16,20},{20,16},{24,28},{28,24},{1,5},{5... | collective-permute-start | bytes 2113544 | tf_op jit(solution)/shard_map/ppermute | solution.py:217
  91.5 6.9 %collective-permute-start.3 = (bf16[256,1024]{1,0:T(8,128)(2,1)S(1)}, bf16[256,1024]{1,0:T(8,128)(2,1)S(1)}, u32[]{:S(2)}, u32[]{:S(2)}) collective-permute-start(bf16[256,1024]{1,0:T(8,128)(2,1)S(1)} %constant_dynamic-slice_fusion.24), channel_id=1, source_target_pairs={{0,1},{1,0},{2,3},{3,2},{4,5},{5,4},{6,7},{7,6},{8,9},{9,8},{10,11... | collective-permute-start | bytes 1572872 | tf_op jit(solution)/shard_map/ppermute | solution.py:217
  94.3 25.6 %collective-permute-start.24 = (bf16[512,688]{0,1:T(8,128)(2,1)}, bf16[512,688]{0,1:T(8,128)(2,1)}, u32[]{:S(2)}, u32[]{:S(2)}) collective-permute-start(bf16[512,688]{0,1:T(8,128)(2,1)} %convolution_convert_fusion.3), channel_id=1, source_target_pairs={{0,4},{4,0},{8,12},{12,8},{16,20},{20,16},{24,28},{28,24},{1,5},{5... | collective-permute-start | bytes 2113544 | tf_op jit(solution)/shard_map/ppermute | solution.py:217
  97.9 33.0 %collective-permute-start.7 = (bf16[256,1024]{1,0:T(8,128)(2,1)}, bf16[256,1024]{1,0:T(8,128)(2,1)}, u32[]{:S(2)}, u32[]{:S(2)}) collective-permute-start(bf16[256,1024]{1,0:T(8,128)(2,1)} %add_convert_fusion.1), channel_id=1, source_target_pairs={{0,2},{1,3},{2,0},{3,1},{4,6},{5,7},{6,4},{7,5},{8,10},{9,11},{10,... | collective-permute-start | bytes 1572872 | tf_op jit(solution)/shard_map/ppermute | solution.py:217
  99.4 33.0 %collective-permute-start.4 = (bf16[256,1024]{1,0:T(8,128)(2,1)}, bf16[256,1024]{1,0:T(8,128)(2,1)}, u32[]{:S(2)}, u32[]{:S(2)}) collective-permute-start(bf16[256,1024]{1,0:T(8,128)(2,1)} %add_convert_fusion.4), channel_id=1, source_target_pairs={{0,2},{1,3},{2,0},{3,1},{4,6},{5,7},{6,4},{7,5},{8,10},{9,11},{10,... | collective-permute-start | bytes 1572872 | tf_op jit(solution)/shard_map/ppermute | solution.py:217
  109.6 25.5 %collective-permute-start.31 = (bf16[688,2,128]{2,0,1:T(8,128)(2,1)}, bf16[688,2,128]{2,0,1:T(8,128)(2,1)}, u32[]{:S(2)}, u32[]{:S(2)}) collective-permute-start(bf16[688,2,128]{2,0,1:T(8,128)(2,1)} %bitcast.107), channel_id=1, source_target_pairs={{0,8},{4,12},{8,0},{12,4},{16,24},{20,28},{24,16},{28,20},{1,9},{5... | collective-permute-start | bytes 1056776 | tf_op jit(solution)/shard_map/ppermute | solution.py:217
  117.6 21.3 %collective-permute-start.28 = (bf16[2,128,688]{1,2,0:T(8,128)(2,1)}, bf16[2,128,688]{1,2,0:T(8,128)(2,1)}, u32[]{:S(2)}, u32[]{:S(2)}) collective-permute-start(bf16[2,128,688]{1,2,0:T(8,128)(2,1)} %bitcast.106), channel_id=1, source_target_pairs={{0,8},{4,12},{8,0},{12,4},{16,24},{20,28},{24,16},{28,20},{1,9},{5... | collective-permute-start | bytes 1056776 | tf_op jit(solution)/shard_map/ppermute | solution.py:217
  128.0 12.3 %collective-permute-start.25 = (bf16[2,128,688]{1,2,0:T(8,128)(2,1)S(1)}, bf16[2,128,688]{1,2,0:T(8,128)(2,1)S(1)}, u32[]{:S(2)}, u32[]{:S(2)}) collective-permute-start(bf16[2,128,688]{1,2,0:T(8,128)(2,1)S(1)} %bitcast.127), channel_id=1, source_target_pairs={{0,8},{4,12},{8,0},{12,4},{16,24},{20,28},{24,16},{28,20},{1,9},{5... | collective-permute-start | bytes 1056776 | tf_op jit(solution)/shard_map/ppermute | solution.py:217
  132.3 30.9 %collective-permute-start.8 = (bf16[256,1024]{1,0:T(8,128)(2,1)S(1)}, bf16[256,1024]{1,0:T(8,128)(2,1)S(1)}, u32[]{:S(2)}, u32[]{:S(2)}) collective-permute-start(bf16[256,1024]{1,0:T(8,128)(2,1)S(1)} %add_convert_fusion.own), channel_id=1, source_target_pairs={{0,1},{1,0},{2,3},{3,2},{4,5},{5,4},{6,7},{7,6},{8,9},{9,8},{10,11... | collective-permute-start | bytes 1572872 | tf_op jit(solution)/shard_map/ppermute | solution.py:217
  134.6 48.2 %collective-permute-start.5 = (bf16[256,1024]{1,0:T(8,128)(2,1)}, bf16[256,1024]{1,0:T(8,128)(2,1)}, u32[]{:S(2)}, u32[]{:S(2)}) collective-permute-start(bf16[256,1024]{1,0:T(8,128)(2,1)} %add_convert_fusion.2), channel_id=1, source_target_pairs={{0,1},{1,0},{2,3},{3,2},{4,5},{5,4},{6,7},{7,6},{8,9},{9,8},{10,11... | collective-permute-start | bytes 1572872 | tf_op jit(solution)/shard_map/ppermute | solution.py:217
  136.2 19.0 %collective-permute-start.32 = (bf16[688,128]{1,0:T(8,128)(2,1)S(1)}, bf16[688,128]{1,0:T(8,128)(2,1)S(1)}, u32[]{:S(2)}, u32[]{:S(2)}) collective-permute-start(bf16[688,128]{1,0:T(8,128)(2,1)S(1)} %fusion.8), channel_id=1, source_target_pairs={{0,16},{4,20},{8,24},{12,28},{16,0},{20,4},{24,8},{28,12},{1,17},{... | collective-permute-start | bytes 528392 | tf_op jit(solution)/shard_map/ppermute | solution.py:217
  139.9 19.0 %collective-permute-start.29 = (bf16[128,688]{0,1:T(8,128)(2,1)S(1)}, bf16[128,688]{0,1:T(8,128)(2,1)S(1)}, u32[]{:S(2)}, u32[]{:S(2)}) collective-permute-start(bf16[128,688]{0,1:T(8,128)(2,1)S(1)} %fusion.7), channel_id=1, source_target_pairs={{0,16},{4,20},{8,24},{12,28},{16,0},{20,4},{24,8},{28,12},{1,17},{... | collective-permute-start | bytes 528392 | tf_op jit(solution)/shard_map/ppermute | solution.py:217
  140.3 22.9 %copy-start.31 = (bf16[512,256]{1,0:T(8,128)(2,1)S(1)}, bf16[512,256]{1,0:T(8,128)(2,1)}, u32[]{:S(2)}) copy-start(bf16[512,256]{1,0:T(8,128)(2,1)} %copy-done.30) | copy-start | bytes 786436
  140.3 22.9 %copy-start.33 = (f32[512,1]{1,0:T(8,128)S(1)}, f32[512,1]{1,0:T(8,128)}, u32[]{:S(2)}) copy-start(f32[512,1]{1,0:T(8,128)} %copy-done.32) | copy-start | bytes 6148
  140.3 22.9 %copy-start.35 = (bf16[512,64]{1,0:T(8,128)(2,1)S(1)}, bf16[512,64]{1,0:T(8,128)(2,1)}, u32[]{:S(2)}) copy-start(bf16[512,64]{1,0:T(8,128)(2,1)} %copy-done.34) | copy-start | bytes 196612
  140.4 22.8 %copy-start.29 = (f32[512,256]{1,0:T(8,128)S(1)}, f32[512,256]{1,0:T(8,128)}, u32[]{:S(2)}) copy-start(f32[512,256]{1,0:T(8,128)} %copy-done.28) | copy-start | bytes 1572868
  140.5 22.7 %copy-start.6 = (bf16[512,1024]{1,0:T(8,128)(2,1)S(1)}, bf16[512,1024]{1,0:T(8,128)(2,1)}, u32[]{:S(2)}) copy-start(bf16[512,1024]{1,0:T(8,128)(2,1)} %cot.1) | copy-start | bytes 3145732
  140.5 22.7 %copy-start.13 = (bf16[256,1024]{1,0:T(8,128)(2,1)S(1)}, bf16[256,1024]{1,0:T(8,128)(2,1)}, u32[]{:S(2)}) copy-start(bf16[256,1024]{1,0:T(8,128)(2,1)} %constant_dynamic-slice_fusion.22.w_own) | copy-start | bytes 1572868
  140.5 22.7 %copy-start.17 = (f32[512,1]{1,0:T(8,128)S(1)}, f32[512,1]{1,0:T(8,128)}, u32[]{:S(2)}) copy-start(f32[512,1]{1,0:T(8,128)} %copy-done.16) | copy-start | bytes 6148
  140.5 22.7 %copy-start.27 = (f32[512,256]{1,0:T(8,128)S(1)}, f32[512,256]{1,0:T(8,128)}, u32[]{:S(2)}) copy-start(f32[512,256]{1,0:T(8,128)} %copy-done.26) | copy-start | bytes 1572868
  140.5 21.9 %collective-permute-start.26 = (bf16[128,688]{0,1:T(8,128)(2,1)S(1)}, bf16[128,688]{0,1:T(8,128)(2,1)S(1)}, u32[]{:S(2)}, u32[]{:S(2)}) collective-permute-start(bf16[128,688]{0,1:T(8,128)(2,1)S(1)} %fusion.6), channel_id=1, source_target_pairs={{0,16},{4,20},{8,24},{12,28},{16,0},{20,4},{24,8},{28,12},{1,17},{... | collective-permute-start | bytes 528392 | tf_op jit(solution)/shard_map/ppermute | solution.py:217
  169.6 39.6 %collective-permute-start.10 = (bf16[512,384]{1,0:T(8,128)(2,1)S(1)}, bf16[512,384]{1,0:T(8,128)(2,1)S(1)}, u32[]{:S(2)}, u32[]{:S(2)}) collective-permute-start(bf16[512,384]{1,0:T(8,128)(2,1)S(1)} %get-tuple-element.40.refs_0_), channel_id=1, source_target_pairs={{0,2},{1,3},{2,0},{3,1},{4,6},{5,7},{6,4},{7,5},{8,10},{9,11},{10,... | collective-permute-start | bytes 1179656 | tf_op jit(solution)/shard_map/ppermute | solution.py:217
  170.1 48.7 %collective-permute-start.9 = (bf16[512,384]{1,0:T(8,128)(2,1)S(1)}, bf16[512,384]{1,0:T(8,128)(2,1)S(1)}, u32[]{:S(2)}, u32[]{:S(2)}) collective-permute-start(bf16[512,384]{1,0:T(8,128)(2,1)S(1)} %get-tuple-element.40.refs_0_), channel_id=1, source_target_pairs={{0,1},{1,0},{2,3},{3,2},{4,5},{5,4},{6,7},{7,6},{8,9},{9,8},{10,11... | collective-permute-start | bytes 1179656 | tf_op jit(solution)/shard_map/ppermute | solution.py:217
  170.2 12.1 %collective-permute-start.21 = (f32[2,2,128]{2,1,0:T(2,128)S(1)}, f32[2,2,128]{2,1,0:T(2,128)S(1)}, u32[]{:S(2)}, u32[]{:S(2)}) collective-permute-start(f32[2,2,128]{2,1,0:T(2,128)S(1)} %fusion.14), channel_id=1, source_target_pairs={{0,8},{4,12},{8,0},{12,4},{16,24},{20,28},{24,16},{28,20},{1,9},{5... | collective-permute-start | bytes 6152 | tf_op jit(solution)/shard_map/ppermute | solution.py:217
  179.1 15.0 %collective-permute-start.18 = (bf16[256,512]{1,0:T(8,128)(2,1)}, bf16[256,512]{1,0:T(8,128)(2,1)S(1)}, u32[]{:S(2)}, u32[]{:S(2)}) collective-permute-start(bf16[256,512]{1,0:T(8,128)(2,1)} %convolution_convert_fusion.5), channel_id=1, source_target_pairs={{0,8},{4,12},{8,0},{12,4},{16,24},{20,28},{24,16},{28,20},{1,9},{5... | collective-permute-start | bytes 786440 | tf_op jit(solution)/shard_map/ppermute | solution.py:217
  182.3 16.0 %collective-permute-start.12 = (bf16[512,384]{1,0:T(8,128)(2,1)}, bf16[512,384]{1,0:T(8,128)(2,1)}, u32[]{:S(2)}, u32[]{:S(2)}) collective-permute-start(bf16[512,384]{1,0:T(8,128)(2,1)} %convolution_convert_fusion.4), channel_id=1, source_target_pairs={{0,4},{4,0},{8,12},{12,8},{16,20},{20,16},{24,28},{28,24},{1,5},{5... | collective-permute-start | bytes 1179656 | tf_op jit(solution)/shard_map/ppermute | solution.py:217
  182.8 4.5 %collective-permute-start.22 = (f32[2,128]{1,0:T(2,128)S(1)}, f32[2,128]{1,0:T(2,128)S(1)}, u32[]{:S(2)}, u32[]{:S(2)}) collective-permute-start(f32[2,128]{1,0:T(2,128)S(1)} %fusion.18), channel_id=1, source_target_pairs={{0,16},{4,20},{8,24},{12,28},{16,0},{20,4},{24,8},{28,12},{1,17},{... | collective-permute-start | bytes 3080 | tf_op jit(solution)/shard_map/ppermute | solution.py:217
  187.4 6.2 %collective-permute-start.23 = (f32[128]{0:T(128)S(1)}, f32[128]{0:T(128)S(1)}, u32[]{:S(2)}, u32[]{:S(2)}) collective-permute-start(f32[128]{0:T(128)S(1)} %fusion.21), channel_id=1, source_target_pairs={{0,4},{4,0},{8,12},{12,8},{16,20},{20,16},{24,28},{28,24},{1,5},{5... | collective-permute-start | bytes 1544 | tf_op jit(solution)/shard_map/ppermute | solution.py:217
  196.7 8.4 %collective-permute-start.19 = (bf16[256,2,128]{2,0,1:T(8,128)(2,1)S(1)}, bf16[256,2,128]{2,0,1:T(8,128)(2,1)S(1)}, u32[]{:S(2)}, u32[]{:S(2)}) collective-permute-start(bf16[256,2,128]{2,0,1:T(8,128)(2,1)S(1)} %bitcast.128), channel_id=1, source_target_pairs={{0,16},{4,20},{8,24},{12,28},{16,0},{20,4},{24,8},{28,12},{1,17},{... | collective-permute-start | bytes 393224 | tf_op jit(solution)/shard_map/ppermute | solution.py:217
  198.3 20.6 %copy-start.4 = (bf16[512,1024]{1,0:T(8,128)(2,1)S(1)}, bf16[512,1024]{1,0:T(8,128)(2,1)}, u32[]{:S(2)}) copy-start(bf16[512,1024]{1,0:T(8,128)(2,1)} %refs_5_.1) | copy-start | bytes 3145732
  199.9 19.0 %copy-start = (f32[512,1024]{1,0:T(8,128)S(1)}, f32[512,1024]{1,0:T(8,128)}, u32[]{:S(2)}) copy-start(f32[512,1024]{1,0:T(8,128)} %get-tuple-element.41.refs_4_) | copy-start | bytes 6291460
  199.9 19.0 %copy-start.15 = (f32[512,1]{1,0:T(8,128)S(1)}, f32[512,1]{1,0:T(8,128)}, u32[]{:S(2)}) copy-start(f32[512,1]{1,0:T(8,128)} %copy-done.14) | copy-start | bytes 6148
  199.9 7.9 %collective-permute-start.13 = (bf16[2,128,384]{2,1,0:T(8,128)(2,1)S(1)}, bf16[2,128,384]{2,1,0:T(8,128)(2,1)S(1)}, u32[]{:S(2)}, u32[]{:S(2)}) collective-permute-start(bf16[2,128,384]{2,1,0:T(8,128)(2,1)S(1)} %fusion.4), channel_id=1, source_target_pairs={{0,8},{4,12},{8,0},{12,4},{16,24},{20,28},{24,16},{28,20},{1,9},{5... | collective-permute-start | bytes 589832 | tf_op jit(solution)/shard_map/ppermute | solution.py:217
  207.9 6.3 %collective-permute-start.14 = (bf16[128,384]{1,0:T(8,128)(2,1)S(1)}, bf16[128,384]{1,0:T(8,128)(2,1)S(1)}, u32[]{:S(2)}, u32[]{:S(2)}) collective-permute-start(bf16[128,384]{1,0:T(8,128)(2,1)S(1)} %fusion.10), channel_id=1, source_target_pairs={{0,16},{4,20},{8,24},{12,28},{16,0},{20,4},{24,8},{28,12},{1,17},{... | collective-permute-start | bytes 294920 | tf_op jit(solution)/shard_map/ppermute | solution.py:217
  208.6 7.2 %collective-permute-start.20 = (bf16[256,128]{1,0:T(8,128)(2,1)S(1)}, bf16[256,128]{1,0:T(8,128)(2,1)S(1)}, u32[]{:S(2)}, u32[]{:S(2)}) collective-permute-start(bf16[256,128]{1,0:T(8,128)(2,1)S(1)} %fusion.11), channel_id=1, source_target_pairs={{0,4},{4,0},{8,12},{12,8},{16,20},{20,16},{24,28},{28,24},{1,5},{5... | collective-permute-start | bytes 196616 | tf_op jit(solution)/shard_map/ppermute | solution.py:217
  209.2 9.7 %collective-permute-start.11 = (bf16[512,384]{1,0:T(8,128)(2,1)S(1)}, bf16[512,384]{1,0:T(8,128)(2,1)S(1)}, u32[]{:S(2)}, u32[]{:S(2)}) collective-permute-start(bf16[512,384]{1,0:T(8,128)(2,1)S(1)} %collective-permute-done.10.refs_2_), channel_id=1, source_target_pairs={{0,1},{1,0},{2,3},{3,2},{4,5},{5,4},{6,7},{7,6},{8,9},{9,8},{10,11... | collective-permute-start | bytes 1179656 | tf_op jit(solution)/shard_map/ppermute | solution.py:217
  214.2 4.7 %collective-permute-start.15 = (bf16[128,384]{1,0:T(8,128)(2,1)S(1)}, bf16[128,384]{1,0:T(8,128)(2,1)S(1)}, u32[]{:S(2)}, u32[]{:S(2)}) collective-permute-start(bf16[128,384]{1,0:T(8,128)(2,1)S(1)} %fusion.5), channel_id=1, source_target_pairs={{0,2},{1,3},{2,0},{3,1},{4,6},{5,7},{6,4},{7,5},{8,10},{9,11},{10,... | collective-permute-start | bytes 294920 | tf_op jit(solution)/shard_map/ppermute | solution.py:217
  216.4 7.5 %collective-permute-start.17 = (bf16[128,384]{1,0:T(8,128)(2,1)S(1)}, bf16[128,384]{1,0:T(8,128)(2,1)S(1)}, u32[]{:S(2)}, u32[]{:S(2)}) collective-permute-start(bf16[128,384]{1,0:T(8,128)(2,1)S(1)} %fusion.5), channel_id=1, source_target_pairs={{0,1},{1,0},{2,3},{3,2},{4,5},{5,4},{6,7},{7,6},{8,9},{9,8},{10,11... | collective-permute-start | bytes 294920 | tf_op jit(solution)/shard_map/ppermute | solution.py:217
  218.9 5.1 %collective-permute-start.16 = (bf16[128,384]{1,0:T(8,128)(2,1)S(1)}, bf16[128,384]{1,0:T(8,128)(2,1)S(1)}, u32[]{:S(2)}, u32[]{:S(2)}) collective-permute-start(bf16[128,384]{1,0:T(8,128)(2,1)S(1)} %collective-permute-done.15), channel_id=1, source_target_pairs={{0,1},{1,0},{2,3},{3,2},{4,5},{5,4},{6,7},{7,6},{8,9},{9,8},{10,11... | collective-permute-start | bytes 294920 | tf_op jit(solution)/shard_map/ppermute | solution.py:217
  (36 other events, 95.9 us)

commit v3 on v2

v3 whole, which is shorter than its diff:
```python
import functools

import jax
import jax.numpy as jnp
from jax import lax
from jax.experimental import pallas as pl
from jax.experimental.pallas import tpu as pltpu
from jax.sharding import PartitionSpec as P

HEADS = 16
QK = 16
VD = 64
EPSILON = 1e-05
F32 = jnp.float32
BF16 = jnp.bfloat16
VMEM_LIMIT = 48 * 1024 * 1024


def dot(a, b):
    return lax.dot_general(a, b, (((1,), (0,)), ((), ())), preferred_element_type=F32)


def dot_nt(a, b):
    return lax.dot_general(a, b, (((1,), (1,)), ((), ())), preferred_element_type=F32)


def dot_tn(a, b):
    return lax.dot_general(a, b, (((0,), (0,)), ((), ())), preferred_element_type=F32)


def lane_mask(shape, width, head):
    return lax.broadcasted_iota(jnp.int32, shape, 1) // width == head


def only_head(array, width, head):
    return jnp.where(lane_mask(array.shape, width, head), array, jnp.zeros_like(array))


def absolute_order(blocks, place):
    blocks = list(blocks)
    mask = 1
    while mask < len(blocks):
        flip = (place & mask) != 0
        blocks = [jnp.where(flip, blocks[j ^ mask], blocks[j]) for j in range(len(blocks))]
        mask *= 2
    return blocks


def bounds_of(lengths):
    bounds, total = [], 0
    for slot in range(lengths.shape[1]):
        total = total + lengths[0, slot]
        bounds.append(total)
    return bounds


def starts_of(bounds, index):
    start = jnp.zeros_like(index)
    for bound in bounds:
        start = jnp.maximum(start, jnp.where(index >= bound, bound, 0))
    return start


def block_columns(ref, index, width):
    if width % 128 == 0:
        return ref[:, pl.ds(pl.multiple_of(index * width, 128), width)]
    each = 128 // width
    wide = ref[:, pl.ds(pl.multiple_of(index // each * 128, 128), 128)]
    picked = wide[:, :width]
    for i in range(1, each):
        picked = jnp.where(index % each == i, wide[:, i * width : (i + 1) * width], picked)
    return picked


def positions(order):
    found = [0]
    for mask in order:
        found = [r for r in found] + [r ^ mask for r in found]
    count = len(found)
    result = []
    for p in range(count):
        r, top = 0, count // 2
        for mask in order:
            if p & top:
                r ^= mask
            top //= 2
        result.append(r)
    return result


def chunk_columns(ref, group, offsets, chunk):
    return jnp.concatenate([block_columns(ref, group ^ r, chunk) for r in offsets], axis=1)


def attend_kernel(
    place, lengths, tok, gain, w_query, w_key, w_value, n_out, r_out, q_out, k_out, v_out, ctx_out, exact_out, den_out
):
    rows = tok.shape[0]
    hq, hv = q_out.shape[1], v_out.shape[1]
    block = rows // 2
    feat = place[0]
    x = tok[...].astype(F32)
    r = lax.rsqrt(jnp.mean(x * x, axis=1, keepdims=True) + EPSILON)
    n = (x * r * gain[...]).astype(BF16)
    n_out[...] = n
    r_out[...] = r
    w_small = jnp.concatenate([block_columns(w_query, feat, hq), block_columns(w_key, feat, hq)], axis=1)
    small = dot(n, w_small)
    v = dot(n, w_value[...]).astype(BF16)
    q = (small[:, :hq] * QK**-0.5).astype(BF16)
    k = small[:, hq:].astype(BF16)
    v_out[...] = v
    q_out[...] = q
    k_out[...] = k
    bounds = bounds_of(lengths)
    for part in range(2):
        low, high = part * block, (part + 1) * block
        row = lax.broadcasted_iota(jnp.int32, (block, high), 0) + low
        col = lax.broadcasted_iota(jnp.int32, (block, high), 1)
        start = starts_of(bounds, lax.broadcasted_iota(jnp.int32, (block, 1), 0) + low)
        allowed = (col <= row) & (col >= start)
        number = jnp.zeros((block, hv), F32)
        total = jnp.zeros((block, hv), F32)
        for head in range(hq // QK):
            t = dot_nt(only_head(q[low:high], QK, head), k[:high]) + 1.0
            p = jnp.where(allowed, t * t + 1.0, 0.0).astype(BF16)
            number = number + dot(p, only_head(v[:high], VD, head))
            ones = jnp.where(lane_mask((high, hv), VD, head), 1.0, 0.0).astype(BF16)
            total = total + dot(p, ones)
        exact = number / total
        exact_out[low:high, :] = exact
        ctx_out[low:high, :] = exact.astype(BF16)
        den_out[low:high, :] = total


def feed_kernel(place, *refs, share):
    lengths = refs[0]
    ctx = refs[1 : 1 + share]
    tok, cot, gain, w_out, w_gate, w_up, w_down = refs[1 + share : 8 + share]
    res_out, r_out, n_out, inner_out, gg_out, gu_out, away_out, own_out = refs[8 + share :]
    step, half = pl.program_id(0), tok.shape[0]
    core = place[0] & 1
    which = jnp.where(step == 0, 1 - core, core)
    index = lax.broadcasted_iota(jnp.int32, (half, 1), 0) + which * half
    live = (index < bounds_of(lengths)[-1]).astype(F32)
    context = jnp.concatenate(absolute_order([c[...] for c in ctx], place[0]), axis=1)
    mixed = dot(context, w_out[...])
    residual = tok[...].astype(F32) + live * mixed
    res_out[...] = residual
    r = lax.rsqrt(jnp.mean(residual * residual, axis=1, keepdims=True) + EPSILON)
    r_out[...] = r
    n = (residual * r * gain[...]).astype(BF16)
    n_out[...] = n
    gate = dot_nt(n, w_gate[...])
    up = dot_nt(n, w_up[...])
    gfeed = (cot[...].astype(F32) * live).astype(BF16)
    ginner = dot_nt(gfeed, w_down[...])
    sig = jax.nn.sigmoid(gate)
    act = gate * sig
    inner_out[...] = (act * up * live).astype(BF16)
    ggate = (ginner * up * sig * (1.0 + gate * (1.0 - sig))).astype(BF16)
    gup = (ginner * act).astype(BF16)
    gg_out[...] = ggate
    gu_out[...] = gup
    back = (dot(ggate, w_gate[...]) + dot(gup, w_up[...])).astype(BF16)

    @pl.when(step == 0)
    def _():
        away_out[...] = back

    @pl.when(step == 1)
    def _():
        own_out[...] = back


def down_kernel(place, inner, w_down, away_out, own_out):
    half = own_out.shape[0]
    core = place[0] & 1
    for which, out in ((1 - core, away_out), (core, own_out)):
        out[...] = dot(inner[pl.ds(pl.multiple_of(which * half, half), half), :], w_down[...]).astype(BF16)


def columns_away_kernel(where, left, right, out, *, order, chunk):
    offsets = positions(order)
    count = len(offsets) // 2
    result = dot_tn(left[...], chunk_columns(right, where[1], offsets[count:], chunk))
    for i in range(count):
        out[i] = result[:, i * chunk : (i + 1) * chunk].astype(BF16)


def columns_keep_kernel(where, left, right, arrived, keep_out, away_out, *, order, chunk):
    offsets = positions(order)
    count = len(offsets) // 2
    result = dot_tn(left[...], chunk_columns(right, where[1], offsets[:count], chunk))
    for i in range(count):
        total = result[:, i * chunk : (i + 1) * chunk] + arrived[i].astype(F32)
        if i < count // 2:
            keep_out[i] = total
        else:
            away_out[i - count // 2] = total.astype(BF16)


def rows_away_kernel(where, left, right, out, *, order, chunk):
    offsets = positions(order)
    count = len(offsets) // 2
    result = dot_tn(chunk_columns(left, where[1], offsets[count:], chunk), right[...])
    for i in range(count):
        out[i] = result[i * chunk : (i + 1) * chunk].astype(BF16)


def rows_keep_kernel(where, left, right, arrived, keep_out, away_out, *, order, chunk):
    offsets = positions(order)
    count = len(offsets) // 2
    result = dot_tn(chunk_columns(left, where[1], offsets[:count], chunk), right[...])
    for i in range(count):
        total = result[i * chunk : (i + 1) * chunk] + arrived[i].astype(F32)
        if i < count // 2:
            keep_out[i] = total
        else:
            away_out[i - count // 2] = total.astype(BF16)


def back_kernel(
    place, lengths, own, other, res, r2, cot, gain, w_own, q_in, k_in, v_in, exact_in, den_in,
    gr_out, gm_out, g_out, gain_out, gctx,
):
    rows = res.shape[0]
    hq, hv = q_in.shape[1], v_in.shape[1]
    half = rows // 2
    core = place[0] & 1
    bounds = bounds_of(lengths)
    gain_sum = jnp.zeros((1, gain_out.shape[1]), F32)
    for which, source in ((core, own), (1 - core, other)):
        here = pl.ds(pl.multiple_of(which * half, half), half)
        live = (lax.broadcasted_iota(jnp.int32, (half, 1), 0) + which * half < bounds[-1]).astype(F32)
        e = source[...].astype(F32)
        residual, r = res[here, :], r2[here, :]
        weighted = e * gain[...]
        gain_sum = gain_sum + jnp.sum(e * residual * r, axis=0, keepdims=True)
        scale = r * r * r * jnp.mean(weighted * residual, axis=1, keepdims=True)
        grad = cot[here, :].astype(F32) + r * weighted - residual * scale
        gr_out[here, :] = grad
        gm = (live * grad).astype(BF16)
        gm_out[here, :] = gm
        gctx[here, :] = dot_nt(gm, w_own[...]).astype(BF16)
    gain_out[...] = gain_sum
    number = gctx[...].astype(F32) / den_in[...]
    gn = number.astype(BF16)
    product = number * exact_in[...]
    leading = product.astype(BF16)
    remainder = (product - leading.astype(F32)).astype(BF16)
    select = (
        lax.broadcasted_iota(jnp.int32, (16, hv), 1) // VD == lax.broadcasted_iota(jnp.int32, (16, hv), 0)
    )
    select = jnp.where(select, 1.0, 0.0).astype(BF16)
    shift = dot_nt(select, leading) + dot_nt(select, remainder)
    q, k, v = q_in[...], k_in[...], v_in[...]
    gq = [jnp.zeros((half, hq), F32) for _ in range(2)]
    for part in range(2):
        low, high = part * half, (part + 1) * half
        row = lax.broadcasted_iota(jnp.int32, (half, rows - low), 0) + low
        col = lax.broadcasted_iota(jnp.int32, (half, rows - low), 1) + low
        start = starts_of(bounds, lax.broadcasted_iota(jnp.int32, (1, rows - low), 1) + low)
        allowed = (row <= col) & (row >= start)
        gk = jnp.zeros((half, hq), F32)
        gv = jnp.zeros((half, hv), F32)
        for head in range(hq // QK):
            q_head = only_head(q[low:], QK, head)
            g_head = only_head(gn[low:], VD, head)
            t = dot_nt(k[low:high], q_head) + 1.0
            p = jnp.where(allowed, t * t + 1.0, 0.0).astype(BF16)
            g = dot_nt(v[low:high], g_head) - shift[head : head + 1, low:]
            ds = jnp.where(allowed, g * t, 0.0).astype(BF16)
            gv = gv + dot(p, g_head)
            gk = gk + dot(ds, q_head)
            k_head = only_head(k[low:high], QK, head)
            for second in range(part, 2):
                piece = ds[:, second * half - low : (second + 1) * half - low]
                gq[second] = gq[second] + dot_tn(piece, k_head)
        g_out[low:high, :hv] = gv.astype(BF16)
        g_out[low:high, hv + hq :] = (gk * 2.0).astype(BF16)
    for part in range(2):
        g_out[part * half : (part + 1) * half, hv : hv + hq] = (gq[part] * (2.0 * QK**-0.5)).astype(BF16)


def out_away_kernel(where, left, right, gain, out, *, order, chunk):
    offsets = positions(order)
    count = len(offsets) // 2
    many = left.shape[1]
    result = dot_tn(left[...], chunk_columns(right, where[1], offsets[count:], chunk))
    gains = chunk_columns(gain, where[1], offsets[count:], chunk)
    for i in range(count):
        out[i, :many, :] = result[:, i * chunk : (i + 1) * chunk].astype(BF16)
        out[i, many:, :] = jnp.broadcast_to(gains[:, i * chunk : (i + 1) * chunk], (16, chunk)).astype(BF16)


def out_keep_kernel(where, left, right, gain, arrived, keep_out, away_out, *, order, chunk):
    offsets = positions(order)
    count = len(offsets) // 2
    many = left.shape[1]
    result = dot_tn(left[...], chunk_columns(right, where[1], offsets[:count], chunk))
    gains = chunk_columns(gain, where[1], offsets[:count], chunk)
    for i in range(count):
        total = result[:, i * chunk : (i + 1) * chunk] + arrived[i, :many, :].astype(F32)
        extra = jnp.broadcast_to(gains[:, i * chunk : (i + 1) * chunk], (16, chunk)) + arrived[i, many:, :].astype(F32)
        if i < count // 2:
            keep_out[i, :many, :] = total
            keep_out[i, many:, :] = extra
        else:
            away_out[i - count // 2, :many, :] = total.astype(BF16)
            away_out[i - count // 2, many:, :] = extra.astype(BF16)


def input_kernel(place, *refs, share, hv, hq):
    grads = refs[:share]
    gr, tok, r1, gain, w_query, w_key, w_value, out = refs[share:]
    blocks = absolute_order([g[...] for g in grads], place[0])
    values = jnp.concatenate([b[:, :hv] for b in blocks], axis=1)
    queries = jnp.concatenate([b[:, hv : hv + hq] for b in blocks], axis=1)
    keys = jnp.concatenate([b[:, hv + hq :] for b in blocks], axis=1)
    e = dot_nt(queries, w_query[...]) + dot_nt(keys, w_key[...]) + dot_nt(values, w_value[...])
    x, r = tok[...].astype(F32), r1[...]
    weighted = e * gain[...]
    scale = r * r * r * jnp.mean(weighted * x, axis=1, keepdims=True)
    out[...] = (gr[...] + r * weighted - x * scale).astype(BF16)


def finish_kernel(where, *refs, share, hv, hq):
    sums = refs[:share]
    gain, w_query, w_key, w_value, q_out, k_out, v_out, gain_out = refs[share:]
    blocks = absolute_order([s[...].astype(F32) for s in sums], where[0])
    values = jnp.concatenate([b[:, :hv] for b in blocks], axis=1)
    queries = jnp.concatenate([b[:, hv : hv + hq] for b in blocks], axis=1)
    keys = jnp.concatenate([b[:, hv + hq :] for b in blocks], axis=1)
    q_out[...] = queries
    k_out[...] = keys
    v_out[...] = values
    total = jnp.sum(values * w_value[...].astype(F32), axis=1, keepdims=True)
    total = total + jnp.sum(queries * w_query[...].astype(F32) + keys * w_key[...].astype(F32), axis=1, keepdims=True)
    spread = jnp.broadcast_to(total, (total.shape[0], total.shape[0]))
    diagonal = lax.broadcasted_iota(jnp.int32, spread.shape, 0) == lax.broadcasted_iota(jnp.int32, spread.shape, 1)
    row = jnp.sum(jnp.where(diagonal, spread, 0.0), axis=0, keepdims=True)
    gain_out[...] = row / block_columns(gain, where[1], gain_out.shape[1])


def whole(array):
    return pl.BlockSpec(array.shape, lambda *_: (0,) * len(array.shape))


SMEM = pl.BlockSpec(memory_space=pltpu.SMEM)


def shape_of(*args):
    return jax.ShapeDtypeStruct(args[:-1], args[-1])


def params():
    return pltpu.CompilerParams(vmem_limit_bytes=VMEM_LIMIT)


def cost(flops, moved):
    return pl.CostEstimate(flops=flops, bytes_accessed=moved, transcendentals=0)


def call(kernel, name, scalars, arrays, shapes, flops, grid=1, specs=None, out_specs=None, scratch=(), **fixed):
    specs, out_specs = specs or {}, out_specs or {}
    moved = sum(a.size * a.dtype.itemsize for a in (*arrays, *shapes))
    return pl.pallas_call(
        functools.partial(kernel, **fixed) if fixed else kernel,
        grid_spec=pltpu.PrefetchScalarGridSpec(
            num_scalar_prefetch=1,
            grid=(grid,),
            in_specs=[specs.get(i, whole(a)) for i, a in enumerate(arrays)],
            out_specs=[out_specs.get(i, whole(s)) for i, s in enumerate(shapes)],
            scratch_shapes=list(scratch),
        ),
        out_shape=list(shapes),
        compiler_params=params(),
        cost_estimate=cost(flops, moved),
        name=name,
    )(scalars, *arrays)


def local(
    tokens, gain_one, w_query, w_key, w_value, w_out, gain_two, w_gate, w_up, w_down, lengths, cotangent
):
    rows, width = tokens.shape
    share, groups = lax.axis_size("feat"), lax.axis_size("dp")
    feat, group = lax.axis_index("feat"), lax.axis_index("dp")
    hq, hv = w_query.shape[1] // share, w_value.shape[1] // share
    hidden = w_gate.shape[1]
    chunk = width // groups
    half = rows // 2
    pack = hv + 2 * hq
    heads = hq // QK
    where = jnp.stack([feat, group]).astype(jnp.int32)
    w_gate, w_up = w_gate.T, w_up.T
    gain_a, gain_b = gain_one[None, :], gain_two[None, :]

    def swap(array, axis, mask):
        count = share if axis == "feat" else groups
        return lax.ppermute(array, axis, [(i, i ^ mask) for i in range(count)])

    def masks_of(count):
        found, mask = [], 1
        while mask < count:
            found.append(mask)
            mask *= 2
        return found

    feat_masks = masks_of(share)[::-1]
    dp_masks = masks_of(groups)
    x_first = dp_masks
    z_first = dp_masks[1:] + dp_masks[:1]

    def gather_feat(own):
        held = {0: own}
        for mask in feat_masks:
            for j in list(held):
                held[j ^ mask] = swap(held[j], "feat", mask)
        return [held[j] for j in range(share)]

    def sum_feat(away, own):
        total = (own.astype(F32) + swap(away, "feat", 1).astype(F32)).astype(BF16)
        for mask in feat_masks[:-1]:
            total = (total.astype(F32) + swap(total, "feat", mask).astype(F32)).astype(BF16)
        return total

    def finish(keep, away, hops):
        for mask in hops:
            total = keep + swap(away, "dp", mask).astype(F32)
            count = total.shape[0] // 2
            keep, away = (total[:count], total[count:].astype(BF16)) if count else (total, None)
        return total[0]

    def reduce_dp(kinds, name, arrays, block, flops, order):
        away_kernel, keep_kernel = kinds
        count = groups // 2
        fixed = dict(order=tuple(order), chunk=chunk)
        [away] = call(
            away_kernel, name + "_away", where, arrays, [shape_of(count, *block, BF16)], flops, **fixed
        )
        arrived = swap(away, "dp", order[0])
        keep, away = call(
            keep_kernel,
            name + "_keep",
            where,
            [*arrays, arrived],
            [shape_of(count // 2, *block, F32), shape_of(count // 2, *block, BF16)],
            flops,
            **fixed,
        )
        return finish(keep, away, order[1:])

    columns = (columns_away_kernel, columns_keep_kernel)

    normed, r_one, q, k, v, ctx, exact, den = call(
        attend_kernel,
        "attend",
        where,
        [lengths, tokens, gain_a, w_query, w_key, w_value],
        [
            shape_of(rows, width, BF16),
            shape_of(rows, 1, F32),
            shape_of(rows, hq, BF16),
            shape_of(rows, hq, BF16),
            shape_of(rows, hv, BF16),
            shape_of(rows, hv, BF16),
            shape_of(rows, hv, F32),
            shape_of(rows, hv, F32),
        ],
        2 * rows * width * pack + heads * 6 * rows * rows * 256,
        specs={0: SMEM, 5: pl.BlockSpec((width, hv), lambda i, p: (0, p[0]))},
    )

    ctx_all = gather_feat(ctx)

    def by_half(array):
        return pl.BlockSpec(
            (half,) + array.shape[1:], lambda i, p: (jnp.where(i == 0, 1 - (p[0] & 1), p[0] & 1), 0)
        )

    feed_in = [lengths, *ctx_all, tokens, cotangent, gain_b, w_out, w_gate, w_up, w_down]
    feed_shapes = [
        shape_of(rows, width, F32),
        shape_of(rows, 1, F32),
        shape_of(rows, width, BF16),
        shape_of(rows, hidden, BF16),
        shape_of(rows, hidden, BF16),
        shape_of(rows, hidden, BF16),
        shape_of(half, width, BF16),
        shape_of(half, width, BF16),
    ]
    residual, r_two, normed_two, inner, grad_gate, grad_up, back_away, back_own = call(
        feed_kernel,
        "feed",
        where,
        feed_in,
        feed_shapes,
        2 * rows * width * (width + 5 * hidden),
        grid=2,
        specs={0: SMEM, **{i: by_half(feed_in[i]) for i in range(1, share + 3)}},
        out_specs={i: by_half(feed_shapes[i]) for i in range(6)},
        share=share,
    )

    back_own = sum_feat(back_away, back_own)
    back_other = swap(back_own, "feat", 1)

    hidden_flops = rows * width * hidden
    sum_gate = reduce_dp(columns, "gate", [grad_gate, normed_two], (hidden, chunk), hidden_flops, x_first)
    sum_down = reduce_dp(columns, "down", [inner, cotangent], (hidden, chunk), hidden_flops, z_first)
    sum_up = reduce_dp(columns, "up", [grad_up, normed_two], (hidden, chunk), hidden_flops, x_first)

    feed_own = sum_feat(
        *call(
            down_kernel,
            "down",
            where,
            [inner, w_down],
            [shape_of(half, width, BF16)] * 2,
            2 * hidden_flops,
        )
    )
    core_start = (feat & 1) * half
    out_own = (lax.dynamic_slice_in_dim(residual, core_start, half, 0) + feed_own.astype(F32)).astype(BF16)
    out_other = swap(out_own, "feat", 1)
    output = jnp.concatenate(absolute_order([out_own, out_other], feat & 1), axis=0)

    grad_res, grad_mixed, grads, gain_part = call(
        back_kernel,
        "back",
        where,
        [lengths, back_own, back_other, residual, r_two, cotangent, gain_b, w_out, q, k, v, exact, den],
        [
            shape_of(rows, width, F32),
            shape_of(rows, width, BF16),
            shape_of(rows, pack, BF16),
            shape_of(1, width, F32),
        ],
        2 * rows * width * hv + heads * 10 * rows * rows * 256,
        specs={0: SMEM, 7: pl.BlockSpec((hv, width), lambda i, p: (p[0], 0))},
        scratch=[pltpu.VMEM((rows, hv), BF16)],
    )

    sum_own = reduce_dp(
        (rows_away_kernel, rows_keep_kernel), "own", [normed, grads], (chunk, pack), rows * width * pack, x_first
    ).astype(BF16)
    sum_out = reduce_dp(
        (out_away_kernel, out_keep_kernel),
        "out",
        [ctx, grad_mixed, gain_part],
        (hv + 16, chunk),
        rows * width * hv,
        z_first,
    )

    grads_all = gather_feat(grads)
    in_args = [*grads_all, grad_res, tokens, r_one, gain_a, w_query, w_key, w_value]

    def by_rows(array):
        return pl.BlockSpec((half,) + array.shape[1:], lambda i, p: (i, 0))

    [grad_input] = call(
        input_kernel,
        "grad_input",
        where,
        in_args,
        [shape_of(rows, width, BF16)],
        2 * rows * width * pack * share,
        grid=2,
        specs={i: by_rows(in_args[i]) for i in range(share + 3)},
        out_specs={0: pl.BlockSpec((half, width), lambda i, p: (i, 0))},
        share=share,
        hv=hv,
        hq=hq,
    )

    def own_rows(array):
        return pl.BlockSpec((chunk, array.shape[1]), lambda i, p: (p[1], 0))

    sum_query, sum_key, sum_value, sum_gain_one = call(
        finish_kernel,
        "finish",
        where,
        [*gather_feat(sum_own), gain_a, w_query, w_key, w_value],
        [
            shape_of(chunk, hq * share, F32),
            shape_of(chunk, hq * share, F32),
            shape_of(chunk, hv * share, F32),
            shape_of(1, chunk, F32),
        ],
        chunk * pack * share,
        specs={
            share + 1: own_rows(w_query),
            share + 2: own_rows(w_key),
            share + 3: own_rows(w_value),
        },
        share=share,
        hv=hv,
        hq=hq,
    )

    return (
        output,
        grad_input,
        sum_gain_one[0],
        sum_query,
        sum_key,
        sum_value,
        sum_out[:hv],
        sum_out[hv],
        sum_gate.T,
        sum_up.T,
        sum_down,
    )


def solution(mesh):
    in_specs = (
        P("dp", None),
        P(),
        P(),
        P(),
        P(),
        P(),
        P(),
        P(None, "feat"),
        P(None, "feat"),
        P("feat", None),
        P("dp", None),
        P("dp", None),
    )
    out_specs = (
        P("dp", None),
        P("dp", None),
        P("dp"),
        P("dp", None),
        P("dp", None),
        P("dp", None),
        P("feat", "dp"),
        P("dp"),
        P("dp", "feat"),
        P("dp", "feat"),
        P("feat", "dp"),
    )
    return jax.shard_map(local, mesh=mesh, in_specs=in_specs, out_specs=out_specs, check_vma=False)
```

time: 233 us -> 149 us (0.64); the launches traced: 229 us -> 149 us
  local copies, waits for them, and re-layouts: 87.6 us -> 10.8 us
  Pallas kernels: 25.5 us -> 49.9 us
  matrix products: 22.9 us -> 0 us
  other arithmetic: 22.3 us -> 8.67 us
  waiting for transfers between devices: 37.4 us -> 49.1 us
    dynamic_slice x17 -> x0, local copies, waits for them, and re-layouts: 28 us -> none  [the longest x12 21.7 us: side(): return lax.dynamic_index_in_dim(array, bit, axis, keepdims=False)]
    unnamed x114 -> x68, local copies, waits for them, and re-layouts: 36 us -> 9.5 us
    pallas_call x4 -> x16, Pallas kernels: 25.5 us -> 49.9 us  [call(): pl.pallas_call(functools.partial(kernel, **fixed) if fixed else kernel, g...]
    dot_general x11 -> x0, matrix products: 22.9 us -> none  [the longest x10 20.9 us: dot_tn(): lax.dot_general(a, b, (((0,), (0,)), ((), ())), preferred_element_type=F32)]
    reshape x10 -> x0, local copies, waits for them, and re-layouts: 22.3 us -> none  [the longest x4 9.13 us: bit_axes(): array.reshape(lead + (2,) * len(masks) + (array.shape[-1] // 2 ** len(mas...]
    ppermute x33 -> x30, waiting for transfers between devices: 37.4 us -> 49.1 us  [swap(): return lax.ppermute(array, axis, [(i, i ^ mask) for i in range(count)])]
    add x12 -> x6, other arithmetic: 5.72 us -> 0.3 us  [finish(): total = keep + swap(away, 'dp', mask).astype(F32)]
    reduce_sum x4 -> x0, other arithmetic: 4.19 us -> none  [the longest x3 3.34 us: local(): jnp.sum(own_chunk(w).astype(F32) * s, axis=1)]
  transfers between devices with their start and end apart: 33 -> 30, of which waited for: 10 -> 12; matrix products, arithmetic and copies ran while one was open for 49% -> 7% of each run, Pallas kernels for 5% -> 21%
where the time goes in v3:
time: 149 us
  Pallas kernels  49.9 us (33%)
  waiting for transfers between devices  49.1 us (33%)
  starting transfers between devices  29.3 us (20%)
  local copies, waits for them, and re-layouts  10.8 us (7%)
  other arithmetic  8.67 us (6%)
    pallas_call x16, Pallas kernels, call(): pl.pallas_call(functools.partial(kernel, **fixed) if fixed else kernel, g...  49.9 us
    ppermute x30, waiting for transfers between devices, swap(): return lax.ppermute(array, axis, [(i, i ^ mask) for i in range(count)])  49.1 us
    ppermute x30, starting transfers between devices, swap(): return lax.ppermute(array, axis, [(i, i ^ mask) for i in range(count)])  29.3 us
    unnamed x68, local copies, waits for them, and re-layouts  9.5 us
  transfers between devices with their start and end apart: 30, of which 12 were waited for; matrix products, arithmetic and copies ran while one was open for 7% of the time, Pallas kernels for 21%

profile of v3, /device:TPU:0, one launch (start us, length us, event | category | flops | bytes accessed | tf_op | source)
XLA Modules:
  0.0 148.8 jit_solution(17849000492671172469)
XLA Ops:
  0.7 1.0 copy-done.8
  1.8 1.0 copy-done.10
  2.8 1.2 copy-done.13
  5.4 4.9 %attend.1 = (bf16[512,1024]{1,0:T(8,128)(2,1)S(1)}, f32[512,1]{1,0:T(8,128)S(1)}, bf16[512,64]{1,0:T(8,128)(2,1)S(1)}, bf16[512,64]{1,0:T(8,128)(2,1)S(1)}, bf16...) custom-call(s32[2]{0:T(128)S(1)} %pad_add_fusion.place.where, ...), custom_call_target="tpu_custom_call" | custom-call | flops 2013265920 | bytes 6952976 | tf_op jit(solution)/shard_map/attend/pallas_call | solution.py:368
  13.3 3.0 %collective-permute-start.1 = (bf16[512,256]{1,0:T(8,128)(2,1)S(1)}, bf16[512,256]{1,0:T(8,128)(2,1)S(1)}, u32[]{:S(2)}, u32[]{:S(2)}) collective-permute-start(bf16[512,256]{1,0:T(8,128)(2,1)S(1)} %get-tuple-element.47.refs_1_.left), channel_id=1, source_target_pairs={{0,2},{1,3},{2,0},{3,1},{4,6},{5,7},{6,4},{7,5},{8,10},{9,11},{10,... | collective-permute-start | bytes 786440 | tf_op jit(solution)/shard_map/ppermute | solution.py:402
  16.2 6.3 %collective-permute-done.1.refs_3_ = bf16[512,256]{1,0:T(8,128)(2,1)S(1)} collective-permute-done((bf16[512,256]{1,0:T(8,128)(2,1)S(1)}, bf16[512,256]{1,0:T(8,128)(2,1)S(1)}, u32[]{:S(2)}, u32[]{:S(2)}) %collective-permute-start.1) | collective-permute-done | bytes 262176 | tf_op jit(solution)/shard_map/ppermute | solution.py:402
  22.5 1.5 %collective-permute-done.2.refs_4_ = bf16[512,256]{1,0:T(8,128)(2,1)S(1)} collective-permute-done((bf16[512,256]{1,0:T(8,128)(2,1)S(1)}, bf16[512,256]{1,0:T(8,128)(2,1)S(1)}, u32[]{:S(2)}, u32[]{:S(2)}) %collective-permute-start.2) | collective-permute-done | bytes 262176 | tf_op jit(solution)/shard_map/ppermute | solution.py:402
  24.1 12.6 %feed.1 = (f32[512,1024]{1,0:T(8,128)}, f32[512,1]{1,0:T(8,128)S(1)}, bf16[512,1024]{1,0:T(8,128)(2,1)S(1)}, bf16[512,688]{1,0:T(8,128)(2,1)S(1)}, bf16[512,688]...) custom-call(s32[2]{0:T(128)S(1)} %pad_add_fusion.place.where, ...), custom_call_target="tpu_custom_call" | custom-call | flops 4680843264 | bytes 15783952 | tf_op jit(solution)/shard_map/feed/pallas_call | solution.py:368
  37.5 1.5 %down.1 = (bf16[256,1024]{1,0:T(8,128)(2,1)S(1)}, bf16[256,1024]{1,0:T(8,128)(2,1)S(1)}) custom-call(s32[2]{0:T(128)S(1)} %pad_add_fusion.place.where, bf16[512,688]{1,0:T(8,128)(2,1)S(1)} %get-tuple-element.49.inner.left, bf16[688,1024]{1,0:T(8,128)(2,1)S(1)} %copy-done.19), custom_call_target="tpu_custom_call" | custom-call | flops 721420288 | bytes 3162112 | tf_op jit(solution)/shard_map/down/pallas_call | solution.py:368
  39.5 2.0 %down_away.1 = bf16[4,688,128]{2,1,0:T(8,128)(2,1)} custom-call(s32[2]{0:T(128)S(1)} %pad_add_fusion.place.where, bf16[512,688]{1,0:T(8,128)(2,1)S(1)} %get-tuple-element.49.inner.left, bf16[512,1024]{1,0:T(8,128)(2,1)S(1)} %copy-done.1), custom_call_target="tpu_custom_call" | custom-call | flops 360710144 | bytes 2457600 | tf_op jit(solution)/shard_map/down_away/pallas_call | solution.py:368
  41.6 1.8 %collective-permute-start.27 = (bf16[4,688,128]{2,1,0:T(8,128)(2,1)}, bf16[4,688,128]{2,1,0:T(8,128)(2,1)}, u32[]{:S(2)}, u32[]{:S(2)}) collective-permute-start(bf16[4,688,128]{2,1,0:T(8,128)(2,1)} %down_away.1), channel_id=1, source_target_pairs={{0,8},{4,12},{8,0},{12,4},{16,24},{20,28},{24,16},{28,20},{1,9},{5... | collective-permute-start | bytes 2113544 | tf_op jit(solution)/shard_map/ppermute | solution.py:402
  43.4 2.1 %up_away.1 = bf16[4,688,128]{2,1,0:T(8,128)(2,1)} custom-call(s32[2]{0:T(128)S(1)} %pad_add_fusion.place.where, bf16[512,688]{1,0:T(8,128)(2,1)S(1)} %get-tuple-element.78.left, bf16[512,1024]{1,0:T(8,128)(2,1)S(1)} %get-tuple-element.75.right), custom_call_target="tpu_custom_call" | custom-call | flops 360710144 | bytes 2457600 | tf_op jit(solution)/shard_map/up_away/pallas_call | solution.py:368
  45.4 1.5 collective-permute-start.24
  46.9 2.0 %gate_away.1 = bf16[4,688,128]{2,1,0:T(8,128)(2,1)} custom-call(s32[2]{0:T(128)S(1)} %pad_add_fusion.place.where, bf16[512,688]{1,0:T(8,128)(2,1)S(1)} %get-tuple-element.74.left, bf16[512,1024]{1,0:T(8,128)(2,1)S(1)} %get-tuple-element.75.right), custom_call_target="tpu_custom_call" | custom-call | flops 360710144 | bytes 2457600 | tf_op jit(solution)/shard_map/gate_away/pallas_call | solution.py:368
  49.5 1.0 add_convert_fusion.1
  50.5 1.5 %collective-permute-start.7 = (bf16[256,1024]{1,0:T(8,128)(2,1)}, bf16[256,1024]{1,0:T(8,128)(2,1)}, u32[]{:S(2)}, u32[]{:S(2)}) collective-permute-start(bf16[256,1024]{1,0:T(8,128)(2,1)} %add_convert_fusion.1), channel_id=1, source_target_pairs={{0,2},{1,3},{2,0},{3,1},{4,6},{5,7},{6,4},{7,5},{8,10},{9,11},{10,... | collective-permute-start | bytes 1572872 | tf_op jit(solution)/shard_map/ppermute | solution.py:402
  52.0 1.0 add_convert_fusion.4
  53.5 6.2 %collective-permute-done.27.arrived = bf16[4,688,128]{2,1,0:T(8,128)(2,1)} collective-permute-done((bf16[4,688,128]{2,1,0:T(8,128)(2,1)}, bf16[4,688,128]{2,1,0:T(8,128)(2,1)}, u32[]{:S(2)}, u32[]{:S(2)}) %collective-permute-start.27) | collective-permute-done | bytes 704544 | tf_op jit(solution)/shard_map/ppermute | solution.py:402
  59.7 1.1 copy-done.7
  60.9 2.2 %down_keep.1 = (f32[2,688,128]{2,1,0:T(8,128)S(1)}, bf16[2,688,128]{2,1,0:T(8,128)(2,1)S(1)}) custom-call(s32[2]{0:T(128)S(1)} %pad_add_fusion.place.where, bf16[512,688]{1,0:T(8,128)(2,1)S(1)} %copy-done.7, bf16[512,1024]{1,0:T(8,128)(2,1)S(1)} %copy-done.1, bf16[4,688,128]{2,1,0:T(8,128)(2,1)} %collective-permute-done.27.arrived), custom_call_target="tpu_custom_call" | custom-call | flops 360710144 | bytes 3514368 | tf_op jit(solution)/shard_map/down_keep/pallas_call | solution.py:368
  63.1 2.8 %collective-permute-start.28 = (bf16[2,688,128]{2,1,0:T(8,128)(2,1)S(1)}, bf16[2,688,128]{2,1,0:T(8,128)(2,1)S(1)}, u32[]{:S(2)}, u32[]{:S(2)}) collective-permute-start(bf16[2,688,128]{2,1,0:T(8,128)(2,1)S(1)} %get-tuple-element.82), channel_id=1, source_target_pairs={{0,16},{4,20},{8,24},{12,28},{16,0},{20,4},{24,8},{28,12},{1,17},{... | collective-permute-start | bytes 1056776 | tf_op jit(solution)/shard_map/ppermute | solution.py:402
  66.0 2.2 %up_keep.1 = (f32[2,688,128]{2,1,0:T(8,128)S(1)}, bf16[2,688,128]{2,1,0:T(8,128)(2,1)S(1)}) custom-call(s32[2]{0:T(128)S(1)} %pad_add_fusion.place.where, bf16[512,688]{1,0:T(8,128)(2,1)S(1)} %copy-done.5, bf16[512,1024]{1,0:T(8,128)(2,1)S(1)} %get-tuple-element.75.right, bf16[4,688,128]{2,1,0:T(8,128)(2,1)} %collective-permute-done.24.arrived), custom_call_target="tpu_custom_call" | custom-call | flops 360710144 | bytes 3514368 | tf_op jit(solution)/shard_map/up_keep/pallas_call | solution.py:368
  68.2 1.7 %collective-permute-start.25 = (bf16[2,688,128]{2,1,0:T(8,128)(2,1)S(1)}, bf16[2,688,128]{2,1,0:T(8,128)(2,1)S(1)}, u32[]{:S(2)}, u32[]{:S(2)}) collective-permute-start(bf16[2,688,128]{2,1,0:T(8,128)(2,1)S(1)} %get-tuple-element.80), channel_id=1, source_target_pairs={{0,8},{4,12},{8,0},{12,4},{16,24},{20,28},{24,16},{28,20},{1,9},{5... | collective-permute-start | bytes 1056776 | tf_op jit(solution)/shard_map/ppermute | solution.py:402
  69.9 8.5 %collective-permute-done.21.arrived = bf16[4,688,128]{2,1,0:T(8,128)(2,1)} collective-permute-done((bf16[4,688,128]{2,1,0:T(8,128)(2,1)}, bf16[4,688,128]{2,1,0:T(8,128)(2,1)}, u32[]{:S(2)}, u32[]{:S(2)}) %collective-permute-start.21) | collective-permute-done | bytes 704544 | tf_op jit(solution)/shard_map/ppermute | solution.py:402
  78.4 2.2 %gate_keep.1 = (f32[2,688,128]{2,1,0:T(8,128)S(1)}, bf16[2,688,128]{2,1,0:T(8,128)(2,1)S(1)}) custom-call(s32[2]{0:T(128)S(1)} %pad_add_fusion.place.where, bf16[512,688]{1,0:T(8,128)(2,1)S(1)} %copy-done.3, bf16[512,1024]{1,0:T(8,128)(2,1)S(1)} %get-tuple-element.75.right, bf16[4,688,128]{2,1,0:T(8,128)(2,1)} %collective-permute-done.21.arrived), custom_call_target="tpu_custom_call" | custom-call | flops 360710144 | bytes 3514368 | tf_op jit(solution)/shard_map/gate_keep/pallas_call | solution.py:368
  81.0 1.4 add_convert_fusion.own
  82.5 1.5 add_convert_fusion.2
  84.6 1.7 %collective-permute-start.29 = (bf16[1,688,128]{2,1,0:T(8,128)(2,1)S(1)}, bf16[1,688,128]{2,1,0:T(8,128)(2,1)S(1)}, u32[]{:S(2)}, u32[]{:S(2)}) collective-permute-start(bf16[1,688,128]{2,1,0:T(8,128)(2,1)S(1)} %slice.92), channel_id=1, source_target_pairs={{0,4},{4,0},{8,12},{12,8},{16,20},{20,16},{24,28},{28,24},{1,5},{5... | collective-permute-start | bytes 528392 | tf_op jit(solution)/shard_map/ppermute | solution.py:402
  86.5 2.7 %collective-permute-start.26 = (bf16[1,688,128]{2,1,0:T(8,128)(2,1)S(1)}, bf16[1,688,128]{2,1,0:T(8,128)(2,1)S(1)}, u32[]{:S(2)}, u32[]{:S(2)}) collective-permute-start(bf16[1,688,128]{2,1,0:T(8,128)(2,1)S(1)} %slice.93), channel_id=1, source_target_pairs={{0,16},{4,20},{8,24},{12,28},{16,0},{20,4},{24,8},{28,12},{1,17},{... | collective-permute-start | bytes 528392 | tf_op jit(solution)/shard_map/ppermute | solution.py:402
  89.2 4.2 %collective-permute-done.22 = bf16[2,688,128]{2,1,0:T(8,128)(2,1)S(1)} collective-permute-done((bf16[2,688,128]{2,1,0:T(8,128)(2,1)S(1)}, bf16[2,688,128]{2,1,0:T(8,128)(2,1)S(1)}, u32[]{:S(2)}, u32[]{:S(2)}) %collective-permute-start.22) | collective-permute-done | bytes 352288 | tf_op jit(solution)/shard_map/ppermute | solution.py:402
  94.3 6.8 %back.1 = (f32[512,1024]{1,0:T(8,128)}, bf16[512,1024]{1,0:T(8,128)(2,1)S(1)}, bf16[512,384]{1,0:T(8,128)(2,1)S(1)}, f32[1,1024]{1,0:T(1,128)S(1)}) custom-call(s32[2]{0:T(128)S(1)} %pad_add_fusion.place.where, s32[1,4]{1,0:T(1,128)S(1)} %copy-done.22, bf16[256,1024]{1,0:T(8,128)(2,1)S(1)} %add_convert_fusion.own, ...), custom_call_target="tpu_custom_call" | custom-call | flops 2952790016 | bytes 11282448 | tf_op jit(solution)/shard_map/back/pallas_call | solution.py:368
  102.1 1.1 collective-permute-start.18
  103.9 1.2 collective-permute-done.23
  105.8 1.5 %collective-permute-start.10 = (bf16[512,384]{1,0:T(8,128)(2,1)S(1)}, bf16[512,384]{1,0:T(8,128)(2,1)S(1)}, u32[]{:S(2)}, u32[]{:S(2)}) collective-permute-start(bf16[512,384]{1,0:T(8,128)(2,1)S(1)} %get-tuple-element.60.refs_0_.right), channel_id=1, source_target_pairs={{0,2},{1,3},{2,0},{3,1},{4,6},{5,7},{6,4},{7,5},{8,10},{9,11},{10,... | collective-permute-start | bytes 1179656 | tf_op jit(solution)/shard_map/ppermute | solution.py:402
  107.4 1.0 own_away.1
  108.9 2.0 %collective-permute-done.18.arrived = bf16[4,272,128]{2,1,0:T(8,128)(2,1)S(1)} collective-permute-done((bf16[4,272,128]{2,1,0:T(8,128)(2,1)S(1)}, bf16[4,272,128]{2,1,0:T(8,128)(2,1)S(1)}, u32[]{:S(2)}, u32[]{:S(2)}) %collective-permute-start.18) | collective-permute-done | bytes 278560 | tf_op jit(solution)/shard_map/ppermute | solution.py:402
  111.8 1.6 %collective-permute-start.19 = (bf16[2,272,128]{2,1,0:T(8,128)(2,1)S(1)}, bf16[2,272,128]{2,1,0:T(8,128)(2,1)S(1)}, u32[]{:S(2)}, u32[]{:S(2)}) collective-permute-start(bf16[2,272,128]{2,1,0:T(8,128)(2,1)S(1)} %get-tuple-element.73), channel_id=1, source_target_pairs={{0,16},{4,20},{8,24},{12,28},{16,0},{20,4},{24,8},{28,12},{1,17},{... | collective-permute-start | bytes 417800 | tf_op jit(solution)/shard_map/ppermute | solution.py:402
  113.5 7.2 %collective-permute-done.19 = bf16[2,272,128]{2,1,0:T(8,128)(2,1)S(1)} collective-permute-done((bf16[2,272,128]{2,1,0:T(8,128)(2,1)S(1)}, bf16[2,272,128]{2,1,0:T(8,128)(2,1)S(1)}, u32[]{:S(2)}, u32[]{:S(2)}) %collective-permute-start.19) | collective-permute-done | bytes 139296 | tf_op jit(solution)/shard_map/ppermute | solution.py:402
  121.5 1.0 pad_maximum_fusion
  122.5 1.0 own_keep.1
  123.7 1.6 %collective-permute-done.20 = bf16[1,272,128]{2,1,0:T(8,128)(2,1)S(1)} collective-permute-done((bf16[1,272,128]{2,1,0:T(8,128)(2,1)S(1)}, bf16[1,272,128]{2,1,0:T(8,128)(2,1)S(1)}, u32[]{:S(2)}, u32[]{:S(2)}) %collective-permute-start.20) | collective-permute-done | bytes 69664 | tf_op jit(solution)/shard_map/ppermute | solution.py:402
  125.4 3.9 %collective-permute-done.13 = bf16[2,128,384]{2,1,0:T(8,128)(2,1)S(1)} collective-permute-done((bf16[2,128,384]{2,1,0:T(8,128)(2,1)S(1)}, bf16[2,128,384]{2,1,0:T(8,128)(2,1)S(1)}, u32[]{:S(2)}, u32[]{:S(2)}) %collective-permute-start.13) | collective-permute-done | bytes 196640 | tf_op jit(solution)/shard_map/ppermute | solution.py:402
  129.4 2.7 %collective-permute-start.14 = (bf16[1,128,384]{2,1,0:T(8,128)(2,1)S(1)}, bf16[1,128,384]{2,1,0:T(8,128)(2,1)S(1)}, u32[]{:S(2)}, u32[]{:S(2)}) collective-permute-start(bf16[1,128,384]{2,1,0:T(8,128)(2,1)S(1)} %slice.95), channel_id=1, source_target_pairs={{0,16},{4,20},{8,24},{12,28},{16,0},{20,4},{24,8},{28,12},{1,17},{... | collective-permute-start | bytes 294920 | tf_op jit(solution)/shard_map/ppermute | solution.py:402
  132.8 3.9 %collective-permute-done.14 = bf16[1,128,384]{2,1,0:T(8,128)(2,1)S(1)} collective-permute-done((bf16[1,128,384]{2,1,0:T(8,128)(2,1)S(1)}, bf16[1,128,384]{2,1,0:T(8,128)(2,1)S(1)}, u32[]{:S(2)}, u32[]{:S(2)}) %collective-permute-start.14) | collective-permute-done | bytes 98336 | tf_op jit(solution)/shard_map/ppermute | solution.py:402
  136.7 1.6 %collective-permute-start.16 = (bf16[128,384]{1,0:T(8,128)(2,1)S(1)}, bf16[128,384]{1,0:T(8,128)(2,1)S(1)}, u32[]{:S(2)}, u32[]{:S(2)}) collective-permute-start(bf16[128,384]{1,0:T(8,128)(2,1)S(1)} %fusion.4.refs_0_), channel_id=1, source_target_pairs={{0,2},{1,3},{2,0},{3,1},{4,6},{5,7},{6,4},{7,5},{8,10},{9,11},{10,... | collective-permute-start | bytes 294920 | tf_op jit(solution)/shard_map/ppermute | solution.py:402
  138.8 2.6 %collective-permute-done.16.refs_2_ = bf16[128,384]{1,0:T(8,128)(2,1)S(1)} collective-permute-done((bf16[128,384]{1,0:T(8,128)(2,1)S(1)}, bf16[128,384]{1,0:T(8,128)(2,1)S(1)}, u32[]{:S(2)}, u32[]{:S(2)}) %collective-permute-start.16) | collective-permute-done | bytes 98336 | tf_op jit(solution)/shard_map/ppermute | solution.py:402
  141.5 5.8 %grad_input.1 = bf16[512,1024]{1,0:T(8,128)(2,1)} custom-call(s32[2]{0:T(128)S(1)} %pad_add_fusion.place.where, bf16[512,384]{1,0:T(8,128)(2,1)S(1)} %get-tuple-element.60.refs_0_.right, bf16[512,384]{1,0:T(8,128)(2,1)S(1)} %collective-permute-done.9.refs_1_, bf16[512,384]{1,0:T(8,128)(2,1)S(1)} %collective-permute-done.10.refs_2_, ...), custom_call_target="tpu_custom_call" | custom-call | flops 1610612736 | bytes 8919040 | tf_op jit(solution)/shard_map/grad_input/pallas_call | solution.py:368
  147.2 1.6 %finish.1 = (f32[128,256]{1,0:T(8,128)}, f32[128,256]{1,0:T(8,128)}, f32[128,1024]{1,0:T(8,128)}, f32[1,128]{1,0:T(1,128)}) custom-call(s32[2]{0:T(128)S(1)} %pad_add_fusion.place.where, bf16[128,384]{1,0:T(8,128)(2,1)S(1)} %fusion.4.refs_0_, bf16[128,384]{1,0:T(8,128)(2,1)S(1)} %collective-permute-done.15.refs_1_, ...), custom_call_target="tpu_custom_call" | custom-call | flops 196608 | bytes 4329984 | tf_op jit(solution)/shard_map/finish/pallas_call | solution.py:368
  (120 shorter events, 15.1 us)
Async XLA Ops:
  5.4 18.7 %copy-start.20 = (f32[1024]{0:T(1024)S(1)}, f32[1024]{0:T(1024)}, u32[]{:S(2)}) copy-start(f32[1024]{0:T(1024)} %param.18) | copy-start | bytes 12292
  13.3 23.4 %copy-start.25 = (f32[512,256]{1,0:T(8,128)}, f32[512,256]{1,0:T(8,128)S(1)}, u32[]{:S(2)}) copy-start(f32[512,256]{1,0:T(8,128)S(1)} %get-tuple-element.59.den_in) | copy-start | bytes 1572868
  13.3 9.3 %collective-permute-start.1 = (bf16[512,256]{1,0:T(8,128)(2,1)S(1)}, bf16[512,256]{1,0:T(8,128)(2,1)S(1)}, u32[]{:S(2)}, u32[]{:S(2)}) collective-permute-start(bf16[512,256]{1,0:T(8,128)(2,1)S(1)} %get-tuple-element.47.refs_1_.left), channel_id=1, source_target_pairs={{0,2},{1,3},{2,0},{3,1},{4,6},{5,7},{6,4},{7,5},{8,10},{9,11},{10,... | collective-permute-start | bytes 786440 | tf_op jit(solution)/shard_map/ppermute | solution.py:402
  16.2 6.3 %collective-permute-start = (bf16[512,256]{1,0:T(8,128)(2,1)S(1)}, bf16[512,256]{1,0:T(8,128)(2,1)S(1)}, u32[]{:S(2)}, u32[]{:S(2)}) collective-permute-start(bf16[512,256]{1,0:T(8,128)(2,1)S(1)} %get-tuple-element.47.refs_1_.left), channel_id=1, source_target_pairs={{0,1},{1,0},{2,3},{3,2},{4,5},{5,4},{6,7},{7,6},{8,9},{9,8},{10,11... | collective-permute-start | bytes 786440 | tf_op jit(solution)/shard_map/ppermute | solution.py:402
  22.5 1.5 %collective-permute-start.2 = (bf16[512,256]{1,0:T(8,128)(2,1)S(1)}, bf16[512,256]{1,0:T(8,128)(2,1)S(1)}, u32[]{:S(2)}, u32[]{:S(2)}) collective-permute-start(bf16[512,256]{1,0:T(8,128)(2,1)S(1)} %collective-permute-done.1.refs_3_), channel_id=1, source_target_pairs={{0,1},{1,0},{2,3},{3,2},{4,5},{5,4},{6,7},{7,6},{8,9},{9,8},{10,11... | collective-permute-start | bytes 786440 | tf_op jit(solution)/shard_map/ppermute | solution.py:402
  24.1 13.5 %copy-start.19 = (bf16[688,1024]{1,0:T(8,128)(2,1)S(1)}, bf16[688,1024]{1,0:T(8,128)(2,1)}, u32[]{:S(2)}) copy-start(bf16[688,1024]{1,0:T(8,128)(2,1)} %w_down.1) | copy-start | bytes 4227076
  37.3 9.5 %copy-start.2 = (bf16[512,688]{1,0:T(8,128)(2,1)}, bf16[512,688]{1,0:T(8,128)(2,1)S(1)}, u32[]{:S(2)}) copy-start(bf16[512,688]{1,0:T(8,128)(2,1)S(1)} %get-tuple-element.74.left) | copy-start | bytes 2113540
  37.4 12.1 %collective-permute-start.6 = (bf16[256,1024]{1,0:T(8,128)(2,1)S(1)}, bf16[256,1024]{1,0:T(8,128)(2,1)S(1)}, u32[]{:S(2)}, u32[]{:S(2)}) collective-permute-start(bf16[256,1024]{1,0:T(8,128)(2,1)S(1)} %get-tuple-element.53), channel_id=1, source_target_pairs={{0,1},{1,0},{2,3},{3,2},{4,5},{5,4},{6,7},{7,6},{8,9},{9,8},{10,11... | collective-permute-start | bytes 1572872 | tf_op jit(solution)/shard_map/ppermute | solution.py:402
  39.0 13.0 %collective-permute-start.3 = (bf16[256,1024]{1,0:T(8,128)(2,1)S(1)}, bf16[256,1024]{1,0:T(8,128)(2,1)S(1)}, u32[]{:S(2)}, u32[]{:S(2)}) collective-permute-start(bf16[256,1024]{1,0:T(8,128)(2,1)S(1)} %get-tuple-element.51), channel_id=1, source_target_pairs={{0,1},{1,0},{2,3},{3,2},{4,5},{5,4},{6,7},{7,6},{8,9},{9,8},{10,11... | collective-permute-start | bytes 1572872 | tf_op jit(solution)/shard_map/ppermute | solution.py:402
  41.6 18.2 %collective-permute-start.27 = (bf16[4,688,128]{2,1,0:T(8,128)(2,1)}, bf16[4,688,128]{2,1,0:T(8,128)(2,1)}, u32[]{:S(2)}, u32[]{:S(2)}) collective-permute-start(bf16[4,688,128]{2,1,0:T(8,128)(2,1)} %down_away.1), channel_id=1, source_target_pairs={{0,8},{4,12},{8,0},{12,4},{16,24},{20,28},{24,16},{28,20},{1,9},{5... | collective-permute-start | bytes 2113544 | tf_op jit(solution)/shard_map/ppermute | solution.py:402
  45.4 20.5 %collective-permute-start.24 = (bf16[4,688,128]{2,1,0:T(8,128)(2,1)}, bf16[4,688,128]{2,1,0:T(8,128)(2,1)}, u32[]{:S(2)}, u32[]{:S(2)}) collective-permute-start(bf16[4,688,128]{2,1,0:T(8,128)(2,1)} %up_away.1), channel_id=1, source_target_pairs={{0,4},{4,0},{8,12},{12,8},{16,20},{20,16},{24,28},{28,24},{1,5},{5... | collective-permute-start | bytes 2113544 | tf_op jit(solution)/shard_map/ppermute | solution.py:402
  48.9 29.4 %collective-permute-start.21 = (bf16[4,688,128]{2,1,0:T(8,128)(2,1)}, bf16[4,688,128]{2,1,0:T(8,128)(2,1)}, u32[]{:S(2)}, u32[]{:S(2)}) collective-permute-start(bf16[4,688,128]{2,1,0:T(8,128)(2,1)} %gate_away.1), channel_id=1, source_target_pairs={{0,4},{4,0},{8,12},{12,8},{16,20},{20,16},{24,28},{28,24},{1,5},{5... | collective-permute-start | bytes 2113544 | tf_op jit(solution)/shard_map/ppermute | solution.py:402
  50.5 30.5 %collective-permute-start.7 = (bf16[256,1024]{1,0:T(8,128)(2,1)}, bf16[256,1024]{1,0:T(8,128)(2,1)}, u32[]{:S(2)}, u32[]{:S(2)}) collective-permute-start(bf16[256,1024]{1,0:T(8,128)(2,1)} %add_convert_fusion.1), channel_id=1, source_target_pairs={{0,2},{1,3},{2,0},{3,1},{4,6},{5,7},{6,4},{7,5},{8,10},{9,11},{10,... | collective-permute-start | bytes 1572872 | tf_op jit(solution)/shard_map/ppermute | solution.py:402
  53.0 29.5 %collective-permute-start.4 = (bf16[256,1024]{1,0:T(8,128)(2,1)}, bf16[256,1024]{1,0:T(8,128)(2,1)}, u32[]{:S(2)}, u32[]{:S(2)}) collective-permute-start(bf16[256,1024]{1,0:T(8,128)(2,1)} %add_convert_fusion.4), channel_id=1, source_target_pairs={{0,2},{1,3},{2,0},{3,1},{4,6},{5,7},{6,4},{7,5},{8,10},{9,11},{10,... | collective-permute-start | bytes 1572872 | tf_op jit(solution)/shard_map/ppermute | solution.py:402
  53.5 12.5 %copy-start.5 = (bf16[512,688]{1,0:T(8,128)(2,1)S(1)}, bf16[512,688]{1,0:T(8,128)(2,1)}, u32[]{:S(2)}) copy-start(bf16[512,688]{1,0:T(8,128)(2,1)} %copy-done.4) | copy-start | bytes 2113540
  53.5 24.9 %copy-start.3 = (bf16[512,688]{1,0:T(8,128)(2,1)S(1)}, bf16[512,688]{1,0:T(8,128)(2,1)}, u32[]{:S(2)}) copy-start(bf16[512,688]{1,0:T(8,128)(2,1)} %copy-done.2) | copy-start | bytes 2113540
  63.1 21.4 %collective-permute-start.28 = (bf16[2,688,128]{2,1,0:T(8,128)(2,1)S(1)}, bf16[2,688,128]{2,1,0:T(8,128)(2,1)S(1)}, u32[]{:S(2)}, u32[]{:S(2)}) collective-permute-start(bf16[2,688,128]{2,1,0:T(8,128)(2,1)S(1)} %get-tuple-element.82), channel_id=1, source_target_pairs={{0,16},{4,20},{8,24},{12,28},{16,0},{20,4},{24,8},{28,12},{1,17},{... | collective-permute-start | bytes 1056776 | tf_op jit(solution)/shard_map/ppermute | solution.py:402
  68.2 14.3 %copy-start.33 = (f32[512,1024]{1,0:T(8,128)S(1)}, f32[512,1024]{1,0:T(8,128)}, u32[]{:S(2)}) copy-start(f32[512,1024]{1,0:T(8,128)} %get-tuple-element.48.res) | copy-start | bytes 6291460
  68.2 18.1 %collective-permute-start.25 = (bf16[2,688,128]{2,1,0:T(8,128)(2,1)S(1)}, bf16[2,688,128]{2,1,0:T(8,128)(2,1)S(1)}, u32[]{:S(2)}, u32[]{:S(2)}) collective-permute-start(bf16[2,688,128]{2,1,0:T(8,128)(2,1)S(1)} %get-tuple-element.80), channel_id=1, source_target_pairs={{0,8},{4,12},{8,0},{12,4},{16,24},{20,28},{24,16},{28,20},{1,9},{5... | collective-permute-start | bytes 1056776 | tf_op jit(solution)/shard_map/ppermute | solution.py:402
  80.6 12.7 %collective-permute-start.22 = (bf16[2,688,128]{2,1,0:T(8,128)(2,1)S(1)}, bf16[2,688,128]{2,1,0:T(8,128)(2,1)S(1)}, u32[]{:S(2)}, u32[]{:S(2)}) collective-permute-start(bf16[2,688,128]{2,1,0:T(8,128)(2,1)S(1)} %get-tuple-element.77), channel_id=1, source_target_pairs={{0,8},{4,12},{8,0},{12,4},{16,24},{20,28},{24,16},{28,20},{1,9},{5... | collective-permute-start | bytes 1056776 | tf_op jit(solution)/shard_map/ppermute | solution.py:402
  82.4 11.9 %collective-permute-start.8 = (bf16[256,1024]{1,0:T(8,128)(2,1)S(1)}, bf16[256,1024]{1,0:T(8,128)(2,1)S(1)}, u32[]{:S(2)}, u32[]{:S(2)}) collective-permute-start(bf16[256,1024]{1,0:T(8,128)(2,1)S(1)} %add_convert_fusion.own), channel_id=1, source_target_pairs={{0,1},{1,0},{2,3},{3,2},{4,5},{5,4},{6,7},{7,6},{8,9},{9,8},{10,11... | collective-permute-start | bytes 1572872 | tf_op jit(solution)/shard_map/ppermute | solution.py:402
  84.0 29.5 %collective-permute-start.5 = (bf16[256,1024]{1,0:T(8,128)(2,1)S(1)}, bf16[256,1024]{1,0:T(8,128)(2,1)S(1)}, u32[]{:S(2)}, u32[]{:S(2)}) collective-permute-start(bf16[256,1024]{1,0:T(8,128)(2,1)S(1)} %add_convert_fusion.2), channel_id=1, source_target_pairs={{0,1},{1,0},{2,3},{3,2},{4,5},{5,4},{6,7},{7,6},{8,9},{9,8},{10,11... | collective-permute-start | bytes 1572872 | tf_op jit(solution)/shard_map/ppermute | solution.py:402
  84.6 8.9 %collective-permute-start.29 = (bf16[1,688,128]{2,1,0:T(8,128)(2,1)S(1)}, bf16[1,688,128]{2,1,0:T(8,128)(2,1)S(1)}, u32[]{:S(2)}, u32[]{:S(2)}) collective-permute-start(bf16[1,688,128]{2,1,0:T(8,128)(2,1)S(1)} %slice.92), channel_id=1, source_target_pairs={{0,4},{4,0},{8,12},{12,8},{16,20},{20,16},{24,28},{28,24},{1,5},{5... | collective-permute-start | bytes 528392 | tf_op jit(solution)/shard_map/ppermute | solution.py:402
  86.4 7.9 %copy-start.22 = (s32[1,4]{1,0:T(1,128)S(1)}, s32[1,4]{1,0:T(1,128)}, u32[]{:S(2)}) copy-start(s32[1,4]{1,0:T(1,128)} %lengths.3) | copy-start | bytes 52
  86.4 7.9 %copy-start.24 = (f32[512,256]{1,0:T(8,128)S(1)}, f32[512,256]{1,0:T(8,128)}, u32[]{:S(2)}) copy-start(f32[512,256]{1,0:T(8,128)} %copy-done.23) | copy-start | bytes 1572868
  86.4 7.9 %copy-start.26 = (f32[512,256]{1,0:T(8,128)S(1)}, f32[512,256]{1,0:T(8,128)}, u32[]{:S(2)}) copy-start(f32[512,256]{1,0:T(8,128)} %copy-done.25) | copy-start | bytes 1572868
  86.4 7.9 %copy-start.28 = (bf16[512,256]{1,0:T(8,128)(2,1)S(1)}, bf16[512,256]{1,0:T(8,128)(2,1)}, u32[]{:S(2)}) copy-start(bf16[512,256]{1,0:T(8,128)(2,1)} %copy-done.27) | copy-start | bytes 786436
  86.4 7.9 %copy-start.30 = (f32[512,1]{1,0:T(8,128)S(1)}, f32[512,1]{1,0:T(8,128)}, u32[]{:S(2)}) copy-start(f32[512,1]{1,0:T(8,128)} %copy-done.29) | copy-start | bytes 6148
  86.5 16.6 %collective-permute-start.26 = (bf16[1,688,128]{2,1,0:T(8,128)(2,1)S(1)}, bf16[1,688,128]{2,1,0:T(8,128)(2,1)S(1)}, u32[]{:S(2)}, u32[]{:S(2)}) collective-permute-start(bf16[1,688,128]{2,1,0:T(8,128)(2,1)S(1)} %slice.93), channel_id=1, source_target_pairs={{0,16},{4,20},{8,24},{12,28},{16,0},{20,4},{24,8},{28,12},{1,17},{... | collective-permute-start | bytes 528392 | tf_op jit(solution)/shard_map/ppermute | solution.py:402
  93.4 11.6 %collective-permute-start.23 = (bf16[1,688,128]{2,1,0:T(8,128)(2,1)S(1)}, bf16[1,688,128]{2,1,0:T(8,128)(2,1)S(1)}, u32[]{:S(2)}, u32[]{:S(2)}) collective-permute-start(bf16[1,688,128]{2,1,0:T(8,128)(2,1)S(1)} %slice.94), channel_id=1, source_target_pairs={{0,16},{4,20},{8,24},{12,28},{16,0},{20,4},{24,8},{28,12},{1,17},{... | collective-permute-start | bytes 528392 | tf_op jit(solution)/shard_map/ppermute | solution.py:402
  102.1 8.9 %collective-permute-start.18 = (bf16[4,272,128]{2,1,0:T(8,128)(2,1)S(1)}, bf16[4,272,128]{2,1,0:T(8,128)(2,1)S(1)}, u32[]{:S(2)}, u32[]{:S(2)}) collective-permute-start(bf16[4,272,128]{2,1,0:T(8,128)(2,1)S(1)} %out_away.1), channel_id=1, source_target_pairs={{0,8},{4,12},{8,0},{12,4},{16,24},{20,28},{24,16},{28,20},{1,9},{5... | collective-permute-start | bytes 835592 | tf_op jit(solution)/shard_map/ppermute | solution.py:402
  105.8 17.8 %collective-permute-start.10 = (bf16[512,384]{1,0:T(8,128)(2,1)S(1)}, bf16[512,384]{1,0:T(8,128)(2,1)S(1)}, u32[]{:S(2)}, u32[]{:S(2)}) collective-permute-start(bf16[512,384]{1,0:T(8,128)(2,1)S(1)} %get-tuple-element.60.refs_0_.right), channel_id=1, source_target_pairs={{0,2},{1,3},{2,0},{3,1},{4,6},{5,7},{6,4},{7,5},{8,10},{9,11},{10,... | collective-permute-start | bytes 1179656 | tf_op jit(solution)/shard_map/ppermute | solution.py:402
  107.4 34.0 %collective-permute-start.9 = (bf16[512,384]{1,0:T(8,128)(2,1)S(1)}, bf16[512,384]{1,0:T(8,128)(2,1)S(1)}, u32[]{:S(2)}, u32[]{:S(2)}) collective-permute-start(bf16[512,384]{1,0:T(8,128)(2,1)S(1)} %get-tuple-element.60.refs_0_.right), channel_id=1, source_target_pairs={{0,1},{1,0},{2,3},{3,2},{4,5},{5,4},{6,7},{7,6},{8,9},{9,8},{10,11... | collective-permute-start | bytes 1179656 | tf_op jit(solution)/shard_map/ppermute | solution.py:402
  108.4 14.2 %collective-permute-start.12 = (bf16[4,128,384]{2,1,0:T(8,128)(2,1)S(1)}, bf16[4,128,384]{2,1,0:T(8,128)(2,1)S(1)}, u32[]{:S(2)}, u32[]{:S(2)}) collective-permute-start(bf16[4,128,384]{2,1,0:T(8,128)(2,1)S(1)} %own_away.1), channel_id=1, source_target_pairs={{0,4},{4,0},{8,12},{12,8},{16,20},{20,16},{24,28},{28,24},{1,5},{5... | collective-permute-start | bytes 1179656 | tf_op jit(solution)/shard_map/ppermute | solution.py:402
  111.8 8.9 %collective-permute-start.19 = (bf16[2,272,128]{2,1,0:T(8,128)(2,1)S(1)}, bf16[2,272,128]{2,1,0:T(8,128)(2,1)S(1)}, u32[]{:S(2)}, u32[]{:S(2)}) collective-permute-start(bf16[2,272,128]{2,1,0:T(8,128)(2,1)S(1)} %get-tuple-element.73), channel_id=1, source_target_pairs={{0,16},{4,20},{8,24},{12,28},{16,0},{20,4},{24,8},{28,12},{1,17},{... | collective-permute-start | bytes 417800 | tf_op jit(solution)/shard_map/ppermute | solution.py:402
  120.7 4.6 %collective-permute-start.20 = (bf16[1,272,128]{2,1,0:T(8,128)(2,1)S(1)}, bf16[1,272,128]{2,1,0:T(8,128)(2,1)S(1)}, u32[]{:S(2)}, u32[]{:S(2)}) collective-permute-start(bf16[1,272,128]{2,1,0:T(8,128)(2,1)S(1)} %slice.96), channel_id=1, source_target_pairs={{0,4},{4,0},{8,12},{12,8},{16,20},{20,16},{24,28},{28,24},{1,5},{5... | collective-permute-start | bytes 208904 | tf_op jit(solution)/shard_map/ppermute | solution.py:402
  121.5 19.9 %copy-start.14 = (bf16[512,1024]{1,0:T(8,128)(2,1)S(1)}, bf16[512,1024]{1,0:T(8,128)(2,1)}, u32[]{:S(2)}) copy-start(bf16[512,1024]{1,0:T(8,128)(2,1)} %refs_5_.4) | copy-start | bytes 3145732
  122.5 18.9 %copy-start.9 = (bf16[1024,256]{1,0:T(8,128)(2,1)S(1)}, bf16[1024,256]{1,0:T(8,128)(2,1)}, u32[]{:S(2)}) copy-start(bf16[1024,256]{1,0:T(8,128)(2,1)} %refs_5_.5) | copy-start | bytes 1572868
  122.5 18.9 %copy-start.11 = (bf16[1024,256]{1,0:T(8,128)(2,1)S(1)}, bf16[1024,256]{1,0:T(8,128)(2,1)}, u32[]{:S(2)}) copy-start(bf16[1024,256]{1,0:T(8,128)(2,1)} %refs_6_.3) | copy-start | bytes 1572868
  122.5 18.9 %copy-start.12 = (f32[512,1024]{1,0:T(8,128)S(1)}, f32[512,1024]{1,0:T(8,128)}, u32[]{:S(2)}) copy-start(f32[512,1024]{1,0:T(8,128)} %get-tuple-element.61.refs_4_) | copy-start | bytes 6291460
  122.5 18.9 %copy-start.16 = (f32[512,1]{1,0:T(8,128)S(1)}, f32[512,1]{1,0:T(8,128)}, u32[]{:S(2)}) copy-start(f32[512,1]{1,0:T(8,128)} %copy-done.15) | copy-start | bytes 6148
  122.5 18.9 %copy-start.18 = (f32[1024]{0:T(1024)S(1)}, f32[1024]{0:T(1024)}, u32[]{:S(2)}) copy-start(f32[1024]{0:T(1024)} %param.13) | copy-start | bytes 12292
  123.6 5.7 %collective-permute-start.13 = (bf16[2,128,384]{2,1,0:T(8,128)(2,1)S(1)}, bf16[2,128,384]{2,1,0:T(8,128)(2,1)S(1)}, u32[]{:S(2)}, u32[]{:S(2)}) collective-permute-start(bf16[2,128,384]{2,1,0:T(8,128)(2,1)S(1)} %get-tuple-element.65), channel_id=1, source_target_pairs={{0,8},{4,12},{8,0},{12,4},{16,24},{20,28},{24,16},{28,20},{1,9},{5... | collective-permute-start | bytes 589832 | tf_op jit(solution)/shard_map/ppermute | solution.py:402
  123.7 17.7 %collective-permute-start.11 = (bf16[512,384]{1,0:T(8,128)(2,1)S(1)}, bf16[512,384]{1,0:T(8,128)(2,1)S(1)}, u32[]{:S(2)}, u32[]{:S(2)}) collective-permute-start(bf16[512,384]{1,0:T(8,128)(2,1)S(1)} %collective-permute-done.10.refs_2_), channel_id=1, source_target_pairs={{0,1},{1,0},{2,3},{3,2},{4,5},{5,4},{6,7},{7,6},{8,9},{9,8},{10,11... | collective-permute-start | bytes 1179656 | tf_op jit(solution)/shard_map/ppermute | solution.py:402
  129.4 7.3 %collective-permute-start.14 = (bf16[1,128,384]{2,1,0:T(8,128)(2,1)S(1)}, bf16[1,128,384]{2,1,0:T(8,128)(2,1)S(1)}, u32[]{:S(2)}, u32[]{:S(2)}) collective-permute-start(bf16[1,128,384]{2,1,0:T(8,128)(2,1)S(1)} %slice.95), channel_id=1, source_target_pairs={{0,16},{4,20},{8,24},{12,28},{16,0},{20,4},{24,8},{28,12},{1,17},{... | collective-permute-start | bytes 294920 | tf_op jit(solution)/shard_map/ppermute | solution.py:402
  136.7 4.7 %collective-permute-start.16 = (bf16[128,384]{1,0:T(8,128)(2,1)S(1)}, bf16[128,384]{1,0:T(8,128)(2,1)S(1)}, u32[]{:S(2)}, u32[]{:S(2)}) collective-permute-start(bf16[128,384]{1,0:T(8,128)(2,1)S(1)} %fusion.4.refs_0_), channel_id=1, source_target_pairs={{0,2},{1,3},{2,0},{3,1},{4,6},{5,7},{6,4},{7,5},{8,10},{9,11},{10,... | collective-permute-start | bytes 294920 | tf_op jit(solution)/shard_map/ppermute | solution.py:402
  138.8 8.4 %collective-permute-start.15 = (bf16[128,384]{1,0:T(8,128)(2,1)S(1)}, bf16[128,384]{1,0:T(8,128)(2,1)S(1)}, u32[]{:S(2)}, u32[]{:S(2)}) collective-permute-start(bf16[128,384]{1,0:T(8,128)(2,1)S(1)} %fusion.4.refs_0_), channel_id=1, source_target_pairs={{0,1},{1,0},{2,3},{3,2},{4,5},{5,4},{6,7},{7,6},{8,9},{9,8},{10,11... | collective-permute-start | bytes 294920 | tf_op jit(solution)/shard_map/ppermute | solution.py:402
  141.4 5.9 %collective-permute-start.17 = (bf16[128,384]{1,0:T(8,128)(2,1)S(1)}, bf16[128,384]{1,0:T(8,128)(2,1)S(1)}, u32[]{:S(2)}, u32[]{:S(2)}) collective-permute-start(bf16[128,384]{1,0:T(8,128)(2,1)S(1)} %collective-permute-done.16.refs_2_), channel_id=1, source_target_pairs={{0,1},{1,0},{2,3},{3,2},{4,5},{5,4},{6,7},{7,6},{8,9},{9,8},{10,11... | collective-permute-start | bytes 294920 | tf_op jit(solution)/shard_map/ppermute | solution.py:402
  (16 other events, 35.5 us)

commit v4 on v3

--- a/solution.py
+++ b/solution.py
@@ -13,7 +13,7 @@
 EPSILON = 1e-05
 F32 = jnp.float32
 BF16 = jnp.bfloat16
-VMEM_LIMIT = 48 * 1024 * 1024
+VMEM_LIMIT = 20 * 1024 * 1024
 
 
 def dot(a, b):
@@ -46,10 +46,10 @@
     return blocks
 
 
-def bounds_of(lengths):
+def bounds_of(where):
     bounds, total = [], 0
-    for slot in range(lengths.shape[1]):
-        total = total + lengths[0, slot]
+    for slot in range(2, where.shape[0]):
+        total = total + where[slot]
         bounds.append(total)
     return bounds
 
@@ -61,15 +61,19 @@
     return start
 
 
+def pick_columns(wide, index, width):
+    each = wide.shape[1] // width
+    picked = wide[:, :width]
+    for i in range(1, each):
+        picked = jnp.where(index % each == i, wide[:, i * width : (i + 1) * width], picked)
+    return picked
+
+
 def block_columns(ref, index, width):
     if width % 128 == 0:
         return ref[:, pl.ds(pl.multiple_of(index * width, 128), width)]
     each = 128 // width
-    wide = ref[:, pl.ds(pl.multiple_of(index // each * 128, 128), 128)]
-    picked = wide[:, :width]
-    for i in range(1, each):
-        picked = jnp.where(index % each == i, wide[:, i * width : (i + 1) * width], picked)
-    return picked
+    return pick_columns(ref[:, pl.ds(pl.multiple_of(index // each * 128, 128), 128)], index, width)
 
 
 def positions(order):
@@ -93,26 +97,29 @@
 
 
 def attend_kernel(
-    place, lengths, tok, gain, w_query, w_key, w_value, n_out, r_out, q_out, k_out, v_out, ctx_out, exact_out, den_out
+    where, tok, gain, w_query, w_key, w_value, *refs
 ):
+    later, (n_out, q_out, k_out, v_out, ctx_out, den_out), kept, sems = refs[:4], refs[4:10], refs[10:14], refs[14]
+    copies = [pltpu.make_async_copy(a, b, sems.at[i]) for i, (a, b) in enumerate(zip(later, kept))]
+    for copy in copies:
+        copy.start()
     rows = tok.shape[0]
     hq, hv = q_out.shape[1], v_out.shape[1]
     block = rows // 2
-    feat = place[0]
+    feat = where[0]
     x = tok[...].astype(F32)
     r = lax.rsqrt(jnp.mean(x * x, axis=1, keepdims=True) + EPSILON)
     n = (x * r * gain[...]).astype(BF16)
     n_out[...] = n
-    r_out[...] = r
-    w_small = jnp.concatenate([block_columns(w_query, feat, hq), block_columns(w_key, feat, hq)], axis=1)
-    small = dot(n, w_small)
+    small = dot(n, jnp.concatenate([w_query[...], w_key[...]], axis=1))
     v = dot(n, w_value[...]).astype(BF16)
-    q = (small[:, :hq] * QK**-0.5).astype(BF16)
-    k = small[:, hq:].astype(BF16)
+    wide = w_query.shape[1]
+    q = (pick_columns(small[:, :wide], feat, hq) * QK**-0.5).astype(BF16)
+    k = pick_columns(small[:, wide:], feat, hq).astype(BF16)
     v_out[...] = v
     q_out[...] = q
     k_out[...] = k
-    bounds = bounds_of(lengths)
+    bounds = bounds_of(where)
     for part in range(2):
         low, high = part * block, (part + 1) * block
         row = lax.broadcasted_iota(jnp.int32, (block, high), 0) + low
@@ -127,28 +134,26 @@
             number = number + dot(p, only_head(v[:high], VD, head))
             ones = jnp.where(lane_mask((high, hv), VD, head), 1.0, 0.0).astype(BF16)
             total = total + dot(p, ones)
-        exact = number / total
-        exact_out[low:high, :] = exact
-        ctx_out[low:high, :] = exact.astype(BF16)
+        ctx_out[low:high, :] = (number / total).astype(BF16)
         den_out[low:high, :] = total
+    for copy in copies:
+        copy.wait()
 
 
 def feed_kernel(place, *refs, share):
-    lengths = refs[0]
-    ctx = refs[1 : 1 + share]
-    tok, cot, gain, w_out, w_gate, w_up, w_down = refs[1 + share : 8 + share]
-    res_out, r_out, n_out, inner_out, gg_out, gu_out, away_out, own_out = refs[8 + share :]
+    ctx = refs[:share]
+    tok, cot, gain, w_out, w_gate, w_up, w_down = refs[share : 7 + share]
+    res_out, n_out, inner_out, gg_out, gu_out, away_out, own_out = refs[7 + share :]
     step, half = pl.program_id(0), tok.shape[0]
     core = place[0] & 1
     which = jnp.where(step == 0, 1 - core, core)
     index = lax.broadcasted_iota(jnp.int32, (half, 1), 0) + which * half
-    live = (index < bounds_of(lengths)[-1]).astype(F32)
+    live = (index < bounds_of(place)[-1]).astype(F32)
     context = jnp.concatenate(absolute_order([c[...] for c in ctx], place[0]), axis=1)
     mixed = dot(context, w_out[...])
     residual = tok[...].astype(F32) + live * mixed
     res_out[...] = residual
     r = lax.rsqrt(jnp.mean(residual * residual, axis=1, keepdims=True) + EPSILON)
-    r_out[...] = r
     n = (residual * r * gain[...]).astype(BF16)
     n_out[...] = n
     gate = dot_nt(n, w_gate[...])
@@ -188,6 +193,11 @@
         out[i] = result[:, i * chunk : (i + 1) * chunk].astype(BF16)
 
 
+def pair_away_kernel(where, first, second, right, first_out, second_out, *, orders, chunk):
+    for left, out, order in ((first, first_out, orders[0]), (second, second_out, orders[1])):
+        columns_away_kernel(where, left, right, out, order=order, chunk=chunk)
+
+
 def columns_keep_kernel(where, left, right, arrived, keep_out, away_out, *, order, chunk):
     offsets = positions(order)
     count = len(offsets) // 2
@@ -208,33 +218,31 @@
         out[i] = result[i * chunk : (i + 1) * chunk].astype(BF16)
 
 
-def rows_keep_kernel(where, left, right, arrived, keep_out, away_out, *, order, chunk):
+def rows_direct_kernel(where, left, right, arrived, *outs, order, chunk):
     offsets = positions(order)
     count = len(offsets) // 2
     result = dot_tn(chunk_columns(left, where[1], offsets[:count], chunk), right[...])
     for i in range(count):
         total = result[i * chunk : (i + 1) * chunk] + arrived[i].astype(F32)
-        if i < count // 2:
-            keep_out[i] = total
-        else:
-            away_out[i - count // 2] = total.astype(BF16)
+        outs[i][...] = total.astype(outs[i].dtype)
 
 
 def back_kernel(
-    place, lengths, own, other, res, r2, cot, gain, w_own, q_in, k_in, v_in, exact_in, den_in,
+    place, own, other, res, cot, gain, w_own, q_in, k_in, v_in, ctx_in, den_in,
     gr_out, gm_out, g_out, gain_out, gctx,
 ):
     rows = res.shape[0]
     hq, hv = q_in.shape[1], v_in.shape[1]
     half = rows // 2
     core = place[0] & 1
-    bounds = bounds_of(lengths)
+    bounds = bounds_of(place)
     gain_sum = jnp.zeros((1, gain_out.shape[1]), F32)
     for which, source in ((core, own), (1 - core, other)):
         here = pl.ds(pl.multiple_of(which * half, half), half)
         live = (lax.broadcasted_iota(jnp.int32, (half, 1), 0) + which * half < bounds[-1]).astype(F32)
         e = source[...].astype(F32)
-        residual, r = res[here, :], r2[here, :]
+        residual = res[here, :]
+        r = lax.rsqrt(jnp.mean(residual * residual, axis=1, keepdims=True) + EPSILON)
         weighted = e * gain[...]
         gain_sum = gain_sum + jnp.sum(e * residual * r, axis=0, keepdims=True)
         scale = r * r * r * jnp.mean(weighted * residual, axis=1, keepdims=True)
@@ -246,7 +254,7 @@
     gain_out[...] = gain_sum
     number = gctx[...].astype(F32) / den_in[...]
     gn = number.astype(BF16)
-    product = number * exact_in[...]
+    product = number * ctx_in[...].astype(F32)
     leading = product.astype(BF16)
     remainder = (product - leading.astype(F32)).astype(BF16)
     select = (
@@ -313,13 +321,14 @@
 
 def input_kernel(place, *refs, share, hv, hq):
     grads = refs[:share]
-    gr, tok, r1, gain, w_query, w_key, w_value, out = refs[share:]
+    gr, tok, gain, w_query, w_key, w_value, out = refs[share:]
     blocks = absolute_order([g[...] for g in grads], place[0])
     values = jnp.concatenate([b[:, :hv] for b in blocks], axis=1)
     queries = jnp.concatenate([b[:, hv : hv + hq] for b in blocks], axis=1)
     keys = jnp.concatenate([b[:, hv + hq :] for b in blocks], axis=1)
     e = dot_nt(queries, w_query[...]) + dot_nt(keys, w_key[...]) + dot_nt(values, w_value[...])
-    x, r = tok[...].astype(F32), r1[...]
+    x = tok[...].astype(F32)
+    r = lax.rsqrt(jnp.mean(x * x, axis=1, keepdims=True) + EPSILON)
     weighted = e * gain[...]
     scale = r * r * r * jnp.mean(weighted * x, axis=1, keepdims=True)
     out[...] = (gr[...] + r * weighted - x * scale).astype(BF16)
@@ -347,24 +356,20 @@
     return pl.BlockSpec(array.shape, lambda *_: (0,) * len(array.shape))
 
 
-SMEM = pl.BlockSpec(memory_space=pltpu.SMEM)
-
-
 def shape_of(*args):
     return jax.ShapeDtypeStruct(args[:-1], args[-1])
 
 
+def hbm_of(*args):
+    return pltpu.HBM(args[:-1], args[-1])
+
+
 def params():
     return pltpu.CompilerParams(vmem_limit_bytes=VMEM_LIMIT)
 
 
-def cost(flops, moved):
-    return pl.CostEstimate(flops=flops, bytes_accessed=moved, transcendentals=0)
-
-
 def call(kernel, name, scalars, arrays, shapes, flops, grid=1, specs=None, out_specs=None, scratch=(), **fixed):
     specs, out_specs = specs or {}, out_specs or {}
-    moved = sum(a.size * a.dtype.itemsize for a in (*arrays, *shapes))
     return pl.pallas_call(
         functools.partial(kernel, **fixed) if fixed else kernel,
         grid_spec=pltpu.PrefetchScalarGridSpec(
@@ -376,9 +381,18 @@
         ),
         out_shape=list(shapes),
         compiler_params=params(),
-        cost_estimate=cost(flops, moved),
+        cost_estimate=pl.CostEstimate(flops=1000, bytes_accessed=1000, transcendentals=0),
         name=name,
     )(scalars, *arrays)
+
+
+def after(arrays, *earlier):
+    held = lax.optimization_barrier((*arrays, *earlier))
+    return held[: len(arrays)]
+
+
+def in_hbm(array):
+    return pltpu.with_memory_space_constraint(array, pltpu.HBM)
 
 
 def local(
@@ -393,7 +407,7 @@
     half = rows // 2
     pack = hv + 2 * hq
     heads = hq // QK
-    where = jnp.stack([feat, group]).astype(jnp.int32)
+    where = jnp.concatenate([jnp.stack([feat, group]).astype(jnp.int32), lengths[0]])
     w_gate, w_up = w_gate.T, w_up.T
     gain_a, gain_b = gain_one[None, :], gain_two[None, :]
 
@@ -433,44 +447,53 @@
             keep, away = (total[:count], total[count:].astype(BF16)) if count else (total, None)
         return total[0]
 
-    def reduce_dp(kinds, name, arrays, block, flops, order):
-        away_kernel, keep_kernel = kinds
-        count = groups // 2
+    def first_hop(kind, name, arrays, block, flops, order):
         fixed = dict(order=tuple(order), chunk=chunk)
         [away] = call(
-            away_kernel, name + "_away", where, arrays, [shape_of(count, *block, BF16)], flops, **fixed
+            kind, name + "_away", where, arrays, [shape_of(groups // 2, *block, BF16)], flops, **fixed
         )
-        arrived = swap(away, "dp", order[0])
+        return away, swap(away, "dp", order[0])
+
+    def last_hops(kind, name, arrays, arrived, block, flops, order):
+        fixed = dict(order=tuple(order), chunk=chunk)
         keep, away = call(
-            keep_kernel,
+            kind,
             name + "_keep",
             where,
             [*arrays, arrived],
-            [shape_of(count // 2, *block, F32), shape_of(count // 2, *block, BF16)],
+            [shape_of(groups // 4, *block, F32), shape_of(groups // 4, *block, BF16)],
             flops,
             **fixed,
         )
-        return finish(keep, away, order[1:])
-
-    columns = (columns_away_kernel, columns_keep_kernel)
-
-    normed, r_one, q, k, v, ctx, exact, den = call(
+        return keep, away
+
+    wide = max(hq, 128)
+    near = pl.BlockSpec((width, wide), lambda i, p: (0, p[0] * hq // wide))
+    anywhere = pl.BlockSpec(memory_space=pl.ANY)
+    later = [w_out, w_gate, w_up, w_down]
+    normed, q, k, v, ctx, den, w_out, w_gate, w_up, w_down = call(
         attend_kernel,
         "attend",
         where,
-        [lengths, tokens, gain_a, w_query, w_key, w_value],
+        [in_hbm(a) for a in (tokens, gain_a, w_query, w_key, w_value, *later)],
         [
-            shape_of(rows, width, BF16),
-            shape_of(rows, 1, F32),
-            shape_of(rows, hq, BF16),
-            shape_of(rows, hq, BF16),
+            hbm_of(rows, width, BF16),
+            hbm_of(rows, hq, BF16),
+            hbm_of(rows, hq, BF16),
+            hbm_of(rows, hv, BF16),
             shape_of(rows, hv, BF16),
-            shape_of(rows, hv, BF16),
-            shape_of(rows, hv, F32),
-            shape_of(rows, hv, F32),
+            hbm_of(rows, hv, F32),
+            *(pltpu.VMEM(a.shape, a.dtype) for a in later),
         ],
         2 * rows * width * pack + heads * 6 * rows * rows * 256,
-        specs={0: SMEM, 5: pl.BlockSpec((width, hv), lambda i, p: (0, p[0]))},
+        specs={
+            2: near,
+            3: near,
+            4: pl.BlockSpec((width, hv), lambda i, p: (0, p[0])),
+            **{5 + i: anywhere for i in range(4)},
+        },
+        out_specs={6 + i: anywhere for i in range(4)},
+        scratch=[pltpu.SemaphoreType.DMA((4,))],
     )
 
     ctx_all = gather_feat(ctx)
@@ -480,10 +503,9 @@
             (half,) + array.shape[1:], lambda i, p: (jnp.where(i == 0, 1 - (p[0] & 1), p[0] & 1), 0)
         )
 
-    feed_in = [lengths, *ctx_all, tokens, cotangent, gain_b, w_out, w_gate, w_up, w_down]
+    feed_in = [*ctx_all, tokens, cotangent, gain_b, w_out, w_gate, w_up, w_down]
     feed_shapes = [
-        shape_of(rows, width, F32),
-        shape_of(rows, 1, F32),
+        hbm_of(rows, width, F32),
         shape_of(rows, width, BF16),
         shape_of(rows, hidden, BF16),
         shape_of(rows, hidden, BF16),
@@ -491,7 +513,7 @@
         shape_of(half, width, BF16),
         shape_of(half, width, BF16),
     ]
-    residual, r_two, normed_two, inner, grad_gate, grad_up, back_away, back_own = call(
+    residual, normed_two, inner, grad_gate, grad_up, back_away, back_own = call(
         feed_kernel,
         "feed",
         where,
@@ -499,39 +521,56 @@
         feed_shapes,
         2 * rows * width * (width + 5 * hidden),
         grid=2,
-        specs={0: SMEM, **{i: by_half(feed_in[i]) for i in range(1, share + 3)}},
-        out_specs={i: by_half(feed_shapes[i]) for i in range(6)},
+        specs={i: by_half(feed_in[i]) for i in range(share + 2)},
+        out_specs={i: by_half(feed_shapes[i]) for i in range(5)},
         share=share,
     )
 
-    back_own = sum_feat(back_away, back_own)
+    hidden_flops = rows * width * hidden
+    block = (hidden, chunk)
+    of_down = ("down", [inner, cotangent])
+    of_gate = ("gate", [grad_gate, normed_two])
+    of_up = ("up", [grad_up, normed_two])
+    arrived = swap(back_away, "feat", 1)
+    sent_down, come_down = first_hop(columns_away_kernel, *of_down, block, hidden_flops, x_first)
+    sent_gate, sent_up = call(
+        pair_away_kernel,
+        "pair_away",
+        where,
+        [grad_gate, grad_up, normed_two],
+        [shape_of(groups // 2, *block, BF16)] * 2,
+        2 * hidden_flops,
+        orders=(tuple(x_first), tuple(z_first)),
+        chunk=chunk,
+    )
+    [arrived] = after([arrived], sent_down, sent_up)
+    back_own = (back_own.astype(F32) + arrived.astype(F32)).astype(BF16)
+    come_gate, come_up = swap(sent_gate, "dp", x_first[0]), swap(sent_up, "dp", z_first[0])
+    [inner_in] = after([inner], sent_up)
+    feed_away, feed_own = call(
+        down_kernel,
+        "down",
+        where,
+        [inner_in, w_down],
+        [shape_of(half, width, BF16)] * 2,
+        2 * hidden_flops,
+    )
+    feed_come = swap(feed_away, "feat", 1)
+    feed_own = (feed_own.astype(F32) + feed_come.astype(F32)).astype(BF16)
+    [back_go] = after([back_own], sent_up)
+    come_back = swap(back_go, "feat", feat_masks[0])
+    [come_back] = after([come_back], feed_own)
+    back_own = (back_own.astype(F32) + come_back.astype(F32)).astype(BF16)
+    for mask in feat_masks[1:-1]:
+        back_own = (back_own.astype(F32) + swap(back_own, "feat", mask).astype(F32)).astype(BF16)
     back_other = swap(back_own, "feat", 1)
-
-    hidden_flops = rows * width * hidden
-    sum_gate = reduce_dp(columns, "gate", [grad_gate, normed_two], (hidden, chunk), hidden_flops, x_first)
-    sum_down = reduce_dp(columns, "down", [inner, cotangent], (hidden, chunk), hidden_flops, z_first)
-    sum_up = reduce_dp(columns, "up", [grad_up, normed_two], (hidden, chunk), hidden_flops, x_first)
-
-    feed_own = sum_feat(
-        *call(
-            down_kernel,
-            "down",
-            where,
-            [inner, w_down],
-            [shape_of(half, width, BF16)] * 2,
-            2 * hidden_flops,
-        )
-    )
-    core_start = (feat & 1) * half
-    out_own = (lax.dynamic_slice_in_dim(residual, core_start, half, 0) + feed_own.astype(F32)).astype(BF16)
-    out_other = swap(out_own, "feat", 1)
-    output = jnp.concatenate(absolute_order([out_own, out_other], feat & 1), axis=0)
+    [feed_own] = after([feed_own], back_own)
 
     grad_res, grad_mixed, grads, gain_part = call(
         back_kernel,
         "back",
         where,
-        [lengths, back_own, back_other, residual, r_two, cotangent, gain_b, w_out, q, k, v, exact, den],
+        [back_own, back_other, residual, cotangent, gain_b, w_out, q, k, v, ctx, den],
         [
             shape_of(rows, width, F32),
             shape_of(rows, width, BF16),
@@ -539,24 +578,55 @@
             shape_of(1, width, F32),
         ],
         2 * rows * width * hv + heads * 10 * rows * rows * 256,
-        specs={0: SMEM, 7: pl.BlockSpec((hv, width), lambda i, p: (p[0], 0))},
+        specs={5: pl.BlockSpec((hv, width), lambda i, p: (p[0], 0))},
         scratch=[pltpu.VMEM((rows, hv), BF16)],
     )
 
-    sum_own = reduce_dp(
-        (rows_away_kernel, rows_keep_kernel), "own", [normed, grads], (chunk, pack), rows * width * pack, x_first
-    ).astype(BF16)
-    sum_out = reduce_dp(
-        (out_away_kernel, out_keep_kernel),
-        "out",
-        [ctx, grad_mixed, gain_part],
-        (hv + 16, chunk),
-        rows * width * hv,
-        z_first,
-    )
+    of_own = ("own", [normed, grads])
+    of_out = ("out", [ctx, grad_mixed, gain_part])
+    own_flops, out_flops = rows * width * pack, rows * width * hv
+    sent_own, come_own = first_hop(rows_away_kernel, *of_own, (chunk, pack), own_flops, x_first)
+    [come_up] = after([come_up], sent_own)
+    keep_up, away_up = last_hops(columns_keep_kernel, *of_up, come_up, block, hidden_flops, z_first)
+    [ctx_in] = after([ctx], away_up)
+    sent_out, come_out = first_hop(
+        out_away_kernel, "out", [ctx_in, grad_mixed, gain_part], (hv + 16, chunk), out_flops, x_first
+    )
+    [come_down] = after([come_down], sent_out)
+    keep_down, away_down = last_hops(columns_keep_kernel, *of_down, come_down, block, hidden_flops, x_first)
+    [come_gate] = after([come_gate], away_down)
+    keep_gate, away_gate = last_hops(columns_keep_kernel, *of_gate, come_gate, block, hidden_flops, x_first)
+    [come_own] = after([come_own], away_gate)
+    kept_own, *direct_own = call(
+        rows_direct_kernel,
+        "own_keep",
+        where,
+        [*of_own[1], come_own],
+        [shape_of(chunk, pack, F32)] + [shape_of(chunk, pack, BF16)] * (groups // 2 - 1),
+        own_flops,
+        order=tuple(x_first),
+        chunk=chunk,
+    )
+    sum_own = kept_own
+    for offset, piece in zip(positions(x_first)[1:], direct_own):
+        sum_own = sum_own + swap(piece, "dp", offset).astype(F32)
+    sum_own = sum_own.astype(BF16)
+    [come_out] = after([come_out], *direct_own)
+    keep_out, away_out = last_hops(out_keep_kernel, *of_out, come_out, (hv + 16, chunk), out_flops, x_first)
+    sum_down = finish(keep_down, away_down, x_first[1:])
+    sum_gate = finish(keep_gate, away_gate, x_first[1:])
+    sum_up = finish(keep_up, away_up, z_first[1:])
+    sum_out = finish(keep_out, away_out, x_first[1:])
+
+    for mask in feat_masks[:-1]:
+        feed_own = (feed_own.astype(F32) + swap(feed_own, "feat", mask).astype(F32)).astype(BF16)
+    core_start = (feat & 1) * half
+    out_own = (lax.dynamic_slice_in_dim(residual, core_start, half, 0) + feed_own.astype(F32)).astype(BF16)
+    out_other = swap(out_own, "feat", 1)
+    output = jnp.concatenate(absolute_order([out_own, out_other], feat & 1), axis=0)
 
     grads_all = gather_feat(grads)
-    in_args = [*grads_all, grad_res, tokens, r_one, gain_a, w_query, w_key, w_value]
+    in_args = [*grads_all, grad_res, tokens, gain_a, w_query, w_key, w_value]
 
     def by_rows(array):
         return pl.BlockSpec((half,) + array.shape[1:], lambda i, p: (i, 0))
@@ -569,7 +639,7 @@
         [shape_of(rows, width, BF16)],
         2 * rows * width * pack * share,
         grid=2,
-        specs={i: by_rows(in_args[i]) for i in range(share + 3)},
+        specs={i: by_rows(in_args[i]) for i in range(share + 2)},
         out_specs={0: pl.BlockSpec((half, width), lambda i, p: (i, 0))},
         share=share,
         hv=hv,

time: 149 us -> 130 us (0.87)
  waiting for transfers between devices: 49.1 us -> 38.9 us
  Pallas kernels: 49.9 us -> 41.5 us
  local copies, waits for them, and re-layouts: 10.8 us -> 4.93 us
  starting transfers between devices: 29.3 us -> 34.8 us
    ppermute x30 -> x31, waiting for transfers between devices: 49.1 us -> 38.9 us  [swap(): return lax.ppermute(array, axis, [(i, i ^ mask) for i in range(count)])]
    pallas_call x16 -> x15, Pallas kernels: 49.9 us -> 41.5 us  [call(): pl.pallas_call(functools.partial(kernel, **fixed) if fixed else kernel, g...]
    unnamed x68 -> x58, local copies, waits for them, and re-layouts: 9.5 us -> 3.69 us
    ppermute x30 -> x31, starting transfers between devices: 29.3 us -> 34.8 us  [swap(): return lax.ppermute(array, axis, [(i, i ^ mask) for i in range(count)])]
    convert_element_type x4, other arithmetic: 3.39 us -> 1.47 us  [the longest x1 1.04 us: local(): feed_own = (feed_own.astype(F32) + feed_come.astype(F32)).astype(BF16)]
  transfers between devices with their start and end apart: 30 -> 31, of which waited for: 12 -> 10; matrix products, arithmetic and copies ran while one was open for 7% -> 7% of each run, Pallas kernels for 21% -> 16%
where the time goes in v4:
time: 130 us
  Pallas kernels  41.5 us (32%)
  waiting for transfers between devices  38.9 us (30%)
  starting transfers between devices  34.8 us (27%)
  other arithmetic  8.3 us (6%)
  local copies, waits for them, and re-layouts  4.93 us (4%)
    pallas_call x15, Pallas kernels, call(): pl.pallas_call(functools.partial(kernel, **fixed) if fixed else kernel, g...  41.5 us
    ppermute x31, waiting for transfers between devices, swap(): return lax.ppermute(array, axis, [(i, i ^ mask) for i in range(count)])  38.9 us
    ppermute x31, starting transfers between devices, swap(): return lax.ppermute(array, axis, [(i, i ^ mask) for i in range(count)])  34.8 us
    unnamed x58, local copies, waits for them, and re-layouts  3.69 us
  transfers between devices with their start and end apart: 31, of which 10 were waited for; matrix products, arithmetic and copies ran while one was open for 7% of the time, Pallas kernels for 16%

profile of v4, /device:TPU:0, one launch (start us, length us, event | category | flops | bytes accessed | tf_op | source)
XLA Modules:
  0.0 129.6 jit_solution(7221807161054999470)
XLA Ops:
  1.4 7.4 %attend.1 = (bf16[512,1024]{1,0:T(8,128)(2,1)}, bf16[512,64]{1,0:T(8,128)(2,1)}, bf16[512,64]{1,0:T(8,128)(2,1)}, bf16[512,256]{1,0:T(8,128)(2,1)}, bf16[512,256...) custom-call(s32[6]{0:T(128)S(1)} %pad_add_fusion.where.place, ...), custom_call_target="tpu_custom_call" | custom-call | flops 1000 | bytes 1000 | tf_op jit(solution)/shard_map/attend/pallas_call | solution.py:373
  8.8 3.0 %collective-permute-start.1 = (bf16[512,256]{1,0:T(8,128)(2,1)S(1)}, bf16[512,256]{1,0:T(8,128)(2,1)S(1)}, u32[]{:S(2)}, u32[]{:S(2)}) collective-permute-start(bf16[512,256]{1,0:T(8,128)(2,1)S(1)} %get-tuple-element.93.refs_0_.ctx_in.left), channel_id=1, source_target_pairs={{0,2},{1,3},{2,0},{3,1},{4,6},{5,7},{6,4},{7,5},{8,10},{9,11},{10,... | collective-permute-start | bytes 786440 | tf_op jit(solution)/shard_map/ppermute | solution.py:416
  11.9 6.3 %collective-permute-done.1.refs_2_ = bf16[512,256]{1,0:T(8,128)(2,1)S(1)} collective-permute-done((bf16[512,256]{1,0:T(8,128)(2,1)S(1)}, bf16[512,256]{1,0:T(8,128)(2,1)S(1)}, u32[]{:S(2)}, u32[]{:S(2)}) %collective-permute-start.1) | collective-permute-done | bytes 262176 | tf_op jit(solution)/shard_map/ppermute | solution.py:416
  18.2 1.5 %collective-permute-done.2.refs_3_ = bf16[512,256]{1,0:T(8,128)(2,1)S(1)} collective-permute-done((bf16[512,256]{1,0:T(8,128)(2,1)S(1)}, bf16[512,256]{1,0:T(8,128)(2,1)S(1)}, u32[]{:S(2)}, u32[]{:S(2)}) %collective-permute-start.2) | collective-permute-done | bytes 262176 | tf_op jit(solution)/shard_map/ppermute | solution.py:416
  19.7 9.5 %feed.1 = (f32[512,1024]{1,0:T(8,128)}, bf16[512,1024]{1,0:T(8,128)(2,1)S(1)}, bf16[512,688]{1,0:T(8,128)(2,1)S(1)}, bf16[512,688]{1,0:T(8,128)(2,1)S(1)}, bf16[...) custom-call(s32[6]{0:T(128)S(1)} %pad_add_fusion.where.place, ...), custom_call_target="tpu_custom_call" | custom-call | flops 1000 | bytes 1000 | tf_op jit(solution)/shard_map/feed/pallas_call | solution.py:373
  29.3 1.1 down_away.1
  30.4 2.0 %pair_away.1 = (bf16[4,688,128]{2,1,0:T(8,128)(2,1)}, bf16[4,688,128]{2,1,0:T(8,128)(2,1)S(1)}) custom-call(s32[6]{0:T(128)S(1)} %pad_add_fusion.where.place, bf16[512,688]{1,0:T(8,128)(2,1)S(1)} %get-tuple-element.70.first.left, bf16[512,688]{1,0:T(8,128)(2,1)S(1)} %get-tuple-element.71.second.left, bf16[512,1024]{1,0:T(8,128)(2,1)S(1)} %get-tuple-element.72.right), custom_call_target="tpu_custom_call" | custom-call | flops 1000 | bytes 1000 | tf_op jit(solution)/shard_map/pair_away/pallas_call | solution.py:373
  32.5 1.5 %down.1 = (bf16[256,1024]{1,0:T(8,128)(2,1)S(1)}, bf16[256,1024]{1,0:T(8,128)(2,1)S(1)}) custom-call(s32[6]{0:T(128)S(1)} %pad_add_fusion.where.place, bf16[512,688]{1,0:T(8,128)(2,1)S(1)} %get-tuple-element.74.inner.left, bf16[688,1024]{1,0:T(8,128)(2,1)S(1)} %get-tuple-element.67.refs_10_.w_down), custom_call_target="tpu_custom_call" | custom-call | flops 1000 | bytes 1000 | tf_op jit(solution)/shard_map/down/pallas_call | solution.py:373
  34.7 1.8 %collective-permute-start.5 = (bf16[256,1024]{1,0:T(8,128)(2,1)S(1)}, bf16[256,1024]{1,0:T(8,128)(2,1)S(1)}, u32[]{:S(2)}, u32[]{:S(2)}) collective-permute-start(bf16[256,1024]{1,0:T(8,128)(2,1)S(1)} %add_convert_fusion.3), channel_id=1, source_target_pairs={{0,2},{1,3},{2,0},{3,1},{4,6},{5,7},{6,4},{7,5},{8,10},{9,11},{10,... | collective-permute-start | bytes 1572872 | tf_op jit(solution)/shard_map/ppermute | solution.py:416
  36.5 1.6 %collective-permute-start.15 = (bf16[4,688,128]{2,1,0:T(8,128)(2,1)S(1)}, bf16[4,688,128]{2,1,0:T(8,128)(2,1)S(1)}, u32[]{:S(2)}, u32[]{:S(2)}) collective-permute-start(bf16[4,688,128]{2,1,0:T(8,128)(2,1)S(1)} %get-tuple-element.73), channel_id=1, source_target_pairs={{0,8},{4,12},{8,0},{12,4},{16,24},{20,28},{24,16},{28,20},{1,9},{5... | collective-permute-start | bytes 2113544 | tf_op jit(solution)/shard_map/ppermute | solution.py:416
  38.1 1.5 %collective-permute-start.14 = (bf16[4,688,128]{2,1,0:T(8,128)(2,1)S(1)}, bf16[4,688,128]{2,1,0:T(8,128)(2,1)S(1)}, u32[]{:S(2)}, u32[]{:S(2)}) collective-permute-start(bf16[4,688,128]{2,1,0:T(8,128)(2,1)S(1)} %down_away.1), channel_id=1, source_target_pairs={{0,4},{4,0},{8,12},{12,8},{16,20},{20,16},{24,28},{28,24},{1,5},{5... | collective-permute-start | bytes 2113544 | tf_op jit(solution)/shard_map/ppermute | solution.py:416
  40.1 1.0 add_convert_fusion.4
  41.2 7.5 %collective-permute-done.5 = bf16[256,1024]{1,0:T(8,128)(2,1)S(1)} collective-permute-done((bf16[256,1024]{1,0:T(8,128)(2,1)S(1)}, bf16[256,1024]{1,0:T(8,128)(2,1)S(1)}, u32[]{:S(2)}, u32[]{:S(2)}) %collective-permute-start.5) | collective-permute-done | bytes 524320 | tf_op jit(solution)/shard_map/ppermute | solution.py:416
  49.0 1.8 %collective-permute-start.6 = (bf16[256,1024]{1,0:T(8,128)(2,1)}, bf16[256,1024]{1,0:T(8,128)(2,1)}, u32[]{:S(2)}, u32[]{:S(2)}) collective-permute-start(bf16[256,1024]{1,0:T(8,128)(2,1)} %add_convert_fusion.4), channel_id=1, source_target_pairs={{0,2},{1,3},{2,0},{3,1},{4,6},{5,7},{6,4},{7,5},{8,10},{9,11},{10,... | collective-permute-start | bytes 1572872 | tf_op jit(solution)/shard_map/ppermute | solution.py:416
  50.9 5.2 %back.1 = (f32[512,1024]{1,0:T(8,128)S(1)}, bf16[512,1024]{1,0:T(8,128)(2,1)S(1)}, bf16[512,384]{1,0:T(8,128)(2,1)S(1)}, f32[1,1024]{1,0:T(1,128)S(1)}) custom-call(s32[6]{0:T(128)S(1)} %pad_add_fusion.where.place, bf16[256,1024]{1,0:T(8,128)(2,1)S(1)} %add_convert_fusion.2.own, bf16[256,1024]{1,0:T(8,128)(2,1)S(1)} %collective-permute-done.8.other, ...), custom_call_target="tpu_custom_call" | custom-call | flops 1000 | bytes 1000 | tf_op jit(solution)/shard_map/back/pallas_call | solution.py:373
  56.2 1.0 own_away.1
  57.2 0.9 copy-done.21
  58.1 1.1 up_keep.1
  59.3 0.9 out_away.1
  60.9 1.9 %down_keep.1 = (f32[2,688,128]{2,1,0:T(8,128)S(1)}, bf16[2,688,128]{2,1,0:T(8,128)(2,1)}) custom-call(s32[6]{0:T(128)S(1)} %pad_add_fusion.where.place, bf16[512,688]{1,0:T(8,128)(2,1)S(1)} %get-tuple-element.74.inner.left, bf16[512,1024]{1,0:T(8,128)(2,1)S(1)} %copy-done.1, bf16[4,688,128]{2,1,0:T(8,128)(2,1)S(1)} %collective-permute-done.14.arrived), custom_call_target="tpu_custom_call" | custom-call | flops 1000 | bytes 1000 | tf_op jit(solution)/shard_map/down_keep/pallas_call | solution.py:373
  62.8 0.9 copy-done.18
  63.7 1.8 %collective-permute-start.29 = (bf16[2,688,128]{2,1,0:T(8,128)(2,1)}, bf16[2,688,128]{2,1,0:T(8,128)(2,1)}, u32[]{:S(2)}, u32[]{:S(2)}) collective-permute-start(bf16[2,688,128]{2,1,0:T(8,128)(2,1)} %get-tuple-element.97), channel_id=1, source_target_pairs={{0,8},{4,12},{8,0},{12,4},{16,24},{20,28},{24,16},{28,20},{1,9},{5... | collective-permute-start | bytes 1056776 | tf_op jit(solution)/shard_map/ppermute | solution.py:416
  65.5 2.6 %collective-permute-start.27 = (bf16[2,688,128]{2,1,0:T(8,128)(2,1)}, bf16[2,688,128]{2,1,0:T(8,128)(2,1)S(1)}, u32[]{:S(2)}, u32[]{:S(2)}) collective-permute-start(bf16[2,688,128]{2,1,0:T(8,128)(2,1)} %copy-done.28), channel_id=1, source_target_pairs={{0,16},{4,20},{8,24},{12,28},{16,0},{20,4},{24,8},{28,12},{1,17},{... | collective-permute-start | bytes 1056776 | tf_op jit(solution)/shard_map/ppermute | solution.py:416
  68.1 1.4 %collective-permute-start.12 = (bf16[4,128,384]{2,1,0:T(8,128)(2,1)}, bf16[4,128,384]{2,1,0:T(8,128)(2,1)S(1)}, u32[]{:S(2)}, u32[]{:S(2)}) collective-permute-start(bf16[4,128,384]{2,1,0:T(8,128)(2,1)} %copy-done.21), channel_id=1, source_target_pairs={{0,4},{4,0},{8,12},{12,8},{16,20},{20,16},{24,28},{28,24},{1,5},{5... | collective-permute-start | bytes 1179656 | tf_op jit(solution)/shard_map/ppermute | solution.py:416
  69.5 1.0 collective-permute-done.13.arrived
  70.5 1.5 %collective-permute-start.22 = (bf16[4,272,128]{2,1,0:T(8,128)(2,1)}, bf16[4,272,128]{2,1,0:T(8,128)(2,1)S(1)}, u32[]{:S(2)}, u32[]{:S(2)}) collective-permute-start(bf16[4,272,128]{2,1,0:T(8,128)(2,1)} %copy-done.22), channel_id=1, source_target_pairs={{0,4},{4,0},{8,12},{12,8},{16,20},{20,16},{24,28},{28,24},{1,5},{5... | collective-permute-start | bytes 835592 | tf_op jit(solution)/shard_map/ppermute | solution.py:416
  72.0 1.1 copy-done.13
  73.1 2.2 %gate_keep.1 = (f32[2,688,128]{2,1,0:T(8,128)S(1)}, bf16[2,688,128]{2,1,0:T(8,128)(2,1)S(1)}) custom-call(s32[6]{0:T(128)S(1)} %pad_add_fusion.where.place, bf16[512,688]{1,0:T(8,128)(2,1)S(1)} %copy-done.13, bf16[512,1024]{1,0:T(8,128)(2,1)S(1)} %get-tuple-element.72.right, bf16[4,688,128]{2,1,0:T(8,128)(2,1)} %collective-permute-done.13.arrived), custom_call_target="tpu_custom_call" | custom-call | flops 1000 | bytes 1000 | tf_op jit(solution)/shard_map/gate_keep/pallas_call | solution.py:373
  75.9 1.5 %add_convert_fusion = bf16[256,1024]{1,0:T(8,128)(2,1)S(1)} fusion(f32[512,1024]{1,0:T(8,128)S(1)} %copy-done.4, s32[]{:T(128)S(6)} %select_n.16, bf16[256,1024]{1,0:T(8,128)(2,1)} %collective-permute-done.6, bf16[256,1024]{1,0:T(8,128)(2,1)} %add_convert_fusion.4), kind=kLoop, calls=%fused_computation.1 | loop fusion | flops 1835008 | bytes 2621444 | tf_op jit(solution)/shard_map/convert_element_type | solution.py:624
  77.4 5.2 %collective-permute-done.29 = bf16[2,688,128]{2,1,0:T(8,128)(2,1)} collective-permute-done((bf16[2,688,128]{2,1,0:T(8,128)(2,1)}, bf16[2,688,128]{2,1,0:T(8,128)(2,1)}, u32[]{:S(2)}, u32[]{:S(2)}) %collective-permute-start.29) | collective-permute-done | bytes 352288 | tf_op jit(solution)/shard_map/ppermute | solution.py:416
  82.5 1.1 convert_add_fusion
  83.7 1.0 own_keep.1
  84.8 1.7 %collective-permute-start.16 = (bf16[128,384]{1,0:T(8,128)(2,1)S(1)}, bf16[128,384]{1,0:T(8,128)(2,1)S(1)}, u32[]{:S(2)}, u32[]{:S(2)}) collective-permute-start(bf16[128,384]{1,0:T(8,128)(2,1)S(1)} %get-tuple-element.102), channel_id=1, source_target_pairs={{0,16},{4,20},{8,24},{12,28},{16,0},{20,4},{24,8},{28,12},{1,17},{... | collective-permute-start | bytes 294920 | tf_op jit(solution)/shard_map/ppermute | solution.py:416
  86.4 2.1 %collective-permute-start.17 = (bf16[128,384]{1,0:T(8,128)(2,1)S(1)}, bf16[128,384]{1,0:T(8,128)(2,1)S(1)}, u32[]{:S(2)}, u32[]{:S(2)}) collective-permute-start(bf16[128,384]{1,0:T(8,128)(2,1)S(1)} %get-tuple-element.103), channel_id=1, source_target_pairs={{0,8},{4,12},{8,0},{12,4},{16,24},{20,28},{24,16},{28,20},{1,9},{5... | collective-permute-start | bytes 294920 | tf_op jit(solution)/shard_map/ppermute | solution.py:416
  88.5 3.2 %collective-permute-done.25 = bf16[2,688,128]{2,1,0:T(8,128)(2,1)S(1)} collective-permute-done((bf16[2,688,128]{2,1,0:T(8,128)(2,1)S(1)}, bf16[2,688,128]{2,1,0:T(8,128)(2,1)S(1)}, u32[]{:S(2)}, u32[]{:S(2)}) %collective-permute-start.25) | collective-permute-done | bytes 352288 | tf_op jit(solution)/shard_map/ppermute | solution.py:416
  91.7 3.8 %collective-permute-start.18 = (bf16[128,384]{1,0:T(8,128)(2,1)S(1)}, bf16[128,384]{1,0:T(8,128)(2,1)S(1)}, u32[]{:S(2)}, u32[]{:S(2)}) collective-permute-start(bf16[128,384]{1,0:T(8,128)(2,1)S(1)} %get-tuple-element.104), channel_id=1, source_target_pairs={{0,24},{4,28},{8,16},{12,20},{16,8},{20,12},{24,0},{28,4},{1,25},{... | collective-permute-start | bytes 294920 | tf_op jit(solution)/shard_map/ppermute | solution.py:416
  95.6 1.6 %collective-permute-start.10 = (bf16[512,384]{1,0:T(8,128)(2,1)S(1)}, bf16[512,384]{1,0:T(8,128)(2,1)S(1)}, u32[]{:S(2)}, u32[]{:S(2)}) collective-permute-start(bf16[512,384]{1,0:T(8,128)(2,1)S(1)} %copy-done.11), channel_id=1, source_target_pairs={{0,2},{1,3},{2,0},{3,1},{4,6},{5,7},{6,4},{7,5},{8,10},{9,11},{10,... | collective-permute-start | bytes 1179656 | tf_op jit(solution)/shard_map/ppermute | solution.py:416
  97.2 0.9 out_keep.1
  98.3 1.8 %collective-permute-start.28 = (bf16[1,688,128]{2,1,0:T(8,128)(2,1)S(1)}, bf16[1,688,128]{2,1,0:T(8,128)(2,1)S(1)}, u32[]{:S(2)}, u32[]{:S(2)}) collective-permute-start(bf16[1,688,128]{2,1,0:T(8,128)(2,1)S(1)} %slice.76), channel_id=1, source_target_pairs={{0,4},{4,0},{8,12},{12,8},{16,20},{20,16},{24,28},{28,24},{1,5},{5... | collective-permute-start | bytes 528392 | tf_op jit(solution)/shard_map/ppermute | solution.py:416
  100.2 2.7 %collective-permute-start.26 = (bf16[1,688,128]{2,1,0:T(8,128)(2,1)S(1)}, bf16[1,688,128]{2,1,0:T(8,128)(2,1)S(1)}, u32[]{:S(2)}, u32[]{:S(2)}) collective-permute-start(bf16[1,688,128]{2,1,0:T(8,128)(2,1)S(1)} %slice.77), channel_id=1, source_target_pairs={{0,16},{4,20},{8,24},{12,28},{16,0},{20,4},{24,8},{28,12},{1,17},{... | collective-permute-start | bytes 528392 | tf_op jit(solution)/shard_map/ppermute | solution.py:416
  103.0 1.0 pad_maximum_fusion
  104.0 1.3 %collective-permute-start.23 = (bf16[2,272,128]{2,1,0:T(8,128)(2,1)S(1)}, bf16[2,272,128]{2,1,0:T(8,128)(2,1)S(1)}, u32[]{:S(2)}, u32[]{:S(2)}) collective-permute-start(bf16[2,272,128]{2,1,0:T(8,128)(2,1)S(1)} %get-tuple-element.111), channel_id=1, source_target_pairs={{0,8},{4,12},{8,0},{12,4},{16,24},{20,28},{24,16},{28,20},{1,9},{5... | collective-permute-start | bytes 417800 | tf_op jit(solution)/shard_map/ppermute | solution.py:416
  105.3 6.0 %collective-permute-done.30 = bf16[1,688,128]{2,1,0:T(8,128)(2,1)S(1)} collective-permute-done((bf16[1,688,128]{2,1,0:T(8,128)(2,1)S(1)}, bf16[1,688,128]{2,1,0:T(8,128)(2,1)S(1)}, u32[]{:S(2)}, u32[]{:S(2)}) %collective-permute-start.30) | collective-permute-done | bytes 176160 | tf_op jit(solution)/shard_map/ppermute | solution.py:416
  113.3 3.4 %collective-permute-done.23 = bf16[2,272,128]{2,1,0:T(8,128)(2,1)S(1)} collective-permute-done((bf16[2,272,128]{2,1,0:T(8,128)(2,1)S(1)}, bf16[2,272,128]{2,1,0:T(8,128)(2,1)S(1)}, u32[]{:S(2)}, u32[]{:S(2)}) %collective-permute-start.23) | collective-permute-done | bytes 139296 | tf_op jit(solution)/shard_map/ppermute | solution.py:416
  116.9 0.8 fusion.2
  118.1 4.7 %collective-permute-done.24 = bf16[1,272,128]{2,1,0:T(8,128)(2,1)S(1)} collective-permute-done((bf16[1,272,128]{2,1,0:T(8,128)(2,1)S(1)}, bf16[1,272,128]{2,1,0:T(8,128)(2,1)S(1)}, u32[]{:S(2)}, u32[]{:S(2)}) %collective-permute-start.24) | collective-permute-done | bytes 69664 | tf_op jit(solution)/shard_map/ppermute | solution.py:416
  124.0 1.6 %finish.1 = (f32[128,256]{1,0:T(8,128)}, f32[128,256]{1,0:T(8,128)}, f32[128,1024]{1,0:T(8,128)}, f32[1,128]{1,0:T(1,128)}) custom-call(s32[6]{0:T(128)S(1)} %pad_add_fusion.where.place, bf16[128,384]{1,0:T(8,128)(2,1)S(1)} %add_convert_fusion.5.refs_0_, bf16[128,384]{1,0:T(8,128)(2,1)S(1)} %collective-permute-done.19.refs_1_, ...), custom_call_target="tpu_custom_call" | custom-call | flops 1000 | bytes 1000 | tf_op jit(solution)/shard_map/finish/pallas_call | solution.py:373
  125.7 3.9 %grad_input.1 = bf16[512,1024]{1,0:T(8,128)(2,1)} custom-call(s32[6]{0:T(128)S(1)} %pad_add_fusion.where.place, bf16[512,384]{1,0:T(8,128)(2,1)S(1)} %copy-done.11, bf16[512,384]{1,0:T(8,128)(2,1)S(1)} %collective-permute-done.9.refs_1_, bf16[512,384]{1,0:T(8,128)(2,1)S(1)} %collective-permute-done.10.refs_2_, ...), custom_call_target="tpu_custom_call" | custom-call | flops 1000 | bytes 1000 | tf_op jit(solution)/shard_map/grad_input/pallas_call | solution.py:373
  (109 shorter events, 8.1 us)
Async XLA Ops:
  1.4 18.3 %copy-start.1 = (bf16[512,1024]{1,0:T(8,128)(2,1)S(1)}, bf16[512,1024]{1,0:T(8,128)(2,1)}, u32[]{:S(2)}) copy-start(bf16[512,1024]{1,0:T(8,128)(2,1)} %right.3) | copy-start | bytes 3145732
  1.4 18.3 %copy-start.2 = (bf16[512,1024]{1,0:T(8,128)(2,1)S(1)}, bf16[512,1024]{1,0:T(8,128)(2,1)}, u32[]{:S(2)}) copy-start(bf16[512,1024]{1,0:T(8,128)(2,1)} %refs_5_.4) | copy-start | bytes 3145732
  1.4 18.3 %copy-start.27 = (f32[1024]{0:T(1024)S(1)}, f32[1024]{0:T(1024)}, u32[]{:S(2)}) copy-start(f32[1024]{0:T(1024)} %param.18) | copy-start | bytes 12292
  8.8 9.3 %collective-permute-start.1 = (bf16[512,256]{1,0:T(8,128)(2,1)S(1)}, bf16[512,256]{1,0:T(8,128)(2,1)S(1)}, u32[]{:S(2)}, u32[]{:S(2)}) collective-permute-start(bf16[512,256]{1,0:T(8,128)(2,1)S(1)} %get-tuple-element.93.refs_0_.ctx_in.left), channel_id=1, source_target_pairs={{0,2},{1,3},{2,0},{3,1},{4,6},{5,7},{6,4},{7,5},{8,10},{9,11},{10,... | collective-permute-start | bytes 786440 | tf_op jit(solution)/shard_map/ppermute | solution.py:416
  11.9 6.3 %collective-permute-start = (bf16[512,256]{1,0:T(8,128)(2,1)S(1)}, bf16[512,256]{1,0:T(8,128)(2,1)S(1)}, u32[]{:S(2)}, u32[]{:S(2)}) collective-permute-start(bf16[512,256]{1,0:T(8,128)(2,1)S(1)} %get-tuple-element.93.refs_0_.ctx_in.left), channel_id=1, source_target_pairs={{0,1},{1,0},{2,3},{3,2},{4,5},{5,4},{6,7},{7,6},{8,9},{9,8},{10,11... | collective-permute-start | bytes 786440 | tf_op jit(solution)/shard_map/ppermute | solution.py:416
  18.2 1.5 %collective-permute-start.2 = (bf16[512,256]{1,0:T(8,128)(2,1)S(1)}, bf16[512,256]{1,0:T(8,128)(2,1)S(1)}, u32[]{:S(2)}, u32[]{:S(2)}) collective-permute-start(bf16[512,256]{1,0:T(8,128)(2,1)S(1)} %collective-permute-done.1.refs_2_), channel_id=1, source_target_pairs={{0,1},{1,0},{2,3},{3,2},{4,5},{5,4},{6,7},{7,6},{8,9},{9,8},{10,11... | collective-permute-start | bytes 786440 | tf_op jit(solution)/shard_map/ppermute | solution.py:416
  29.2 5.3 %collective-permute-start.4 = (bf16[256,1024]{1,0:T(8,128)(2,1)S(1)}, bf16[256,1024]{1,0:T(8,128)(2,1)S(1)}, u32[]{:S(2)}, u32[]{:S(2)}) collective-permute-start(bf16[256,1024]{1,0:T(8,128)(2,1)S(1)} %get-tuple-element.78), channel_id=1, source_target_pairs={{0,1},{1,0},{2,3},{3,2},{4,5},{5,4},{6,7},{7,6},{8,9},{9,8},{10,11... | collective-permute-start | bytes 1572872 | tf_op jit(solution)/shard_map/ppermute | solution.py:416
  34.0 6.1 %collective-permute-start.3 = (bf16[256,1024]{1,0:T(8,128)(2,1)S(1)}, bf16[256,1024]{1,0:T(8,128)(2,1)S(1)}, u32[]{:S(2)}, u32[]{:S(2)}) collective-permute-start(bf16[256,1024]{1,0:T(8,128)(2,1)S(1)} %get-tuple-element.76), channel_id=1, source_target_pairs={{0,1},{1,0},{2,3},{3,2},{4,5},{5,4},{6,7},{7,6},{8,9},{9,8},{10,11... | collective-permute-start | bytes 1572872 | tf_op jit(solution)/shard_map/ppermute | solution.py:416
  34.5 16.4 %copy-start.3 = (f32[512,1024]{1,0:T(8,128)S(1)}, f32[512,1024]{1,0:T(8,128)}, u32[]{:S(2)}) copy-start(f32[512,1024]{1,0:T(8,128)} %get-tuple-element.68.res) | copy-start | bytes 6291460
  34.5 16.4 %copy-start.20 = (f32[512,256]{1,0:T(8,128)S(1)}, f32[512,256]{1,0:T(8,128)}, u32[]{:S(2)}) copy-start(f32[512,256]{1,0:T(8,128)} %get-tuple-element.86.den_in) | copy-start | bytes 1572868
  34.5 16.4 %copy-start.23 = (bf16[512,256]{1,0:T(8,128)(2,1)S(1)}, bf16[512,256]{1,0:T(8,128)(2,1)}, u32[]{:S(2)}) copy-start(bf16[512,256]{1,0:T(8,128)(2,1)} %get-tuple-element.85.v_in) | copy-start | bytes 786436
  34.5 16.4 %copy-start.24 = (bf16[512,64]{1,0:T(8,128)(2,1)S(1)}, bf16[512,64]{1,0:T(8,128)(2,1)}, u32[]{:S(2)}) copy-start(bf16[512,64]{1,0:T(8,128)(2,1)} %get-tuple-element.83.q_in) | copy-start | bytes 196612
  34.5 16.4 %copy-start.25 = (bf16[512,64]{1,0:T(8,128)(2,1)S(1)}, bf16[512,64]{1,0:T(8,128)(2,1)}, u32[]{:S(2)}) copy-start(bf16[512,64]{1,0:T(8,128)(2,1)} %get-tuple-element.84.k_in) | copy-start | bytes 196612
  34.7 14.0 %collective-permute-start.5 = (bf16[256,1024]{1,0:T(8,128)(2,1)S(1)}, bf16[256,1024]{1,0:T(8,128)(2,1)S(1)}, u32[]{:S(2)}, u32[]{:S(2)}) collective-permute-start(bf16[256,1024]{1,0:T(8,128)(2,1)S(1)} %add_convert_fusion.3), channel_id=1, source_target_pairs={{0,2},{1,3},{2,0},{3,1},{4,6},{5,7},{6,4},{7,5},{8,10},{9,11},{10,... | collective-permute-start | bytes 1572872 | tf_op jit(solution)/shard_map/ppermute | solution.py:416
  36.5 21.6 %collective-permute-start.15 = (bf16[4,688,128]{2,1,0:T(8,128)(2,1)S(1)}, bf16[4,688,128]{2,1,0:T(8,128)(2,1)S(1)}, u32[]{:S(2)}, u32[]{:S(2)}) collective-permute-start(bf16[4,688,128]{2,1,0:T(8,128)(2,1)S(1)} %get-tuple-element.73), channel_id=1, source_target_pairs={{0,8},{4,12},{8,0},{12,4},{16,24},{20,28},{24,16},{28,20},{1,9},{5... | collective-permute-start | bytes 2113544 | tf_op jit(solution)/shard_map/ppermute | solution.py:416
  38.1 22.8 %collective-permute-start.14 = (bf16[4,688,128]{2,1,0:T(8,128)(2,1)S(1)}, bf16[4,688,128]{2,1,0:T(8,128)(2,1)S(1)}, u32[]{:S(2)}, u32[]{:S(2)}) collective-permute-start(bf16[4,688,128]{2,1,0:T(8,128)(2,1)S(1)} %down_away.1), channel_id=1, source_target_pairs={{0,4},{4,0},{8,12},{12,8},{16,20},{20,16},{24,28},{28,24},{1,5},{5... | collective-permute-start | bytes 2113544 | tf_op jit(solution)/shard_map/ppermute | solution.py:416
  39.6 31.0 %collective-permute-start.13 = (bf16[4,688,128]{2,1,0:T(8,128)(2,1)}, bf16[4,688,128]{2,1,0:T(8,128)(2,1)}, u32[]{:S(2)}, u32[]{:S(2)}) collective-permute-start(bf16[4,688,128]{2,1,0:T(8,128)(2,1)} %get-tuple-element.90), channel_id=1, source_target_pairs={{0,4},{4,0},{8,12},{12,8},{16,20},{20,16},{24,28},{28,24},{1,5},{5... | collective-permute-start | bytes 2113544 | tf_op jit(solution)/shard_map/ppermute | solution.py:416
  48.9 2.0 %collective-permute-start.8 = (bf16[256,1024]{1,0:T(8,128)(2,1)S(1)}, bf16[256,1024]{1,0:T(8,128)(2,1)S(1)}, u32[]{:S(2)}, u32[]{:S(2)}) collective-permute-start(bf16[256,1024]{1,0:T(8,128)(2,1)S(1)} %add_convert_fusion.2.own), channel_id=1, source_target_pairs={{0,1},{1,0},{2,3},{3,2},{4,5},{5,4},{6,7},{7,6},{8,9},{9,8},{10,11... | collective-permute-start | bytes 1572872 | tf_op jit(solution)/shard_map/ppermute | solution.py:416
  49.0 26.4 %collective-permute-start.6 = (bf16[256,1024]{1,0:T(8,128)(2,1)}, bf16[256,1024]{1,0:T(8,128)(2,1)}, u32[]{:S(2)}, u32[]{:S(2)}) collective-permute-start(bf16[256,1024]{1,0:T(8,128)(2,1)} %add_convert_fusion.4), channel_id=1, source_target_pairs={{0,2},{1,3},{2,0},{3,1},{4,6},{5,7},{6,4},{7,5},{8,10},{9,11},{10,... | collective-permute-start | bytes 1572872 | tf_op jit(solution)/shard_map/ppermute | solution.py:416
  63.7 18.8 %collective-permute-start.29 = (bf16[2,688,128]{2,1,0:T(8,128)(2,1)}, bf16[2,688,128]{2,1,0:T(8,128)(2,1)}, u32[]{:S(2)}, u32[]{:S(2)}) collective-permute-start(bf16[2,688,128]{2,1,0:T(8,128)(2,1)} %get-tuple-element.97), channel_id=1, source_target_pairs={{0,8},{4,12},{8,0},{12,4},{16,24},{20,28},{24,16},{28,20},{1,9},{5... | collective-permute-start | bytes 1056776 | tf_op jit(solution)/shard_map/ppermute | solution.py:416
  65.5 10.4 %copy-start.4 = (f32[512,1024]{1,0:T(8,128)S(1)}, f32[512,1024]{1,0:T(8,128)}, u32[]{:S(2)}) copy-start(f32[512,1024]{1,0:T(8,128)} %get-tuple-element.68.res) | copy-start | bytes 6291460
  65.5 18.1 %collective-permute-start.27 = (bf16[2,688,128]{2,1,0:T(8,128)(2,1)}, bf16[2,688,128]{2,1,0:T(8,128)(2,1)S(1)}, u32[]{:S(2)}, u32[]{:S(2)}) collective-permute-start(bf16[2,688,128]{2,1,0:T(8,128)(2,1)} %copy-done.28), channel_id=1, source_target_pairs={{0,16},{4,20},{8,24},{12,28},{16,0},{20,4},{24,8},{28,12},{1,17},{... | collective-permute-start | bytes 1056776 | tf_op jit(solution)/shard_map/ppermute | solution.py:416
  68.1 15.6 %collective-permute-start.12 = (bf16[4,128,384]{2,1,0:T(8,128)(2,1)}, bf16[4,128,384]{2,1,0:T(8,128)(2,1)S(1)}, u32[]{:S(2)}, u32[]{:S(2)}) collective-permute-start(bf16[4,128,384]{2,1,0:T(8,128)(2,1)} %copy-done.21), channel_id=1, source_target_pairs={{0,4},{4,0},{8,12},{12,8},{16,20},{20,16},{24,28},{28,24},{1,5},{5... | collective-permute-start | bytes 1179656 | tf_op jit(solution)/shard_map/ppermute | solution.py:416
  70.5 25.1 %collective-permute-start.22 = (bf16[4,272,128]{2,1,0:T(8,128)(2,1)}, bf16[4,272,128]{2,1,0:T(8,128)(2,1)S(1)}, u32[]{:S(2)}, u32[]{:S(2)}) collective-permute-start(bf16[4,272,128]{2,1,0:T(8,128)(2,1)} %copy-done.22), channel_id=1, source_target_pairs={{0,4},{4,0},{8,12},{12,8},{16,20},{20,16},{24,28},{28,24},{1,5},{5... | collective-permute-start | bytes 835592 | tf_op jit(solution)/shard_map/ppermute | solution.py:416
  73.1 9.4 %copy-start.19 = (f32[2,688,128]{2,1,0:T(8,128)S(1)}, f32[2,688,128]{2,1,0:T(8,128)}, u32[]{:S(2)}) copy-start(f32[2,688,128]{2,1,0:T(8,128)} %copy-done.18) | copy-start | bytes 2113540
  75.4 8.2 %copy-start.17 = (f32[2,688,128]{2,1,0:T(8,128)S(1)}, f32[2,688,128]{2,1,0:T(8,128)}, u32[]{:S(2)}) copy-start(f32[2,688,128]{2,1,0:T(8,128)} %copy-done.16) | copy-start | bytes 2113540
  75.4 16.3 %collective-permute-start.25 = (bf16[2,688,128]{2,1,0:T(8,128)(2,1)S(1)}, bf16[2,688,128]{2,1,0:T(8,128)(2,1)S(1)}, u32[]{:S(2)}, u32[]{:S(2)}) collective-permute-start(bf16[2,688,128]{2,1,0:T(8,128)(2,1)S(1)} %get-tuple-element.99), channel_id=1, source_target_pairs={{0,8},{4,12},{8,0},{12,4},{16,24},{20,28},{24,16},{28,20},{1,9},{5... | collective-permute-start | bytes 1056776 | tf_op jit(solution)/shard_map/ppermute | solution.py:416
  82.5 17.7 %collective-permute-start.7 = (bf16[256,1024]{1,0:T(8,128)(2,1)S(1)}, bf16[256,1024]{1,0:T(8,128)(2,1)S(1)}, u32[]{:S(2)}, u32[]{:S(2)}) collective-permute-start(bf16[256,1024]{1,0:T(8,128)(2,1)S(1)} %add_convert_fusion), channel_id=1, source_target_pairs={{0,1},{1,0},{2,3},{3,2},{4,5},{5,4},{6,7},{7,6},{8,9},{9,8},{10,11... | collective-permute-start | bytes 1572872 | tf_op jit(solution)/shard_map/ppermute | solution.py:416
  83.7 13.5 %copy-start.9 = (bf16[512,1024]{1,0:T(8,128)(2,1)S(1)}, bf16[512,1024]{1,0:T(8,128)(2,1)}, u32[]{:S(2)}) copy-start(bf16[512,1024]{1,0:T(8,128)(2,1)} %copy-done.8) | copy-start | bytes 3145732
  84.8 13.4 %collective-permute-start.16 = (bf16[128,384]{1,0:T(8,128)(2,1)S(1)}, bf16[128,384]{1,0:T(8,128)(2,1)S(1)}, u32[]{:S(2)}, u32[]{:S(2)}) collective-permute-start(bf16[128,384]{1,0:T(8,128)(2,1)S(1)} %get-tuple-element.102), channel_id=1, source_target_pairs={{0,16},{4,20},{8,24},{12,28},{16,0},{20,4},{24,8},{28,12},{1,17},{... | collective-permute-start | bytes 294920 | tf_op jit(solution)/shard_map/ppermute | solution.py:416
  86.4 11.8 %collective-permute-start.17 = (bf16[128,384]{1,0:T(8,128)(2,1)S(1)}, bf16[128,384]{1,0:T(8,128)(2,1)S(1)}, u32[]{:S(2)}, u32[]{:S(2)}) collective-permute-start(bf16[128,384]{1,0:T(8,128)(2,1)S(1)} %get-tuple-element.103), channel_id=1, source_target_pairs={{0,8},{4,12},{8,0},{12,4},{16,24},{20,28},{24,16},{28,20},{1,9},{5... | collective-permute-start | bytes 294920 | tf_op jit(solution)/shard_map/ppermute | solution.py:416
  91.7 6.6 %collective-permute-start.18 = (bf16[128,384]{1,0:T(8,128)(2,1)S(1)}, bf16[128,384]{1,0:T(8,128)(2,1)S(1)}, u32[]{:S(2)}, u32[]{:S(2)}) collective-permute-start(bf16[128,384]{1,0:T(8,128)(2,1)S(1)} %get-tuple-element.104), channel_id=1, source_target_pairs={{0,24},{4,28},{8,16},{12,20},{16,8},{20,12},{24,0},{28,4},{1,25},{... | collective-permute-start | bytes 294920 | tf_op jit(solution)/shard_map/ppermute | solution.py:416
  95.6 8.4 %collective-permute-start.10 = (bf16[512,384]{1,0:T(8,128)(2,1)S(1)}, bf16[512,384]{1,0:T(8,128)(2,1)S(1)}, u32[]{:S(2)}, u32[]{:S(2)}) collective-permute-start(bf16[512,384]{1,0:T(8,128)(2,1)S(1)} %copy-done.11), channel_id=1, source_target_pairs={{0,2},{1,3},{2,0},{3,1},{4,6},{5,7},{6,4},{7,5},{8,10},{9,11},{10,... | collective-permute-start | bytes 1179656 | tf_op jit(solution)/shard_map/ppermute | solution.py:416
  98.1 27.5 %collective-permute-start.9 = (bf16[512,384]{1,0:T(8,128)(2,1)S(1)}, bf16[512,384]{1,0:T(8,128)(2,1)S(1)}, u32[]{:S(2)}, u32[]{:S(2)}) collective-permute-start(bf16[512,384]{1,0:T(8,128)(2,1)S(1)} %copy-done.11), channel_id=1, source_target_pairs={{0,1},{1,0},{2,3},{3,2},{4,5},{5,4},{6,7},{7,6},{8,9},{9,8},{10,11... | collective-permute-start | bytes 1179656 | tf_op jit(solution)/shard_map/ppermute | solution.py:416
  98.2 13.1 %collective-permute-start.30 = (bf16[1,688,128]{2,1,0:T(8,128)(2,1)S(1)}, bf16[1,688,128]{2,1,0:T(8,128)(2,1)S(1)}, u32[]{:S(2)}, u32[]{:S(2)}) collective-permute-start(bf16[1,688,128]{2,1,0:T(8,128)(2,1)S(1)} %slice.75), channel_id=1, source_target_pairs={{0,16},{4,20},{8,24},{12,28},{16,0},{20,4},{24,8},{28,12},{1,17},{... | collective-permute-start | bytes 528392 | tf_op jit(solution)/shard_map/ppermute | solution.py:416
  98.3 13.7 %collective-permute-start.28 = (bf16[1,688,128]{2,1,0:T(8,128)(2,1)S(1)}, bf16[1,688,128]{2,1,0:T(8,128)(2,1)S(1)}, u32[]{:S(2)}, u32[]{:S(2)}) collective-permute-start(bf16[1,688,128]{2,1,0:T(8,128)(2,1)S(1)} %slice.76), channel_id=1, source_target_pairs={{0,4},{4,0},{8,12},{12,8},{16,20},{20,16},{24,28},{28,24},{1,5},{5... | collective-permute-start | bytes 528392 | tf_op jit(solution)/shard_map/ppermute | solution.py:416
  100.2 16.6 %collective-permute-start.26 = (bf16[1,688,128]{2,1,0:T(8,128)(2,1)S(1)}, bf16[1,688,128]{2,1,0:T(8,128)(2,1)S(1)}, u32[]{:S(2)}, u32[]{:S(2)}) collective-permute-start(bf16[1,688,128]{2,1,0:T(8,128)(2,1)S(1)} %slice.77), channel_id=1, source_target_pairs={{0,16},{4,20},{8,24},{12,28},{16,0},{20,4},{24,8},{28,12},{1,17},{... | collective-permute-start | bytes 528392 | tf_op jit(solution)/shard_map/ppermute | solution.py:416
  104.0 20.0 %copy-start = (bf16[1024,1024]{1,0:T(8,128)(2,1)S(1)}, bf16[1024,1024]{1,0:T(8,128)(2,1)}, u32[]{:S(2)}) copy-start(bf16[1024,1024]{1,0:T(8,128)(2,1)} %refs_7_.3) | copy-start | bytes 6291460
  104.0 20.0 %copy-start.5 = (bf16[1024,256]{1,0:T(8,128)(2,1)S(1)}, bf16[1024,256]{1,0:T(8,128)(2,1)}, u32[]{:S(2)}) copy-start(bf16[1024,256]{1,0:T(8,128)(2,1)} %refs_5_.5) | copy-start | bytes 1572868
  104.0 20.0 %copy-start.6 = (bf16[1024,256]{1,0:T(8,128)(2,1)S(1)}, bf16[1024,256]{1,0:T(8,128)(2,1)}, u32[]{:S(2)}) copy-start(bf16[1024,256]{1,0:T(8,128)(2,1)} %refs_6_.1) | copy-start | bytes 1572868
  104.0 20.0 %copy-start.26 = (f32[1024]{0:T(1024)S(1)}, f32[1024]{0:T(1024)}, u32[]{:S(2)}) copy-start(f32[1024]{0:T(1024)} %param.13) | copy-start | bytes 12292
  104.0 12.7 %collective-permute-start.23 = (bf16[2,272,128]{2,1,0:T(8,128)(2,1)S(1)}, bf16[2,272,128]{2,1,0:T(8,128)(2,1)S(1)}, u32[]{:S(2)}, u32[]{:S(2)}) collective-permute-start(bf16[2,272,128]{2,1,0:T(8,128)(2,1)S(1)} %get-tuple-element.111), channel_id=1, source_target_pairs={{0,8},{4,12},{8,0},{12,4},{16,24},{20,28},{24,16},{28,20},{1,9},{5... | collective-permute-start | bytes 417800 | tf_op jit(solution)/shard_map/ppermute | solution.py:416
  111.3 14.4 %collective-permute-start.11 = (bf16[512,384]{1,0:T(8,128)(2,1)S(1)}, bf16[512,384]{1,0:T(8,128)(2,1)S(1)}, u32[]{:S(2)}, u32[]{:S(2)}) collective-permute-start(bf16[512,384]{1,0:T(8,128)(2,1)S(1)} %collective-permute-done.10.refs_2_), channel_id=1, source_target_pairs={{0,1},{1,0},{2,3},{3,2},{4,5},{5,4},{6,7},{7,6},{8,9},{9,8},{10,11... | collective-permute-start | bytes 1179656 | tf_op jit(solution)/shard_map/ppermute | solution.py:416
  112.1 5.6 %collective-permute-start.20 = (bf16[128,384]{1,0:T(8,128)(2,1)S(1)}, bf16[128,384]{1,0:T(8,128)(2,1)S(1)}, u32[]{:S(2)}, u32[]{:S(2)}) collective-permute-start(bf16[128,384]{1,0:T(8,128)(2,1)S(1)} %add_convert_fusion.5.refs_0_), channel_id=1, source_target_pairs={{0,2},{1,3},{2,0},{3,1},{4,6},{5,7},{6,4},{7,5},{8,10},{9,11},{10,... | collective-permute-start | bytes 294920 | tf_op jit(solution)/shard_map/ppermute | solution.py:416
  116.7 7.3 %collective-permute-start.19 = (bf16[128,384]{1,0:T(8,128)(2,1)S(1)}, bf16[128,384]{1,0:T(8,128)(2,1)S(1)}, u32[]{:S(2)}, u32[]{:S(2)}) collective-permute-start(bf16[128,384]{1,0:T(8,128)(2,1)S(1)} %add_convert_fusion.5.refs_0_), channel_id=1, source_target_pairs={{0,1},{1,0},{2,3},{3,2},{4,5},{5,4},{6,7},{7,6},{8,9},{9,8},{10,11... | collective-permute-start | bytes 294920 | tf_op jit(solution)/shard_map/ppermute | solution.py:416
  116.8 6.0 %collective-permute-start.24 = (bf16[1,272,128]{2,1,0:T(8,128)(2,1)S(1)}, bf16[1,272,128]{2,1,0:T(8,128)(2,1)S(1)}, u32[]{:S(2)}, u32[]{:S(2)}) collective-permute-start(bf16[1,272,128]{2,1,0:T(8,128)(2,1)S(1)} %slice.78), channel_id=1, source_target_pairs={{0,16},{4,20},{8,24},{12,28},{16,0},{20,4},{24,8},{28,12},{1,17},{... | collective-permute-start | bytes 208904 | tf_op jit(solution)/shard_map/ppermute | solution.py:416
  117.6 8.0 %copy-start.15 = (f32[512,1024]{1,0:T(8,128)S(1)}, f32[512,1024]{1,0:T(8,128)}, u32[]{:S(2)}) copy-start(f32[512,1024]{1,0:T(8,128)} %copy-done.14) | copy-start | bytes 6291460
  117.6 6.4 %collective-permute-start.21 = (bf16[128,384]{1,0:T(8,128)(2,1)S(1)}, bf16[128,384]{1,0:T(8,128)(2,1)S(1)}, u32[]{:S(2)}, u32[]{:S(2)}) collective-permute-start(bf16[128,384]{1,0:T(8,128)(2,1)S(1)} %collective-permute-done.20.refs_2_), channel_id=1, source_target_pairs={{0,1},{1,0},{2,3},{3,2},{4,5},{5,4},{6,7},{7,6},{8,9},{9,8},{10,11... | collective-permute-start | bytes 294920 | tf_op jit(solution)/shard_map/ppermute | solution.py:416
  (12 other events, 32.3 us)

commit v5 on v4

v5 whole, which is shorter than its diff:
```python
import functools

import jax
import jax.numpy as jnp
from jax import lax
from jax.experimental import pallas as pl
from jax.experimental.pallas import tpu as pltpu
from jax.sharding import PartitionSpec as P

HEADS = 16
QK = 16
VD = 64
EPSILON = 1e-05
F32 = jnp.float32
BF16 = jnp.bfloat16
COSTS = {"feed": 3000000000, "late": 10000000000}
VMEM_LIMIT = 20 * 1024 * 1024


def dot(a, b):
    return lax.dot_general(a, b, (((1,), (0,)), ((), ())), preferred_element_type=F32)


def dot_nt(a, b):
    return lax.dot_general(a, b, (((1,), (1,)), ((), ())), preferred_element_type=F32)


def dot_tn(a, b):
    return lax.dot_general(a, b, (((0,), (0,)), ((), ())), preferred_element_type=F32)


def lane_mask(shape, width, head):
    return lax.broadcasted_iota(jnp.int32, shape, 1) // width == head


def only_head(array, width, head):
    return jnp.where(lane_mask(array.shape, width, head), array, jnp.zeros_like(array))


def absolute_order(blocks, place):
    blocks = list(blocks)
    mask = 1
    while mask < len(blocks):
        flip = (place & mask) != 0
        blocks = [jnp.where(flip, blocks[j ^ mask], blocks[j]) for j in range(len(blocks))]
        mask *= 2
    return blocks


def bounds_of(where):
    bounds, total = [], 0
    for slot in range(2, where.shape[0]):
        total = total + where[slot]
        bounds.append(total)
    return bounds


def starts_of(bounds, index):
    start = jnp.zeros_like(index)
    for bound in bounds:
        start = jnp.maximum(start, jnp.where(index >= bound, bound, 0))
    return start


def pick_columns(wide, index, width):
    each = wide.shape[1] // width
    picked = wide[:, :width]
    for i in range(1, each):
        picked = jnp.where(index % each == i, wide[:, i * width : (i + 1) * width], picked)
    return picked


def block_columns(ref, index, width):
    if width % 128 == 0:
        return ref[:, pl.ds(pl.multiple_of(index * width, 128), width)]
    each = 128 // width
    return pick_columns(ref[:, pl.ds(pl.multiple_of(index // each * 128, 128), 128)], index, width)


def positions(order):
    found = [0]
    for mask in order:
        found = [r for r in found] + [r ^ mask for r in found]
    count = len(found)
    result = []
    for p in range(count):
        r, top = 0, count // 2
        for mask in order:
            if p & top:
                r ^= mask
            top //= 2
        result.append(r)
    return result


def chunk_columns(ref, group, offsets, chunk):
    return jnp.concatenate([block_columns(ref, group ^ r, chunk) for r in offsets], axis=1)


def attend_kernel(
    where, tok, gain, w_query, w_key, w_value, *refs
):
    n_out, q_out, k_out, v_out, ctx_out, den_out = refs
    rows = tok.shape[0]
    hq, hv = q_out.shape[1], v_out.shape[1]
    block = rows // 2
    feat = where[0]
    x = tok[...].astype(F32)
    r = lax.rsqrt(jnp.mean(x * x, axis=1, keepdims=True) + EPSILON)
    n = (x * r * gain[...]).astype(BF16)
    n_out[...] = n
    small = dot(n, jnp.concatenate([w_query[...], w_key[...]], axis=1))
    v = dot(n, w_value[...]).astype(BF16)
    wide = w_query.shape[1]
    q = (pick_columns(small[:, :wide], feat, hq) * QK**-0.5).astype(BF16)
    k = pick_columns(small[:, wide:], feat, hq).astype(BF16)
    v_out[...] = v
    q_out[...] = q
    k_out[...] = k
    bounds = bounds_of(where)
    for part in range(2):
        low, high = part * block, (part + 1) * block
        row = lax.broadcasted_iota(jnp.int32, (block, high), 0) + low
        col = lax.broadcasted_iota(jnp.int32, (block, high), 1)
        start = starts_of(bounds, lax.broadcasted_iota(jnp.int32, (block, 1), 0) + low)
        allowed = (col <= row) & (col >= start)
        number = jnp.zeros((block, hv), F32)
        total = jnp.zeros((block, hv), F32)
        for head in range(hq // QK):
            t = dot_nt(only_head(q[low:high], QK, head), k[:high]) + 1.0
            p = jnp.where(allowed, t * t + 1.0, 0.0).astype(BF16)
            number = number + dot(p, only_head(v[:high], VD, head))
            ones = jnp.where(lane_mask((high, hv), VD, head), 1.0, 0.0).astype(BF16)
            total = total + dot(p, ones)
        ctx_out[low:high, :] = (number / total).astype(BF16)
        den_out[low:high, :] = total


def fetch_kernel(where, ctx, cot, *refs):
    *refs, ginner_out, sems = refs
    count = len(refs) // 2
    copies = [pltpu.make_async_copy(refs[i], refs[count + i], sems.at[i]) for i in range(count)]
    for copy in copies:
        copy.start()
    copies[0].wait()
    live = lax.broadcasted_iota(jnp.int32, (cot.shape[0], 1), 0) < bounds_of(where)[-1]
    gfeed = jnp.where(live, cot[...], jnp.zeros_like(cot))
    ginner_out[...] = dot_nt(gfeed, refs[count][...])
    for copy in copies[1:]:
        copy.wait()


def feed_kernel(place, *refs, share):
    ctx = refs[:share]
    tok, ginner_in, gain, w_out, w_gate, w_up = refs[share : 6 + share]
    res_out, n_out, inner_out, gg_out, gu_out, away_out, own_out = refs[6 + share :]
    half = tok.shape[0] // 2
    core = place[0] & 1
    contexts = absolute_order([c[...] for c in ctx], place[0])
    context = jnp.concatenate(contexts, axis=1)
    rows = slice(None)
    index = lax.broadcasted_iota(jnp.int32, (2 * half, 1), 0)
    live = (index < bounds_of(place)[-1]).astype(F32)
    residual = tok[...].astype(F32) + live * dot(context, w_out[...])
    res_out[...] = residual
    r = lax.rsqrt(jnp.mean(residual * residual, axis=1, keepdims=True) + EPSILON)
    n = (residual * r * gain[...]).astype(BF16)
    n_out[...] = n
    gate = dot_nt(n, w_gate[...])
    up = dot_nt(n, w_up[...])
    ginner = ginner_in[...]
    sig = jax.nn.sigmoid(gate)
    act = gate * sig
    inner_out[...] = (act * up * live).astype(BF16)
    ggate = (ginner * up * sig * (1.0 + gate * (1.0 - sig))).astype(BF16)
    gup = (ginner * act).astype(BF16)
    gg_out[...] = ggate
    gu_out[...] = gup
    for which, out in ((1 - core, away_out), (core, own_out)):
        here = pl.ds(pl.multiple_of(which * half, half), half)
        out[...] = (dot(gg_out[here, :], w_gate[...]) + dot(gu_out[here, :], w_up[...])).astype(BF16)


def down_kernel(place, inner, w_down, away_out, own_out):
    half = own_out.shape[0]
    core = place[0] & 1
    for which, out in ((1 - core, away_out), (core, own_out)):
        out[...] = dot(inner[pl.ds(pl.multiple_of(which * half, half), half), :], w_down[...]).astype(BF16)


def products(where, pairs, offsets, chunk):
    found = []
    for left, right in pairs:
        part = chunk_columns(right, where[1], offsets, chunk)
        found.append(jnp.broadcast_to(part, (16, part.shape[1])) if left is None else dot_tn(left, part))
    return found


def away_kernel(where, *refs, pairs, order, chunk):
    out = refs[-1]
    offsets = positions(order)
    count = len(offsets) // 2
    low = 0
    for part in products(where, pairs(refs), offsets[count:], chunk):
        high = low + part.shape[0]
        for i in range(count):
            out[i, low:high, :] = part[:, i * chunk : (i + 1) * chunk].astype(BF16)
        low = high


def keep_kernel(where, *refs, pairs, order, chunk):
    arrived, keep_out, away_out = refs[-3:]
    offsets = positions(order)
    count = len(offsets) // 2
    low = 0
    for part in products(where, pairs(refs), offsets[:count], chunk):
        high = low + part.shape[0]
        for i in range(count):
            total = part[:, i * chunk : (i + 1) * chunk] + arrived[i, low:high, :].astype(F32)
            if i < count // 2:
                keep_out[i, low:high, :] = total.astype(keep_out.dtype)
            else:
                away_out[i - count // 2, low:high, :] = total.astype(BF16)
        low = high


def direct_kernel(where, *refs, pairs, order, chunk, inputs):
    arrived, outs = refs[inputs], refs[inputs + 1 :]
    offsets = positions(order)
    count = len(offsets) // 2
    low = 0
    for part in products(where, pairs(refs), offsets[:count], chunk):
        high = low + part.shape[0]
        for i in range(count):
            total = part[:, i * chunk : (i + 1) * chunk] + arrived[i, low:high, :].astype(F32)
            outs[i][low:high, :] = total.astype(outs[i].dtype)
        low = high


def hop_kernel(where, held, come, keep_out, away_out):
    count = keep_out.shape[0]
    for i in range(count):
        keep_out[i] = (held[i].astype(F32) + come[i].astype(F32)).astype(keep_out.dtype)
        away_out[i] = (held[count + i].astype(F32) + come[count + i].astype(F32)).astype(BF16)


def hidden_kernel(where, x_held, x_come, z_held, z_come, down_out, gate_out, up_out):
    hidden = down_out.shape[0]
    split = x_held.shape[1] - hidden
    x = x_held[0].astype(F32) + x_come[0].astype(F32)
    z = z_held[0].astype(F32) + z_come[0].astype(F32)
    down_out[...] = x[:hidden]
    gate_out[:split, :] = x[hidden:]
    gate_out[split:, :] = z[: hidden - split]
    up_out[...] = z[hidden - split :]


def late_kernel(where, held, *refs):
    comes, (out, gain_out, own_out) = refs[:-3], refs[-3:]
    total = held[...].reshape(held.shape[-2:]).astype(F32)
    for come in comes:
        total = total + come[...].reshape(come.shape[-2:]).astype(F32)
    many = out.shape[0]
    out[...] = total[:many]
    gain_out[...] = total[many : many + 1]
    own_out[...] = total[many + 16 :].astype(BF16)


def back_kernel(
    place, own, other, res, cot, gain, w_own, q_in, k_in, v_in, ctx_in, den_in,
    gr_out, gm_out, g_out, gain_out, gctx,
):
    rows = res.shape[0]
    hq, hv = q_in.shape[1], v_in.shape[1]
    half = rows // 2
    core = place[0] & 1
    bounds = bounds_of(place)
    gain_sum = jnp.zeros((1, gain_out.shape[1]), F32)
    for which, source in ((core, own), (1 - core, other)):
        here = pl.ds(pl.multiple_of(which * half, half), half)
        live = (lax.broadcasted_iota(jnp.int32, (half, 1), 0) + which * half < bounds[-1]).astype(F32)
        e = source[...].astype(F32)
        residual = res[here, :]
        r = lax.rsqrt(jnp.mean(residual * residual, axis=1, keepdims=True) + EPSILON)
        weighted = e * gain[...]
        gain_sum = gain_sum + jnp.sum(e * residual * r, axis=0, keepdims=True)
        scale = r * r * r * jnp.mean(weighted * residual, axis=1, keepdims=True)
        grad = cot[here, :].astype(F32) + r * weighted - residual * scale
        gr_out[here, :] = grad
        gm = (live * grad).astype(BF16)
        gm_out[here, :] = gm
        gctx[here, :] = dot_nt(gm, w_own[...]).astype(BF16)
    gain_out[...] = gain_sum
    number = gctx[...].astype(F32) / den_in[...]
    gn = number.astype(BF16)
    product = number * ctx_in[...].astype(F32)
    leading = product.astype(BF16)
    remainder = (product - leading.astype(F32)).astype(BF16)
    select = (
        lax.broadcasted_iota(jnp.int32, (16, hv), 1) // VD == lax.broadcasted_iota(jnp.int32, (16, hv), 0)
    )
    select = jnp.where(select, 1.0, 0.0).astype(BF16)
    shift = dot_nt(select, leading) + dot_nt(select, remainder)
    q, k, v = q_in[...], k_in[...], v_in[...]
    gq = [jnp.zeros((half, hq), F32) for _ in range(2)]
    for part in range(2):
        low, high = part * half, (part + 1) * half
        row = lax.broadcasted_iota(jnp.int32, (half, rows - low), 0) + low
        col = lax.broadcasted_iota(jnp.int32, (half, rows - low), 1) + low
        start = starts_of(bounds, lax.broadcasted_iota(jnp.int32, (1, rows - low), 1) + low)
        allowed = (row <= col) & (row >= start)
        gk = jnp.zeros((half, hq), F32)
        gv = jnp.zeros((half, hv), F32)
        for head in range(hq // QK):
            q_head = only_head(q[low:], QK, head)
            g_head = only_head(gn[low:], VD, head)
            t = dot_nt(k[low:high], q_head) + 1.0
            p = jnp.where(allowed, t * t + 1.0, 0.0).astype(BF16)
            g = dot_nt(v[low:high], g_head) - shift[head : head + 1, low:]
            ds = jnp.where(allowed, g * t, 0.0).astype(BF16)
            gv = gv + dot(p, g_head)
            gk = gk + dot(ds, q_head)
            k_head = only_head(k[low:high], QK, head)
            for second in range(part, 2):
                piece = ds[:, second * half - low : (second + 1) * half - low]
                gq[second] = gq[second] + dot_tn(piece, k_head)
        g_out[low:high, :hv] = gv.astype(BF16)
        g_out[low:high, hv + hq :] = (gk * 2.0).astype(BF16)
    for part in range(2):
        g_out[part * half : (part + 1) * half, hv : hv + hq] = (gq[part] * (2.0 * QK**-0.5)).astype(BF16)


def input_kernel(place, *refs, share, hv, hq):
    grads = refs[:share]
    gr, tok, res, own, other, gain, w_query, w_key, w_value, out, output = refs[share:]
    blocks = absolute_order([g[...] for g in grads], place[0])
    values = jnp.concatenate([b[:, :hv] for b in blocks], axis=1)
    queries = jnp.concatenate([b[:, hv : hv + hq] for b in blocks], axis=1)
    keys = jnp.concatenate([b[:, hv + hq :] for b in blocks], axis=1)
    e = dot_nt(queries, w_query[...]) + dot_nt(keys, w_key[...]) + dot_nt(values, w_value[...])
    x = tok[...].astype(F32)
    r = lax.rsqrt(jnp.mean(x * x, axis=1, keepdims=True) + EPSILON)
    weighted = e * gain[...]
    scale = r * r * r * jnp.mean(weighted * x, axis=1, keepdims=True)
    out[...] = (gr[...] + r * weighted - x * scale).astype(BF16)
    step, half = pl.program_id(0), tok.shape[0]
    index = lax.broadcasted_iota(jnp.int32, (half, 1), 0) + step * half
    live = (index < bounds_of(place)[-1]).astype(F32)
    feed = jnp.where(step == (place[0] & 1), own[...], other[...]).astype(F32)
    output[...] = (res[...] + live * feed).astype(BF16)


def finish_kernel(where, *refs, share, hv, hq):
    sums = refs[:share]
    gain, w_query, w_key, w_value, q_out, k_out, v_out, gain_out = refs[share:]
    blocks = [b.T for b in absolute_order([s[...].astype(F32) for s in sums], where[0])]
    values = jnp.concatenate([b[:, :hv] for b in blocks], axis=1)
    queries = jnp.concatenate([b[:, hv : hv + hq] for b in blocks], axis=1)
    keys = jnp.concatenate([b[:, hv + hq :] for b in blocks], axis=1)
    q_out[...] = queries
    k_out[...] = keys
    v_out[...] = values
    total = jnp.sum(values * w_value[...].astype(F32), axis=1, keepdims=True)
    total = total + jnp.sum(queries * w_query[...].astype(F32) + keys * w_key[...].astype(F32), axis=1, keepdims=True)
    spread = jnp.broadcast_to(total, (total.shape[0], total.shape[0]))
    diagonal = lax.broadcasted_iota(jnp.int32, spread.shape, 0) == lax.broadcasted_iota(jnp.int32, spread.shape, 1)
    row = jnp.sum(jnp.where(diagonal, spread, 0.0), axis=0, keepdims=True)
    gain_out[...] = row / block_columns(gain, where[1], gain_out.shape[1])


def whole(array):
    return pl.BlockSpec(array.shape, lambda *_: (0,) * len(array.shape))


def shape_of(*args):
    return jax.ShapeDtypeStruct(args[:-1], args[-1])


def vmem_of(*args):
    return pltpu.VMEM(args[:-1], args[-1])


def params():
    return pltpu.CompilerParams(vmem_limit_bytes=VMEM_LIMIT)


def call(kernel, name, scalars, arrays, shapes, grid=1, specs=None, out_specs=None, scratch=(), **fixed):
    specs, out_specs = specs or {}, out_specs or {}
    return pl.pallas_call(
        functools.partial(kernel, **fixed) if fixed else kernel,
        grid_spec=pltpu.PrefetchScalarGridSpec(
            num_scalar_prefetch=1,
            grid=(grid,),
            in_specs=[specs.get(i, whole(a)) for i, a in enumerate(arrays)],
            out_specs=[out_specs.get(i, whole(s)) for i, s in enumerate(shapes)],
            scratch_shapes=list(scratch),
        ),
        out_shape=list(shapes),
        compiler_params=params(),
        cost_estimate=pl.CostEstimate(flops=COSTS.get(name, 1000), bytes_accessed=1000, transcendentals=0),
        name=name,
    )(scalars, *arrays)


def after(arrays, *earlier):
    held = lax.optimization_barrier((*arrays, *earlier))
    return held[: len(arrays)]


def in_hbm(array):
    return pltpu.with_memory_space_constraint(array, pltpu.HBM)


def local(
    tokens, gain_one, w_query, w_key, w_value, w_out, gain_two, w_gate, w_up, w_down, lengths, cotangent
):
    rows, width = tokens.shape
    share, groups = lax.axis_size("feat"), lax.axis_size("dp")
    feat, group = lax.axis_index("feat"), lax.axis_index("dp")
    hq, hv = w_query.shape[1] // share, w_value.shape[1] // share
    hidden = w_gate.shape[1]
    chunk = width // groups
    half = rows // 2
    pack = hv + 2 * hq
    where = jnp.concatenate([jnp.stack([feat, group]).astype(jnp.int32), lengths[0]])
    w_gate, w_up = w_gate.T, w_up.T
    gain_a, gain_b = gain_one[None, :], gain_two[None, :]

    def swap(array, axis, mask):
        count = share if axis == "feat" else groups
        return lax.ppermute(array, axis, [(i, i ^ mask) for i in range(count)])

    def masks_of(count):
        found, mask = [], 1
        while mask < count:
            found.append(mask)
            mask *= 2
        return found

    feat_masks = masks_of(share)[::-1]
    dp_masks = masks_of(groups)
    x_first = tuple(dp_masks)
    z_first = tuple(dp_masks[1:] + dp_masks[:1])

    def gather_feat(own, *earlier):
        held = {0: own}
        for mask in feat_masks:
            for j in list(held):
                [held[j ^ mask]] = after([swap(held[j], "feat", mask)], *earlier)
        return [held[j] for j in range(share)]

    def plus(array, come):
        return (array.astype(F32) + come.astype(F32)).astype(BF16)

    wide = max(hq, 128)
    near = pl.BlockSpec((width, wide), lambda i, p: (0, p[0] * hq // wide))
    anywhere = pl.BlockSpec(memory_space=pl.ANY)
    later = [w_down, w_out, w_gate, w_up]
    normed, q, k, v, ctx, den = call(
        attend_kernel,
        "attend",
        where,
        [in_hbm(a) for a in (tokens, gain_a, w_query, w_key, w_value)],
        [
            vmem_of(rows, width, BF16),
            vmem_of(rows, hq, BF16),
            vmem_of(rows, hq, BF16),
            vmem_of(rows, hv, BF16),
            vmem_of(rows, hv, BF16),
            vmem_of(rows, hv, F32),
        ],
        specs={2: near, 3: near, 4: pl.BlockSpec((width, hv), lambda i, p: (0, p[0]))},
    )
    whole_vmem = pl.BlockSpec(memory_space=pltpu.VMEM)
    w_down, w_out, w_gate, w_up, ginner = call(
        fetch_kernel,
        "fetch",
        where,
        [ctx, in_hbm(cotangent), *map(in_hbm, later)],
        [*(pltpu.VMEM(a.shape, a.dtype) for a in later), vmem_of(rows, hidden, F32)],
        specs={i: anywhere for i in (0, 2, 3, 4, 5)},
        out_specs={0: whole_vmem, **{i: anywhere for i in range(1, 4)}},
        scratch=[pltpu.SemaphoreType.DMA((4,))],
    )
    ctx_all = gather_feat(ctx, w_down)

    feed_in = [*ctx_all, tokens, ginner, gain_b, w_out, w_gate, w_up]
    feed_shapes = [
        vmem_of(rows, width, F32),
        vmem_of(rows, width, BF16),
        vmem_of(rows, hidden, BF16),
        vmem_of(rows, hidden, BF16),
        vmem_of(rows, hidden, BF16),
        shape_of(half, width, BF16),
        shape_of(half, width, BF16),
    ]
    residual, normed_two, inner, grad_gate, grad_up, back_away, back_own = call(
        feed_kernel,
        "feed",
        where,
        feed_in,
        feed_shapes,
        share=share,
    )

    z_order = z_first
    split = max(hidden // 256, 1) * 128 + (128 if hidden % 256 >= 128 else 0)
    few = groups // 4
    x_args = [inner, grad_gate, cotangent, normed_two]
    z_args = [grad_gate, grad_up, normed_two]
    x_pairs = lambda refs: [(refs[0][...], refs[2]), (refs[1][:, :split], refs[3])]
    z_pairs = lambda refs: [(refs[0][:, split:], refs[2]), (refs[1][...], refs[2])]
    x_fixed = dict(pairs=x_pairs, order=x_first, chunk=chunk)
    z_fixed = dict(pairs=z_pairs, order=z_order, chunk=chunk)
    x_many, z_many, late_many = hidden + split, 2 * hidden - split, hv + 16 + pack

    def hops(name, held, sent, masks, earlier):
        [come] = after([swap(sent, "dp", masks[0])], earlier)
        for mask in masks[1:]:
            count = held.shape[0] // 2
            shapes = [shape_of(count, *held.shape[1:], BF16)] * 2
            held, sent = call(hop_kernel, name, where, [held, come], shapes)
            come = swap(sent, "dp", mask)
        return held, come, sent

    last = back_own
    feed_away, feed_own = call(
        down_kernel, "down", where, [*after([inner], last), w_down], [shape_of(half, width, BF16)] * 2
    )
    last = feed_own
    [x_sent] = call(
        away_kernel,
        "x_away",
        where,
        [*after(x_args[:1], last), *x_args[1:]],
        [shape_of(2 * few, x_many, chunk, BF16)],
        **x_fixed,
    )
    last = x_sent
    [z_sent] = call(
        away_kernel,
        "z_away",
        where,
        [*after(z_args[:1], last), *z_args[1:]],
        [shape_of(2 * few, z_many, chunk, BF16)],
        **z_fixed,
    )
    last = z_sent
    [come] = after([swap(back_away, "feat", 1)], last)
    last = back_own = plus(back_own, come)
    [come] = after([swap(feed_away, "feat", 1)], last)
    last = feed_own = plus(feed_own, come)
    for mask in feat_masks[:-1]:
        [come] = after([swap(back_own, "feat", mask)], last)
        last = back_own = plus(back_own, come)
    [back_other] = after([swap(back_own, "feat", 1)], last)
    grad_res, grad_mixed, grads, gain_part = call(
        back_kernel,
        "back",
        where,
        [back_own, back_other, residual, cotangent, gain_b, w_out, q, k, v, ctx, den],
        [
            vmem_of(rows, width, F32),
            vmem_of(rows, width, BF16),
            vmem_of(rows, pack, BF16),
            shape_of(1, width, F32),
        ],
        specs={5: pl.BlockSpec((hv, width), lambda i, p: (p[0], 0))},
        scratch=[pltpu.VMEM((rows, hv), BF16)],
    )
    last = gain_part
    late_args = [ctx, grads, normed, grad_mixed, gain_part]
    late_pairs = lambda refs: [(refs[0][...], refs[3]), (None, refs[4]), (refs[1][...], refs[2])]
    late_fixed = dict(pairs=late_pairs, order=x_first, chunk=chunk)
    held = {0: grads}
    for mask in feat_masks[:-1]:
        for j in list(held):
            held[j ^ mask] = swap(held[j], "feat", mask)
    far = [j for j in held if j]
    [late_sent] = call(
        away_kernel,
        "late_away",
        where,
        [*after(late_args[:1], last), *late_args[1:]],
        [shape_of(2 * few, late_many, chunk, BF16)],
        **late_fixed,
    )
    late_come = swap(late_sent, "dp", x_first[0])
    last = late_sent
    [come] = after([swap(z_sent, "dp", z_order[0])], last)
    shapes = [shape_of(few, z_many, chunk, BF16)] * 2
    z_held, z_sent = call(keep_kernel, "z_keep", where, [*z_args, come], shapes, **z_fixed)
    last = z_sent
    [come] = after([swap(x_sent, "dp", x_first[0])], last)
    shapes = [shape_of(few, x_many, chunk, BF16)] * 2
    x_held, x_sent = call(keep_kernel, "x_keep", where, [*x_args, come], shapes, **x_fixed)
    last = x_sent
    for mask in feat_masks[:-1]:
        [come] = after([swap(feed_own, "feat", mask)], last)
        last = feed_own = plus(feed_own, come)
    held.update(zip(far, after([held[j] for j in far], last)))
    last = held[far[-1]]
    [come] = after([late_come], last)
    late, *direct = call(
        direct_kernel,
        "late_keep",
        where,
        [*late_args, come],
        [shape_of(late_many, chunk, F32)] + [shape_of(late_many, chunk, BF16)] * (2 * few - 1),
        inputs=len(late_args),
        **late_fixed,
    )
    comes = [swap(piece, "dp", offset) for offset, piece in zip(positions(x_first)[1:], direct)]
    last = direct[-1]
    z_held, z_come, last = hops("z_hop", z_held, z_sent, z_order[1:], last)
    for j in list(held):
        [held[j ^ 1]] = after([swap(held[j], "feat", 1)], last)
    last = held[1]
    x_held, x_come, last = hops("x_hop", x_held, x_sent, x_first[1:], last)
    sum_out, sum_gain_two, sum_own = call(
        late_kernel,
        "late",
        where,
        [late, *after(comes, last)],
        [shape_of(hv, chunk, F32), shape_of(1, chunk, F32), shape_of(pack, chunk, BF16)],
    )
    last = sum_own
    sums = {0: sum_own}
    for mask in feat_masks[:-1]:
        for j in list(sums):
            sums[j ^ mask] = swap(sums[j], "feat", mask)
    sums_far = [j for j in sums if j]
    [feed_other] = after([swap(feed_own, "feat", 1)], last)
    last = feed_other
    def by_rows(array):
        return pl.BlockSpec((half,) + array.shape[1:], lambda i, p: (i, 0))

    in_args = [*[held[j] for j in range(share)], *after([grad_res], last), tokens, residual, feed_own, feed_other, gain_a, w_query, w_key, w_value]
    grad_input, output = call(
        input_kernel,
        "grad_input",
        where,
        in_args,
        [shape_of(rows, width, BF16)] * 2,
        grid=2,
        specs={i: by_rows(in_args[i]) for i in range(share + 3)},
        out_specs={i: pl.BlockSpec((half, width), lambda i, p: (i, 0)) for i in range(2)},
        share=share,
        hv=hv,
        hq=hq,
    )
    last = grad_input
    for j in list(sums):
        sums[j ^ 1] = swap(sums[j], "feat", 1)

    def own_rows(array):
        return pl.BlockSpec((chunk, array.shape[1]), lambda i, p: (p[1], 0))

    sum_query, sum_key, sum_value, sum_gain_one = call(
        finish_kernel,
        "finish",
        where,
        [*after([sums[j] for j in range(share)], last), gain_a, w_query, w_key, w_value],
        [
            shape_of(chunk, hq * share, F32),
            shape_of(chunk, hq * share, F32),
            shape_of(chunk, hv * share, F32),
            shape_of(1, chunk, F32),
        ],
        specs={
            share + 1: own_rows(w_query),
            share + 2: own_rows(w_key),
            share + 3: own_rows(w_value),
        },
        share=share,
        hv=hv,
        hq=hq,
    )
    last = sum_query
    x_come, z_come = after([x_come, z_come], last)
    sum_down, sum_gate, sum_up = call(
        hidden_kernel, "hidden", where, [x_held, x_come, z_held, z_come], [shape_of(hidden, chunk, F32)] * 3
    )
    last = sum_down

    return (
        output,
        grad_input,
        sum_gain_one[0],
        sum_query,
        sum_key,
        sum_value,
        sum_out,
        sum_gain_two[0],
        sum_gate.T,
        sum_up.T,
        sum_down,
    )


def solution(mesh):
    in_specs = (
        P("dp", None),
        P(),
        P(),
        P(),
        P(),
        P(),
        P(),
        P(None, "feat"),
        P(None, "feat"),
        P("feat", None),
        P("dp", None),
        P("dp", None),
    )
    out_specs = (
        P("dp", None),
        P("dp", None),
        P("dp"),
        P("dp", None),
        P("dp", None),
        P("dp", None),
        P("feat", "dp"),
        P("dp"),
        P("dp", "feat"),
        P("dp", "feat"),
        P("feat", "dp"),
    )
    return jax.shard_map(local, mesh=mesh, in_specs=in_specs, out_specs=out_specs, check_vma=False)
```

time: 130 us -> 114 us (0.88)
  the two profiles are of different devices: /device:TPU:0 before, /device:TPU:17 now
where the time goes in v5:
time: 114 us
  Pallas kernels  40.7 us (36%)
  waiting for transfers between devices  37.2 us (33%)
  starting transfers between devices  33.3 us (29%)
  other arithmetic  1.5 us (1%)
    pallas_call x17, Pallas kernels, call(): pl.pallas_call(functools.partial(kernel, **fixed) if fixed else kernel, g...  40.7 us
    ppermute x25, waiting for transfers between devices, swap(): return lax.ppermute(array, axis, [(i, i ^ mask) for i in range(count)])  37.2 us
    ppermute x25, starting transfers between devices, swap(): return lax.ppermute(array, axis, [(i, i ^ mask) for i in range(count)])  33.3 us
  transfers between devices with their start and end apart: 25, of which 11 were waited for; matrix products, arithmetic and copies ran while one was open for 1% of the time, Pallas kernels for 25%

profile of v5, /device:TPU:17, one launch (start us, length us, event | category | flops | bytes accessed | tf_op | source)
XLA Modules:
  0.0 113.6 jit_solution(5049703300416500472)
XLA Ops:
  0.6 0.7 pad_add_fusion.where.place
  1.4 5.2 %attend.1 = (bf16[512,1024]{1,0:T(8,128)(2,1)S(1)}, bf16[512,64]{1,0:T(8,128)(2,1)S(1)}, bf16[512,64]{1,0:T(8,128)(2,1)S(1)}, bf16[512,256]{1,0:T(8,128)(2,1)S(1...) custom-call(s32[6]{0:T(128)S(1)} %pad_add_fusion.where.place, bf16[512,1024]{1,0:T(8,128)(2,1)} %refs_5_.2, ...), custom_call_target="tpu_custom_call" | custom-call | flops 1000 | bytes 1000 | tf_op jit(solution)/shard_map/attend/pallas_call | solution.py:389
  6.6 1.3 %collective-permute-start.1 = (bf16[512,256]{1,0:T(8,128)(2,1)S(1)}, bf16[512,256]{1,0:T(8,128)(2,1)S(1)}, u32[]{:S(2)}, u32[]{:S(2)}) collective-permute-start(bf16[512,256]{1,0:T(8,128)(2,1)S(1)} %get-tuple-element.121.ctx.refs_0_.ctx_in), channel_id=1, source_target_pairs={{0,2},{1,3},{2,0},{3,1},{4,6},{5,7},{6,4},{7,5},{8,10},{9,11},{10,... | collective-permute-start | bytes 786440 | tf_op jit(solution)/shard_map/ppermute | solution.py:431
  7.9 0.9 collective-permute-start
  8.8 4.6 %fetch.1 = (bf16[688,1024]{1,0:T(8,128)(2,1)S(1)}, bf16[1024,1024]{1,0:T(8,128)(2,1)S(1)}, bf16[688,1024]{1,0:T(8,128)(2,1)S(1)}, bf16[688,1024]{1,0:T(8,128)(2,1)S(1)}, f32[512,688]{1,0:T(8,128)S(1)}) custom-call(s32[6]{0:T(128)S(1)} %pad_add_fusion.where.place, bf16[512,256]{1,0:T(8,128)(2,1)S(1)} %get-tuple-element.121.ctx.refs_0_.ctx_in, ...), custom_call_target="tpu_custom_call" | custom-call | flops 1000 | bytes 1000 | tf_op jit(solution)/shard_map/fetch/pallas_call | solution.py:389
  13.5 0.3 collective-permute-done.1.refs_2_
  13.8 1.6 %collective-permute-start.2 = (bf16[512,256]{1,0:T(8,128)(2,1)S(1)}, bf16[512,256]{1,0:T(8,128)(2,1)S(1)}, u32[]{:S(2)}, u32[]{:S(2)}) collective-permute-start(bf16[512,256]{1,0:T(8,128)(2,1)S(1)} %collective-permute-done.1.refs_2_), channel_id=1, source_target_pairs={{0,1},{1,0},{2,3},{3,2},{4,5},{5,4},{6,7},{7,6},{8,9},{9,8},{10,11... | collective-permute-start | bytes 786440 | tf_op jit(solution)/shard_map/ppermute | solution.py:431
  15.3 1.2 %collective-permute-done.2.refs_3_ = bf16[512,256]{1,0:T(8,128)(2,1)S(1)} collective-permute-done((bf16[512,256]{1,0:T(8,128)(2,1)S(1)}, bf16[512,256]{1,0:T(8,128)(2,1)S(1)}, u32[]{:S(2)}, u32[]{:S(2)}) %collective-permute-start.2) | collective-permute-done | bytes 262176 | tf_op jit(solution)/shard_map/ppermute | solution.py:431
  16.5 6.0 %feed.1 = (f32[512,1024]{1,0:T(8,128)S(1)}, bf16[512,1024]{1,0:T(8,128)(2,1)S(1)}, bf16[512,688]{1,0:T(8,128)(2,1)S(1)}, bf16[512,688]{1,0:T(8,128)(2,1)S(1)}, b...) custom-call(s32[6]{0:T(128)S(1)} %pad_add_fusion.where.place, ...), custom_call_target="tpu_custom_call" | custom-call | flops 3000000000 | bytes 1000 | tf_op jit(solution)/shard_map/feed/pallas_call | solution.py:389
  22.5 0.4 collective-permute-start.3
  23.0 1.5 %down.1 = (bf16[256,1024]{1,0:T(8,128)(2,1)S(1)}, bf16[256,1024]{1,0:T(8,128)(2,1)S(1)}) custom-call(s32[6]{0:T(128)S(1)} %pad_add_fusion.where.place, bf16[512,688]{1,0:T(8,128)(2,1)S(1)} %get-tuple-element.105.inner.refs_0_, bf16[688,1024]{1,0:T(8,128)(2,1)S(1)} %get-tuple-element.91.w_down), custom_call_target="tpu_custom_call" | custom-call | flops 1000 | bytes 1000 | tf_op jit(solution)/shard_map/down/pallas_call | solution.py:389
  24.5 1.4 %x_away.1 = bf16[4,1072,128]{2,1,0:T(8,128)(2,1)S(1)} custom-call(s32[6]{0:T(128)S(1)} %pad_add_fusion.where.place, bf16[512,688]{1,0:T(8,128)(2,1)S(1)} %get-tuple-element.105.inner.refs_0_, bf16[512,688]{1,0:T(8,128)(2,1)S(1)} %get-tuple-element.107.refs_1_.refs_0_, bf16[512,1024]{1,0:T(8,128)(2,1)S(1)} %copy-done.1, ...), custom_call_target="tpu_custom_call" | custom-call | flops 1000 | bytes 1000 | tf_op jit(solution)/shard_map/x_away/pallas_call | solution.py:389
  26.1 1.3 %z_away.1 = bf16[4,992,128]{2,1,0:T(8,128)(2,1)S(1)} custom-call(s32[6]{0:T(128)S(1)} %pad_add_fusion.where.place, bf16[512,688]{1,0:T(8,128)(2,1)S(1)} %get-tuple-element.107.refs_1_.refs_0_, bf16[512,688]{1,0:T(8,128)(2,1)S(1)} %get-tuple-element.108.refs_1_, bf16[512,1024]{1,0:T(8,128)(2,1)S(1)} %get-tuple-element.106.refs_3_.refs_2_), custom_call_target="tpu_custom_call" | custom-call | flops 1000 | bytes 1000 | tf_op jit(solution)/shard_map/z_away/pallas_call | solution.py:389
  27.6 1.3 %collective-permute-start.4 = (bf16[256,1024]{1,0:T(8,128)(2,1)S(1)}, bf16[256,1024]{1,0:T(8,128)(2,1)S(1)}, u32[]{:S(2)}, u32[]{:S(2)}) collective-permute-start(bf16[256,1024]{1,0:T(8,128)(2,1)S(1)} %add_convert_fusion.3), channel_id=1, source_target_pairs={{0,2},{1,3},{2,0},{3,1},{4,6},{5,7},{6,4},{7,5},{8,10},{9,11},{10,... | collective-permute-start | bytes 1572872 | tf_op jit(solution)/shard_map/ppermute | solution.py:431
  28.9 1.3 %collective-permute-start.8 = (bf16[4,992,128]{2,1,0:T(8,128)(2,1)S(1)}, bf16[4,992,128]{2,1,0:T(8,128)(2,1)S(1)}, u32[]{:S(2)}, u32[]{:S(2)}) collective-permute-start(bf16[4,992,128]{2,1,0:T(8,128)(2,1)S(1)} %z_away.1), channel_id=1, source_target_pairs={{0,8},{4,12},{8,0},{12,4},{16,24},{20,28},{24,16},{28,20},{1,9},{5... | collective-permute-start | bytes 3047432 | tf_op jit(solution)/shard_map/ppermute | solution.py:431
  30.2 1.2 %collective-permute-start.13 = (bf16[4,1072,128]{2,1,0:T(8,128)(2,1)S(1)}, bf16[4,1072,128]{2,1,0:T(8,128)(2,1)S(1)}, u32[]{:S(2)}, u32[]{:S(2)}) collective-permute-start(bf16[4,1072,128]{2,1,0:T(8,128)(2,1)S(1)} %x_away.1), channel_id=1, source_target_pairs={{0,4},{4,0},{8,12},{12,8},{16,20},{20,16},{24,28},{28,24},{1,5},{5... | collective-permute-start | bytes 3293192 | tf_op jit(solution)/shard_map/ppermute | solution.py:431
  31.6 9.2 %collective-permute-done.4 = bf16[256,1024]{1,0:T(8,128)(2,1)S(1)} collective-permute-done((bf16[256,1024]{1,0:T(8,128)(2,1)S(1)}, bf16[256,1024]{1,0:T(8,128)(2,1)S(1)}, u32[]{:S(2)}, u32[]{:S(2)}) %collective-permute-start.4) | collective-permute-done | bytes 524320 | tf_op jit(solution)/shard_map/ppermute | solution.py:431
  41.0 1.3 %collective-permute-start.6 = (bf16[256,1024]{1,0:T(8,128)(2,1)S(1)}, bf16[256,1024]{1,0:T(8,128)(2,1)S(1)}, u32[]{:S(2)}, u32[]{:S(2)}) collective-permute-start(bf16[256,1024]{1,0:T(8,128)(2,1)S(1)} %add_convert_fusion.1.own), channel_id=1, source_target_pairs={{0,1},{1,0},{2,3},{3,2},{4,5},{5,4},{6,7},{7,6},{8,9},{9,8},{10,11... | collective-permute-start | bytes 1572872 | tf_op jit(solution)/shard_map/ppermute | solution.py:431
  42.3 1.3 %collective-permute-start.12 = (bf16[256,1024]{1,0:T(8,128)(2,1)S(1)}, bf16[256,1024]{1,0:T(8,128)(2,1)S(1)}, u32[]{:S(2)}, u32[]{:S(2)}) collective-permute-start(bf16[256,1024]{1,0:T(8,128)(2,1)S(1)} %add_convert_fusion.2), channel_id=1, source_target_pairs={{0,2},{1,3},{2,0},{3,1},{4,6},{5,7},{6,4},{7,5},{8,10},{9,11},{10,... | collective-permute-start | bytes 1572872 | tf_op jit(solution)/shard_map/ppermute | solution.py:431
  43.5 0.3 collective-permute-done.6.other
  43.8 5.4 %back.1 = (f32[512,1024]{1,0:T(8,128)S(1)}, bf16[512,1024]{1,0:T(8,128)(2,1)S(1)}, bf16[512,384]{1,0:T(8,128)(2,1)S(1)}, f32[1,1024]{1,0:T(1,128)S(1)}) custom-call(s32[6]{0:T(128)S(1)} %pad_add_fusion.where.place, bf16[256,1024]{1,0:T(8,128)(2,1)S(1)} %add_convert_fusion.1.own, bf16[256,1024]{1,0:T(8,128)(2,1)S(1)} %collective-permute-done.6.other, ...), custom_call_target="tpu_custom_call" | custom-call | flops 1000 | bytes 1000 | tf_op jit(solution)/shard_map/back/pallas_call | solution.py:389
  49.2 1.1 late_away.1
  50.3 1.3 %collective-permute-start.10 = (bf16[4,656,128]{2,1,0:T(8,128)(2,1)S(1)}, bf16[4,656,128]{2,1,0:T(8,128)(2,1)S(1)}, u32[]{:S(2)}, u32[]{:S(2)}) collective-permute-start(bf16[4,656,128]{2,1,0:T(8,128)(2,1)S(1)} %late_away.1), channel_id=1, source_target_pairs={{0,4},{4,0},{8,12},{12,8},{16,20},{20,16},{24,28},{28,24},{1,5},{5... | collective-permute-start | bytes 2015240 | tf_op jit(solution)/shard_map/ppermute | solution.py:431
  51.6 0.7 collective-permute-done.8.refs_3_
  52.3 1.3 %z_keep.1 = (bf16[2,992,128]{2,1,0:T(8,128)(2,1)S(1)}, bf16[2,992,128]{2,1,0:T(8,128)(2,1)S(1)}) custom-call(s32[6]{0:T(128)S(1)} %pad_add_fusion.where.place, bf16[512,688]{1,0:T(8,128)(2,1)S(1)} %get-tuple-element.107.refs_1_.refs_0_, bf16[512,688]{1,0:T(8,128)(2,1)S(1)} %get-tuple-element.108.refs_1_, ...), custom_call_target="tpu_custom_call" | custom-call | flops 1000 | bytes 1000 | tf_op jit(solution)/shard_map/z_keep/pallas_call | solution.py:389
  53.7 0.5 collective-permute-start.11
  54.3 0.7 collective-permute-done.13.refs_4_
  55.0 1.4 %x_keep.1 = (bf16[2,1072,128]{2,1,0:T(8,128)(2,1)S(1)}, bf16[2,1072,128]{2,1,0:T(8,128)(2,1)S(1)}) custom-call(s32[6]{0:T(128)S(1)} %pad_add_fusion.where.place, bf16[512,688]{1,0:T(8,128)(2,1)S(1)} %get-tuple-element.105.inner.refs_0_, bf16[512,688]{1,0:T(8,128)(2,1)S(1)} %get-tuple-element.107.refs_1_.refs_0_, bf16[512,1024]{1,0:T(8,128)(2,1)S(1)} %copy-done.1, ...), custom_call_target="tpu_custom_call" | custom-call | flops 1000 | bytes 1000 | tf_op jit(solution)/shard_map/x_keep/pallas_call | solution.py:389
  56.4 0.6 collective-permute-start.19
  57.0 3.1 %collective-permute-start.7 = (bf16[512,384]{1,0:T(8,128)(2,1)S(1)}, bf16[512,384]{1,0:T(8,128)(2,1)S(1)}, u32[]{:S(2)}, u32[]{:S(2)}) collective-permute-start(bf16[512,384]{1,0:T(8,128)(2,1)S(1)} %get-tuple-element.119.refs_1_.refs_0_), channel_id=1, source_target_pairs={{0,1},{1,0},{2,3},{3,2},{4,5},{5,4},{6,7},{7,6},{8,9},{9,8},{10,11... | collective-permute-start | bytes 1179656 | tf_op jit(solution)/shard_map/ppermute | solution.py:431
  60.4 2.2 %collective-permute-done.11.refs_2_ = bf16[512,384]{1,0:T(8,128)(2,1)S(1)} collective-permute-done((bf16[512,384]{1,0:T(8,128)(2,1)S(1)}, bf16[512,384]{1,0:T(8,128)(2,1)S(1)}, u32[]{:S(2)}, u32[]{:S(2)}) %collective-permute-start.11) | collective-permute-done | bytes 393248 | tf_op jit(solution)/shard_map/ppermute | solution.py:431
  62.6 6.8 %collective-permute-done.10.refs_5_ = bf16[4,656,128]{2,1,0:T(8,128)(2,1)S(1)} collective-permute-done((bf16[4,656,128]{2,1,0:T(8,128)(2,1)S(1)}, bf16[4,656,128]{2,1,0:T(8,128)(2,1)S(1)}, u32[]{:S(2)}, u32[]{:S(2)}) %collective-permute-start.10) | collective-permute-done | bytes 671776 | tf_op jit(solution)/shard_map/ppermute | solution.py:431
  69.4 1.1 late_keep.1
  70.9 4.0 %collective-permute-done.9.come = bf16[2,992,128]{2,1,0:T(8,128)(2,1)S(1)} collective-permute-done((bf16[2,992,128]{2,1,0:T(8,128)(2,1)S(1)}, bf16[2,992,128]{2,1,0:T(8,128)(2,1)S(1)}, u32[]{:S(2)}, u32[]{:S(2)}) %collective-permute-start.9) | collective-permute-done | bytes 507936 | tf_op jit(solution)/shard_map/ppermute | solution.py:431
  74.9 3.9 %collective-permute-start.18 = (bf16[656,128]{1,0:T(8,128)(2,1)S(1)}, bf16[656,128]{1,0:T(8,128)(2,1)S(1)}, u32[]{:S(2)}, u32[]{:S(2)}) collective-permute-start(bf16[656,128]{1,0:T(8,128)(2,1)S(1)} %get-tuple-element.132), channel_id=1, source_target_pairs={{0,24},{4,28},{8,16},{12,20},{16,8},{20,12},{24,0},{28,4},{1,25},{... | collective-permute-start | bytes 503816 | tf_op jit(solution)/shard_map/ppermute | solution.py:431
  78.8 0.7 z_hop.1
  79.5 1.3 %collective-permute-start.15 = (bf16[256,1024]{1,0:T(8,128)(2,1)S(1)}, bf16[256,1024]{1,0:T(8,128)(2,1)S(1)}, u32[]{:S(2)}, u32[]{:S(2)}) collective-permute-start(bf16[256,1024]{1,0:T(8,128)(2,1)S(1)} %add_convert_fusion.refs_7_), channel_id=1, source_target_pairs={{0,1},{1,0},{2,3},{3,2},{4,5},{5,4},{6,7},{7,6},{8,9},{9,8},{10,11... | collective-permute-start | bytes 1572872 | tf_op jit(solution)/shard_map/ppermute | solution.py:431
  80.8 4.4 %collective-permute-start.14 = (bf16[512,384]{1,0:T(8,128)(2,1)S(1)}, bf16[512,384]{1,0:T(8,128)(2,1)S(1)}, u32[]{:S(2)}, u32[]{:S(2)}) collective-permute-start(bf16[512,384]{1,0:T(8,128)(2,1)S(1)} %collective-permute-done.11.refs_2_), channel_id=1, source_target_pairs={{0,1},{1,0},{2,3},{3,2},{4,5},{5,4},{6,7},{7,6},{8,9},{9,8},{10,11... | collective-permute-start | bytes 1179656 | tf_op jit(solution)/shard_map/ppermute | solution.py:431
  85.1 0.7 x_hop.1
  86.0 4.4 %collective-permute-start.23 = (bf16[1,1072,128]{2,1,0:T(8,128)(2,1)S(1)}, bf16[1,1072,128]{2,1,0:T(8,128)(2,1)S(1)}, u32[]{:S(2)}, u32[]{:S(2)}) collective-permute-start(bf16[1,1072,128]{2,1,0:T(8,128)(2,1)S(1)} %get-tuple-element.143), channel_id=1, source_target_pairs={{0,16},{4,20},{8,24},{12,28},{16,0},{20,4},{24,8},{28,12},{1,17},{... | collective-permute-start | bytes 823304 | tf_op jit(solution)/shard_map/ppermute | solution.py:431
  90.4 8.9 %collective-permute-done.18.refs_2_ = bf16[656,128]{1,0:T(8,128)(2,1)S(1)} collective-permute-done((bf16[656,128]{1,0:T(8,128)(2,1)S(1)}, bf16[656,128]{1,0:T(8,128)(2,1)S(1)}, u32[]{:S(2)}, u32[]{:S(2)}) %collective-permute-start.18) | collective-permute-done | bytes 167968 | tf_op jit(solution)/shard_map/ppermute | solution.py:431
  99.3 1.2 %late.1 = (f32[256,128]{1,0:T(8,128)}, f32[1,128]{1,0:T(1,128)}, bf16[384,128]{1,0:T(8,128)(2,1)S(1)}) custom-call(s32[6]{0:T(128)S(1)} %pad_add_fusion.where.place, f32[656,128]{1,0:T(8,128)S(1)} %get-tuple-element.138.held, bf16[656,128]{1,0:T(8,128)(2,1)S(1)} %collective-permute-done.16.refs_0_, bf16[656,128]{1,0:T(8,128)(2,1)S(1)} %collective-permute-done.17.refs_1_, ...), custom_call_target="tpu_custom_call" | custom-call | flops 10000000000 | bytes 1000 | tf_op jit(solution)/shard_map/late/pallas_call | solution.py:389
  100.5 0.6 collective-permute-start.20
  101.2 2.8 %collective-permute-done.21.refs_2_ = bf16[384,128]{1,0:T(8,128)(2,1)S(1)} collective-permute-done((bf16[384,128]{1,0:T(8,128)(2,1)S(1)}, bf16[384,128]{1,0:T(8,128)(2,1)S(1)}, u32[]{:S(2)}, u32[]{:S(2)}) %collective-permute-start.21) | collective-permute-done | bytes 98336 | tf_op jit(solution)/shard_map/ppermute | solution.py:431
  104.0 1.7 %collective-permute-start.22 = (bf16[384,128]{1,0:T(8,128)(2,1)S(1)}, bf16[384,128]{1,0:T(8,128)(2,1)S(1)}, u32[]{:S(2)}, u32[]{:S(2)}) collective-permute-start(bf16[384,128]{1,0:T(8,128)(2,1)S(1)} %collective-permute-done.21.refs_2_), channel_id=1, source_target_pairs={{0,1},{1,0},{2,3},{3,2},{4,5},{5,4},{6,7},{7,6},{8,9},{9,8},{10,11... | collective-permute-start | bytes 294920 | tf_op jit(solution)/shard_map/ppermute | solution.py:431
  105.8 4.6 %grad_input.1 = (bf16[512,1024]{1,0:T(8,128)(2,1)}, bf16[512,1024]{1,0:T(8,128)(2,1)}) custom-call(s32[6]{0:T(128)S(1)} %pad_add_fusion.where.place, bf16[512,384]{1,0:T(8,128)(2,1)S(1)} %get-tuple-element.119.refs_1_.refs_0_, bf16[512,384]{1,0:T(8,128)(2,1)S(1)} %collective-permute-done.7.refs_1_, bf16[512,384]{1,0:T(8,128)(2,1)S(1)} %collective-permute-done.11.refs_2_, ...), custom_call_target="tpu_custom_call" | custom-call | flops 1000 | bytes 1000 | tf_op jit(solution)/shard_map/grad_input/pallas_call | solution.py:389
  110.4 1.7 %finish.1 = (f32[128,256]{1,0:T(8,128)}, f32[128,256]{1,0:T(8,128)}, f32[128,1024]{1,0:T(8,128)}, f32[1,128]{1,0:T(1,128)}) custom-call(s32[6]{0:T(128)S(1)} %pad_add_fusion.where.place, bf16[384,128]{1,0:T(8,128)(2,1)S(1)} %get-tuple-element.152.refs_0_, bf16[384,128]{1,0:T(8,128)(2,1)S(1)} %collective-permute-done.20.refs_1_, ...), custom_call_target="tpu_custom_call" | custom-call | flops 1000 | bytes 1000 | tf_op jit(solution)/shard_map/finish/pallas_call | solution.py:389
  112.1 1.6 %hidden.1 = (f32[688,128]{1,0:T(8,128)}, f32[688,128]{1,0:T(8,128)}, f32[688,128]{1,0:T(8,128)}) custom-call(s32[6]{0:T(128)S(1)} %pad_add_fusion.where.place, bf16[1,1072,128]{2,1,0:T(8,128)(2,1)S(1)} %get-tuple-element.162.x_held, bf16[1,1072,128]{2,1,0:T(8,128)(2,1)S(1)} %collective-permute-done.23.x_come, ...), custom_call_target="tpu_custom_call" | custom-call | flops 1000 | bytes 1000 | tf_op jit(solution)/shard_map/hidden/pallas_call | solution.py:389
  (38 shorter events, 1.6 us)
Async XLA Ops:
  6.6 7.2 %collective-permute-start.1 = (bf16[512,256]{1,0:T(8,128)(2,1)S(1)}, bf16[512,256]{1,0:T(8,128)(2,1)S(1)}, u32[]{:S(2)}, u32[]{:S(2)}) collective-permute-start(bf16[512,256]{1,0:T(8,128)(2,1)S(1)} %get-tuple-element.121.ctx.refs_0_.ctx_in), channel_id=1, source_target_pairs={{0,2},{1,3},{2,0},{3,1},{4,6},{5,7},{6,4},{7,5},{8,10},{9,11},{10,... | collective-permute-start | bytes 786440 | tf_op jit(solution)/shard_map/ppermute | solution.py:431
  7.9 7.5 %collective-permute-start = (bf16[512,256]{1,0:T(8,128)(2,1)S(1)}, bf16[512,256]{1,0:T(8,128)(2,1)S(1)}, u32[]{:S(2)}, u32[]{:S(2)}) collective-permute-start(bf16[512,256]{1,0:T(8,128)(2,1)S(1)} %get-tuple-element.121.ctx.refs_0_.ctx_in), channel_id=1, source_target_pairs={{0,1},{1,0},{2,3},{3,2},{4,5},{5,4},{6,7},{7,6},{8,9},{9,8},{10,11... | collective-permute-start | bytes 786440 | tf_op jit(solution)/shard_map/ppermute | solution.py:431
  8.8 7.7 %copy-start.4 = (bf16[512,1024]{1,0:T(8,128)(2,1)S(1)}, bf16[512,1024]{1,0:T(8,128)(2,1)}, u32[]{:S(2)}) copy-start(bf16[512,1024]{1,0:T(8,128)(2,1)} %refs_5_.2) | copy-start | bytes 3145732
  8.8 7.7 %copy-start.6 = (f32[1024]{0:T(1024)S(1)}, f32[1024]{0:T(1024)}, u32[]{:S(2)}) copy-start(f32[1024]{0:T(1024)} %param.18) | copy-start | bytes 12292
  13.8 2.7 %collective-permute-start.2 = (bf16[512,256]{1,0:T(8,128)(2,1)S(1)}, bf16[512,256]{1,0:T(8,128)(2,1)S(1)}, u32[]{:S(2)}, u32[]{:S(2)}) collective-permute-start(bf16[512,256]{1,0:T(8,128)(2,1)S(1)} %collective-permute-done.1.refs_2_), channel_id=1, source_target_pairs={{0,1},{1,0},{2,3},{3,2},{4,5},{5,4},{6,7},{7,6},{8,9},{9,8},{10,11... | collective-permute-start | bytes 786440 | tf_op jit(solution)/shard_map/ppermute | solution.py:431
  22.5 2.0 %copy-start.1 = (bf16[512,1024]{1,0:T(8,128)(2,1)S(1)}, bf16[512,1024]{1,0:T(8,128)(2,1)}, u32[]{:S(2)}) copy-start(bf16[512,1024]{1,0:T(8,128)(2,1)} %refs_2_.3) | copy-start | bytes 3145732
  22.5 4.9 %collective-permute-start.3 = (bf16[256,1024]{1,0:T(8,128)(2,1)S(1)}, bf16[256,1024]{1,0:T(8,128)(2,1)S(1)}, u32[]{:S(2)}, u32[]{:S(2)}) collective-permute-start(bf16[256,1024]{1,0:T(8,128)(2,1)S(1)} %get-tuple-element.100), channel_id=1, source_target_pairs={{0,1},{1,0},{2,3},{3,2},{4,5},{5,4},{6,7},{7,6},{8,9},{9,8},{10,11... | collective-permute-start | bytes 1572872 | tf_op jit(solution)/shard_map/ppermute | solution.py:431
  25.9 5.5 %collective-permute-start.5 = (bf16[256,1024]{1,0:T(8,128)(2,1)S(1)}, bf16[256,1024]{1,0:T(8,128)(2,1)S(1)}, u32[]{:S(2)}, u32[]{:S(2)}) collective-permute-start(bf16[256,1024]{1,0:T(8,128)(2,1)S(1)} %get-tuple-element.110), channel_id=1, source_target_pairs={{0,1},{1,0},{2,3},{3,2},{4,5},{5,4},{6,7},{7,6},{8,9},{9,8},{10,11... | collective-permute-start | bytes 1572872 | tf_op jit(solution)/shard_map/ppermute | solution.py:431
  27.6 13.2 %collective-permute-start.4 = (bf16[256,1024]{1,0:T(8,128)(2,1)S(1)}, bf16[256,1024]{1,0:T(8,128)(2,1)S(1)}, u32[]{:S(2)}, u32[]{:S(2)}) collective-permute-start(bf16[256,1024]{1,0:T(8,128)(2,1)S(1)} %add_convert_fusion.3), channel_id=1, source_target_pairs={{0,2},{1,3},{2,0},{3,1},{4,6},{5,7},{6,4},{7,5},{8,10},{9,11},{10,... | collective-permute-start | bytes 1572872 | tf_op jit(solution)/shard_map/ppermute | solution.py:431
  28.9 23.4 %collective-permute-start.8 = (bf16[4,992,128]{2,1,0:T(8,128)(2,1)S(1)}, bf16[4,992,128]{2,1,0:T(8,128)(2,1)S(1)}, u32[]{:S(2)}, u32[]{:S(2)}) collective-permute-start(bf16[4,992,128]{2,1,0:T(8,128)(2,1)S(1)} %z_away.1), channel_id=1, source_target_pairs={{0,8},{4,12},{8,0},{12,4},{16,24},{20,28},{24,16},{28,20},{1,9},{5... | collective-permute-start | bytes 3047432 | tf_op jit(solution)/shard_map/ppermute | solution.py:431
  30.2 24.8 %collective-permute-start.13 = (bf16[4,1072,128]{2,1,0:T(8,128)(2,1)S(1)}, bf16[4,1072,128]{2,1,0:T(8,128)(2,1)S(1)}, u32[]{:S(2)}, u32[]{:S(2)}) collective-permute-start(bf16[4,1072,128]{2,1,0:T(8,128)(2,1)S(1)} %x_away.1), channel_id=1, source_target_pairs={{0,4},{4,0},{8,12},{12,8},{16,20},{20,16},{24,28},{28,24},{1,5},{5... | collective-permute-start | bytes 3293192 | tf_op jit(solution)/shard_map/ppermute | solution.py:431
  41.0 2.8 %collective-permute-start.6 = (bf16[256,1024]{1,0:T(8,128)(2,1)S(1)}, bf16[256,1024]{1,0:T(8,128)(2,1)S(1)}, u32[]{:S(2)}, u32[]{:S(2)}) collective-permute-start(bf16[256,1024]{1,0:T(8,128)(2,1)S(1)} %add_convert_fusion.1.own), channel_id=1, source_target_pairs={{0,1},{1,0},{2,3},{3,2},{4,5},{5,4},{6,7},{7,6},{8,9},{9,8},{10,11... | collective-permute-start | bytes 1572872 | tf_op jit(solution)/shard_map/ppermute | solution.py:431
  42.3 14.7 %collective-permute-start.12 = (bf16[256,1024]{1,0:T(8,128)(2,1)S(1)}, bf16[256,1024]{1,0:T(8,128)(2,1)S(1)}, u32[]{:S(2)}, u32[]{:S(2)}) collective-permute-start(bf16[256,1024]{1,0:T(8,128)(2,1)S(1)} %add_convert_fusion.2), channel_id=1, source_target_pairs={{0,2},{1,3},{2,0},{3,1},{4,6},{5,7},{6,4},{7,5},{8,10},{9,11},{10,... | collective-permute-start | bytes 1572872 | tf_op jit(solution)/shard_map/ppermute | solution.py:431
  50.3 19.1 %collective-permute-start.10 = (bf16[4,656,128]{2,1,0:T(8,128)(2,1)S(1)}, bf16[4,656,128]{2,1,0:T(8,128)(2,1)S(1)}, u32[]{:S(2)}, u32[]{:S(2)}) collective-permute-start(bf16[4,656,128]{2,1,0:T(8,128)(2,1)S(1)} %late_away.1), channel_id=1, source_target_pairs={{0,4},{4,0},{8,12},{12,8},{16,20},{20,16},{24,28},{28,24},{1,5},{5... | collective-permute-start | bytes 2015240 | tf_op jit(solution)/shard_map/ppermute | solution.py:431
  53.6 21.3 %collective-permute-start.9 = (bf16[2,992,128]{2,1,0:T(8,128)(2,1)S(1)}, bf16[2,992,128]{2,1,0:T(8,128)(2,1)S(1)}, u32[]{:S(2)}, u32[]{:S(2)}) collective-permute-start(bf16[2,992,128]{2,1,0:T(8,128)(2,1)S(1)} %get-tuple-element.126), channel_id=1, source_target_pairs={{0,16},{4,20},{8,24},{12,28},{16,0},{20,4},{24,8},{28,12},{1,17},{... | collective-permute-start | bytes 1523720 | tf_op jit(solution)/shard_map/ppermute | solution.py:431
  53.7 8.8 %collective-permute-start.11 = (bf16[512,384]{1,0:T(8,128)(2,1)S(1)}, bf16[512,384]{1,0:T(8,128)(2,1)S(1)}, u32[]{:S(2)}, u32[]{:S(2)}) collective-permute-start(bf16[512,384]{1,0:T(8,128)(2,1)S(1)} %get-tuple-element.119.refs_1_.refs_0_), channel_id=1, source_target_pairs={{0,2},{1,3},{2,0},{3,1},{4,6},{5,7},{6,4},{7,5},{8,10},{9,11},{10,... | collective-permute-start | bytes 1179656 | tf_op jit(solution)/shard_map/ppermute | solution.py:431
  56.4 24.4 %collective-permute-start.19 = (bf16[2,1072,128]{2,1,0:T(8,128)(2,1)S(1)}, bf16[2,1072,128]{2,1,0:T(8,128)(2,1)S(1)}, u32[]{:S(2)}, u32[]{:S(2)}) collective-permute-start(bf16[2,1072,128]{2,1,0:T(8,128)(2,1)S(1)} %get-tuple-element.128), channel_id=1, source_target_pairs={{0,8},{4,12},{8,0},{12,4},{16,24},{20,28},{24,16},{28,20},{1,9},{5... | collective-permute-start | bytes 1646600 | tf_op jit(solution)/shard_map/ppermute | solution.py:431
  57.0 22.4 %collective-permute-start.7 = (bf16[512,384]{1,0:T(8,128)(2,1)S(1)}, bf16[512,384]{1,0:T(8,128)(2,1)S(1)}, u32[]{:S(2)}, u32[]{:S(2)}) collective-permute-start(bf16[512,384]{1,0:T(8,128)(2,1)S(1)} %get-tuple-element.119.refs_1_.refs_0_), channel_id=1, source_target_pairs={{0,1},{1,0},{2,3},{3,2},{4,5},{5,4},{6,7},{7,6},{8,9},{9,8},{10,11... | collective-permute-start | bytes 1179656 | tf_op jit(solution)/shard_map/ppermute | solution.py:431
  70.5 15.3 %collective-permute-start.16 = (bf16[656,128]{1,0:T(8,128)(2,1)S(1)}, bf16[656,128]{1,0:T(8,128)(2,1)S(1)}, u32[]{:S(2)}, u32[]{:S(2)}) collective-permute-start(bf16[656,128]{1,0:T(8,128)(2,1)S(1)} %get-tuple-element.139), channel_id=1, source_target_pairs={{0,16},{4,20},{8,24},{12,28},{16,0},{20,4},{24,8},{28,12},{1,17},{... | collective-permute-start | bytes 503816 | tf_op jit(solution)/shard_map/ppermute | solution.py:431
  70.7 15.3 %collective-permute-start.17 = (bf16[656,128]{1,0:T(8,128)(2,1)S(1)}, bf16[656,128]{1,0:T(8,128)(2,1)S(1)}, u32[]{:S(2)}, u32[]{:S(2)}) collective-permute-start(bf16[656,128]{1,0:T(8,128)(2,1)S(1)} %get-tuple-element.140), channel_id=1, source_target_pairs={{0,8},{4,12},{8,0},{12,4},{16,24},{20,28},{24,16},{28,20},{1,9},{5... | collective-permute-start | bytes 503816 | tf_op jit(solution)/shard_map/ppermute | solution.py:431
  74.9 24.4 %collective-permute-start.18 = (bf16[656,128]{1,0:T(8,128)(2,1)S(1)}, bf16[656,128]{1,0:T(8,128)(2,1)S(1)}, u32[]{:S(2)}, u32[]{:S(2)}) collective-permute-start(bf16[656,128]{1,0:T(8,128)(2,1)S(1)} %get-tuple-element.132), channel_id=1, source_target_pairs={{0,24},{4,28},{8,16},{12,20},{16,8},{20,12},{24,0},{28,4},{1,25},{... | collective-permute-start | bytes 503816 | tf_op jit(solution)/shard_map/ppermute | solution.py:431
  79.5 26.3 %collective-permute-start.15 = (bf16[256,1024]{1,0:T(8,128)(2,1)S(1)}, bf16[256,1024]{1,0:T(8,128)(2,1)S(1)}, u32[]{:S(2)}, u32[]{:S(2)}) collective-permute-start(bf16[256,1024]{1,0:T(8,128)(2,1)S(1)} %add_convert_fusion.refs_7_), channel_id=1, source_target_pairs={{0,1},{1,0},{2,3},{3,2},{4,5},{5,4},{6,7},{7,6},{8,9},{9,8},{10,11... | collective-permute-start | bytes 1572872 | tf_op jit(solution)/shard_map/ppermute | solution.py:431
  80.8 19.8 %collective-permute-start.14 = (bf16[512,384]{1,0:T(8,128)(2,1)S(1)}, bf16[512,384]{1,0:T(8,128)(2,1)S(1)}, u32[]{:S(2)}, u32[]{:S(2)}) collective-permute-start(bf16[512,384]{1,0:T(8,128)(2,1)S(1)} %collective-permute-done.11.refs_2_), channel_id=1, source_target_pairs={{0,1},{1,0},{2,3},{3,2},{4,5},{5,4},{6,7},{7,6},{8,9},{9,8},{10,11... | collective-permute-start | bytes 1179656 | tf_op jit(solution)/shard_map/ppermute | solution.py:431
  85.8 26.3 %collective-permute-start.24 = (bf16[1,992,128]{2,1,0:T(8,128)(2,1)S(1)}, bf16[1,992,128]{2,1,0:T(8,128)(2,1)S(1)}, u32[]{:S(2)}, u32[]{:S(2)}) collective-permute-start(bf16[1,992,128]{2,1,0:T(8,128)(2,1)S(1)} %get-tuple-element.134), channel_id=1, source_target_pairs={{0,4},{4,0},{8,12},{12,8},{16,20},{20,16},{24,28},{28,24},{1,5},{5... | collective-permute-start | bytes 761864 | tf_op jit(solution)/shard_map/ppermute | solution.py:431
  86.0 26.1 %collective-permute-start.23 = (bf16[1,1072,128]{2,1,0:T(8,128)(2,1)S(1)}, bf16[1,1072,128]{2,1,0:T(8,128)(2,1)S(1)}, u32[]{:S(2)}, u32[]{:S(2)}) collective-permute-start(bf16[1,1072,128]{2,1,0:T(8,128)(2,1)S(1)} %get-tuple-element.143), channel_id=1, source_target_pairs={{0,16},{4,20},{8,24},{12,28},{16,0},{20,4},{24,8},{28,12},{1,17},{... | collective-permute-start | bytes 823304 | tf_op jit(solution)/shard_map/ppermute | solution.py:431
  99.3 6.5 %copy-start = (bf16[1024,1024]{1,0:T(8,128)(2,1)S(1)}, bf16[1024,1024]{1,0:T(8,128)(2,1)}, u32[]{:S(2)}) copy-start(bf16[1024,1024]{1,0:T(8,128)(2,1)} %refs_7_.1) | copy-start | bytes 6291460
  99.3 6.5 %copy-start.2 = (bf16[1024,256]{1,0:T(8,128)(2,1)S(1)}, bf16[1024,256]{1,0:T(8,128)(2,1)}, u32[]{:S(2)}) copy-start(bf16[1024,256]{1,0:T(8,128)(2,1)} %refs_5_.3) | copy-start | bytes 1572868
  99.3 6.5 %copy-start.3 = (bf16[1024,256]{1,0:T(8,128)(2,1)S(1)}, bf16[1024,256]{1,0:T(8,128)(2,1)}, u32[]{:S(2)}) copy-start(bf16[1024,256]{1,0:T(8,128)(2,1)} %refs_6_.1) | copy-start | bytes 1572868
  99.3 6.5 %copy-start.5 = (f32[1024]{0:T(1024)S(1)}, f32[1024]{0:T(1024)}, u32[]{:S(2)}) copy-start(f32[1024]{0:T(1024)} %param.13) | copy-start | bytes 12292
  100.5 3.5 %collective-permute-start.21 = (bf16[384,128]{1,0:T(8,128)(2,1)S(1)}, bf16[384,128]{1,0:T(8,128)(2,1)S(1)}, u32[]{:S(2)}, u32[]{:S(2)}) collective-permute-start(bf16[384,128]{1,0:T(8,128)(2,1)S(1)} %get-tuple-element.152.refs_0_), channel_id=1, source_target_pairs={{0,2},{1,3},{2,0},{3,1},{4,6},{5,7},{6,4},{7,5},{8,10},{9,11},{10,... | collective-permute-start | bytes 294920 | tf_op jit(solution)/shard_map/ppermute | solution.py:431
  100.5 9.8 %collective-permute-start.20 = (bf16[384,128]{1,0:T(8,128)(2,1)S(1)}, bf16[384,128]{1,0:T(8,128)(2,1)S(1)}, u32[]{:S(2)}, u32[]{:S(2)}) collective-permute-start(bf16[384,128]{1,0:T(8,128)(2,1)S(1)} %get-tuple-element.152.refs_0_), channel_id=1, source_target_pairs={{0,1},{1,0},{2,3},{3,2},{4,5},{5,4},{6,7},{7,6},{8,9},{9,8},{10,11... | collective-permute-start | bytes 294920 | tf_op jit(solution)/shard_map/ppermute | solution.py:431
  104.0 6.4 %collective-permute-start.22 = (bf16[384,128]{1,0:T(8,128)(2,1)S(1)}, bf16[384,128]{1,0:T(8,128)(2,1)S(1)}, u32[]{:S(2)}, u32[]{:S(2)}) collective-permute-start(bf16[384,128]{1,0:T(8,128)(2,1)S(1)} %collective-permute-done.21.refs_2_), channel_id=1, source_target_pairs={{0,1},{1,0},{2,3},{3,2},{4,5},{5,4},{6,7},{7,6},{8,9},{9,8},{10,11... | collective-permute-start | bytes 294920 | tf_op jit(solution)/shard_map/ppermute | solution.py:431

commit v6 on v5

--- a/solution.py
+++ b/solution.py
@@ -13,7 +13,7 @@
 EPSILON = 1e-05
 F32 = jnp.float32
 BF16 = jnp.bfloat16
-COSTS = {"feed": 3000000000, "late": 10000000000}
+COSTS = {"feed": 3000000000, "grad_input": 1000, "hidden": 10000000000, "late": 3000000000}
 VMEM_LIMIT = 20 * 1024 * 1024
 
 
@@ -49,7 +49,7 @@
 
 def bounds_of(where):
     bounds, total = [], 0
-    for slot in range(2, where.shape[0]):
+    for slot in range(2, len(where) if isinstance(where, tuple) else where.shape[0]):
         total = total + where[slot]
         bounds.append(total)
     return bounds
@@ -97,14 +97,13 @@
     return jnp.concatenate([block_columns(ref, group ^ r, chunk) for r in offsets], axis=1)
 
 
-def attend_kernel(
-    where, tok, gain, w_query, w_key, w_value, *refs
-):
+def attend_kernel(lengths, tok, gain, w_query, w_key, w_value, *refs):
     n_out, q_out, k_out, v_out, ctx_out, den_out = refs
     rows = tok.shape[0]
     hq, hv = q_out.shape[1], v_out.shape[1]
     block = rows // 2
-    feat = where[0]
+    feat = lax.axis_index("feat")
+    where = (0, 0, *[lengths[0, i] for i in range(lengths.shape[1])])
     x = tok[...].astype(F32)
     r = lax.rsqrt(jnp.mean(x * x, axis=1, keepdims=True) + EPSILON)
     n = (x * r * gain[...]).astype(BF16)
@@ -118,22 +117,27 @@
     q_out[...] = q
     k_out[...] = k
     bounds = bounds_of(where)
+    start = starts_of(bounds, lax.broadcasted_iota(jnp.int32, (rows, 1), 0))
+    number = [jnp.zeros((block, hv), F32) for _ in range(2)]
+    total = [jnp.zeros((block, hv), F32) for _ in range(2)]
     for part in range(2):
         low, high = part * block, (part + 1) * block
-        row = lax.broadcasted_iota(jnp.int32, (block, high), 0) + low
-        col = lax.broadcasted_iota(jnp.int32, (block, high), 1)
-        start = starts_of(bounds, lax.broadcasted_iota(jnp.int32, (block, 1), 0) + low)
-        allowed = (col <= row) & (col >= start)
-        number = jnp.zeros((block, hv), F32)
-        total = jnp.zeros((block, hv), F32)
+        row = lax.broadcasted_iota(jnp.int32, (rows - low, block), 0) + low
+        col = lax.broadcasted_iota(jnp.int32, (rows - low, block), 1) + low
+        allowed = (col <= row) & (col >= start[low:])
         for head in range(hq // QK):
-            t = dot_nt(only_head(q[low:high], QK, head), k[:high]) + 1.0
-            p = jnp.where(allowed, t * t + 1.0, 0.0).astype(BF16)
-            number = number + dot(p, only_head(v[:high], VD, head))
-            ones = jnp.where(lane_mask((high, hv), VD, head), 1.0, 0.0).astype(BF16)
-            total = total + dot(p, ones)
-        ctx_out[low:high, :] = (number / total).astype(BF16)
-        den_out[low:high, :] = total
+            t = dot_nt(only_head(q[low:], QK, head), k[low:high]) + 1.0
+            exact = jnp.where(allowed, t * t + 1.0, 0.0)
+            p = exact.astype(BF16)
+            part_number = dot(p, only_head(v[low:high], VD, head))
+            part_total = jnp.where(lane_mask((rows - low, hv), VD, head), jnp.sum(exact, axis=1, keepdims=True), 0.0)
+            for i in range(part, 2):
+                here = slice(i * block - low, (i + 1) * block - low)
+                number[i] = number[i] + part_number[here]
+                total[i] = total[i] + part_total[here]
+    for i in range(2):
+        ctx_out[i * block : (i + 1) * block, :] = (number[i] / total[i]).astype(BF16)
+        den_out[i * block : (i + 1) * block, :] = total[i]
 
 
 def fetch_kernel(where, ctx, cot, *refs):
@@ -208,6 +212,12 @@
         low = high
 
 
+def aways_kernel(where, inner, gate, up, cot, normed, w_down, x_out, z_out, feed_away, feed_own, *, x_fixed, z_fixed):
+    away_kernel(where, inner, gate, cot, normed, x_out, **x_fixed)
+    away_kernel(where, gate, up, normed, z_out, **z_fixed)
+    down_kernel(where, inner, w_down, feed_away, feed_own)
+
+
 def keep_kernel(where, *refs, pairs, order, chunk):
     arrived, keep_out, away_out = refs[-3:]
     offsets = positions(order)
@@ -266,8 +276,28 @@
     own_out[...] = total[many + 16 :].astype(BF16)
 
 
+def prepare_kernel(where, q_in, k_in, res, p_out, t_out, r_out):
+    rows, hq = q_in.shape
+    half = rows // 2
+    bounds = bounds_of(where)
+    residual = res[...]
+    r_out[...] = lax.rsqrt(jnp.mean(residual * residual, axis=1, keepdims=True) + EPSILON)
+    q, k = q_in[...], k_in[...]
+    for part in range(2):
+        low, high = part * half, (part + 1) * half
+        row = lax.broadcasted_iota(jnp.int32, (high, half), 0)
+        col = lax.broadcasted_iota(jnp.int32, (high, half), 1) + low
+        start = starts_of(bounds, lax.broadcasted_iota(jnp.int32, (1, half), 1) + low)
+        allowed = (row <= col) & (row >= start)
+        for head in range(hq // QK):
+            t = dot_nt(k[:high], only_head(q[low:high], QK, head)) + 1.0
+            here = slice(part * half, part * half + high)
+            p_out[head, here, :] = jnp.where(allowed, t * t + 1.0, 0.0).astype(BF16)
+            t_out[head, here, :] = jnp.where(allowed, t, 0.0).astype(BF16)
+
+
 def back_kernel(
-    place, own, other, res, cot, gain, w_own, q_in, k_in, v_in, ctx_in, den_in,
+    place, own, other, res, r_in, cot, gain, w_own, q_in, k_in, v_in, ctx_in, den_in, p_in, t_in,
     gr_out, gm_out, g_out, gain_out, gctx,
 ):
     rows = res.shape[0]
@@ -280,8 +310,7 @@
         here = pl.ds(pl.multiple_of(which * half, half), half)
         live = (lax.broadcasted_iota(jnp.int32, (half, 1), 0) + which * half < bounds[-1]).astype(F32)
         e = source[...].astype(F32)
-        residual = res[here, :]
-        r = lax.rsqrt(jnp.mean(residual * residual, axis=1, keepdims=True) + EPSILON)
+        residual, r = res[here, :], r_in[here, :]
         weighted = e * gain[...]
         gain_sum = gain_sum + jnp.sum(e * residual * r, axis=0, keepdims=True)
         scale = r * r * r * jnp.mean(weighted * residual, axis=1, keepdims=True)
@@ -302,32 +331,27 @@
     select = jnp.where(select, 1.0, 0.0).astype(BF16)
     shift = dot_nt(select, leading) + dot_nt(select, remainder)
     q, k, v = q_in[...], k_in[...], v_in[...]
-    gq = [jnp.zeros((half, hq), F32) for _ in range(2)]
+    gk = [jnp.zeros((half, hq), F32) for _ in range(2)]
+    gv = [jnp.zeros((half, hv), F32) for _ in range(2)]
     for part in range(2):
         low, high = part * half, (part + 1) * half
-        row = lax.broadcasted_iota(jnp.int32, (half, rows - low), 0) + low
-        col = lax.broadcasted_iota(jnp.int32, (half, rows - low), 1) + low
-        start = starts_of(bounds, lax.broadcasted_iota(jnp.int32, (1, rows - low), 1) + low)
-        allowed = (row <= col) & (row >= start)
-        gk = jnp.zeros((half, hq), F32)
-        gv = jnp.zeros((half, hv), F32)
+        gq = jnp.zeros((half, hq), F32)
         for head in range(hq // QK):
-            q_head = only_head(q[low:], QK, head)
-            g_head = only_head(gn[low:], VD, head)
-            t = dot_nt(k[low:high], q_head) + 1.0
-            p = jnp.where(allowed, t * t + 1.0, 0.0).astype(BF16)
-            g = dot_nt(v[low:high], g_head) - shift[head : head + 1, low:]
-            ds = jnp.where(allowed, g * t, 0.0).astype(BF16)
-            gv = gv + dot(p, g_head)
-            gk = gk + dot(ds, q_head)
-            k_head = only_head(k[low:high], QK, head)
-            for second in range(part, 2):
-                piece = ds[:, second * half - low : (second + 1) * half - low]
-                gq[second] = gq[second] + dot_tn(piece, k_head)
-        g_out[low:high, :hv] = gv.astype(BF16)
-        g_out[low:high, hv + hq :] = (gk * 2.0).astype(BF16)
-    for part in range(2):
-        g_out[part * half : (part + 1) * half, hv : hv + hq] = (gq[part] * (2.0 * QK**-0.5)).astype(BF16)
+            q_head = only_head(q[low:high], QK, head)
+            g_head = only_head(gn[low:high], VD, head)
+            p = p_in[head, part * half : part * half + high, :]
+            t = t_in[head, part * half : part * half + high, :]
+            g = dot_nt(v[:high], g_head) - shift[head : head + 1, low:high]
+            ds = (g * t.astype(F32)).astype(BF16)
+            part_gv, part_gk = dot(p, g_head), dot(ds, q_head)
+            for j in range(part + 1):
+                gv[j] = gv[j] + part_gv[j * half : (j + 1) * half]
+                gk[j] = gk[j] + part_gk[j * half : (j + 1) * half]
+            gq = gq + dot_tn(ds, only_head(k[:high], QK, head))
+        g_out[low:high, hv : hv + hq] = (gq * (2.0 * QK**-0.5)).astype(BF16)
+    for j in range(2):
+        g_out[j * half : (j + 1) * half, :hv] = gv[j].astype(BF16)
+        g_out[j * half : (j + 1) * half, hv + hq :] = (gk[j] * 2.0).astype(BF16)
 
 
 def input_kernel(place, *refs, share, hv, hq):
@@ -453,24 +477,35 @@
         return (array.astype(F32) + come.astype(F32)).astype(BF16)
 
     wide = max(hq, 128)
-    near = pl.BlockSpec((width, wide), lambda i, p: (0, p[0] * hq // wide))
     anywhere = pl.BlockSpec(memory_space=pl.ANY)
     later = [w_down, w_out, w_gate, w_up]
-    normed, q, k, v, ctx, den = call(
+    near = pl.BlockSpec((width, wide), lambda i: (0, lax.axis_index("feat") * hq // wide))
+    attend_args = [in_hbm(a) for a in (lengths, tokens, gain_a, w_query, w_key, w_value)]
+    attend_shapes = [
+        vmem_of(rows, width, BF16),
+        vmem_of(rows, hq, BF16),
+        vmem_of(rows, hq, BF16),
+        vmem_of(rows, hv, BF16),
+        vmem_of(rows, hv, BF16),
+        vmem_of(rows, hv, F32),
+    ]
+    normed, q, k, v, ctx, den = pl.pallas_call(
         attend_kernel,
-        "attend",
-        where,
-        [in_hbm(a) for a in (tokens, gain_a, w_query, w_key, w_value)],
-        [
-            vmem_of(rows, width, BF16),
-            vmem_of(rows, hq, BF16),
-            vmem_of(rows, hq, BF16),
-            vmem_of(rows, hv, BF16),
-            vmem_of(rows, hv, BF16),
-            vmem_of(rows, hv, F32),
+        grid=(1,),
+        in_specs=[
+            pl.BlockSpec(memory_space=pltpu.SMEM),
+            whole(tokens),
+            whole(gain_a),
+            near,
+            near,
+            pl.BlockSpec((width, hv), lambda i: (0, lax.axis_index("feat"))),
         ],
-        specs={2: near, 3: near, 4: pl.BlockSpec((width, hv), lambda i, p: (0, p[0]))},
-    )
+        out_specs=[whole(a) for a in attend_shapes],
+        out_shape=attend_shapes,
+        compiler_params=params(),
+        cost_estimate=pl.CostEstimate(flops=1000, bytes_accessed=1000, transcendentals=0),
+        name="attend",
+    )(*attend_args)
     whole_vmem = pl.BlockSpec(memory_space=pltpu.VMEM)
     w_down, w_out, w_gate, w_up, ginner = call(
         fetch_kernel,
@@ -524,48 +559,53 @@
         return held, come, sent
 
     last = back_own
-    feed_away, feed_own = call(
-        down_kernel, "down", where, [*after([inner], last), w_down], [shape_of(half, width, BF16)] * 2
-    )
-    last = feed_own
-    [x_sent] = call(
-        away_kernel,
-        "x_away",
-        where,
-        [*after(x_args[:1], last), *x_args[1:]],
-        [shape_of(2 * few, x_many, chunk, BF16)],
-        **x_fixed,
-    )
-    last = x_sent
-    [z_sent] = call(
-        away_kernel,
-        "z_away",
-        where,
-        [*after(z_args[:1], last), *z_args[1:]],
-        [shape_of(2 * few, z_many, chunk, BF16)],
-        **z_fixed,
+    x_sent, z_sent, feed_away, feed_own = call(
+        aways_kernel,
+        "aways",
+        where,
+        [inner, grad_gate, grad_up, cotangent, normed_two, w_down],
+        [
+            shape_of(2 * few, x_many, chunk, BF16),
+            shape_of(2 * few, z_many, chunk, BF16),
+            shape_of(half, width, BF16),
+            shape_of(half, width, BF16),
+        ],
+        x_fixed=x_fixed,
+        z_fixed=z_fixed,
     )
     last = z_sent
     [come] = after([swap(back_away, "feat", 1)], last)
     last = back_own = plus(back_own, come)
-    [come] = after([swap(feed_away, "feat", 1)], last)
-    last = feed_own = plus(feed_own, come)
+    scores, slopes, r_two = call(
+        prepare_kernel,
+        "prepare",
+        where,
+        [*after([q], last), k, residual],
+        [
+            vmem_of(hq // QK, 3 * half, half, BF16),
+            vmem_of(hq // QK, 3 * half, half, BF16),
+            vmem_of(rows, 1, F32),
+        ],
+    )
+    last = scores
     for mask in feat_masks[:-1]:
         [come] = after([swap(back_own, "feat", mask)], last)
         last = back_own = plus(back_own, come)
+    [come] = after([swap(feed_away, "feat", 1)], last)
+    last = feed_own = plus(feed_own, come)
     [back_other] = after([swap(back_own, "feat", 1)], last)
     grad_res, grad_mixed, grads, gain_part = call(
         back_kernel,
         "back",
         where,
-        [back_own, back_other, residual, cotangent, gain_b, w_out, q, k, v, ctx, den],
+        [back_own, back_other, residual, r_two, cotangent, gain_b, w_out, q, k, v, ctx, den, scores, slopes],
         [
             vmem_of(rows, width, F32),
             vmem_of(rows, width, BF16),
             vmem_of(rows, pack, BF16),
             shape_of(1, width, F32),
         ],
-        specs={5: pl.BlockSpec((hv, width), lambda i, p: (p[0], 0))},
+        specs={6: pl.BlockSpec((hv, width), lambda i, p: (p[0], 0))},
         scratch=[pltpu.VMEM((rows, hv), BF16)],
     )
     last = gain_part
@@ -613,10 +653,10 @@
     comes = [swap(piece, "dp", offset) for offset, piece in zip(positions(x_first)[1:], direct)]
     last = direct[-1]
     z_held, z_come, last = hops("z_hop", z_held, z_sent, z_order[1:], last)
+    x_held, x_come, last = hops("x_hop", x_held, x_sent, x_first[1:], last)
     for j in list(held):
         [held[j ^ 1]] = after([swap(held[j], "feat", 1)], last)
     last = held[1]
-    x_held, x_come, last = hops("x_hop", x_held, x_sent, x_first[1:], last)
     sum_out, sum_gain_two, sum_own = call(
         late_kernel,
         "late",
@@ -650,6 +690,11 @@
         hq=hq,
     )
     last = grad_input
+    x_come, z_come = after([x_come, z_come], last)
+    sum_down, sum_gate, sum_up = call(
+        hidden_kernel, "hidden", where, [x_held, x_come, z_held, z_come], [shape_of(hidden, chunk, F32)] * 3
+    )
+    last = sum_down
     for j in list(sums):
         sums[j ^ 1] = swap(sums[j], "feat", 1)
 
@@ -677,11 +722,6 @@
         hq=hq,
     )
     last = sum_query
-    x_come, z_come = after([x_come, z_come], last)
-    sum_down, sum_gate, sum_up = call(
-        hidden_kernel, "hidden", where, [x_held, x_come, z_held, z_come], [shape_of(hidden, chunk, F32)] * 3
-    )
-    last = sum_down
 
     return (
         output,

time: 114 us -> 107 us (0.939)
  the two profiles are of different devices: /device:TPU:17 before, /device:TPU:0 now
where the time goes in v6:
time: 107 us
  waiting for transfers between devices  43.2 us (40%)
  Pallas kernels  38.8 us (36%)
  starting transfers between devices  23.3 us (22%)
    ppermute x25, waiting for transfers between devices, swap(): return lax.ppermute(array, axis, [(i, i ^ mask) for i in range(count)])  43.2 us
    pallas_call x15, Pallas kernels, call(): pl.pallas_call(functools.partial(kernel, **fixed) if fixed else kernel, g...  34.9 us
    ppermute x25, starting transfers between devices, swap(): return lax.ppermute(array, axis, [(i, i ^ mask) for i in range(count)])  23.3 us
    pallas_call x1, Pallas kernels, local(): pl.pallas_call(attend_kernel, grid=(1,), in_specs=[pl.BlockSpec(memory_sp...  3.94 us
  transfers between devices with their start and end apart: 25, of which 11 were waited for; matrix products, arithmetic and copies ran while one was open for 1% of the time, Pallas kernels for 25%

profile of v6, /device:TPU:0, one launch (start us, length us, event | category | flops | bytes accessed | tf_op | source)
XLA Modules:
  0.0 107.2 jit_solution(7232283227233858342)
XLA Ops:
  0.7 3.9 %attend.1 = (bf16[512,1024]{1,0:T(8,128)(2,1)S(1)}, bf16[512,64]{1,0:T(8,128)(2,1)S(1)}, bf16[512,64]{1,0:T(8,128)(2,1)S(1)}, bf16[512,256]{1,0:T(8,128)(2,1)S(1...) custom-call(s32[1,4]{1,0:T(1,128)} %lengths.1, bf16[512,1024]{1,0:T(8,128)(2,1)} %refs_5_.2, f32[1,1024]{1,0:T(1,128)} %bitcast.11, ...), custom_call_target="tpu_custom_call" | custom-call | flops 1000 | bytes 1000 | tf_op jit(solution)/shard_map/attend/pallas_call | solution.py:492
  4.6 3.0 %collective-permute-start.1 = (bf16[512,256]{1,0:T(8,128)(2,1)S(1)}, bf16[512,256]{1,0:T(8,128)(2,1)S(1)}, u32[]{:S(2)}, u32[]{:S(2)}) collective-permute-start(bf16[512,256]{1,0:T(8,128)(2,1)S(1)} %get-tuple-element.127.ctx.refs_0_.ctx_in), channel_id=1, source_target_pairs={{0,2},{1,3},{2,0},{3,1},{4,6},{5,7},{6,4},{7,5},{8,10},{9,11},{10,... | collective-permute-start | bytes 786440 | tf_op jit(solution)/shard_map/ppermute | solution.py:455
  7.7 4.6 %fetch.1 = (bf16[688,1024]{1,0:T(8,128)(2,1)S(1)}, bf16[1024,1024]{1,0:T(8,128)(2,1)S(1)}, bf16[688,1024]{1,0:T(8,128)(2,1)S(1)}, bf16[688,1024]{1,0:T(8,128)(2,1)S(1)}, f32[512,688]{1,0:T(8,128)S(1)}) custom-call(s32[6]{0:T(128)S(1)} %pad_add_fusion.where.place, bf16[512,256]{1,0:T(8,128)(2,1)S(1)} %get-tuple-element.127.ctx.refs_0_.ctx_in, ...), custom_call_target="tpu_custom_call" | custom-call | flops 1000 | bytes 1000 | tf_op jit(solution)/shard_map/fetch/pallas_call | solution.py:413
  12.4 1.6 %collective-permute-done.1.refs_2_ = bf16[512,256]{1,0:T(8,128)(2,1)S(1)} collective-permute-done((bf16[512,256]{1,0:T(8,128)(2,1)S(1)}, bf16[512,256]{1,0:T(8,128)(2,1)S(1)}, u32[]{:S(2)}, u32[]{:S(2)}) %collective-permute-start.1) | collective-permute-done | bytes 262176 | tf_op jit(solution)/shard_map/ppermute | solution.py:455
  13.9 1.5 %collective-permute-done.2.refs_3_ = bf16[512,256]{1,0:T(8,128)(2,1)S(1)} collective-permute-done((bf16[512,256]{1,0:T(8,128)(2,1)S(1)}, bf16[512,256]{1,0:T(8,128)(2,1)S(1)}, u32[]{:S(2)}, u32[]{:S(2)}) %collective-permute-start.2) | collective-permute-done | bytes 262176 | tf_op jit(solution)/shard_map/ppermute | solution.py:455
  15.5 6.0 %feed.1 = (f32[512,1024]{1,0:T(8,128)S(1)}, bf16[512,1024]{1,0:T(8,128)(2,1)S(1)}, bf16[512,688]{1,0:T(8,128)(2,1)S(1)}, bf16[512,688]{1,0:T(8,128)(2,1)S(1)}, b...) custom-call(s32[6]{0:T(128)S(1)} %pad_add_fusion.where.place, ...), custom_call_target="tpu_custom_call" | custom-call | flops 3000000000 | bytes 1000 | tf_op jit(solution)/shard_map/feed/pallas_call | solution.py:413
  21.5 0.2 collective-permute-start.3
  21.7 2.8 %aways.1 = (bf16[4,1072,128]{2,1,0:T(8,128)(2,1)S(1)}, bf16[4,992,128]{2,1,0:T(8,128)(2,1)S(1)}, bf16[256,1024]{1,0:T(8,128)(2,1)S(1)}, bf16[256,1024]{1,0:T(8,128)(2,1)S(1)}) custom-call(s32[6]{0:T(128)S(1)} %pad_add_fusion.where.place, bf16[512,688]{1,0:T(8,128)(2,1)S(1)} %get-tuple-element.104.inner.refs_0_, ...), custom_call_target="tpu_custom_call" | custom-call | flops 1000 | bytes 1000 | tf_op jit(solution)/shard_map/aways/pallas_call | solution.py:413
  24.5 0.2 add_convert_fusion.3
  24.7 1.8 %collective-permute-start.4 = (bf16[256,1024]{1,0:T(8,128)(2,1)S(1)}, bf16[256,1024]{1,0:T(8,128)(2,1)S(1)}, u32[]{:S(2)}, u32[]{:S(2)}) collective-permute-start(bf16[256,1024]{1,0:T(8,128)(2,1)S(1)} %add_convert_fusion.3), channel_id=1, source_target_pairs={{0,2},{1,3},{2,0},{3,1},{4,6},{5,7},{6,4},{7,5},{8,10},{9,11},{10,... | collective-permute-start | bytes 1572872 | tf_op jit(solution)/shard_map/ppermute | solution.py:455
  26.6 1.6 %collective-permute-start.9 = (bf16[4,992,128]{2,1,0:T(8,128)(2,1)S(1)}, bf16[4,992,128]{2,1,0:T(8,128)(2,1)S(1)}, u32[]{:S(2)}, u32[]{:S(2)}) collective-permute-start(bf16[4,992,128]{2,1,0:T(8,128)(2,1)S(1)} %get-tuple-element.108), channel_id=1, source_target_pairs={{0,8},{4,12},{8,0},{12,4},{16,24},{20,28},{24,16},{28,20},{1,9},{5... | collective-permute-start | bytes 3047432 | tf_op jit(solution)/shard_map/ppermute | solution.py:455
  28.1 1.5 %collective-permute-start.8 = (bf16[4,1072,128]{2,1,0:T(8,128)(2,1)S(1)}, bf16[4,1072,128]{2,1,0:T(8,128)(2,1)S(1)}, u32[]{:S(2)}, u32[]{:S(2)}) collective-permute-start(bf16[4,1072,128]{2,1,0:T(8,128)(2,1)S(1)} %get-tuple-element.125), channel_id=1, source_target_pairs={{0,4},{4,0},{8,12},{12,8},{16,20},{20,16},{24,28},{28,24},{1,5},{5... | collective-permute-start | bytes 3293192 | tf_op jit(solution)/shard_map/ppermute | solution.py:455
  29.6 1.6 %prepare.1 = (bf16[4,768,256]{2,1,0:T(8,128)(2,1)S(1)}, bf16[4,768,256]{2,1,0:T(8,128)(2,1)S(1)}, f32[512,1]{1,0:T(8,128)S(1)}) custom-call(s32[6]{0:T(128)S(1)} %pad_add_fusion.where.place, bf16[512,64]{1,0:T(8,128)(2,1)S(1)} %get-tuple-element.111.q_in, bf16[512,64]{1,0:T(8,128)(2,1)S(1)} %get-tuple-element.112.k_in, ...), custom_call_target="tpu_custom_call" | custom-call | flops 1000 | bytes 1000 | tf_op jit(solution)/shard_map/prepare/pallas_call | solution.py:413
  31.2 7.8 %collective-permute-done.4 = bf16[256,1024]{1,0:T(8,128)(2,1)S(1)} collective-permute-done((bf16[256,1024]{1,0:T(8,128)(2,1)S(1)}, bf16[256,1024]{1,0:T(8,128)(2,1)S(1)}, u32[]{:S(2)}, u32[]{:S(2)}) %collective-permute-start.4) | collective-permute-done | bytes 524320 | tf_op jit(solution)/shard_map/ppermute | solution.py:455
  38.9 0.2 add_convert_fusion.2.own
  39.2 0.2 add_convert_fusion.1
  39.4 1.8 %collective-permute-start.14 = (bf16[256,1024]{1,0:T(8,128)(2,1)S(1)}, bf16[256,1024]{1,0:T(8,128)(2,1)S(1)}, u32[]{:S(2)}, u32[]{:S(2)}) collective-permute-start(bf16[256,1024]{1,0:T(8,128)(2,1)S(1)} %add_convert_fusion.1), channel_id=1, source_target_pairs={{0,2},{1,3},{2,0},{3,1},{4,6},{5,7},{6,4},{7,5},{8,10},{9,11},{10,... | collective-permute-start | bytes 1572872 | tf_op jit(solution)/shard_map/ppermute | solution.py:455
  41.2 4.5 %back.1 = (f32[512,1024]{1,0:T(8,128)S(1)}, bf16[512,1024]{1,0:T(8,128)(2,1)S(1)}, bf16[512,384]{1,0:T(8,128)(2,1)S(1)}, f32[1,1024]{1,0:T(1,128)S(1)}) custom-call(s32[6]{0:T(128)S(1)} %pad_add_fusion.where.place, bf16[256,1024]{1,0:T(8,128)(2,1)S(1)} %add_convert_fusion.2.own, bf16[256,1024]{1,0:T(8,128)(2,1)S(1)} %collective-permute-done.5.other, ...), custom_call_target="tpu_custom_call" | custom-call | flops 1000 | bytes 1000 | tf_op jit(solution)/shard_map/back/pallas_call | solution.py:413
  45.8 1.1 %late_away.1 = bf16[4,656,128]{2,1,0:T(8,128)(2,1)S(1)} custom-call(s32[6]{0:T(128)S(1)} %pad_add_fusion.where.place, bf16[512,256]{1,0:T(8,128)(2,1)S(1)} %get-tuple-element.127.ctx.refs_0_.ctx_in, bf16[512,384]{1,0:T(8,128)(2,1)S(1)} %get-tuple-element.124.refs_1_.refs_0_, bf16[512,1024]{1,0:T(8,128)(2,1)S(1)} %get-tuple-element.128.refs_2_, ...), custom_call_target="tpu_custom_call" | custom-call | flops 1000 | bytes 1000 | tf_op jit(solution)/shard_map/late_away/pallas_call | solution.py:413
  46.9 1.6 %collective-permute-start.12 = (bf16[4,656,128]{2,1,0:T(8,128)(2,1)S(1)}, bf16[4,656,128]{2,1,0:T(8,128)(2,1)S(1)}, u32[]{:S(2)}, u32[]{:S(2)}) collective-permute-start(bf16[4,656,128]{2,1,0:T(8,128)(2,1)S(1)} %late_away.1), channel_id=1, source_target_pairs={{0,4},{4,0},{8,12},{12,8},{16,20},{20,16},{24,28},{28,24},{1,5},{5... | collective-permute-start | bytes 2015240 | tf_op jit(solution)/shard_map/ppermute | solution.py:455
  48.6 2.8 %collective-permute-done.9.refs_3_ = bf16[4,992,128]{2,1,0:T(8,128)(2,1)S(1)} collective-permute-done((bf16[4,992,128]{2,1,0:T(8,128)(2,1)S(1)}, bf16[4,992,128]{2,1,0:T(8,128)(2,1)S(1)}, u32[]{:S(2)}, u32[]{:S(2)}) %collective-permute-start.9) | collective-permute-done | bytes 1015840 | tf_op jit(solution)/shard_map/ppermute | solution.py:455
  51.4 1.3 %z_keep.1 = (bf16[2,992,128]{2,1,0:T(8,128)(2,1)S(1)}, bf16[2,992,128]{2,1,0:T(8,128)(2,1)S(1)}) custom-call(s32[6]{0:T(128)S(1)} %pad_add_fusion.where.place, bf16[512,688]{1,0:T(8,128)(2,1)S(1)} %get-tuple-element.105.gate.refs_0_.refs_1_, bf16[512,688]{1,0:T(8,128)(2,1)S(1)} %get-tuple-element.106.up.refs_1_, ...), custom_call_target="tpu_custom_call" | custom-call | flops 1000 | bytes 1000 | tf_op jit(solution)/shard_map/z_keep/pallas_call | solution.py:413
  52.7 2.6 %collective-permute-start.11 = (bf16[2,992,128]{2,1,0:T(8,128)(2,1)S(1)}, bf16[2,992,128]{2,1,0:T(8,128)(2,1)S(1)}, u32[]{:S(2)}, u32[]{:S(2)}) collective-permute-start(bf16[2,992,128]{2,1,0:T(8,128)(2,1)S(1)} %get-tuple-element.131), channel_id=1, source_target_pairs={{0,16},{4,20},{8,24},{12,28},{16,0},{20,4},{24,8},{28,12},{1,17},{... | collective-permute-start | bytes 1523720 | tf_op jit(solution)/shard_map/ppermute | solution.py:455
  55.4 1.4 %x_keep.1 = (bf16[2,1072,128]{2,1,0:T(8,128)(2,1)S(1)}, bf16[2,1072,128]{2,1,0:T(8,128)(2,1)S(1)}) custom-call(s32[6]{0:T(128)S(1)} %pad_add_fusion.where.place, bf16[512,688]{1,0:T(8,128)(2,1)S(1)} %get-tuple-element.104.inner.refs_0_, bf16[512,688]{1,0:T(8,128)(2,1)S(1)} %get-tuple-element.105.gate.refs_0_.refs_1_, bf16[512,1024]{1,0:T(8,128)(2,1)S(1)} %copy-done.1, ...), custom_call_target="tpu_custom_call" | custom-call | flops 1000 | bytes 1000 | tf_op jit(solution)/shard_map/x_keep/pallas_call | solution.py:413
  56.7 1.6 %collective-permute-start.10 = (bf16[2,1072,128]{2,1,0:T(8,128)(2,1)S(1)}, bf16[2,1072,128]{2,1,0:T(8,128)(2,1)S(1)}, u32[]{:S(2)}, u32[]{:S(2)}) collective-permute-start(bf16[2,1072,128]{2,1,0:T(8,128)(2,1)S(1)} %get-tuple-element.134), channel_id=1, source_target_pairs={{0,8},{4,12},{8,0},{12,4},{16,24},{20,28},{24,16},{28,20},{1,9},{5... | collective-permute-start | bytes 1646600 | tf_op jit(solution)/shard_map/ppermute | solution.py:455
  58.4 0.5 collective-permute-start.13
  58.9 0.2 add_convert_fusion.refs_7_
  59.1 9.4 %collective-permute-done.13.refs_2_ = bf16[512,384]{1,0:T(8,128)(2,1)S(1)} collective-permute-done((bf16[512,384]{1,0:T(8,128)(2,1)S(1)}, bf16[512,384]{1,0:T(8,128)(2,1)S(1)}, u32[]{:S(2)}, u32[]{:S(2)}) %collective-permute-start.13) | collective-permute-done | bytes 393248 | tf_op jit(solution)/shard_map/ppermute | solution.py:455
  68.5 0.3 collective-permute-done.12.refs_5_
  68.8 1.1 %late_keep.1 = (f32[656,128]{1,0:T(8,128)S(1)}, bf16[656,128]{1,0:T(8,128)(2,1)S(1)}, bf16[656,128]{1,0:T(8,128)(2,1)S(1)}, bf16[656,128]{1,0:T(8,128)(2,1)S(1)}) custom-call(s32[6]{0:T(128)S(1)} %pad_add_fusion.where.place, bf16[512,256]{1,0:T(8,128)(2,1)S(1)} %get-tuple-element.127.ctx.refs_0_.ctx_in, ...), custom_call_target="tpu_custom_call" | custom-call | flops 1000 | bytes 1000 | tf_op jit(solution)/shard_map/late_keep/pallas_call | solution.py:413
  70.0 2.7 %collective-permute-start.17 = (bf16[656,128]{1,0:T(8,128)(2,1)S(1)}, bf16[656,128]{1,0:T(8,128)(2,1)S(1)}, u32[]{:S(2)}, u32[]{:S(2)}) collective-permute-start(bf16[656,128]{1,0:T(8,128)(2,1)S(1)} %get-tuple-element.148), channel_id=1, source_target_pairs={{0,16},{4,20},{8,24},{12,28},{16,0},{20,4},{24,8},{28,12},{1,17},{... | collective-permute-start | bytes 503816 | tf_op jit(solution)/shard_map/ppermute | solution.py:455
  72.6 0.5 collective-permute-start.18
  73.1 1.4 %collective-permute-start.19 = (bf16[656,128]{1,0:T(8,128)(2,1)S(1)}, bf16[656,128]{1,0:T(8,128)(2,1)S(1)}, u32[]{:S(2)}, u32[]{:S(2)}) collective-permute-start(bf16[656,128]{1,0:T(8,128)(2,1)S(1)} %get-tuple-element.139), channel_id=1, source_target_pairs={{0,24},{4,28},{8,16},{12,20},{16,8},{20,12},{24,0},{28,4},{1,25},{... | collective-permute-start | bytes 503816 | tf_op jit(solution)/shard_map/ppermute | solution.py:455
  74.4 5.0 %collective-permute-done.11.come = bf16[2,992,128]{2,1,0:T(8,128)(2,1)S(1)} collective-permute-done((bf16[2,992,128]{2,1,0:T(8,128)(2,1)S(1)}, bf16[2,992,128]{2,1,0:T(8,128)(2,1)S(1)}, u32[]{:S(2)}, u32[]{:S(2)}) %collective-permute-start.11) | collective-permute-done | bytes 507936 | tf_op jit(solution)/shard_map/ppermute | solution.py:455
  79.5 5.6 %collective-permute-done.10.come = bf16[2,1072,128]{2,1,0:T(8,128)(2,1)S(1)} collective-permute-done((bf16[2,1072,128]{2,1,0:T(8,128)(2,1)S(1)}, bf16[2,1072,128]{2,1,0:T(8,128)(2,1)S(1)}, u32[]{:S(2)}, u32[]{:S(2)}) %collective-permute-start.10) | collective-permute-done | bytes 548896 | tf_op jit(solution)/shard_map/ppermute | solution.py:455
  85.1 0.7 z_hop.1
  85.7 0.7 x_hop.1
  86.4 0.2 collective-permute-done.17.refs_0_
  86.6 4.4 %collective-permute-done.18.refs_1_ = bf16[656,128]{1,0:T(8,128)(2,1)S(1)} collective-permute-done((bf16[656,128]{1,0:T(8,128)(2,1)S(1)}, bf16[656,128]{1,0:T(8,128)(2,1)S(1)}, u32[]{:S(2)}, u32[]{:S(2)}) %collective-permute-start.18) | collective-permute-done | bytes 167968 | tf_op jit(solution)/shard_map/ppermute | solution.py:455
  91.0 1.6 %collective-permute-start.24 = (bf16[1,992,128]{2,1,0:T(8,128)(2,1)S(1)}, bf16[1,992,128]{2,1,0:T(8,128)(2,1)S(1)}, u32[]{:S(2)}, u32[]{:S(2)}) collective-permute-start(bf16[1,992,128]{2,1,0:T(8,128)(2,1)S(1)} %get-tuple-element.141), channel_id=1, source_target_pairs={{0,4},{4,0},{8,12},{12,8},{16,20},{20,16},{24,28},{28,24},{1,5},{5... | collective-permute-start | bytes 761864 | tf_op jit(solution)/shard_map/ppermute | solution.py:455
  92.6 1.2 %late.1 = (f32[256,128]{1,0:T(8,128)}, f32[1,128]{1,0:T(1,128)}, bf16[384,128]{1,0:T(8,128)(2,1)S(1)}) custom-call(s32[6]{0:T(128)S(1)} %pad_add_fusion.where.place, f32[656,128]{1,0:T(8,128)S(1)} %get-tuple-element.147.held, bf16[656,128]{1,0:T(8,128)(2,1)S(1)} %collective-permute-done.17.refs_0_, bf16[656,128]{1,0:T(8,128)(2,1)S(1)} %collective-permute-done.18.refs_1_, ...), custom_call_target="tpu_custom_call" | custom-call | flops 3000000000 | bytes 1000 | tf_op jit(solution)/shard_map/late/pallas_call | solution.py:413
  93.8 0.4 collective-permute-start.21
  94.3 0.2 copy-done.3
  94.4 4.6 %grad_input.1 = (bf16[512,1024]{1,0:T(8,128)(2,1)}, bf16[512,1024]{1,0:T(8,128)(2,1)}) custom-call(s32[6]{0:T(128)S(1)} %pad_add_fusion.where.place, bf16[512,384]{1,0:T(8,128)(2,1)S(1)} %get-tuple-element.124.refs_1_.refs_0_, bf16[512,384]{1,0:T(8,128)(2,1)S(1)} %collective-permute-done.7.refs_1_, bf16[512,384]{1,0:T(8,128)(2,1)S(1)} %collective-permute-done.13.refs_2_, ...), custom_call_target="tpu_custom_call" | custom-call | flops 1000 | bytes 1000 | tf_op jit(solution)/shard_map/grad_input/pallas_call | solution.py:413
  99.0 0.4 collective-permute-start.22
  99.4 4.5 %collective-permute-done.23.x_come = bf16[1,1072,128]{2,1,0:T(8,128)(2,1)S(1)} collective-permute-done((bf16[1,1072,128]{2,1,0:T(8,128)(2,1)S(1)}, bf16[1,1072,128]{2,1,0:T(8,128)(2,1)S(1)}, u32[]{:S(2)}, u32[]{:S(2)}) %collective-permute-start.23) | collective-permute-done | bytes 274464 | tf_op jit(solution)/shard_map/ppermute | solution.py:455
  103.9 1.6 %hidden.1 = (f32[688,128]{1,0:T(8,128)}, f32[688,128]{1,0:T(8,128)}, f32[688,128]{1,0:T(8,128)}) custom-call(s32[6]{0:T(128)S(1)} %pad_add_fusion.where.place, bf16[1,1072,128]{2,1,0:T(8,128)(2,1)S(1)} %get-tuple-element.158.x_held, bf16[1,1072,128]{2,1,0:T(8,128)(2,1)S(1)} %collective-permute-done.23.x_come, ...), custom_call_target="tpu_custom_call" | custom-call | flops 10000000000 | bytes 1000 | tf_op jit(solution)/shard_map/hidden/pallas_call | solution.py:413
  105.5 1.7 %finish.1 = (f32[128,256]{1,0:T(8,128)}, f32[128,256]{1,0:T(8,128)}, f32[128,1024]{1,0:T(8,128)}, f32[1,128]{1,0:T(1,128)}) custom-call(s32[6]{0:T(128)S(1)} %pad_add_fusion.where.place, bf16[384,128]{1,0:T(8,128)(2,1)S(1)} %get-tuple-element.163.refs_0_, bf16[384,128]{1,0:T(8,128)(2,1)S(1)} %collective-permute-done.20.refs_1_, ...), custom_call_target="tpu_custom_call" | custom-call | flops 1000 | bytes 1000 | tf_op jit(solution)/shard_map/finish/pallas_call | solution.py:413
  (39 shorter events, 0.3 us)
Async XLA Ops:
  0.6 7.0 %copy-start.7 = (s32[1,4]{1,0:T(1,128)S(1)}, s32[1,4]{1,0:T(1,128)}, u32[]{:S(2)}) copy-start(s32[1,4]{1,0:T(1,128)} %lengths.1) | copy-start | bytes 52
  4.6 9.3 %collective-permute-start.1 = (bf16[512,256]{1,0:T(8,128)(2,1)S(1)}, bf16[512,256]{1,0:T(8,128)(2,1)S(1)}, u32[]{:S(2)}, u32[]{:S(2)}) collective-permute-start(bf16[512,256]{1,0:T(8,128)(2,1)S(1)} %get-tuple-element.127.ctx.refs_0_.ctx_in), channel_id=1, source_target_pairs={{0,2},{1,3},{2,0},{3,1},{4,6},{5,7},{6,4},{7,5},{8,10},{9,11},{10,... | collective-permute-start | bytes 786440 | tf_op jit(solution)/shard_map/ppermute | solution.py:455
  7.6 6.3 %collective-permute-start = (bf16[512,256]{1,0:T(8,128)(2,1)S(1)}, bf16[512,256]{1,0:T(8,128)(2,1)S(1)}, u32[]{:S(2)}, u32[]{:S(2)}) collective-permute-start(bf16[512,256]{1,0:T(8,128)(2,1)S(1)} %get-tuple-element.127.ctx.refs_0_.ctx_in), channel_id=1, source_target_pairs={{0,1},{1,0},{2,3},{3,2},{4,5},{5,4},{6,7},{7,6},{8,9},{9,8},{10,11... | collective-permute-start | bytes 786440 | tf_op jit(solution)/shard_map/ppermute | solution.py:455
  7.7 7.8 %copy-start.4 = (bf16[512,1024]{1,0:T(8,128)(2,1)S(1)}, bf16[512,1024]{1,0:T(8,128)(2,1)}, u32[]{:S(2)}) copy-start(bf16[512,1024]{1,0:T(8,128)(2,1)} %refs_5_.2) | copy-start | bytes 3145732
  7.7 7.8 %copy-start.6 = (f32[1024]{0:T(1024)S(1)}, f32[1024]{0:T(1024)}, u32[]{:S(2)}) copy-start(f32[1024]{0:T(1024)} %param.18) | copy-start | bytes 12292
  13.9 1.5 %collective-permute-start.2 = (bf16[512,256]{1,0:T(8,128)(2,1)S(1)}, bf16[512,256]{1,0:T(8,128)(2,1)S(1)}, u32[]{:S(2)}, u32[]{:S(2)}) collective-permute-start(bf16[512,256]{1,0:T(8,128)(2,1)S(1)} %collective-permute-done.1.refs_2_), channel_id=1, source_target_pairs={{0,1},{1,0},{2,3},{3,2},{4,5},{5,4},{6,7},{7,6},{8,9},{9,8},{10,11... | collective-permute-start | bytes 786440 | tf_op jit(solution)/shard_map/ppermute | solution.py:455
  15.5 6.2 %copy-start.1 = (bf16[512,1024]{1,0:T(8,128)(2,1)S(1)}, bf16[512,1024]{1,0:T(8,128)(2,1)}, u32[]{:S(2)}) copy-start(bf16[512,1024]{1,0:T(8,128)(2,1)} %refs_2_.1) | copy-start | bytes 3145732
  21.5 3.0 %collective-permute-start.3 = (bf16[256,1024]{1,0:T(8,128)(2,1)S(1)}, bf16[256,1024]{1,0:T(8,128)(2,1)S(1)}, u32[]{:S(2)}, u32[]{:S(2)}) collective-permute-start(bf16[256,1024]{1,0:T(8,128)(2,1)S(1)} %get-tuple-element.103), channel_id=1, source_target_pairs={{0,1},{1,0},{2,3},{3,2},{4,5},{5,4},{6,7},{7,6},{8,9},{9,8},{10,11... | collective-permute-start | bytes 1572872 | tf_op jit(solution)/shard_map/ppermute | solution.py:455
  24.7 14.3 %collective-permute-start.4 = (bf16[256,1024]{1,0:T(8,128)(2,1)S(1)}, bf16[256,1024]{1,0:T(8,128)(2,1)S(1)}, u32[]{:S(2)}, u32[]{:S(2)}) collective-permute-start(bf16[256,1024]{1,0:T(8,128)(2,1)S(1)} %add_convert_fusion.3), channel_id=1, source_target_pairs={{0,2},{1,3},{2,0},{3,1},{4,6},{5,7},{6,4},{7,5},{8,10},{9,11},{10,... | collective-permute-start | bytes 1572872 | tf_op jit(solution)/shard_map/ppermute | solution.py:455
  26.5 12.7 %collective-permute-start.6 = (bf16[256,1024]{1,0:T(8,128)(2,1)S(1)}, bf16[256,1024]{1,0:T(8,128)(2,1)S(1)}, u32[]{:S(2)}, u32[]{:S(2)}) collective-permute-start(bf16[256,1024]{1,0:T(8,128)(2,1)S(1)} %get-tuple-element.117), channel_id=1, source_target_pairs={{0,1},{1,0},{2,3},{3,2},{4,5},{5,4},{6,7},{7,6},{8,9},{9,8},{10,11... | collective-permute-start | bytes 1572872 | tf_op jit(solution)/shard_map/ppermute | solution.py:455
  26.6 24.8 %collective-permute-start.9 = (bf16[4,992,128]{2,1,0:T(8,128)(2,1)S(1)}, bf16[4,992,128]{2,1,0:T(8,128)(2,1)S(1)}, u32[]{:S(2)}, u32[]{:S(2)}) collective-permute-start(bf16[4,992,128]{2,1,0:T(8,128)(2,1)S(1)} %get-tuple-element.108), channel_id=1, source_target_pairs={{0,8},{4,12},{8,0},{12,4},{16,24},{20,28},{24,16},{28,20},{1,9},{5... | collective-permute-start | bytes 3047432 | tf_op jit(solution)/shard_map/ppermute | solution.py:455
  28.1 27.2 %collective-permute-start.8 = (bf16[4,1072,128]{2,1,0:T(8,128)(2,1)S(1)}, bf16[4,1072,128]{2,1,0:T(8,128)(2,1)S(1)}, u32[]{:S(2)}, u32[]{:S(2)}) collective-permute-start(bf16[4,1072,128]{2,1,0:T(8,128)(2,1)S(1)} %get-tuple-element.125), channel_id=1, source_target_pairs={{0,4},{4,0},{8,12},{12,8},{16,20},{20,16},{24,28},{28,24},{1,5},{5... | collective-permute-start | bytes 3293192 | tf_op jit(solution)/shard_map/ppermute | solution.py:455
  39.1 2.1 %collective-permute-start.5 = (bf16[256,1024]{1,0:T(8,128)(2,1)S(1)}, bf16[256,1024]{1,0:T(8,128)(2,1)S(1)}, u32[]{:S(2)}, u32[]{:S(2)}) collective-permute-start(bf16[256,1024]{1,0:T(8,128)(2,1)S(1)} %add_convert_fusion.2.own), channel_id=1, source_target_pairs={{0,1},{1,0},{2,3},{3,2},{4,5},{5,4},{6,7},{7,6},{8,9},{9,8},{10,11... | collective-permute-start | bytes 1572872 | tf_op jit(solution)/shard_map/ppermute | solution.py:455
  39.4 19.5 %collective-permute-start.14 = (bf16[256,1024]{1,0:T(8,128)(2,1)S(1)}, bf16[256,1024]{1,0:T(8,128)(2,1)S(1)}, u32[]{:S(2)}, u32[]{:S(2)}) collective-permute-start(bf16[256,1024]{1,0:T(8,128)(2,1)S(1)} %add_convert_fusion.1), channel_id=1, source_target_pairs={{0,2},{1,3},{2,0},{3,1},{4,6},{5,7},{6,4},{7,5},{8,10},{9,11},{10,... | collective-permute-start | bytes 1572872 | tf_op jit(solution)/shard_map/ppermute | solution.py:455
  46.9 21.9 %collective-permute-start.12 = (bf16[4,656,128]{2,1,0:T(8,128)(2,1)S(1)}, bf16[4,656,128]{2,1,0:T(8,128)(2,1)S(1)}, u32[]{:S(2)}, u32[]{:S(2)}) collective-permute-start(bf16[4,656,128]{2,1,0:T(8,128)(2,1)S(1)} %late_away.1), channel_id=1, source_target_pairs={{0,4},{4,0},{8,12},{12,8},{16,20},{20,16},{24,28},{28,24},{1,5},{5... | collective-permute-start | bytes 2015240 | tf_op jit(solution)/shard_map/ppermute | solution.py:455
  52.7 26.8 %collective-permute-start.11 = (bf16[2,992,128]{2,1,0:T(8,128)(2,1)S(1)}, bf16[2,992,128]{2,1,0:T(8,128)(2,1)S(1)}, u32[]{:S(2)}, u32[]{:S(2)}) collective-permute-start(bf16[2,992,128]{2,1,0:T(8,128)(2,1)S(1)} %get-tuple-element.131), channel_id=1, source_target_pairs={{0,16},{4,20},{8,24},{12,28},{16,0},{20,4},{24,8},{28,12},{1,17},{... | collective-permute-start | bytes 1523720 | tf_op jit(solution)/shard_map/ppermute | solution.py:455
  56.7 28.3 %collective-permute-start.10 = (bf16[2,1072,128]{2,1,0:T(8,128)(2,1)S(1)}, bf16[2,1072,128]{2,1,0:T(8,128)(2,1)S(1)}, u32[]{:S(2)}, u32[]{:S(2)}) collective-permute-start(bf16[2,1072,128]{2,1,0:T(8,128)(2,1)S(1)} %get-tuple-element.134), channel_id=1, source_target_pairs={{0,8},{4,12},{8,0},{12,4},{16,24},{20,28},{24,16},{28,20},{1,9},{5... | collective-permute-start | bytes 1646600 | tf_op jit(solution)/shard_map/ppermute | solution.py:455
  58.4 10.1 %collective-permute-start.13 = (bf16[512,384]{1,0:T(8,128)(2,1)S(1)}, bf16[512,384]{1,0:T(8,128)(2,1)S(1)}, u32[]{:S(2)}, u32[]{:S(2)}) collective-permute-start(bf16[512,384]{1,0:T(8,128)(2,1)S(1)} %get-tuple-element.124.refs_1_.refs_0_), channel_id=1, source_target_pairs={{0,2},{1,3},{2,0},{3,1},{4,6},{5,7},{6,4},{7,5},{8,10},{9,11},{10,... | collective-permute-start | bytes 1179656 | tf_op jit(solution)/shard_map/ppermute | solution.py:455
  58.9 14.2 %collective-permute-start.7 = (bf16[512,384]{1,0:T(8,128)(2,1)S(1)}, bf16[512,384]{1,0:T(8,128)(2,1)S(1)}, u32[]{:S(2)}, u32[]{:S(2)}) collective-permute-start(bf16[512,384]{1,0:T(8,128)(2,1)S(1)} %get-tuple-element.124.refs_1_.refs_0_), channel_id=1, source_target_pairs={{0,1},{1,0},{2,3},{3,2},{4,5},{5,4},{6,7},{7,6},{8,9},{9,8},{10,11... | collective-permute-start | bytes 1179656 | tf_op jit(solution)/shard_map/ppermute | solution.py:455
  70.0 16.7 %collective-permute-start.17 = (bf16[656,128]{1,0:T(8,128)(2,1)S(1)}, bf16[656,128]{1,0:T(8,128)(2,1)S(1)}, u32[]{:S(2)}, u32[]{:S(2)}) collective-permute-start(bf16[656,128]{1,0:T(8,128)(2,1)S(1)} %get-tuple-element.148), channel_id=1, source_target_pairs={{0,16},{4,20},{8,24},{12,28},{16,0},{20,4},{24,8},{28,12},{1,17},{... | collective-permute-start | bytes 503816 | tf_op jit(solution)/shard_map/ppermute | solution.py:455
  72.6 18.4 %collective-permute-start.18 = (bf16[656,128]{1,0:T(8,128)(2,1)S(1)}, bf16[656,128]{1,0:T(8,128)(2,1)S(1)}, u32[]{:S(2)}, u32[]{:S(2)}) collective-permute-start(bf16[656,128]{1,0:T(8,128)(2,1)S(1)} %get-tuple-element.149), channel_id=1, source_target_pairs={{0,8},{4,12},{8,0},{12,4},{16,24},{20,28},{24,16},{28,20},{1,9},{5... | collective-permute-start | bytes 503816 | tf_op jit(solution)/shard_map/ppermute | solution.py:455
  73.1 19.5 %collective-permute-start.19 = (bf16[656,128]{1,0:T(8,128)(2,1)S(1)}, bf16[656,128]{1,0:T(8,128)(2,1)S(1)}, u32[]{:S(2)}, u32[]{:S(2)}) collective-permute-start(bf16[656,128]{1,0:T(8,128)(2,1)S(1)} %get-tuple-element.139), channel_id=1, source_target_pairs={{0,24},{4,28},{8,16},{12,20},{16,8},{20,12},{24,0},{28,4},{1,25},{... | collective-permute-start | bytes 503816 | tf_op jit(solution)/shard_map/ppermute | solution.py:455
  79.5 14.8 %collective-permute-start.16 = (bf16[256,1024]{1,0:T(8,128)(2,1)S(1)}, bf16[256,1024]{1,0:T(8,128)(2,1)S(1)}, u32[]{:S(2)}, u32[]{:S(2)}) collective-permute-start(bf16[256,1024]{1,0:T(8,128)(2,1)S(1)} %add_convert_fusion.refs_7_), channel_id=1, source_target_pairs={{0,1},{1,0},{2,3},{3,2},{4,5},{5,4},{6,7},{7,6},{8,9},{9,8},{10,11... | collective-permute-start | bytes 1572872 | tf_op jit(solution)/shard_map/ppermute | solution.py:455
  85.1 9.2 %collective-permute-start.15 = (bf16[512,384]{1,0:T(8,128)(2,1)S(1)}, bf16[512,384]{1,0:T(8,128)(2,1)S(1)}, u32[]{:S(2)}, u32[]{:S(2)}) collective-permute-start(bf16[512,384]{1,0:T(8,128)(2,1)S(1)} %collective-permute-done.13.refs_2_), channel_id=1, source_target_pairs={{0,1},{1,0},{2,3},{3,2},{4,5},{5,4},{6,7},{7,6},{8,9},{9,8},{10,11... | collective-permute-start | bytes 1179656 | tf_op jit(solution)/shard_map/ppermute | solution.py:455
  86.6 17.3 %collective-permute-start.23 = (bf16[1,1072,128]{2,1,0:T(8,128)(2,1)S(1)}, bf16[1,1072,128]{2,1,0:T(8,128)(2,1)S(1)}, u32[]{:S(2)}, u32[]{:S(2)}) collective-permute-start(bf16[1,1072,128]{2,1,0:T(8,128)(2,1)S(1)} %get-tuple-element.143), channel_id=1, source_target_pairs={{0,16},{4,20},{8,24},{12,28},{16,0},{20,4},{24,8},{28,12},{1,17},{... | collective-permute-start | bytes 823304 | tf_op jit(solution)/shard_map/ppermute | solution.py:455
  91.0 8.4 %collective-permute-start.24 = (bf16[1,992,128]{2,1,0:T(8,128)(2,1)S(1)}, bf16[1,992,128]{2,1,0:T(8,128)(2,1)S(1)}, u32[]{:S(2)}, u32[]{:S(2)}) collective-permute-start(bf16[1,992,128]{2,1,0:T(8,128)(2,1)S(1)} %get-tuple-element.141), channel_id=1, source_target_pairs={{0,4},{4,0},{8,12},{12,8},{16,20},{20,16},{24,28},{28,24},{1,5},{5... | collective-permute-start | bytes 761864 | tf_op jit(solution)/shard_map/ppermute | solution.py:455
  92.5 1.7 %copy-start = (bf16[1024,1024]{1,0:T(8,128)(2,1)S(1)}, bf16[1024,1024]{1,0:T(8,128)(2,1)}, u32[]{:S(2)}) copy-start(bf16[1024,1024]{1,0:T(8,128)(2,1)} %refs_7_.1) | copy-start | bytes 6291460
  92.5 1.7 %copy-start.2 = (bf16[1024,256]{1,0:T(8,128)(2,1)S(1)}, bf16[1024,256]{1,0:T(8,128)(2,1)}, u32[]{:S(2)}) copy-start(bf16[1024,256]{1,0:T(8,128)(2,1)} %refs_5_.3) | copy-start | bytes 1572868
  92.5 1.9 %copy-start.3 = (bf16[1024,256]{1,0:T(8,128)(2,1)S(1)}, bf16[1024,256]{1,0:T(8,128)(2,1)}, u32[]{:S(2)}) copy-start(bf16[1024,256]{1,0:T(8,128)(2,1)} %refs_6_.1) | copy-start | bytes 1572868
  92.5 1.9 %copy-start.5 = (f32[1024]{0:T(1024)S(1)}, f32[1024]{0:T(1024)}, u32[]{:S(2)}) copy-start(f32[1024]{0:T(1024)} %param.13) | copy-start | bytes 12292
  93.8 5.2 %collective-permute-start.21 = (bf16[384,128]{1,0:T(8,128)(2,1)S(1)}, bf16[384,128]{1,0:T(8,128)(2,1)S(1)}, u32[]{:S(2)}, u32[]{:S(2)}) collective-permute-start(bf16[384,128]{1,0:T(8,128)(2,1)S(1)} %get-tuple-element.163.refs_0_), channel_id=1, source_target_pairs={{0,2},{1,3},{2,0},{3,1},{4,6},{5,7},{6,4},{7,5},{8,10},{9,11},{10,... | collective-permute-start | bytes 294920 | tf_op jit(solution)/shard_map/ppermute | solution.py:455
  94.2 11.2 %collective-permute-start.20 = (bf16[384,128]{1,0:T(8,128)(2,1)S(1)}, bf16[384,128]{1,0:T(8,128)(2,1)S(1)}, u32[]{:S(2)}, u32[]{:S(2)}) collective-permute-start(bf16[384,128]{1,0:T(8,128)(2,1)S(1)} %get-tuple-element.163.refs_0_), channel_id=1, source_target_pairs={{0,1},{1,0},{2,3},{3,2},{4,5},{5,4},{6,7},{7,6},{8,9},{9,8},{10,11... | collective-permute-start | bytes 294920 | tf_op jit(solution)/shard_map/ppermute | solution.py:455
  99.0 6.5 %collective-permute-start.22 = (bf16[384,128]{1,0:T(8,128)(2,1)S(1)}, bf16[384,128]{1,0:T(8,128)(2,1)S(1)}, u32[]{:S(2)}, u32[]{:S(2)}) collective-permute-start(bf16[384,128]{1,0:T(8,128)(2,1)S(1)} %collective-permute-done.21.refs_2_), channel_id=1, source_target_pairs={{0,1},{1,0},{2,3},{3,2},{4,5},{5,4},{6,7},{7,6},{8,9},{9,8},{10,11... | collective-permute-start | bytes 294920 | tf_op jit(solution)/shard_map/ppermute | solution.py:455

commit v7 on v6

--- a/solution.py
+++ b/solution.py
@@ -13,7 +13,7 @@
 EPSILON = 1e-05
 F32 = jnp.float32
 BF16 = jnp.bfloat16
-COSTS = {"feed": 3000000000, "grad_input": 1000, "hidden": 10000000000, "late": 3000000000}
+COSTS = {"feed": 3000000000, "grad_input": 1000, "hidden": 10000000000, "late": 10000000000}
 VMEM_LIMIT = 20 * 1024 * 1024
 
 
@@ -170,16 +170,17 @@
     r = lax.rsqrt(jnp.mean(residual * residual, axis=1, keepdims=True) + EPSILON)
     n = (residual * r * gain[...]).astype(BF16)
     n_out[...] = n
-    gate = dot_nt(n, w_gate[...])
-    up = dot_nt(n, w_up[...])
-    ginner = ginner_in[...]
-    sig = jax.nn.sigmoid(gate)
-    act = gate * sig
-    inner_out[...] = (act * up * live).astype(BF16)
-    ggate = (ginner * up * sig * (1.0 + gate * (1.0 - sig))).astype(BF16)
-    gup = (ginner * act).astype(BF16)
-    gg_out[...] = ggate
-    gu_out[...] = gup
+    hidden = w_gate.shape[0]
+    for low in range(0, hidden, 256):
+        part = slice(low, min(low + 256, hidden))
+        gate = dot_nt(n, w_gate[part, :])
+        up = dot_nt(n, w_up[part, :])
+        ginner = ginner_in[:, part]
+        sig = jax.nn.sigmoid(gate)
+        act = gate * sig
+        inner_out[:, part] = (act * up * live).astype(BF16)
+        gg_out[:, part] = (ginner * up * sig * (1.0 + gate * (1.0 - sig))).astype(BF16)
+        gu_out[:, part] = (ginner * act).astype(BF16)
     for which, out in ((1 - core, away_out), (core, own_out)):
         here = pl.ds(pl.multiple_of(which * half, half), half)
         out[...] = (dot(gg_out[here, :], w_gate[...]) + dot(gu_out[here, :], w_up[...])).astype(BF16)
@@ -200,12 +201,12 @@
     return found
 
 
-def away_kernel(where, *refs, pairs, order, chunk):
+def away_kernel(where, *refs, pairs, order, chunk, away=True):
     out = refs[-1]
     offsets = positions(order)
     count = len(offsets) // 2
     low = 0
-    for part in products(where, pairs(refs), offsets[count:], chunk):
+    for part in products(where, pairs(refs), offsets[count:] if away else offsets[:count], chunk):
         high = low + part.shape[0]
         for i in range(count):
             out[i, low:high, :] = part[:, i * chunk : (i + 1) * chunk].astype(BF16)
@@ -216,6 +217,16 @@
     away_kernel(where, inner, gate, cot, normed, x_out, **x_fixed)
     away_kernel(where, gate, up, normed, z_out, **z_fixed)
     down_kernel(where, inner, w_down, feed_away, feed_own)
+
+
+def pair_keeps_kernel(where, inner, gate, up, cot, normed, x_out, z_out, *, x_fixed, z_fixed):
+    away_kernel(where, inner, gate, cot, normed, x_out, **x_fixed, away=False)
+    away_kernel(where, gate, up, normed, z_out, **z_fixed, away=False)
+
+
+def pair_aways_kernel(where, inner, gate, up, cot, normed, x_out, z_out, *, x_fixed, z_fixed):
+    away_kernel(where, inner, gate, cot, normed, x_out, **x_fixed)
+    away_kernel(where, gate, up, normed, z_out, **z_fixed)
 
 
 def keep_kernel(where, *refs, pairs, order, chunk):
@@ -273,7 +284,7 @@
     many = out.shape[0]
     out[...] = total[:many]
     gain_out[...] = total[many : many + 1]
-    own_out[...] = total[many + 16 :].astype(BF16)
+    own_out[...] = total[many + 16 :].T.astype(BF16)
 
 
 def prepare_kernel(where, q_in, k_in, res, p_out, t_out, r_out):
@@ -377,7 +388,7 @@
 def finish_kernel(where, *refs, share, hv, hq):
     sums = refs[:share]
     gain, w_query, w_key, w_value, q_out, k_out, v_out, gain_out = refs[share:]
-    blocks = [b.T for b in absolute_order([s[...].astype(F32) for s in sums], where[0])]
+    blocks = absolute_order([s[...].astype(F32) for s in sums], where[0])
     values = jnp.concatenate([b[:, :hv] for b in blocks], axis=1)
     queries = jnp.concatenate([b[:, hv : hv + hq] for b in blocks], axis=1)
     keys = jnp.concatenate([b[:, hv + hq :] for b in blocks], axis=1)
@@ -390,6 +401,11 @@
     diagonal = lax.broadcasted_iota(jnp.int32, spread.shape, 0) == lax.broadcasted_iota(jnp.int32, spread.shape, 1)
     row = jnp.sum(jnp.where(diagonal, spread, 0.0), axis=0, keepdims=True)
     gain_out[...] = row / block_columns(gain, where[1], gain_out.shape[1])
+
+
+def last_kernel(where, *refs, share, hv, hq):
+    hidden_kernel(where, *refs[:4], *refs[8 + share : 11 + share])
+    finish_kernel(where, *refs[4 : 8 + share], *refs[11 + share :], share=share, hv=hv, hq=hq)
 
 
 def whole(array):
@@ -588,6 +604,16 @@
         ],
     )
     last = scores
+    x_held, z_held = call(
+        pair_keeps_kernel,
+        "keeps",
+        where,
+        [*after([inner], last), grad_gate, grad_up, cotangent, normed_two],
+        [shape_of(2 * few, x_many, chunk, BF16), shape_of(2 * few, z_many, chunk, BF16)],
+        x_fixed=x_fixed,
+        z_fixed=z_fixed,
+    )
+    last = z_held
     for mask in feat_masks[:-1]:
         [come] = after([swap(back_own, "feat", mask)], last)
         last = back_own = plus(back_own, come)
@@ -629,11 +655,11 @@
     last = late_sent
     [come] = after([swap(z_sent, "dp", z_order[0])], last)
     shapes = [shape_of(few, z_many, chunk, BF16)] * 2
-    z_held, z_sent = call(keep_kernel, "z_keep", where, [*z_args, come], shapes, **z_fixed)
+    z_held, z_sent = call(hop_kernel, "z_keep", where, [z_held, come], shapes)
     last = z_sent
     [come] = after([swap(x_sent, "dp", x_first[0])], last)
     shapes = [shape_of(few, x_many, chunk, BF16)] * 2
-    x_held, x_sent = call(keep_kernel, "x_keep", where, [*x_args, come], shapes, **x_fixed)
+    x_held, x_sent = call(hop_kernel, "x_keep", where, [x_held, come], shapes)
     last = x_sent
     for mask in feat_masks[:-1]:
         [come] = after([swap(feed_own, "feat", mask)], last)
@@ -662,7 +688,7 @@
         "late",
         where,
         [late, *after(comes, last)],
-        [shape_of(hv, chunk, F32), shape_of(1, chunk, F32), shape_of(pack, chunk, BF16)],
+        [shape_of(hv, chunk, F32), shape_of(1, chunk, F32), shape_of(chunk, pack, BF16)],
     )
     last = sum_own
     sums = {0: sum_own}

time: 107 us -> 106 us (level)
  waiting for transfers between devices: 43.2 us -> 36.6 us
  starting transfers between devices: 23.3 us -> 28.6 us
    ppermute x25, waiting for transfers between devices: 43.2 us -> 36.6 us  [swap(): return lax.ppermute(array, axis, [(i, i ^ mask) for i in range(count)])]
    ppermute x25, starting transfers between devices: 23.3 us -> 28.6 us  [swap(): return lax.ppermute(array, axis, [(i, i ^ mask) for i in range(count)])]
    pallas_call x15 -> x16, Pallas kernels: 34.9 us -> 35.2 us  [call(): pl.pallas_call(functools.partial(kernel, **fixed) if fixed else kernel, g...]
  transfers between devices with their start and end apart: 25 -> 25, of which waited for: 11 -> 11; matrix products, arithmetic and copies ran while one was open for 1% -> 1% of each run, Pallas kernels for 25% -> 26%
where the time goes in v7:
time: 106 us
  Pallas kernels  39.1 us (37%)
  waiting for transfers between devices  36.6 us (35%)
  starting transfers between devices  28.6 us (27%)
    ppermute x25, waiting for transfers between devices, swap(): return lax.ppermute(array, axis, [(i, i ^ mask) for i in range(count)])  36.6 us
    pallas_call x16, Pallas kernels, call(): pl.pallas_call(functools.partial(kernel, **fixed) if fixed else kernel, g...  35.2 us
    ppermute x25, starting transfers between devices, swap(): return lax.ppermute(array, axis, [(i, i ^ mask) for i in range(count)])  28.6 us
    pallas_call x1, Pallas kernels, local(): pl.pallas_call(attend_kernel, grid=(1,), in_specs=[pl.BlockSpec(memory_sp...  3.94 us
  transfers between devices with their start and end apart: 25, of which 11 were waited for; matrix products, arithmetic and copies ran while one was open for 1% of the time, Pallas kernels for 26%

profile of v7, /device:TPU:0, one launch (start us, length us, event | category | flops | bytes accessed | tf_op | source)
XLA Modules:
  0.0 106.2 jit_solution(6179872296536707236)
XLA Ops:
  0.7 3.9 %attend.1 = (bf16[512,1024]{1,0:T(8,128)(2,1)S(1)}, bf16[512,64]{1,0:T(8,128)(2,1)S(1)}, bf16[512,64]{1,0:T(8,128)(2,1)S(1)}, bf16[512,256]{1,0:T(8,128)(2,1)S(1...) custom-call(s32[1,4]{1,0:T(1,128)} %lengths.1, bf16[512,1024]{1,0:T(8,128)(2,1)} %refs_5_.2, f32[1,1024]{1,0:T(1,128)} %bitcast.11, ...), custom_call_target="tpu_custom_call" | custom-call | flops 1000 | bytes 1000 | tf_op jit(solution)/shard_map/attend/pallas_call | solution.py:508
  4.6 3.0 %collective-permute-start.1 = (bf16[512,256]{1,0:T(8,128)(2,1)S(1)}, bf16[512,256]{1,0:T(8,128)(2,1)S(1)}, u32[]{:S(2)}, u32[]{:S(2)}) collective-permute-start(bf16[512,256]{1,0:T(8,128)(2,1)S(1)} %get-tuple-element.133.ctx.refs_0_.ctx_in), channel_id=1, source_target_pairs={{0,2},{1,3},{2,0},{3,1},{4,6},{5,7},{6,4},{7,5},{8,10},{9,11},{10,... | collective-permute-start | bytes 786440 | tf_op jit(solution)/shard_map/ppermute | solution.py:471
  7.7 4.6 %fetch.1 = (bf16[688,1024]{1,0:T(8,128)(2,1)S(1)}, bf16[1024,1024]{1,0:T(8,128)(2,1)S(1)}, bf16[688,1024]{1,0:T(8,128)(2,1)S(1)}, bf16[688,1024]{1,0:T(8,128)(2,1)S(1)}, f32[512,688]{1,0:T(8,128)S(1)}) custom-call(s32[6]{0:T(128)S(1)} %pad_add_fusion.where.place, bf16[512,256]{1,0:T(8,128)(2,1)S(1)} %get-tuple-element.133.ctx.refs_0_.ctx_in, ...), custom_call_target="tpu_custom_call" | custom-call | flops 1000 | bytes 1000 | tf_op jit(solution)/shard_map/fetch/pallas_call | solution.py:429
  12.4 1.6 %collective-permute-done.1.refs_2_ = bf16[512,256]{1,0:T(8,128)(2,1)S(1)} collective-permute-done((bf16[512,256]{1,0:T(8,128)(2,1)S(1)}, bf16[512,256]{1,0:T(8,128)(2,1)S(1)}, u32[]{:S(2)}, u32[]{:S(2)}) %collective-permute-start.1) | collective-permute-done | bytes 262176 | tf_op jit(solution)/shard_map/ppermute | solution.py:471
  13.9 1.5 %collective-permute-done.2.refs_3_ = bf16[512,256]{1,0:T(8,128)(2,1)S(1)} collective-permute-done((bf16[512,256]{1,0:T(8,128)(2,1)S(1)}, bf16[512,256]{1,0:T(8,128)(2,1)S(1)}, u32[]{:S(2)}, u32[]{:S(2)}) %collective-permute-start.2) | collective-permute-done | bytes 262176 | tf_op jit(solution)/shard_map/ppermute | solution.py:471
  15.5 5.8 %feed.1 = (f32[512,1024]{1,0:T(8,128)S(1)}, bf16[512,1024]{1,0:T(8,128)(2,1)S(1)}, bf16[512,688]{1,0:T(8,128)(2,1)S(1)}, bf16[512,688]{1,0:T(8,128)(2,1)S(1)}, b...) custom-call(s32[6]{0:T(128)S(1)} %pad_add_fusion.where.place, ...), custom_call_target="tpu_custom_call" | custom-call | flops 3000000000 | bytes 1000 | tf_op jit(solution)/shard_map/feed/pallas_call | solution.py:429
  21.5 2.7 %aways.1 = (bf16[4,1072,128]{2,1,0:T(8,128)(2,1)S(1)}, bf16[4,992,128]{2,1,0:T(8,128)(2,1)S(1)}, bf16[256,1024]{1,0:T(8,128)(2,1)S(1)}, bf16[256,1024]{1,0:T(8,128)(2,1)S(1)}) custom-call(s32[6]{0:T(128)S(1)} %pad_add_fusion.where.place, bf16[512,688]{1,0:T(8,128)(2,1)S(1)} %get-tuple-element.118.inner, bf16[512,688]{1,0:T(8,128)(2,1)S(1)} %get-tuple-element.108.gate, ...), custom_call_target="tpu_custom_call" | custom-call | flops 1000 | bytes 1000 | tf_op jit(solution)/shard_map/aways/pallas_call | solution.py:429
  24.2 0.2 add_convert_fusion.3
  24.4 1.8 %collective-permute-start.4 = (bf16[256,1024]{1,0:T(8,128)(2,1)S(1)}, bf16[256,1024]{1,0:T(8,128)(2,1)S(1)}, u32[]{:S(2)}, u32[]{:S(2)}) collective-permute-start(bf16[256,1024]{1,0:T(8,128)(2,1)S(1)} %add_convert_fusion.3), channel_id=1, source_target_pairs={{0,2},{1,3},{2,0},{3,1},{4,6},{5,7},{6,4},{7,5},{8,10},{9,11},{10,... | collective-permute-start | bytes 1572872 | tf_op jit(solution)/shard_map/ppermute | solution.py:471
  26.3 1.6 %collective-permute-start.9 = (bf16[4,992,128]{2,1,0:T(8,128)(2,1)S(1)}, bf16[4,992,128]{2,1,0:T(8,128)(2,1)S(1)}, u32[]{:S(2)}, u32[]{:S(2)}) collective-permute-start(bf16[4,992,128]{2,1,0:T(8,128)(2,1)S(1)} %get-tuple-element.111), channel_id=1, source_target_pairs={{0,8},{4,12},{8,0},{12,4},{16,24},{20,28},{24,16},{28,20},{1,9},{5... | collective-permute-start | bytes 3047432 | tf_op jit(solution)/shard_map/ppermute | solution.py:471
  27.9 1.5 %collective-permute-start.8 = (bf16[4,1072,128]{2,1,0:T(8,128)(2,1)S(1)}, bf16[4,1072,128]{2,1,0:T(8,128)(2,1)S(1)}, u32[]{:S(2)}, u32[]{:S(2)}) collective-permute-start(bf16[4,1072,128]{2,1,0:T(8,128)(2,1)S(1)} %get-tuple-element.131), channel_id=1, source_target_pairs={{0,4},{4,0},{8,12},{12,8},{16,20},{20,16},{24,28},{28,24},{1,5},{5... | collective-permute-start | bytes 3293192 | tf_op jit(solution)/shard_map/ppermute | solution.py:471
  29.4 1.6 %prepare.1 = (bf16[4,768,256]{2,1,0:T(8,128)(2,1)S(1)}, bf16[4,768,256]{2,1,0:T(8,128)(2,1)S(1)}, f32[512,1]{1,0:T(8,128)S(1)}) custom-call(s32[6]{0:T(128)S(1)} %pad_add_fusion.where.place, bf16[512,64]{1,0:T(8,128)(2,1)S(1)} %get-tuple-element.114.q_in, bf16[512,64]{1,0:T(8,128)(2,1)S(1)} %get-tuple-element.115.k_in, ...), custom_call_target="tpu_custom_call" | custom-call | flops 1000 | bytes 1000 | tf_op jit(solution)/shard_map/prepare/pallas_call | solution.py:429
  30.9 1.9 %keeps.1 = (bf16[4,1072,128]{2,1,0:T(8,128)(2,1)S(1)}, bf16[4,992,128]{2,1,0:T(8,128)(2,1)S(1)}) custom-call(s32[6]{0:T(128)S(1)} %pad_add_fusion.where.place, bf16[512,688]{1,0:T(8,128)(2,1)S(1)} %get-tuple-element.118.inner, bf16[512,688]{1,0:T(8,128)(2,1)S(1)} %get-tuple-element.108.gate, bf16[512,688]{1,0:T(8,128)(2,1)S(1)} %get-tuple-element.109.up, ...), custom_call_target="tpu_custom_call" | custom-call | flops 1000 | bytes 1000 | tf_op jit(solution)/shard_map/keeps/pallas_call | solution.py:429
  32.9 5.8 %collective-permute-done.4 = bf16[256,1024]{1,0:T(8,128)(2,1)S(1)} collective-permute-done((bf16[256,1024]{1,0:T(8,128)(2,1)S(1)}, bf16[256,1024]{1,0:T(8,128)(2,1)S(1)}, u32[]{:S(2)}, u32[]{:S(2)}) %collective-permute-start.4) | collective-permute-done | bytes 524320 | tf_op jit(solution)/shard_map/ppermute | solution.py:471
  38.7 0.4 add_convert_fusion.2.own
  39.2 0.2 add_convert_fusion.1
  39.4 1.8 %collective-permute-start.14 = (bf16[256,1024]{1,0:T(8,128)(2,1)S(1)}, bf16[256,1024]{1,0:T(8,128)(2,1)S(1)}, u32[]{:S(2)}, u32[]{:S(2)}) collective-permute-start(bf16[256,1024]{1,0:T(8,128)(2,1)S(1)} %add_convert_fusion.1), channel_id=1, source_target_pairs={{0,2},{1,3},{2,0},{3,1},{4,6},{5,7},{6,4},{7,5},{8,10},{9,11},{10,... | collective-permute-start | bytes 1572872 | tf_op jit(solution)/shard_map/ppermute | solution.py:471
  41.2 4.4 %back.1 = (f32[512,1024]{1,0:T(8,128)S(1)}, bf16[512,1024]{1,0:T(8,128)(2,1)S(1)}, bf16[512,384]{1,0:T(8,128)(2,1)S(1)}, f32[1,1024]{1,0:T(1,128)S(1)}) custom-call(s32[6]{0:T(128)S(1)} %pad_add_fusion.where.place, bf16[256,1024]{1,0:T(8,128)(2,1)S(1)} %add_convert_fusion.2.own, bf16[256,1024]{1,0:T(8,128)(2,1)S(1)} %collective-permute-done.5.other, ...), custom_call_target="tpu_custom_call" | custom-call | flops 1000 | bytes 1000 | tf_op jit(solution)/shard_map/back/pallas_call | solution.py:429
  45.5 1.1 %late_away.1 = bf16[4,656,128]{2,1,0:T(8,128)(2,1)S(1)} custom-call(s32[6]{0:T(128)S(1)} %pad_add_fusion.where.place, bf16[512,256]{1,0:T(8,128)(2,1)S(1)} %get-tuple-element.133.ctx.refs_0_.ctx_in, bf16[512,384]{1,0:T(8,128)(2,1)S(1)} %get-tuple-element.129.refs_1_.refs_0_, bf16[512,1024]{1,0:T(8,128)(2,1)S(1)} %get-tuple-element.134.refs_2_, ...), custom_call_target="tpu_custom_call" | custom-call | flops 1000 | bytes 1000 | tf_op jit(solution)/shard_map/late_away/pallas_call | solution.py:429
  46.7 1.6 %collective-permute-start.12 = (bf16[4,656,128]{2,1,0:T(8,128)(2,1)S(1)}, bf16[4,656,128]{2,1,0:T(8,128)(2,1)S(1)}, u32[]{:S(2)}, u32[]{:S(2)}) collective-permute-start(bf16[4,656,128]{2,1,0:T(8,128)(2,1)S(1)} %late_away.1), channel_id=1, source_target_pairs={{0,4},{4,0},{8,12},{12,8},{16,20},{20,16},{24,28},{28,24},{1,5},{5... | collective-permute-start | bytes 2015240 | tf_op jit(solution)/shard_map/ppermute | solution.py:471
  48.3 2.8 %collective-permute-done.9.come = bf16[4,992,128]{2,1,0:T(8,128)(2,1)S(1)} collective-permute-done((bf16[4,992,128]{2,1,0:T(8,128)(2,1)S(1)}, bf16[4,992,128]{2,1,0:T(8,128)(2,1)S(1)}, u32[]{:S(2)}, u32[]{:S(2)}) %collective-permute-start.9) | collective-permute-done | bytes 1015840 | tf_op jit(solution)/shard_map/ppermute | solution.py:471
  51.1 0.8 z_keep.1
  51.9 2.7 %collective-permute-start.11 = (bf16[2,992,128]{2,1,0:T(8,128)(2,1)S(1)}, bf16[2,992,128]{2,1,0:T(8,128)(2,1)S(1)}, u32[]{:S(2)}, u32[]{:S(2)}) collective-permute-start(bf16[2,992,128]{2,1,0:T(8,128)(2,1)S(1)} %get-tuple-element.137), channel_id=1, source_target_pairs={{0,16},{4,20},{8,24},{12,28},{16,0},{20,4},{24,8},{28,12},{1,17},{... | collective-permute-start | bytes 1523720 | tf_op jit(solution)/shard_map/ppermute | solution.py:471
  54.6 0.5 collective-permute-start.13
  55.0 0.8 x_keep.1
  55.8 1.7 %collective-permute-start.10 = (bf16[2,1072,128]{2,1,0:T(8,128)(2,1)S(1)}, bf16[2,1072,128]{2,1,0:T(8,128)(2,1)S(1)}, u32[]{:S(2)}, u32[]{:S(2)}) collective-permute-start(bf16[2,1072,128]{2,1,0:T(8,128)(2,1)S(1)} %get-tuple-element.140), channel_id=1, source_target_pairs={{0,8},{4,12},{8,0},{12,4},{16,24},{20,28},{24,16},{28,20},{1,9},{5... | collective-permute-start | bytes 1646600 | tf_op jit(solution)/shard_map/ppermute | solution.py:471
  57.5 0.2 add_convert_fusion.refs_7_
  57.7 7.2 %collective-permute-done.13.refs_2_ = bf16[512,384]{1,0:T(8,128)(2,1)S(1)} collective-permute-done((bf16[512,384]{1,0:T(8,128)(2,1)S(1)}, bf16[512,384]{1,0:T(8,128)(2,1)S(1)}, u32[]{:S(2)}, u32[]{:S(2)}) %collective-permute-start.13) | collective-permute-done | bytes 393248 | tf_op jit(solution)/shard_map/ppermute | solution.py:471
  65.0 3.6 %collective-permute-done.12.refs_5_ = bf16[4,656,128]{2,1,0:T(8,128)(2,1)S(1)} collective-permute-done((bf16[4,656,128]{2,1,0:T(8,128)(2,1)S(1)}, bf16[4,656,128]{2,1,0:T(8,128)(2,1)S(1)}, u32[]{:S(2)}, u32[]{:S(2)}) %collective-permute-start.12) | collective-permute-done | bytes 671776 | tf_op jit(solution)/shard_map/ppermute | solution.py:471
  68.6 1.1 %late_keep.1 = (f32[656,128]{1,0:T(8,128)S(1)}, bf16[656,128]{1,0:T(8,128)(2,1)S(1)}, bf16[656,128]{1,0:T(8,128)(2,1)S(1)}, bf16[656,128]{1,0:T(8,128)(2,1)S(1)}) custom-call(s32[6]{0:T(128)S(1)} %pad_add_fusion.where.place, bf16[512,256]{1,0:T(8,128)(2,1)S(1)} %get-tuple-element.133.ctx.refs_0_.ctx_in, ...), custom_call_target="tpu_custom_call" | custom-call | flops 1000 | bytes 1000 | tf_op jit(solution)/shard_map/late_keep/pallas_call | solution.py:429
  69.7 2.7 %collective-permute-start.17 = (bf16[656,128]{1,0:T(8,128)(2,1)S(1)}, bf16[656,128]{1,0:T(8,128)(2,1)S(1)}, u32[]{:S(2)}, u32[]{:S(2)}) collective-permute-start(bf16[656,128]{1,0:T(8,128)(2,1)S(1)} %get-tuple-element.154), channel_id=1, source_target_pairs={{0,16},{4,20},{8,24},{12,28},{16,0},{20,4},{24,8},{28,12},{1,17},{... | collective-permute-start | bytes 503816 | tf_op jit(solution)/shard_map/ppermute | solution.py:471
  72.4 0.5 collective-permute-start.18
  72.8 5.8 %collective-permute-done.11.come = bf16[2,992,128]{2,1,0:T(8,128)(2,1)S(1)} collective-permute-done((bf16[2,992,128]{2,1,0:T(8,128)(2,1)S(1)}, bf16[2,992,128]{2,1,0:T(8,128)(2,1)S(1)}, u32[]{:S(2)}, u32[]{:S(2)}) %collective-permute-start.11) | collective-permute-done | bytes 507936 | tf_op jit(solution)/shard_map/ppermute | solution.py:471
  78.7 2.4 %collective-permute-start.19 = (bf16[656,128]{1,0:T(8,128)(2,1)S(1)}, bf16[656,128]{1,0:T(8,128)(2,1)S(1)}, u32[]{:S(2)}, u32[]{:S(2)}) collective-permute-start(bf16[656,128]{1,0:T(8,128)(2,1)S(1)} %get-tuple-element.145), channel_id=1, source_target_pairs={{0,24},{4,28},{8,16},{12,20},{16,8},{20,12},{24,0},{28,4},{1,25},{... | collective-permute-start | bytes 503816 | tf_op jit(solution)/shard_map/ppermute | solution.py:471
  81.1 0.7 z_hop.1
  81.8 1.8 %collective-permute-done.10.come = bf16[2,1072,128]{2,1,0:T(8,128)(2,1)S(1)} collective-permute-done((bf16[2,1072,128]{2,1,0:T(8,128)(2,1)S(1)}, bf16[2,1072,128]{2,1,0:T(8,128)(2,1)S(1)}, u32[]{:S(2)}, u32[]{:S(2)}) %collective-permute-start.10) | collective-permute-done | bytes 548896 | tf_op jit(solution)/shard_map/ppermute | solution.py:471
  83.6 0.7 x_hop.1
  84.3 0.6 collective-permute-start.15
  84.8 1.0 collective-permute-done.17.refs_0_
  85.8 1.7 %collective-permute-done.18.refs_1_ = bf16[656,128]{1,0:T(8,128)(2,1)S(1)} collective-permute-done((bf16[656,128]{1,0:T(8,128)(2,1)S(1)}, bf16[656,128]{1,0:T(8,128)(2,1)S(1)}, u32[]{:S(2)}, u32[]{:S(2)}) %collective-permute-start.18) | collective-permute-done | bytes 167968 | tf_op jit(solution)/shard_map/ppermute | solution.py:471
  87.5 3.4 %collective-permute-start.24 = (bf16[1,992,128]{2,1,0:T(8,128)(2,1)S(1)}, bf16[1,992,128]{2,1,0:T(8,128)(2,1)S(1)}, u32[]{:S(2)}, u32[]{:S(2)}) collective-permute-start(bf16[1,992,128]{2,1,0:T(8,128)(2,1)S(1)} %get-tuple-element.147), channel_id=1, source_target_pairs={{0,4},{4,0},{8,12},{12,8},{16,20},{20,16},{24,28},{28,24},{1,5},{5... | collective-permute-start | bytes 761864 | tf_op jit(solution)/shard_map/ppermute | solution.py:471
  90.9 1.3 %late.1 = (f32[256,128]{1,0:T(8,128)}, f32[1,128]{1,0:T(1,128)}, bf16[128,384]{1,0:T(8,128)(2,1)S(1)}) custom-call(s32[6]{0:T(128)S(1)} %pad_add_fusion.where.place, f32[656,128]{1,0:T(8,128)S(1)} %get-tuple-element.153.held, bf16[656,128]{1,0:T(8,128)(2,1)S(1)} %collective-permute-done.17.refs_0_, bf16[656,128]{1,0:T(8,128)(2,1)S(1)} %collective-permute-done.18.refs_1_, ...), custom_call_target="tpu_custom_call" | custom-call | flops 10000000000 | bytes 1000 | tf_op jit(solution)/shard_map/late/pallas_call | solution.py:429
  92.2 2.0 %collective-permute-start.21 = (bf16[128,384]{1,0:T(8,128)(2,1)S(1)}, bf16[128,384]{1,0:T(8,128)(2,1)S(1)}, u32[]{:S(2)}, u32[]{:S(2)}) collective-permute-start(bf16[128,384]{1,0:T(8,128)(2,1)S(1)} %get-tuple-element.169.refs_0_), channel_id=1, source_target_pairs={{0,2},{1,3},{2,0},{3,1},{4,6},{5,7},{6,4},{7,5},{8,10},{9,11},{10,... | collective-permute-start | bytes 294920 | tf_op jit(solution)/shard_map/ppermute | solution.py:471
  94.3 4.6 %grad_input.1 = (bf16[512,1024]{1,0:T(8,128)(2,1)}, bf16[512,1024]{1,0:T(8,128)(2,1)}) custom-call(s32[6]{0:T(128)S(1)} %pad_add_fusion.where.place, bf16[512,384]{1,0:T(8,128)(2,1)S(1)} %get-tuple-element.129.refs_1_.refs_0_, bf16[512,384]{1,0:T(8,128)(2,1)S(1)} %collective-permute-done.7.refs_1_, bf16[512,384]{1,0:T(8,128)(2,1)S(1)} %collective-permute-done.13.refs_2_, ...), custom_call_target="tpu_custom_call" | custom-call | flops 1000 | bytes 1000 | tf_op jit(solution)/shard_map/grad_input/pallas_call | solution.py:429
  98.9 0.5 collective-permute-start.22
  99.4 3.7 %collective-permute-done.23.x_come = bf16[1,1072,128]{2,1,0:T(8,128)(2,1)S(1)} collective-permute-done((bf16[1,1072,128]{2,1,0:T(8,128)(2,1)S(1)}, bf16[1,1072,128]{2,1,0:T(8,128)(2,1)S(1)}, u32[]{:S(2)}, u32[]{:S(2)}) %collective-permute-start.23) | collective-permute-done | bytes 274464 | tf_op jit(solution)/shard_map/ppermute | solution.py:471
  103.1 1.6 %hidden.1 = (f32[688,128]{1,0:T(8,128)}, f32[688,128]{1,0:T(8,128)}, f32[688,128]{1,0:T(8,128)}) custom-call(s32[6]{0:T(128)S(1)} %pad_add_fusion.where.place, bf16[1,1072,128]{2,1,0:T(8,128)(2,1)S(1)} %get-tuple-element.164.x_held, bf16[1,1072,128]{2,1,0:T(8,128)(2,1)S(1)} %collective-permute-done.23.x_come, ...), custom_call_target="tpu_custom_call" | custom-call | flops 10000000000 | bytes 1000 | tf_op jit(solution)/shard_map/hidden/pallas_call | solution.py:429
  104.6 1.6 %finish.1 = (f32[128,256]{1,0:T(8,128)}, f32[128,256]{1,0:T(8,128)}, f32[128,1024]{1,0:T(8,128)}, f32[1,128]{1,0:T(1,128)}) custom-call(s32[6]{0:T(128)S(1)} %pad_add_fusion.where.place, bf16[128,384]{1,0:T(8,128)(2,1)S(1)} %get-tuple-element.169.refs_0_, bf16[128,384]{1,0:T(8,128)(2,1)S(1)} %collective-permute-done.20.refs_1_, ...), custom_call_target="tpu_custom_call" | custom-call | flops 1000 | bytes 1000 | tf_op jit(solution)/shard_map/finish/pallas_call | solution.py:429
  (40 shorter events, 0.5 us)
Async XLA Ops:
  0.6 7.0 %copy-start.7 = (s32[1,4]{1,0:T(1,128)S(1)}, s32[1,4]{1,0:T(1,128)}, u32[]{:S(2)}) copy-start(s32[1,4]{1,0:T(1,128)} %lengths.1) | copy-start | bytes 52
  4.6 9.3 %collective-permute-start.1 = (bf16[512,256]{1,0:T(8,128)(2,1)S(1)}, bf16[512,256]{1,0:T(8,128)(2,1)S(1)}, u32[]{:S(2)}, u32[]{:S(2)}) collective-permute-start(bf16[512,256]{1,0:T(8,128)(2,1)S(1)} %get-tuple-element.133.ctx.refs_0_.ctx_in), channel_id=1, source_target_pairs={{0,2},{1,3},{2,0},{3,1},{4,6},{5,7},{6,4},{7,5},{8,10},{9,11},{10,... | collective-permute-start | bytes 786440 | tf_op jit(solution)/shard_map/ppermute | solution.py:471
  7.6 6.3 %collective-permute-start = (bf16[512,256]{1,0:T(8,128)(2,1)S(1)}, bf16[512,256]{1,0:T(8,128)(2,1)S(1)}, u32[]{:S(2)}, u32[]{:S(2)}) collective-permute-start(bf16[512,256]{1,0:T(8,128)(2,1)S(1)} %get-tuple-element.133.ctx.refs_0_.ctx_in), channel_id=1, source_target_pairs={{0,1},{1,0},{2,3},{3,2},{4,5},{5,4},{6,7},{7,6},{8,9},{9,8},{10,11... | collective-permute-start | bytes 786440 | tf_op jit(solution)/shard_map/ppermute | solution.py:471
  7.7 7.8 %copy-start.4 = (bf16[512,1024]{1,0:T(8,128)(2,1)S(1)}, bf16[512,1024]{1,0:T(8,128)(2,1)}, u32[]{:S(2)}) copy-start(bf16[512,1024]{1,0:T(8,128)(2,1)} %refs_5_.2) | copy-start | bytes 3145732
  7.7 7.8 %copy-start.6 = (f32[1024]{0:T(1024)S(1)}, f32[1024]{0:T(1024)}, u32[]{:S(2)}) copy-start(f32[1024]{0:T(1024)} %param.18) | copy-start | bytes 12292
  13.9 1.5 %collective-permute-start.2 = (bf16[512,256]{1,0:T(8,128)(2,1)S(1)}, bf16[512,256]{1,0:T(8,128)(2,1)S(1)}, u32[]{:S(2)}, u32[]{:S(2)}) collective-permute-start(bf16[512,256]{1,0:T(8,128)(2,1)S(1)} %collective-permute-done.1.refs_2_), channel_id=1, source_target_pairs={{0,1},{1,0},{2,3},{3,2},{4,5},{5,4},{6,7},{7,6},{8,9},{9,8},{10,11... | collective-permute-start | bytes 786440 | tf_op jit(solution)/shard_map/ppermute | solution.py:471
  15.5 6.0 %copy-start.1 = (bf16[512,1024]{1,0:T(8,128)(2,1)S(1)}, bf16[512,1024]{1,0:T(8,128)(2,1)}, u32[]{:S(2)}) copy-start(bf16[512,1024]{1,0:T(8,128)(2,1)} %cot.7) | copy-start | bytes 3145732
  21.3 2.9 %collective-permute-start.3 = (bf16[256,1024]{1,0:T(8,128)(2,1)S(1)}, bf16[256,1024]{1,0:T(8,128)(2,1)S(1)}, u32[]{:S(2)}, u32[]{:S(2)}) collective-permute-start(bf16[256,1024]{1,0:T(8,128)(2,1)S(1)} %get-tuple-element.106), channel_id=1, source_target_pairs={{0,1},{1,0},{2,3},{3,2},{4,5},{5,4},{6,7},{7,6},{8,9},{9,8},{10,11... | collective-permute-start | bytes 1572872 | tf_op jit(solution)/shard_map/ppermute | solution.py:471
  24.4 14.3 %collective-permute-start.4 = (bf16[256,1024]{1,0:T(8,128)(2,1)S(1)}, bf16[256,1024]{1,0:T(8,128)(2,1)S(1)}, u32[]{:S(2)}, u32[]{:S(2)}) collective-permute-start(bf16[256,1024]{1,0:T(8,128)(2,1)S(1)} %add_convert_fusion.3), channel_id=1, source_target_pairs={{0,2},{1,3},{2,0},{3,1},{4,6},{5,7},{6,4},{7,5},{8,10},{9,11},{10,... | collective-permute-start | bytes 1572872 | tf_op jit(solution)/shard_map/ppermute | solution.py:471
  26.2 12.9 %collective-permute-start.6 = (bf16[256,1024]{1,0:T(8,128)(2,1)S(1)}, bf16[256,1024]{1,0:T(8,128)(2,1)S(1)}, u32[]{:S(2)}, u32[]{:S(2)}) collective-permute-start(bf16[256,1024]{1,0:T(8,128)(2,1)S(1)} %get-tuple-element.122), channel_id=1, source_target_pairs={{0,1},{1,0},{2,3},{3,2},{4,5},{5,4},{6,7},{7,6},{8,9},{9,8},{10,11... | collective-permute-start | bytes 1572872 | tf_op jit(solution)/shard_map/ppermute | solution.py:471
  26.3 24.8 %collective-permute-start.9 = (bf16[4,992,128]{2,1,0:T(8,128)(2,1)S(1)}, bf16[4,992,128]{2,1,0:T(8,128)(2,1)S(1)}, u32[]{:S(2)}, u32[]{:S(2)}) collective-permute-start(bf16[4,992,128]{2,1,0:T(8,128)(2,1)S(1)} %get-tuple-element.111), channel_id=1, source_target_pairs={{0,8},{4,12},{8,0},{12,4},{16,24},{20,28},{24,16},{28,20},{1,9},{5... | collective-permute-start | bytes 3047432 | tf_op jit(solution)/shard_map/ppermute | solution.py:471
  27.9 27.1 %collective-permute-start.8 = (bf16[4,1072,128]{2,1,0:T(8,128)(2,1)S(1)}, bf16[4,1072,128]{2,1,0:T(8,128)(2,1)S(1)}, u32[]{:S(2)}, u32[]{:S(2)}) collective-permute-start(bf16[4,1072,128]{2,1,0:T(8,128)(2,1)S(1)} %get-tuple-element.131), channel_id=1, source_target_pairs={{0,4},{4,0},{8,12},{12,8},{16,20},{20,16},{24,28},{28,24},{1,5},{5... | collective-permute-start | bytes 3293192 | tf_op jit(solution)/shard_map/ppermute | solution.py:471
  39.1 2.1 %collective-permute-start.5 = (bf16[256,1024]{1,0:T(8,128)(2,1)S(1)}, bf16[256,1024]{1,0:T(8,128)(2,1)S(1)}, u32[]{:S(2)}, u32[]{:S(2)}) collective-permute-start(bf16[256,1024]{1,0:T(8,128)(2,1)S(1)} %add_convert_fusion.2.own), channel_id=1, source_target_pairs={{0,1},{1,0},{2,3},{3,2},{4,5},{5,4},{6,7},{7,6},{8,9},{9,8},{10,11... | collective-permute-start | bytes 1572872 | tf_op jit(solution)/shard_map/ppermute | solution.py:471
  39.4 18.2 %collective-permute-start.14 = (bf16[256,1024]{1,0:T(8,128)(2,1)S(1)}, bf16[256,1024]{1,0:T(8,128)(2,1)S(1)}, u32[]{:S(2)}, u32[]{:S(2)}) collective-permute-start(bf16[256,1024]{1,0:T(8,128)(2,1)S(1)} %add_convert_fusion.1), channel_id=1, source_target_pairs={{0,2},{1,3},{2,0},{3,1},{4,6},{5,7},{6,4},{7,5},{8,10},{9,11},{10,... | collective-permute-start | bytes 1572872 | tf_op jit(solution)/shard_map/ppermute | solution.py:471
  46.7 21.9 %collective-permute-start.12 = (bf16[4,656,128]{2,1,0:T(8,128)(2,1)S(1)}, bf16[4,656,128]{2,1,0:T(8,128)(2,1)S(1)}, u32[]{:S(2)}, u32[]{:S(2)}) collective-permute-start(bf16[4,656,128]{2,1,0:T(8,128)(2,1)S(1)} %late_away.1), channel_id=1, source_target_pairs={{0,4},{4,0},{8,12},{12,8},{16,20},{20,16},{24,28},{28,24},{1,5},{5... | collective-permute-start | bytes 2015240 | tf_op jit(solution)/shard_map/ppermute | solution.py:471
  51.9 26.8 %collective-permute-start.11 = (bf16[2,992,128]{2,1,0:T(8,128)(2,1)S(1)}, bf16[2,992,128]{2,1,0:T(8,128)(2,1)S(1)}, u32[]{:S(2)}, u32[]{:S(2)}) collective-permute-start(bf16[2,992,128]{2,1,0:T(8,128)(2,1)S(1)} %get-tuple-element.137), channel_id=1, source_target_pairs={{0,16},{4,20},{8,24},{12,28},{16,0},{20,4},{24,8},{28,12},{1,17},{... | collective-permute-start | bytes 1523720 | tf_op jit(solution)/shard_map/ppermute | solution.py:471
  54.6 10.4 %collective-permute-start.13 = (bf16[512,384]{1,0:T(8,128)(2,1)S(1)}, bf16[512,384]{1,0:T(8,128)(2,1)S(1)}, u32[]{:S(2)}, u32[]{:S(2)}) collective-permute-start(bf16[512,384]{1,0:T(8,128)(2,1)S(1)} %get-tuple-element.129.refs_1_.refs_0_), channel_id=1, source_target_pairs={{0,2},{1,3},{2,0},{3,1},{4,6},{5,7},{6,4},{7,5},{8,10},{9,11},{10,... | collective-permute-start | bytes 1179656 | tf_op jit(solution)/shard_map/ppermute | solution.py:471
  55.8 27.7 %collective-permute-start.10 = (bf16[2,1072,128]{2,1,0:T(8,128)(2,1)S(1)}, bf16[2,1072,128]{2,1,0:T(8,128)(2,1)S(1)}, u32[]{:S(2)}, u32[]{:S(2)}) collective-permute-start(bf16[2,1072,128]{2,1,0:T(8,128)(2,1)S(1)} %get-tuple-element.140), channel_id=1, source_target_pairs={{0,8},{4,12},{8,0},{12,4},{16,24},{20,28},{24,16},{28,20},{1,9},{5... | collective-permute-start | bytes 1646600 | tf_op jit(solution)/shard_map/ppermute | solution.py:471
  57.5 26.7 %collective-permute-start.7 = (bf16[512,384]{1,0:T(8,128)(2,1)S(1)}, bf16[512,384]{1,0:T(8,128)(2,1)S(1)}, u32[]{:S(2)}, u32[]{:S(2)}) collective-permute-start(bf16[512,384]{1,0:T(8,128)(2,1)S(1)} %get-tuple-element.129.refs_1_.refs_0_), channel_id=1, source_target_pairs={{0,1},{1,0},{2,3},{3,2},{4,5},{5,4},{6,7},{7,6},{8,9},{9,8},{10,11... | collective-permute-start | bytes 1179656 | tf_op jit(solution)/shard_map/ppermute | solution.py:471
  69.7 16.1 %collective-permute-start.17 = (bf16[656,128]{1,0:T(8,128)(2,1)S(1)}, bf16[656,128]{1,0:T(8,128)(2,1)S(1)}, u32[]{:S(2)}, u32[]{:S(2)}) collective-permute-start(bf16[656,128]{1,0:T(8,128)(2,1)S(1)} %get-tuple-element.154), channel_id=1, source_target_pairs={{0,16},{4,20},{8,24},{12,28},{16,0},{20,4},{24,8},{28,12},{1,17},{... | collective-permute-start | bytes 503816 | tf_op jit(solution)/shard_map/ppermute | solution.py:471
  72.4 15.1 %collective-permute-start.18 = (bf16[656,128]{1,0:T(8,128)(2,1)S(1)}, bf16[656,128]{1,0:T(8,128)(2,1)S(1)}, u32[]{:S(2)}, u32[]{:S(2)}) collective-permute-start(bf16[656,128]{1,0:T(8,128)(2,1)S(1)} %get-tuple-element.155), channel_id=1, source_target_pairs={{0,8},{4,12},{8,0},{12,4},{16,24},{20,28},{24,16},{28,20},{1,9},{5... | collective-permute-start | bytes 503816 | tf_op jit(solution)/shard_map/ppermute | solution.py:471
  78.7 12.2 %collective-permute-start.19 = (bf16[656,128]{1,0:T(8,128)(2,1)S(1)}, bf16[656,128]{1,0:T(8,128)(2,1)S(1)}, u32[]{:S(2)}, u32[]{:S(2)}) collective-permute-start(bf16[656,128]{1,0:T(8,128)(2,1)S(1)} %get-tuple-element.145), channel_id=1, source_target_pairs={{0,24},{4,28},{8,16},{12,20},{16,8},{20,12},{24,0},{28,4},{1,25},{... | collective-permute-start | bytes 503816 | tf_op jit(solution)/shard_map/ppermute | solution.py:471
  83.6 10.7 %collective-permute-start.16 = (bf16[256,1024]{1,0:T(8,128)(2,1)S(1)}, bf16[256,1024]{1,0:T(8,128)(2,1)S(1)}, u32[]{:S(2)}, u32[]{:S(2)}) collective-permute-start(bf16[256,1024]{1,0:T(8,128)(2,1)S(1)} %add_convert_fusion.refs_7_), channel_id=1, source_target_pairs={{0,1},{1,0},{2,3},{3,2},{4,5},{5,4},{6,7},{7,6},{8,9},{9,8},{10,11... | collective-permute-start | bytes 1572872 | tf_op jit(solution)/shard_map/ppermute | solution.py:471
  84.3 10.0 %collective-permute-start.15 = (bf16[512,384]{1,0:T(8,128)(2,1)S(1)}, bf16[512,384]{1,0:T(8,128)(2,1)S(1)}, u32[]{:S(2)}, u32[]{:S(2)}) collective-permute-start(bf16[512,384]{1,0:T(8,128)(2,1)S(1)} %collective-permute-done.13.refs_2_), channel_id=1, source_target_pairs={{0,1},{1,0},{2,3},{3,2},{4,5},{5,4},{6,7},{7,6},{8,9},{9,8},{10,11... | collective-permute-start | bytes 1179656 | tf_op jit(solution)/shard_map/ppermute | solution.py:471
  85.8 17.2 %collective-permute-start.23 = (bf16[1,1072,128]{2,1,0:T(8,128)(2,1)S(1)}, bf16[1,1072,128]{2,1,0:T(8,128)(2,1)S(1)}, u32[]{:S(2)}, u32[]{:S(2)}) collective-permute-start(bf16[1,1072,128]{2,1,0:T(8,128)(2,1)S(1)} %get-tuple-element.149), channel_id=1, source_target_pairs={{0,16},{4,20},{8,24},{12,28},{16,0},{20,4},{24,8},{28,12},{1,17},{... | collective-permute-start | bytes 823304 | tf_op jit(solution)/shard_map/ppermute | solution.py:471
  87.5 11.9 %collective-permute-start.24 = (bf16[1,992,128]{2,1,0:T(8,128)(2,1)S(1)}, bf16[1,992,128]{2,1,0:T(8,128)(2,1)S(1)}, u32[]{:S(2)}, u32[]{:S(2)}) collective-permute-start(bf16[1,992,128]{2,1,0:T(8,128)(2,1)S(1)} %get-tuple-element.147), channel_id=1, source_target_pairs={{0,4},{4,0},{8,12},{12,8},{16,20},{20,16},{24,28},{28,24},{1,5},{5... | collective-permute-start | bytes 761864 | tf_op jit(solution)/shard_map/ppermute | solution.py:471
  90.9 3.3 %copy-start = (bf16[1024,1024]{1,0:T(8,128)(2,1)S(1)}, bf16[1024,1024]{1,0:T(8,128)(2,1)}, u32[]{:S(2)}) copy-start(bf16[1024,1024]{1,0:T(8,128)(2,1)} %refs_7_.1) | copy-start | bytes 6291460
  90.9 3.4 %copy-start.2 = (bf16[1024,256]{1,0:T(8,128)(2,1)S(1)}, bf16[1024,256]{1,0:T(8,128)(2,1)}, u32[]{:S(2)}) copy-start(bf16[1024,256]{1,0:T(8,128)(2,1)} %refs_5_.3) | copy-start | bytes 1572868
  90.9 3.4 %copy-start.3 = (bf16[1024,256]{1,0:T(8,128)(2,1)S(1)}, bf16[1024,256]{1,0:T(8,128)(2,1)}, u32[]{:S(2)}) copy-start(bf16[1024,256]{1,0:T(8,128)(2,1)} %refs_6_.1) | copy-start | bytes 1572868
  90.9 3.4 %copy-start.5 = (f32[1024]{0:T(1024)S(1)}, f32[1024]{0:T(1024)}, u32[]{:S(2)}) copy-start(f32[1024]{0:T(1024)} %param.13) | copy-start | bytes 12292
  92.2 6.7 %collective-permute-start.21 = (bf16[128,384]{1,0:T(8,128)(2,1)S(1)}, bf16[128,384]{1,0:T(8,128)(2,1)S(1)}, u32[]{:S(2)}, u32[]{:S(2)}) collective-permute-start(bf16[128,384]{1,0:T(8,128)(2,1)S(1)} %get-tuple-element.169.refs_0_), channel_id=1, source_target_pairs={{0,2},{1,3},{2,0},{3,1},{4,6},{5,7},{6,4},{7,5},{8,10},{9,11},{10,... | collective-permute-start | bytes 294920 | tf_op jit(solution)/shard_map/ppermute | solution.py:471
  94.3 10.4 %collective-permute-start.20 = (bf16[128,384]{1,0:T(8,128)(2,1)S(1)}, bf16[128,384]{1,0:T(8,128)(2,1)S(1)}, u32[]{:S(2)}, u32[]{:S(2)}) collective-permute-start(bf16[128,384]{1,0:T(8,128)(2,1)S(1)} %get-tuple-element.169.refs_0_), channel_id=1, source_target_pairs={{0,1},{1,0},{2,3},{3,2},{4,5},{5,4},{6,7},{7,6},{8,9},{9,8},{10,11... | collective-permute-start | bytes 294920 | tf_op jit(solution)/shard_map/ppermute | solution.py:471
  98.9 5.7 %collective-permute-start.22 = (bf16[128,384]{1,0:T(8,128)(2,1)S(1)}, bf16[128,384]{1,0:T(8,128)(2,1)S(1)}, u32[]{:S(2)}, u32[]{:S(2)}) collective-permute-start(bf16[128,384]{1,0:T(8,128)(2,1)S(1)} %collective-permute-done.21.refs_2_), channel_id=1, source_target_pairs={{0,1},{1,0},{2,3},{3,2},{4,5},{5,4},{6,7},{7,6},{8,9},{9,8},{10,11... | collective-permute-start | bytes 294920 | tf_op jit(solution)/shard_map/ppermute | solution.py:471

commit v8 on v7

--- a/solution.py
+++ b/solution.py
@@ -13,7 +13,7 @@
 EPSILON = 1e-05
 F32 = jnp.float32
 BF16 = jnp.bfloat16
-COSTS = {"feed": 3000000000, "grad_input": 1000, "hidden": 10000000000, "late": 10000000000}
+COSTS = {"feed": 3000000000, "grad_input": 1000, "hidden": 10000000000, "late": 10000000000, "late_keep": 10000000000}
 VMEM_LIMIT = 20 * 1024 * 1024
 
 
@@ -258,6 +258,11 @@
         low = high
 
 
+def add_kernel(where, held, come, *outs):
+    for i, out in enumerate(outs):
+        out[...] = (held[i].astype(F32) + come[i].astype(F32)).astype(out.dtype)
+
+
 def hop_kernel(where, held, come, keep_out, away_out):
     count = keep_out.shape[0]
     for i in range(count):
@@ -575,23 +580,24 @@
         return held, come, sent
 
     last = back_own
-    x_sent, z_sent, feed_away, feed_own = call(
-        aways_kernel,
-        "aways",
-        where,
-        [inner, grad_gate, grad_up, cotangent, normed_two, w_down],
-        [
-            shape_of(2 * few, x_many, chunk, BF16),
-            shape_of(2 * few, z_many, chunk, BF16),
-            shape_of(half, width, BF16),
-            shape_of(half, width, BF16),
-        ],
+    x_sent, z_sent = call(
+        pair_aways_kernel,
+        "pair",
+        where,
+        [inner, grad_gate, grad_up, cotangent, normed_two],
+        [shape_of(2 * few, x_many, chunk, BF16), shape_of(2 * few, z_many, chunk, BF16)],
         x_fixed=x_fixed,
         z_fixed=z_fixed,
     )
     last = z_sent
     [come] = after([swap(back_away, "feat", 1)], last)
     last = back_own = plus(back_own, come)
+    feed_away, feed_own = call(
+        down_kernel, "down", where, [*after([inner], last), w_down], [shape_of(half, width, BF16)] * 2
+    )
+    last = feed_own
+    [come] = after([swap(feed_away, "feat", 1)], last)
+    last = feed_own = plus(feed_own, come)
     scores, slopes, r_two = call(
         prepare_kernel,
         "prepare",
@@ -617,8 +623,6 @@
     for mask in feat_masks[:-1]:
         [come] = after([swap(back_own, "feat", mask)], last)
         last = back_own = plus(back_own, come)
-    [come] = after([swap(feed_away, "feat", 1)], last)
-    last = feed_own = plus(feed_own, come)
     [back_other] = after([swap(back_own, "feat", 1)], last)
     grad_res, grad_mixed, grads, gain_part = call(
         back_kernel,
@@ -661,6 +665,16 @@
     shapes = [shape_of(few, x_many, chunk, BF16)] * 2
     x_held, x_sent = call(hop_kernel, "x_keep", where, [x_held, come], shapes)
     last = x_sent
+    [late_held] = call(
+        away_kernel,
+        "late_product",
+        where,
+        [*after(late_args[:1], last), *late_args[1:]],
+        [shape_of(2 * few, late_many, chunk, BF16)],
+        **late_fixed,
+        away=False,
+    )
+    last = late_held
     for mask in feat_masks[:-1]:
         [come] = after([swap(feed_own, "feat", mask)], last)
         last = feed_own = plus(feed_own, come)
@@ -668,13 +682,11 @@
     last = held[far[-1]]
     [come] = after([late_come], last)
     late, *direct = call(
-        direct_kernel,
+        add_kernel,
         "late_keep",
         where,
-        [*late_args, come],
+        [late_held, come],
         [shape_of(late_many, chunk, F32)] + [shape_of(late_many, chunk, BF16)] * (2 * few - 1),
-        inputs=len(late_args),
-        **late_fixed,
     )
     comes = [swap(piece, "dp", offset) for offset, piece in zip(positions(x_first)[1:], direct)]
     last = direct[-1]

time: 106 us -> 106 us (level)
  starting transfers between devices: 28.6 us -> 25.4 us
  Pallas kernels: 39.1 us -> 40.7 us
  waiting for transfers between devices: 36.6 us -> 38.1 us
    ppermute x25, starting transfers between devices: 28.6 us -> 25.4 us  [swap(): return lax.ppermute(array, axis, [(i, i ^ mask) for i in range(count)])]
    pallas_call x16 -> x18, Pallas kernels: 35.2 us -> 36.8 us  [call(): pl.pallas_call(functools.partial(kernel, **fixed) if fixed else kernel, g...]
    ppermute x25, waiting for transfers between devices: 36.6 us -> 38.1 us  [swap(): return lax.ppermute(array, axis, [(i, i ^ mask) for i in range(count)])]
  transfers between devices with their start and end apart: 25 -> 25, of which waited for: 11 -> 13; matrix products, arithmetic and copies ran while one was open for 1% -> 1% of each run, Pallas kernels for 26% -> 26%
where the time goes in v8:
time: 106 us
  Pallas kernels  40.7 us (38%)
  waiting for transfers between devices  38.1 us (36%)
  starting transfers between devices  25.4 us (24%)
    ppermute x25, waiting for transfers between devices, swap(): return lax.ppermute(array, axis, [(i, i ^ mask) for i in range(count)])  38.1 us
    pallas_call x18, Pallas kernels, call(): pl.pallas_call(functools.partial(kernel, **fixed) if fixed else kernel, g...  36.8 us
    ppermute x25, starting transfers between devices, swap(): return lax.ppermute(array, axis, [(i, i ^ mask) for i in range(count)])  25.4 us
    pallas_call x1, Pallas kernels, local(): pl.pallas_call(attend_kernel, grid=(1,), in_specs=[pl.BlockSpec(memory_sp...  3.94 us
  transfers between devices with their start and end apart: 25, of which 13 were waited for; matrix products, arithmetic and copies ran while one was open for 1% of the time, Pallas kernels for 26%

profile of v8, /device:TPU:0, one launch (start us, length us, event | category | flops | bytes accessed | tf_op | source)
XLA Modules:
  0.0 106.0 jit_solution(10840466720793348479)
XLA Ops:
  0.7 3.9 %attend.1 = (bf16[512,1024]{1,0:T(8,128)(2,1)S(1)}, bf16[512,64]{1,0:T(8,128)(2,1)S(1)}, bf16[512,64]{1,0:T(8,128)(2,1)S(1)}, bf16[512,256]{1,0:T(8,128)(2,1)S(1...) custom-call(s32[1,4]{1,0:T(1,128)} %lengths.1, bf16[512,1024]{1,0:T(8,128)(2,1)} %refs_5_.2, f32[1,1024]{1,0:T(1,128)} %bitcast.11, ...), custom_call_target="tpu_custom_call" | custom-call | flops 1000 | bytes 1000 | tf_op jit(solution)/shard_map/attend/pallas_call | solution.py:513
  4.6 3.0 %collective-permute-start.1 = (bf16[512,256]{1,0:T(8,128)(2,1)S(1)}, bf16[512,256]{1,0:T(8,128)(2,1)S(1)}, u32[]{:S(2)}, u32[]{:S(2)}) collective-permute-start(bf16[512,256]{1,0:T(8,128)(2,1)S(1)} %get-tuple-element.145.ctx.refs_0_.ctx_in), channel_id=1, source_target_pairs={{0,2},{1,3},{2,0},{3,1},{4,6},{5,7},{6,4},{7,5},{8,10},{9,11},{10,... | collective-permute-start | bytes 786440 | tf_op jit(solution)/shard_map/ppermute | solution.py:476
  7.7 4.6 %fetch.1 = (bf16[688,1024]{1,0:T(8,128)(2,1)S(1)}, bf16[1024,1024]{1,0:T(8,128)(2,1)S(1)}, bf16[688,1024]{1,0:T(8,128)(2,1)S(1)}, bf16[688,1024]{1,0:T(8,128)(2,1)S(1)}, f32[512,688]{1,0:T(8,128)S(1)}) custom-call(s32[6]{0:T(128)S(1)} %pad_add_fusion.where.place, bf16[512,256]{1,0:T(8,128)(2,1)S(1)} %get-tuple-element.145.ctx.refs_0_.ctx_in, ...), custom_call_target="tpu_custom_call" | custom-call | flops 1000 | bytes 1000 | tf_op jit(solution)/shard_map/fetch/pallas_call | solution.py:434
  12.4 1.6 %collective-permute-done.1.refs_2_ = bf16[512,256]{1,0:T(8,128)(2,1)S(1)} collective-permute-done((bf16[512,256]{1,0:T(8,128)(2,1)S(1)}, bf16[512,256]{1,0:T(8,128)(2,1)S(1)}, u32[]{:S(2)}, u32[]{:S(2)}) %collective-permute-start.1) | collective-permute-done | bytes 262176 | tf_op jit(solution)/shard_map/ppermute | solution.py:476
  13.9 1.5 %collective-permute-done.2.refs_3_ = bf16[512,256]{1,0:T(8,128)(2,1)S(1)} collective-permute-done((bf16[512,256]{1,0:T(8,128)(2,1)S(1)}, bf16[512,256]{1,0:T(8,128)(2,1)S(1)}, u32[]{:S(2)}, u32[]{:S(2)}) %collective-permute-start.2) | collective-permute-done | bytes 262176 | tf_op jit(solution)/shard_map/ppermute | solution.py:476
  15.5 5.8 %feed.1 = (f32[512,1024]{1,0:T(8,128)S(1)}, bf16[512,1024]{1,0:T(8,128)(2,1)S(1)}, bf16[512,688]{1,0:T(8,128)(2,1)S(1)}, bf16[512,688]{1,0:T(8,128)(2,1)S(1)}, b...) custom-call(s32[6]{0:T(128)S(1)} %pad_add_fusion.where.place, ...), custom_call_target="tpu_custom_call" | custom-call | flops 3000000000 | bytes 1000 | tf_op jit(solution)/shard_map/feed/pallas_call | solution.py:434
  21.5 1.9 %pair.1 = (bf16[4,1072,128]{2,1,0:T(8,128)(2,1)S(1)}, bf16[4,992,128]{2,1,0:T(8,128)(2,1)S(1)}) custom-call(s32[6]{0:T(128)S(1)} %pad_add_fusion.where.place, bf16[512,688]{1,0:T(8,128)(2,1)S(1)} %get-tuple-element.124.inner, bf16[512,688]{1,0:T(8,128)(2,1)S(1)} %get-tuple-element.110.gate, bf16[512,688]{1,0:T(8,128)(2,1)S(1)} %get-tuple-element.111.up, ...), custom_call_target="tpu_custom_call" | custom-call | flops 1000 | bytes 1000 | tf_op jit(solution)/shard_map/pair/pallas_call | solution.py:434
  23.6 1.5 %down.1 = (bf16[256,1024]{1,0:T(8,128)(2,1)S(1)}, bf16[256,1024]{1,0:T(8,128)(2,1)S(1)}) custom-call(s32[6]{0:T(128)S(1)} %pad_add_fusion.where.place, bf16[512,688]{1,0:T(8,128)(2,1)S(1)} %get-tuple-element.124.inner, bf16[688,1024]{1,0:T(8,128)(2,1)S(1)} %get-tuple-element.99.w_down), custom_call_target="tpu_custom_call" | custom-call | flops 1000 | bytes 1000 | tf_op jit(solution)/shard_map/down/pallas_call | solution.py:434
  25.2 0.4 collective-permute-start.5
  25.6 1.7 %collective-permute-start.4 = (bf16[256,1024]{1,0:T(8,128)(2,1)S(1)}, bf16[256,1024]{1,0:T(8,128)(2,1)S(1)}, u32[]{:S(2)}, u32[]{:S(2)}) collective-permute-start(bf16[256,1024]{1,0:T(8,128)(2,1)S(1)} %add_convert_fusion.3), channel_id=1, source_target_pairs={{0,2},{1,3},{2,0},{3,1},{4,6},{5,7},{6,4},{7,5},{8,10},{9,11},{10,... | collective-permute-start | bytes 1572872 | tf_op jit(solution)/shard_map/ppermute | solution.py:476
  27.3 1.6 %collective-permute-start.9 = (bf16[4,992,128]{2,1,0:T(8,128)(2,1)S(1)}, bf16[4,992,128]{2,1,0:T(8,128)(2,1)S(1)}, u32[]{:S(2)}, u32[]{:S(2)}) collective-permute-start(bf16[4,992,128]{2,1,0:T(8,128)(2,1)S(1)} %get-tuple-element.113), channel_id=1, source_target_pairs={{0,8},{4,12},{8,0},{12,4},{16,24},{20,28},{24,16},{28,20},{1,9},{5... | collective-permute-start | bytes 3047432 | tf_op jit(solution)/shard_map/ppermute | solution.py:476
  28.9 1.5 %collective-permute-start.8 = (bf16[4,1072,128]{2,1,0:T(8,128)(2,1)S(1)}, bf16[4,1072,128]{2,1,0:T(8,128)(2,1)S(1)}, u32[]{:S(2)}, u32[]{:S(2)}) collective-permute-start(bf16[4,1072,128]{2,1,0:T(8,128)(2,1)S(1)} %get-tuple-element.134), channel_id=1, source_target_pairs={{0,4},{4,0},{8,12},{12,8},{16,20},{20,16},{24,28},{28,24},{1,5},{5... | collective-permute-start | bytes 3293192 | tf_op jit(solution)/shard_map/ppermute | solution.py:476
  30.6 1.6 %prepare.1 = (bf16[4,768,256]{2,1,0:T(8,128)(2,1)S(1)}, bf16[4,768,256]{2,1,0:T(8,128)(2,1)S(1)}, f32[512,1]{1,0:T(8,128)S(1)}) custom-call(s32[6]{0:T(128)S(1)} %pad_add_fusion.where.place, bf16[512,64]{1,0:T(8,128)(2,1)S(1)} %get-tuple-element.120.q_in, bf16[512,64]{1,0:T(8,128)(2,1)S(1)} %get-tuple-element.121.k_in, ...), custom_call_target="tpu_custom_call" | custom-call | flops 1000 | bytes 1000 | tf_op jit(solution)/shard_map/prepare/pallas_call | solution.py:434
  32.1 2.1 %keeps.1 = (bf16[4,1072,128]{2,1,0:T(8,128)(2,1)S(1)}, bf16[4,992,128]{2,1,0:T(8,128)(2,1)S(1)}) custom-call(s32[6]{0:T(128)S(1)} %pad_add_fusion.where.place, bf16[512,688]{1,0:T(8,128)(2,1)S(1)} %get-tuple-element.124.inner, bf16[512,688]{1,0:T(8,128)(2,1)S(1)} %get-tuple-element.110.gate, bf16[512,688]{1,0:T(8,128)(2,1)S(1)} %get-tuple-element.111.up, ...), custom_call_target="tpu_custom_call" | custom-call | flops 1000 | bytes 1000 | tf_op jit(solution)/shard_map/keeps/pallas_call | solution.py:434
  34.2 5.3 %collective-permute-done.4 = bf16[256,1024]{1,0:T(8,128)(2,1)S(1)} collective-permute-done((bf16[256,1024]{1,0:T(8,128)(2,1)S(1)}, bf16[256,1024]{1,0:T(8,128)(2,1)S(1)}, u32[]{:S(2)}, u32[]{:S(2)}) %collective-permute-start.4) | collective-permute-done | bytes 524320 | tf_op jit(solution)/shard_map/ppermute | solution.py:476
  39.8 1.8 %collective-permute-start.14 = (bf16[256,1024]{1,0:T(8,128)(2,1)S(1)}, bf16[256,1024]{1,0:T(8,128)(2,1)S(1)}, u32[]{:S(2)}, u32[]{:S(2)}) collective-permute-start(bf16[256,1024]{1,0:T(8,128)(2,1)S(1)} %add_convert_fusion.2), channel_id=1, source_target_pairs={{0,2},{1,3},{2,0},{3,1},{4,6},{5,7},{6,4},{7,5},{8,10},{9,11},{10,... | collective-permute-start | bytes 1572872 | tf_op jit(solution)/shard_map/ppermute | solution.py:476
  41.7 4.4 %back.1 = (f32[512,1024]{1,0:T(8,128)S(1)}, bf16[512,1024]{1,0:T(8,128)(2,1)S(1)}, bf16[512,384]{1,0:T(8,128)(2,1)S(1)}, f32[1,1024]{1,0:T(1,128)S(1)}) custom-call(s32[6]{0:T(128)S(1)} %pad_add_fusion.where.place, bf16[256,1024]{1,0:T(8,128)(2,1)S(1)} %add_convert_fusion.1.own, bf16[256,1024]{1,0:T(8,128)(2,1)S(1)} %collective-permute-done.6.other, ...), custom_call_target="tpu_custom_call" | custom-call | flops 1000 | bytes 1000 | tf_op jit(solution)/shard_map/back/pallas_call | solution.py:434
  46.1 1.1 %late_away.1 = bf16[4,656,128]{2,1,0:T(8,128)(2,1)S(1)} custom-call(s32[6]{0:T(128)S(1)} %pad_add_fusion.where.place, bf16[512,256]{1,0:T(8,128)(2,1)S(1)} %get-tuple-element.145.ctx.refs_0_.ctx_in, bf16[512,384]{1,0:T(8,128)(2,1)S(1)} %get-tuple-element.132.refs_1_.refs_0_, bf16[512,1024]{1,0:T(8,128)(2,1)S(1)} %get-tuple-element.137.refs_2_, ...), custom_call_target="tpu_custom_call" | custom-call | flops 1000 | bytes 1000 | tf_op jit(solution)/shard_map/late_away/pallas_call | solution.py:434
  47.2 1.7 %collective-permute-start.12 = (bf16[4,656,128]{2,1,0:T(8,128)(2,1)S(1)}, bf16[4,656,128]{2,1,0:T(8,128)(2,1)S(1)}, u32[]{:S(2)}, u32[]{:S(2)}) collective-permute-start(bf16[4,656,128]{2,1,0:T(8,128)(2,1)S(1)} %late_away.1), channel_id=1, source_target_pairs={{0,4},{4,0},{8,12},{12,8},{16,20},{20,16},{24,28},{28,24},{1,5},{5... | collective-permute-start | bytes 2015240 | tf_op jit(solution)/shard_map/ppermute | solution.py:476
  49.0 1.5 %collective-permute-start.13 = (bf16[512,384]{1,0:T(8,128)(2,1)S(1)}, bf16[512,384]{1,0:T(8,128)(2,1)S(1)}, u32[]{:S(2)}, u32[]{:S(2)}) collective-permute-start(bf16[512,384]{1,0:T(8,128)(2,1)S(1)} %get-tuple-element.132.refs_1_.refs_0_), channel_id=1, source_target_pairs={{0,2},{1,3},{2,0},{3,1},{4,6},{5,7},{6,4},{7,5},{8,10},{9,11},{10,... | collective-permute-start | bytes 1179656 | tf_op jit(solution)/shard_map/ppermute | solution.py:476
  50.5 1.0 collective-permute-done.9.come
  51.5 0.8 z_keep.1
  52.3 2.7 %collective-permute-start.11 = (bf16[2,992,128]{2,1,0:T(8,128)(2,1)S(1)}, bf16[2,992,128]{2,1,0:T(8,128)(2,1)S(1)}, u32[]{:S(2)}, u32[]{:S(2)}) collective-permute-start(bf16[2,992,128]{2,1,0:T(8,128)(2,1)S(1)} %get-tuple-element.140), channel_id=1, source_target_pairs={{0,16},{4,20},{8,24},{12,28},{16,0},{20,4},{24,8},{28,12},{1,17},{... | collective-permute-start | bytes 1523720 | tf_op jit(solution)/shard_map/ppermute | solution.py:476
  55.0 1.1 %collective-permute-done.8.come = bf16[4,1072,128]{2,1,0:T(8,128)(2,1)S(1)} collective-permute-done((bf16[4,1072,128]{2,1,0:T(8,128)(2,1)S(1)}, bf16[4,1072,128]{2,1,0:T(8,128)(2,1)S(1)}, u32[]{:S(2)}, u32[]{:S(2)}) %collective-permute-start.8) | collective-permute-done | bytes 1097760 | tf_op jit(solution)/shard_map/ppermute | solution.py:476
  56.0 0.8 x_keep.1
  56.8 0.6 collective-permute-start.10
  57.4 1.1 %late_product.1.held = bf16[4,656,128]{2,1,0:T(8,128)(2,1)S(1)} custom-call(s32[6]{0:T(128)S(1)} %pad_add_fusion.where.place, bf16[512,256]{1,0:T(8,128)(2,1)S(1)} %get-tuple-element.145.ctx.refs_0_.ctx_in, bf16[512,384]{1,0:T(8,128)(2,1)S(1)} %get-tuple-element.132.refs_1_.refs_0_, bf16[512,1024]{1,0:T(8,128)(2,1)S(1)} %get-tuple-element.137.refs_2_, ...), custom_call_target="tpu_custom_call" | custom-call | flops 1000 | bytes 1000 | tf_op jit(solution)/shard_map/late_product/pallas_call | solution.py:434
  58.8 3.8 %collective-permute-done.13.refs_2_ = bf16[512,384]{1,0:T(8,128)(2,1)S(1)} collective-permute-done((bf16[512,384]{1,0:T(8,128)(2,1)S(1)}, bf16[512,384]{1,0:T(8,128)(2,1)S(1)}, u32[]{:S(2)}, u32[]{:S(2)}) %collective-permute-start.13) | collective-permute-done | bytes 393248 | tf_op jit(solution)/shard_map/ppermute | solution.py:476
  62.6 6.4 %collective-permute-done.12.come = bf16[4,656,128]{2,1,0:T(8,128)(2,1)S(1)} collective-permute-done((bf16[4,656,128]{2,1,0:T(8,128)(2,1)S(1)}, bf16[4,656,128]{2,1,0:T(8,128)(2,1)S(1)}, u32[]{:S(2)}, u32[]{:S(2)}) %collective-permute-start.12) | collective-permute-done | bytes 671776 | tf_op jit(solution)/shard_map/ppermute | solution.py:476
  69.0 0.7 late_keep.1
  69.7 2.7 %collective-permute-start.17 = (bf16[656,128]{1,0:T(8,128)(2,1)S(1)}, bf16[656,128]{1,0:T(8,128)(2,1)S(1)}, u32[]{:S(2)}, u32[]{:S(2)}) collective-permute-start(bf16[656,128]{1,0:T(8,128)(2,1)S(1)} %get-tuple-element.158), channel_id=1, source_target_pairs={{0,16},{4,20},{8,24},{12,28},{16,0},{20,4},{24,8},{28,12},{1,17},{... | collective-permute-start | bytes 503816 | tf_op jit(solution)/shard_map/ppermute | solution.py:476
  72.4 0.4 collective-permute-start.18
  72.8 6.3 %collective-permute-done.11.come = bf16[2,992,128]{2,1,0:T(8,128)(2,1)S(1)} collective-permute-done((bf16[2,992,128]{2,1,0:T(8,128)(2,1)S(1)}, bf16[2,992,128]{2,1,0:T(8,128)(2,1)S(1)}, u32[]{:S(2)}, u32[]{:S(2)}) %collective-permute-start.11) | collective-permute-done | bytes 507936 | tf_op jit(solution)/shard_map/ppermute | solution.py:476
  79.1 2.3 %collective-permute-start.19 = (bf16[656,128]{1,0:T(8,128)(2,1)S(1)}, bf16[656,128]{1,0:T(8,128)(2,1)S(1)}, u32[]{:S(2)}, u32[]{:S(2)}) collective-permute-start(bf16[656,128]{1,0:T(8,128)(2,1)S(1)} %get-tuple-element.149), channel_id=1, source_target_pairs={{0,24},{4,28},{8,16},{12,20},{16,8},{20,12},{24,0},{28,4},{1,25},{... | collective-permute-start | bytes 503816 | tf_op jit(solution)/shard_map/ppermute | solution.py:476
  81.5 0.7 z_hop.1
  82.1 1.3 %collective-permute-done.10.come = bf16[2,1072,128]{2,1,0:T(8,128)(2,1)S(1)} collective-permute-done((bf16[2,1072,128]{2,1,0:T(8,128)(2,1)S(1)}, bf16[2,1072,128]{2,1,0:T(8,128)(2,1)S(1)}, u32[]{:S(2)}, u32[]{:S(2)}) %collective-permute-start.10) | collective-permute-done | bytes 548896 | tf_op jit(solution)/shard_map/ppermute | solution.py:476
  83.4 0.7 x_hop.1
  84.1 0.6 collective-permute-start.15
  84.7 1.6 %collective-permute-done.17.refs_0_ = bf16[656,128]{1,0:T(8,128)(2,1)S(1)} collective-permute-done((bf16[656,128]{1,0:T(8,128)(2,1)S(1)}, bf16[656,128]{1,0:T(8,128)(2,1)S(1)}, u32[]{:S(2)}, u32[]{:S(2)}) %collective-permute-start.17) | collective-permute-done | bytes 167968 | tf_op jit(solution)/shard_map/ppermute | solution.py:476
  86.3 3.1 %collective-permute-done.18.refs_1_ = bf16[656,128]{1,0:T(8,128)(2,1)S(1)} collective-permute-done((bf16[656,128]{1,0:T(8,128)(2,1)S(1)}, bf16[656,128]{1,0:T(8,128)(2,1)S(1)}, u32[]{:S(2)}, u32[]{:S(2)}) %collective-permute-start.18) | collective-permute-done | bytes 167968 | tf_op jit(solution)/shard_map/ppermute | solution.py:476
  89.4 1.5 %collective-permute-start.24 = (bf16[1,992,128]{2,1,0:T(8,128)(2,1)S(1)}, bf16[1,992,128]{2,1,0:T(8,128)(2,1)S(1)}, u32[]{:S(2)}, u32[]{:S(2)}) collective-permute-start(bf16[1,992,128]{2,1,0:T(8,128)(2,1)S(1)} %get-tuple-element.151), channel_id=1, source_target_pairs={{0,4},{4,0},{8,12},{12,8},{16,20},{20,16},{24,28},{28,24},{1,5},{5... | collective-permute-start | bytes 761864 | tf_op jit(solution)/shard_map/ppermute | solution.py:476
  91.0 1.3 %late.1 = (f32[256,128]{1,0:T(8,128)}, f32[1,128]{1,0:T(1,128)}, bf16[128,384]{1,0:T(8,128)(2,1)S(1)}) custom-call(s32[6]{0:T(128)S(1)} %pad_add_fusion.where.place, f32[656,128]{1,0:T(8,128)S(1)} %get-tuple-element.157.held, bf16[656,128]{1,0:T(8,128)(2,1)S(1)} %collective-permute-done.17.refs_0_, bf16[656,128]{1,0:T(8,128)(2,1)S(1)} %collective-permute-done.18.refs_1_, ...), custom_call_target="tpu_custom_call" | custom-call | flops 10000000000 | bytes 1000 | tf_op jit(solution)/shard_map/late/pallas_call | solution.py:434
  92.2 0.5 collective-permute-start.21
  92.8 4.6 %grad_input.1 = (bf16[512,1024]{1,0:T(8,128)(2,1)}, bf16[512,1024]{1,0:T(8,128)(2,1)}) custom-call(s32[6]{0:T(128)S(1)} %pad_add_fusion.where.place, bf16[512,384]{1,0:T(8,128)(2,1)S(1)} %get-tuple-element.132.refs_1_.refs_0_, bf16[512,384]{1,0:T(8,128)(2,1)S(1)} %collective-permute-done.7.refs_1_, bf16[512,384]{1,0:T(8,128)(2,1)S(1)} %collective-permute-done.13.refs_2_, ...), custom_call_target="tpu_custom_call" | custom-call | flops 1000 | bytes 1000 | tf_op jit(solution)/shard_map/grad_input/pallas_call | solution.py:434
  97.4 0.5 collective-permute-start.22
  97.9 4.9 %collective-permute-done.23.x_come = bf16[1,1072,128]{2,1,0:T(8,128)(2,1)S(1)} collective-permute-done((bf16[1,1072,128]{2,1,0:T(8,128)(2,1)S(1)}, bf16[1,1072,128]{2,1,0:T(8,128)(2,1)S(1)}, u32[]{:S(2)}, u32[]{:S(2)}) %collective-permute-start.23) | collective-permute-done | bytes 274464 | tf_op jit(solution)/shard_map/ppermute | solution.py:476
  102.8 1.5 %hidden.1 = (f32[688,128]{1,0:T(8,128)}, f32[688,128]{1,0:T(8,128)}, f32[688,128]{1,0:T(8,128)}) custom-call(s32[6]{0:T(128)S(1)} %pad_add_fusion.where.place, bf16[1,1072,128]{2,1,0:T(8,128)(2,1)S(1)} %get-tuple-element.168.x_held, bf16[1,1072,128]{2,1,0:T(8,128)(2,1)S(1)} %collective-permute-done.23.x_come, ...), custom_call_target="tpu_custom_call" | custom-call | flops 10000000000 | bytes 1000 | tf_op jit(solution)/shard_map/hidden/pallas_call | solution.py:434
  104.4 1.6 %finish.1 = (f32[128,256]{1,0:T(8,128)}, f32[128,256]{1,0:T(8,128)}, f32[128,1024]{1,0:T(8,128)}, f32[1,128]{1,0:T(1,128)}) custom-call(s32[6]{0:T(128)S(1)} %pad_add_fusion.where.place, bf16[128,384]{1,0:T(8,128)(2,1)S(1)} %get-tuple-element.173.refs_0_, bf16[128,384]{1,0:T(8,128)(2,1)S(1)} %collective-permute-done.20.refs_1_, ...), custom_call_target="tpu_custom_call" | custom-call | flops 1000 | bytes 1000 | tf_op jit(solution)/shard_map/finish/pallas_call | solution.py:434
  (42 shorter events, 1.4 us)
Async XLA Ops:
  0.6 7.0 %copy-start.7 = (s32[1,4]{1,0:T(1,128)S(1)}, s32[1,4]{1,0:T(1,128)}, u32[]{:S(2)}) copy-start(s32[1,4]{1,0:T(1,128)} %lengths.1) | copy-start | bytes 52
  4.6 9.3 %collective-permute-start.1 = (bf16[512,256]{1,0:T(8,128)(2,1)S(1)}, bf16[512,256]{1,0:T(8,128)(2,1)S(1)}, u32[]{:S(2)}, u32[]{:S(2)}) collective-permute-start(bf16[512,256]{1,0:T(8,128)(2,1)S(1)} %get-tuple-element.145.ctx.refs_0_.ctx_in), channel_id=1, source_target_pairs={{0,2},{1,3},{2,0},{3,1},{4,6},{5,7},{6,4},{7,5},{8,10},{9,11},{10,... | collective-permute-start | bytes 786440 | tf_op jit(solution)/shard_map/ppermute | solution.py:476
  7.6 6.3 %collective-permute-start = (bf16[512,256]{1,0:T(8,128)(2,1)S(1)}, bf16[512,256]{1,0:T(8,128)(2,1)S(1)}, u32[]{:S(2)}, u32[]{:S(2)}) collective-permute-start(bf16[512,256]{1,0:T(8,128)(2,1)S(1)} %get-tuple-element.145.ctx.refs_0_.ctx_in), channel_id=1, source_target_pairs={{0,1},{1,0},{2,3},{3,2},{4,5},{5,4},{6,7},{7,6},{8,9},{9,8},{10,11... | collective-permute-start | bytes 786440 | tf_op jit(solution)/shard_map/ppermute | solution.py:476
  7.7 7.8 %copy-start.4 = (bf16[512,1024]{1,0:T(8,128)(2,1)S(1)}, bf16[512,1024]{1,0:T(8,128)(2,1)}, u32[]{:S(2)}) copy-start(bf16[512,1024]{1,0:T(8,128)(2,1)} %refs_5_.2) | copy-start | bytes 3145732
  7.7 7.8 %copy-start.6 = (f32[1024]{0:T(1024)S(1)}, f32[1024]{0:T(1024)}, u32[]{:S(2)}) copy-start(f32[1024]{0:T(1024)} %param.18) | copy-start | bytes 12292
  13.9 1.5 %collective-permute-start.2 = (bf16[512,256]{1,0:T(8,128)(2,1)S(1)}, bf16[512,256]{1,0:T(8,128)(2,1)S(1)}, u32[]{:S(2)}, u32[]{:S(2)}) collective-permute-start(bf16[512,256]{1,0:T(8,128)(2,1)S(1)} %collective-permute-done.1.refs_2_), channel_id=1, source_target_pairs={{0,1},{1,0},{2,3},{3,2},{4,5},{5,4},{6,7},{7,6},{8,9},{9,8},{10,11... | collective-permute-start | bytes 786440 | tf_op jit(solution)/shard_map/ppermute | solution.py:476
  15.5 6.0 %copy-start.1 = (bf16[512,1024]{1,0:T(8,128)(2,1)S(1)}, bf16[512,1024]{1,0:T(8,128)(2,1)}, u32[]{:S(2)}) copy-start(bf16[512,1024]{1,0:T(8,128)(2,1)} %cot.7) | copy-start | bytes 3145732
  21.3 2.1 %collective-permute-start.3 = (bf16[256,1024]{1,0:T(8,128)(2,1)S(1)}, bf16[256,1024]{1,0:T(8,128)(2,1)S(1)}, u32[]{:S(2)}, u32[]{:S(2)}) collective-permute-start(bf16[256,1024]{1,0:T(8,128)(2,1)S(1)} %get-tuple-element.108), channel_id=1, source_target_pairs={{0,1},{1,0},{2,3},{3,2},{4,5},{5,4},{6,7},{7,6},{8,9},{9,8},{10,11... | collective-permute-start | bytes 1572872 | tf_op jit(solution)/shard_map/ppermute | solution.py:476
  25.2 5.2 %collective-permute-start.5 = (bf16[256,1024]{1,0:T(8,128)(2,1)S(1)}, bf16[256,1024]{1,0:T(8,128)(2,1)S(1)}, u32[]{:S(2)}, u32[]{:S(2)}) collective-permute-start(bf16[256,1024]{1,0:T(8,128)(2,1)S(1)} %get-tuple-element.118), channel_id=1, source_target_pairs={{0,1},{1,0},{2,3},{3,2},{4,5},{5,4},{6,7},{7,6},{8,9},{9,8},{10,11... | collective-permute-start | bytes 1572872 | tf_op jit(solution)/shard_map/ppermute | solution.py:476
  25.6 14.0 %collective-permute-start.4 = (bf16[256,1024]{1,0:T(8,128)(2,1)S(1)}, bf16[256,1024]{1,0:T(8,128)(2,1)S(1)}, u32[]{:S(2)}, u32[]{:S(2)}) collective-permute-start(bf16[256,1024]{1,0:T(8,128)(2,1)S(1)} %add_convert_fusion.3), channel_id=1, source_target_pairs={{0,2},{1,3},{2,0},{3,1},{4,6},{5,7},{6,4},{7,5},{8,10},{9,11},{10,... | collective-permute-start | bytes 1572872 | tf_op jit(solution)/shard_map/ppermute | solution.py:476
  27.3 24.2 %collective-permute-start.9 = (bf16[4,992,128]{2,1,0:T(8,128)(2,1)S(1)}, bf16[4,992,128]{2,1,0:T(8,128)(2,1)S(1)}, u32[]{:S(2)}, u32[]{:S(2)}) collective-permute-start(bf16[4,992,128]{2,1,0:T(8,128)(2,1)S(1)} %get-tuple-element.113), channel_id=1, source_target_pairs={{0,8},{4,12},{8,0},{12,4},{16,24},{20,28},{24,16},{28,20},{1,9},{5... | collective-permute-start | bytes 3047432 | tf_op jit(solution)/shard_map/ppermute | solution.py:476
  28.9 27.1 %collective-permute-start.8 = (bf16[4,1072,128]{2,1,0:T(8,128)(2,1)S(1)}, bf16[4,1072,128]{2,1,0:T(8,128)(2,1)S(1)}, u32[]{:S(2)}, u32[]{:S(2)}) collective-permute-start(bf16[4,1072,128]{2,1,0:T(8,128)(2,1)S(1)} %get-tuple-element.134), channel_id=1, source_target_pairs={{0,4},{4,0},{8,12},{12,8},{16,20},{20,16},{24,28},{28,24},{1,5},{5... | collective-permute-start | bytes 3293192 | tf_op jit(solution)/shard_map/ppermute | solution.py:476
  39.8 2.0 %collective-permute-start.6 = (bf16[256,1024]{1,0:T(8,128)(2,1)S(1)}, bf16[256,1024]{1,0:T(8,128)(2,1)S(1)}, u32[]{:S(2)}, u32[]{:S(2)}) collective-permute-start(bf16[256,1024]{1,0:T(8,128)(2,1)S(1)} %add_convert_fusion.1.own), channel_id=1, source_target_pairs={{0,1},{1,0},{2,3},{3,2},{4,5},{5,4},{6,7},{7,6},{8,9},{9,8},{10,11... | collective-permute-start | bytes 1572872 | tf_op jit(solution)/shard_map/ppermute | solution.py:476
  39.8 18.7 %collective-permute-start.14 = (bf16[256,1024]{1,0:T(8,128)(2,1)S(1)}, bf16[256,1024]{1,0:T(8,128)(2,1)S(1)}, u32[]{:S(2)}, u32[]{:S(2)}) collective-permute-start(bf16[256,1024]{1,0:T(8,128)(2,1)S(1)} %add_convert_fusion.2), channel_id=1, source_target_pairs={{0,2},{1,3},{2,0},{3,1},{4,6},{5,7},{6,4},{7,5},{8,10},{9,11},{10,... | collective-permute-start | bytes 1572872 | tf_op jit(solution)/shard_map/ppermute | solution.py:476
  47.2 21.7 %collective-permute-start.12 = (bf16[4,656,128]{2,1,0:T(8,128)(2,1)S(1)}, bf16[4,656,128]{2,1,0:T(8,128)(2,1)S(1)}, u32[]{:S(2)}, u32[]{:S(2)}) collective-permute-start(bf16[4,656,128]{2,1,0:T(8,128)(2,1)S(1)} %late_away.1), channel_id=1, source_target_pairs={{0,4},{4,0},{8,12},{12,8},{16,20},{20,16},{24,28},{28,24},{1,5},{5... | collective-permute-start | bytes 2015240 | tf_op jit(solution)/shard_map/ppermute | solution.py:476
  49.0 13.6 %collective-permute-start.13 = (bf16[512,384]{1,0:T(8,128)(2,1)S(1)}, bf16[512,384]{1,0:T(8,128)(2,1)S(1)}, u32[]{:S(2)}, u32[]{:S(2)}) collective-permute-start(bf16[512,384]{1,0:T(8,128)(2,1)S(1)} %get-tuple-element.132.refs_1_.refs_0_), channel_id=1, source_target_pairs={{0,2},{1,3},{2,0},{3,1},{4,6},{5,7},{6,4},{7,5},{8,10},{9,11},{10,... | collective-permute-start | bytes 1179656 | tf_op jit(solution)/shard_map/ppermute | solution.py:476
  52.3 26.8 %collective-permute-start.11 = (bf16[2,992,128]{2,1,0:T(8,128)(2,1)S(1)}, bf16[2,992,128]{2,1,0:T(8,128)(2,1)S(1)}, u32[]{:S(2)}, u32[]{:S(2)}) collective-permute-start(bf16[2,992,128]{2,1,0:T(8,128)(2,1)S(1)} %get-tuple-element.140), channel_id=1, source_target_pairs={{0,16},{4,20},{8,24},{12,28},{16,0},{20,4},{24,8},{28,12},{1,17},{... | collective-permute-start | bytes 1523720 | tf_op jit(solution)/shard_map/ppermute | solution.py:476
  56.8 26.6 %collective-permute-start.10 = (bf16[2,1072,128]{2,1,0:T(8,128)(2,1)S(1)}, bf16[2,1072,128]{2,1,0:T(8,128)(2,1)S(1)}, u32[]{:S(2)}, u32[]{:S(2)}) collective-permute-start(bf16[2,1072,128]{2,1,0:T(8,128)(2,1)S(1)} %get-tuple-element.143), channel_id=1, source_target_pairs={{0,8},{4,12},{8,0},{12,4},{16,24},{20,28},{24,16},{28,20},{1,9},{5... | collective-permute-start | bytes 1646600 | tf_op jit(solution)/shard_map/ppermute | solution.py:476
  58.5 25.6 %collective-permute-start.7 = (bf16[512,384]{1,0:T(8,128)(2,1)S(1)}, bf16[512,384]{1,0:T(8,128)(2,1)S(1)}, u32[]{:S(2)}, u32[]{:S(2)}) collective-permute-start(bf16[512,384]{1,0:T(8,128)(2,1)S(1)} %get-tuple-element.132.refs_1_.refs_0_), channel_id=1, source_target_pairs={{0,1},{1,0},{2,3},{3,2},{4,5},{5,4},{6,7},{7,6},{8,9},{9,8},{10,11... | collective-permute-start | bytes 1179656 | tf_op jit(solution)/shard_map/ppermute | solution.py:476
  69.7 16.6 %collective-permute-start.17 = (bf16[656,128]{1,0:T(8,128)(2,1)S(1)}, bf16[656,128]{1,0:T(8,128)(2,1)S(1)}, u32[]{:S(2)}, u32[]{:S(2)}) collective-permute-start(bf16[656,128]{1,0:T(8,128)(2,1)S(1)} %get-tuple-element.158), channel_id=1, source_target_pairs={{0,16},{4,20},{8,24},{12,28},{16,0},{20,4},{24,8},{28,12},{1,17},{... | collective-permute-start | bytes 503816 | tf_op jit(solution)/shard_map/ppermute | solution.py:476
  72.4 17.1 %collective-permute-start.18 = (bf16[656,128]{1,0:T(8,128)(2,1)S(1)}, bf16[656,128]{1,0:T(8,128)(2,1)S(1)}, u32[]{:S(2)}, u32[]{:S(2)}) collective-permute-start(bf16[656,128]{1,0:T(8,128)(2,1)S(1)} %get-tuple-element.159), channel_id=1, source_target_pairs={{0,8},{4,12},{8,0},{12,4},{16,24},{20,28},{24,16},{28,20},{1,9},{5... | collective-permute-start | bytes 503816 | tf_op jit(solution)/shard_map/ppermute | solution.py:476
  79.1 11.8 %collective-permute-start.19 = (bf16[656,128]{1,0:T(8,128)(2,1)S(1)}, bf16[656,128]{1,0:T(8,128)(2,1)S(1)}, u32[]{:S(2)}, u32[]{:S(2)}) collective-permute-start(bf16[656,128]{1,0:T(8,128)(2,1)S(1)} %get-tuple-element.149), channel_id=1, source_target_pairs={{0,24},{4,28},{8,16},{12,20},{16,8},{20,12},{24,0},{28,4},{1,25},{... | collective-permute-start | bytes 503816 | tf_op jit(solution)/shard_map/ppermute | solution.py:476
  83.4 9.3 %collective-permute-start.16 = (bf16[256,1024]{1,0:T(8,128)(2,1)S(1)}, bf16[256,1024]{1,0:T(8,128)(2,1)S(1)}, u32[]{:S(2)}, u32[]{:S(2)}) collective-permute-start(bf16[256,1024]{1,0:T(8,128)(2,1)S(1)} %add_convert_fusion.refs_7_), channel_id=1, source_target_pairs={{0,1},{1,0},{2,3},{3,2},{4,5},{5,4},{6,7},{7,6},{8,9},{9,8},{10,11... | collective-permute-start | bytes 1572872 | tf_op jit(solution)/shard_map/ppermute | solution.py:476
  84.1 8.6 %collective-permute-start.15 = (bf16[512,384]{1,0:T(8,128)(2,1)S(1)}, bf16[512,384]{1,0:T(8,128)(2,1)S(1)}, u32[]{:S(2)}, u32[]{:S(2)}) collective-permute-start(bf16[512,384]{1,0:T(8,128)(2,1)S(1)} %collective-permute-done.13.refs_2_), channel_id=1, source_target_pairs={{0,1},{1,0},{2,3},{3,2},{4,5},{5,4},{6,7},{7,6},{8,9},{9,8},{10,11... | collective-permute-start | bytes 1179656 | tf_op jit(solution)/shard_map/ppermute | solution.py:476
  86.3 16.5 %collective-permute-start.23 = (bf16[1,1072,128]{2,1,0:T(8,128)(2,1)S(1)}, bf16[1,1072,128]{2,1,0:T(8,128)(2,1)S(1)}, u32[]{:S(2)}, u32[]{:S(2)}) collective-permute-start(bf16[1,1072,128]{2,1,0:T(8,128)(2,1)S(1)} %get-tuple-element.153), channel_id=1, source_target_pairs={{0,16},{4,20},{8,24},{12,28},{16,0},{20,4},{24,8},{28,12},{1,17},{... | collective-permute-start | bytes 823304 | tf_op jit(solution)/shard_map/ppermute | solution.py:476
  89.4 8.5 %collective-permute-start.24 = (bf16[1,992,128]{2,1,0:T(8,128)(2,1)S(1)}, bf16[1,992,128]{2,1,0:T(8,128)(2,1)S(1)}, u32[]{:S(2)}, u32[]{:S(2)}) collective-permute-start(bf16[1,992,128]{2,1,0:T(8,128)(2,1)S(1)} %get-tuple-element.151), channel_id=1, source_target_pairs={{0,4},{4,0},{8,12},{12,8},{16,20},{20,16},{24,28},{28,24},{1,5},{5... | collective-permute-start | bytes 761864 | tf_op jit(solution)/shard_map/ppermute | solution.py:476
  90.9 1.8 %copy-start = (bf16[1024,1024]{1,0:T(8,128)(2,1)S(1)}, bf16[1024,1024]{1,0:T(8,128)(2,1)}, u32[]{:S(2)}) copy-start(bf16[1024,1024]{1,0:T(8,128)(2,1)} %refs_7_.1) | copy-start | bytes 6291460
  90.9 1.8 %copy-start.2 = (bf16[1024,256]{1,0:T(8,128)(2,1)S(1)}, bf16[1024,256]{1,0:T(8,128)(2,1)}, u32[]{:S(2)}) copy-start(bf16[1024,256]{1,0:T(8,128)(2,1)} %refs_5_.3) | copy-start | bytes 1572868
  90.9 1.9 %copy-start.3 = (bf16[1024,256]{1,0:T(8,128)(2,1)S(1)}, bf16[1024,256]{1,0:T(8,128)(2,1)}, u32[]{:S(2)}) copy-start(bf16[1024,256]{1,0:T(8,128)(2,1)} %refs_6_.1) | copy-start | bytes 1572868
  90.9 1.9 %copy-start.5 = (f32[1024]{0:T(1024)S(1)}, f32[1024]{0:T(1024)}, u32[]{:S(2)}) copy-start(f32[1024]{0:T(1024)} %param.13) | copy-start | bytes 12292
  92.2 5.2 %collective-permute-start.21 = (bf16[128,384]{1,0:T(8,128)(2,1)S(1)}, bf16[128,384]{1,0:T(8,128)(2,1)S(1)}, u32[]{:S(2)}, u32[]{:S(2)}) collective-permute-start(bf16[128,384]{1,0:T(8,128)(2,1)S(1)} %get-tuple-element.173.refs_0_), channel_id=1, source_target_pairs={{0,2},{1,3},{2,0},{3,1},{4,6},{5,7},{6,4},{7,5},{8,10},{9,11},{10,... | collective-permute-start | bytes 294920 | tf_op jit(solution)/shard_map/ppermute | solution.py:476
  92.7 11.6 %collective-permute-start.20 = (bf16[128,384]{1,0:T(8,128)(2,1)S(1)}, bf16[128,384]{1,0:T(8,128)(2,1)S(1)}, u32[]{:S(2)}, u32[]{:S(2)}) collective-permute-start(bf16[128,384]{1,0:T(8,128)(2,1)S(1)} %get-tuple-element.173.refs_0_), channel_id=1, source_target_pairs={{0,1},{1,0},{2,3},{3,2},{4,5},{5,4},{6,7},{7,6},{8,9},{9,8},{10,11... | collective-permute-start | bytes 294920 | tf_op jit(solution)/shard_map/ppermute | solution.py:476
  97.4 7.0 %collective-permute-start.22 = (bf16[128,384]{1,0:T(8,128)(2,1)S(1)}, bf16[128,384]{1,0:T(8,128)(2,1)S(1)}, u32[]{:S(2)}, u32[]{:S(2)}) collective-permute-start(bf16[128,384]{1,0:T(8,128)(2,1)S(1)} %collective-permute-done.21.refs_2_), channel_id=1, source_target_pairs={{0,1},{1,0},{2,3},{3,2},{4,5},{5,4},{6,7},{7,6},{8,9},{9,8},{10,11... | collective-permute-start | bytes 294920 | tf_op jit(solution)/shard_map/ppermute | solution.py:476

commit v9 on v8

--- a/solution.py
+++ b/solution.py
@@ -413,6 +413,13 @@
     finish_kernel(where, *refs[4 : 8 + share], *refs[11 + share :], share=share, hv=hv, hq=hq)
 
 
+def back_late_kernel(where, *refs, order, chunk):
+    *ins, normed, gr_out, gm_out, g_out, gain_out, late_out, gctx = refs
+    back_kernel(where, *ins, gr_out, gm_out, g_out, gain_out, gctx)
+    pairs = lambda _: [(ins[10][...], gm_out), (None, gain_out), (g_out[...], normed)]
+    away_kernel(where, late_out, pairs=pairs, order=order, chunk=chunk)
+
+
 def whole(array):
     return pl.BlockSpec(array.shape, lambda *_: (0,) * len(array.shape))
 
@@ -624,21 +631,23 @@
         [come] = after([swap(back_own, "feat", mask)], last)
         last = back_own = plus(back_own, come)
     [back_other] = after([swap(back_own, "feat", 1)], last)
-    grad_res, grad_mixed, grads, gain_part = call(
-        back_kernel,
+    grad_res, grad_mixed, grads, gain_part, late_sent = call(
+        back_late_kernel,
         "back",
         where,
-        [back_own, back_other, residual, r_two, cotangent, gain_b, w_out, q, k, v, ctx, den, scores, slopes],
+        [back_own, back_other, residual, r_two, cotangent, gain_b, w_out, q, k, v, ctx, den, scores, slopes, normed],
         [
             vmem_of(rows, width, F32),
             vmem_of(rows, width, BF16),
             vmem_of(rows, pack, BF16),
             shape_of(1, width, F32),
+            shape_of(2 * few, hv + 16 + pack, chunk, BF16),
         ],
         specs={6: pl.BlockSpec((hv, width), lambda i, p: (p[0], 0))},
         scratch=[pltpu.VMEM((rows, hv), BF16)],
-    )
-    last = gain_part
+        order=x_first,
+        chunk=chunk,
+    )
     late_args = [ctx, grads, normed, grad_mixed, gain_part]
     late_pairs = lambda refs: [(refs[0][...], refs[3]), (None, refs[4]), (refs[1][...], refs[2])]
     late_fixed = dict(pairs=late_pairs, order=x_first, chunk=chunk)
@@ -647,14 +656,6 @@
         for j in list(held):
             held[j ^ mask] = swap(held[j], "feat", mask)
     far = [j for j in held if j]
-    [late_sent] = call(
-        away_kernel,
-        "late_away",
-        where,
-        [*after(late_args[:1], last), *late_args[1:]],
-        [shape_of(2 * few, late_many, chunk, BF16)],
-        **late_fixed,
-    )
     late_come = swap(late_sent, "dp", x_first[0])
     last = late_sent
     [come] = after([swap(z_sent, "dp", z_order[0])], last)

time: 106 us -> 106 us (level)
    pallas_call x18 -> x17, Pallas kernels: 36.8 us -> 36.1 us  [call(): pl.pallas_call(functools.partial(kernel, **fixed) if fixed else kernel, g...]
where the time goes in v9:
time: 106 us
  Pallas kernels  40 us (38%)
  waiting for transfers between devices  38.7 us (37%)
  starting transfers between devices  25.4 us (24%)
    ppermute x25, waiting for transfers between devices, swap(): return lax.ppermute(array, axis, [(i, i ^ mask) for i in range(count)])  38.7 us
    pallas_call x17, Pallas kernels, call(): pl.pallas_call(functools.partial(kernel, **fixed) if fixed else kernel, g...  36.1 us
    ppermute x25, starting transfers between devices, swap(): return lax.ppermute(array, axis, [(i, i ^ mask) for i in range(count)])  25.4 us
    pallas_call x1, Pallas kernels, local(): pl.pallas_call(attend_kernel, grid=(1,), in_specs=[pl.BlockSpec(memory_sp...  3.94 us
  transfers between devices with their start and end apart: 25, of which 13 were waited for; matrix products, arithmetic and copies ran while one was open for 1% of the time, Pallas kernels for 26%

profile of v9, /device:TPU:0, one launch (start us, length us, event | category | flops | bytes accessed | tf_op | source)
XLA Modules:
  0.0 105.9 jit_solution(3849079321722849140)
XLA Ops:
  0.7 3.9 %attend.1 = (bf16[512,1024]{1,0:T(8,128)(2,1)S(1)}, bf16[512,64]{1,0:T(8,128)(2,1)S(1)}, bf16[512,64]{1,0:T(8,128)(2,1)S(1)}, bf16[512,256]{1,0:T(8,128)(2,1)S(1...) custom-call(s32[1,4]{1,0:T(1,128)} %lengths.1, bf16[512,1024]{1,0:T(8,128)(2,1)} %refs_5_.2, f32[1,1024]{1,0:T(1,128)} %bitcast.11, ...), custom_call_target="tpu_custom_call" | custom-call | flops 1000 | bytes 1000 | tf_op jit(solution)/shard_map/attend/pallas_call | solution.py:520
  4.6 3.0 %collective-permute-start.1 = (bf16[512,256]{1,0:T(8,128)(2,1)S(1)}, bf16[512,256]{1,0:T(8,128)(2,1)S(1)}, u32[]{:S(2)}, u32[]{:S(2)}) collective-permute-start(bf16[512,256]{1,0:T(8,128)(2,1)S(1)} %get-tuple-element.143.ctx.refs_0_.refs_10_), channel_id=1, source_target_pairs={{0,2},{1,3},{2,0},{3,1},{4,6},{5,7},{6,4},{7,5},{8,10},{9,11},{10,... | collective-permute-start | bytes 786440 | tf_op jit(solution)/shard_map/ppermute | solution.py:483
  7.7 4.6 %fetch.1 = (bf16[688,1024]{1,0:T(8,128)(2,1)S(1)}, bf16[1024,1024]{1,0:T(8,128)(2,1)S(1)}, bf16[688,1024]{1,0:T(8,128)(2,1)S(1)}, bf16[688,1024]{1,0:T(8,128)(2,1)S(1)}, f32[512,688]{1,0:T(8,128)S(1)}) custom-call(s32[6]{0:T(128)S(1)} %pad_add_fusion.where.place, bf16[512,256]{1,0:T(8,128)(2,1)S(1)} %get-tuple-element.143.ctx.refs_0_.refs_10_, ...), custom_call_target="tpu_custom_call" | custom-call | flops 1000 | bytes 1000 | tf_op jit(solution)/shard_map/fetch/pallas_call | solution.py:441
  12.4 1.6 %collective-permute-done.1.refs_2_ = bf16[512,256]{1,0:T(8,128)(2,1)S(1)} collective-permute-done((bf16[512,256]{1,0:T(8,128)(2,1)S(1)}, bf16[512,256]{1,0:T(8,128)(2,1)S(1)}, u32[]{:S(2)}, u32[]{:S(2)}) %collective-permute-start.1) | collective-permute-done | bytes 262176 | tf_op jit(solution)/shard_map/ppermute | solution.py:483
  13.9 1.5 %collective-permute-done.2.refs_3_ = bf16[512,256]{1,0:T(8,128)(2,1)S(1)} collective-permute-done((bf16[512,256]{1,0:T(8,128)(2,1)S(1)}, bf16[512,256]{1,0:T(8,128)(2,1)S(1)}, u32[]{:S(2)}, u32[]{:S(2)}) %collective-permute-start.2) | collective-permute-done | bytes 262176 | tf_op jit(solution)/shard_map/ppermute | solution.py:483
  15.5 5.7 %feed.1 = (f32[512,1024]{1,0:T(8,128)S(1)}, bf16[512,1024]{1,0:T(8,128)(2,1)S(1)}, bf16[512,688]{1,0:T(8,128)(2,1)S(1)}, bf16[512,688]{1,0:T(8,128)(2,1)S(1)}, b...) custom-call(s32[6]{0:T(128)S(1)} %pad_add_fusion.where.place, ...), custom_call_target="tpu_custom_call" | custom-call | flops 3000000000 | bytes 1000 | tf_op jit(solution)/shard_map/feed/pallas_call | solution.py:441
  21.2 0.2 collective-permute-start.3
  21.4 1.9 %pair.1 = (bf16[4,1072,128]{2,1,0:T(8,128)(2,1)S(1)}, bf16[4,992,128]{2,1,0:T(8,128)(2,1)S(1)}) custom-call(s32[6]{0:T(128)S(1)} %pad_add_fusion.where.place, bf16[512,688]{1,0:T(8,128)(2,1)S(1)} %get-tuple-element.124.inner, bf16[512,688]{1,0:T(8,128)(2,1)S(1)} %get-tuple-element.110.gate, bf16[512,688]{1,0:T(8,128)(2,1)S(1)} %get-tuple-element.111.up, ...), custom_call_target="tpu_custom_call" | custom-call | flops 1000 | bytes 1000 | tf_op jit(solution)/shard_map/pair/pallas_call | solution.py:441
  23.6 1.5 %down.1 = (bf16[256,1024]{1,0:T(8,128)(2,1)S(1)}, bf16[256,1024]{1,0:T(8,128)(2,1)S(1)}) custom-call(s32[6]{0:T(128)S(1)} %pad_add_fusion.where.place, bf16[512,688]{1,0:T(8,128)(2,1)S(1)} %get-tuple-element.124.inner, bf16[688,1024]{1,0:T(8,128)(2,1)S(1)} %get-tuple-element.99.w_down), custom_call_target="tpu_custom_call" | custom-call | flops 1000 | bytes 1000 | tf_op jit(solution)/shard_map/down/pallas_call | solution.py:441
  25.1 0.5 collective-permute-start.5
  25.6 1.7 %collective-permute-start.4 = (bf16[256,1024]{1,0:T(8,128)(2,1)S(1)}, bf16[256,1024]{1,0:T(8,128)(2,1)S(1)}, u32[]{:S(2)}, u32[]{:S(2)}) collective-permute-start(bf16[256,1024]{1,0:T(8,128)(2,1)S(1)} %add_convert_fusion.3), channel_id=1, source_target_pairs={{0,2},{1,3},{2,0},{3,1},{4,6},{5,7},{6,4},{7,5},{8,10},{9,11},{10,... | collective-permute-start | bytes 1572872 | tf_op jit(solution)/shard_map/ppermute | solution.py:483
  27.3 1.6 %collective-permute-start.9 = (bf16[4,992,128]{2,1,0:T(8,128)(2,1)S(1)}, bf16[4,992,128]{2,1,0:T(8,128)(2,1)S(1)}, u32[]{:S(2)}, u32[]{:S(2)}) collective-permute-start(bf16[4,992,128]{2,1,0:T(8,128)(2,1)S(1)} %get-tuple-element.113), channel_id=1, source_target_pairs={{0,8},{4,12},{8,0},{12,4},{16,24},{20,28},{24,16},{28,20},{1,9},{5... | collective-permute-start | bytes 3047432 | tf_op jit(solution)/shard_map/ppermute | solution.py:483
  28.9 1.5 %collective-permute-start.8 = (bf16[4,1072,128]{2,1,0:T(8,128)(2,1)S(1)}, bf16[4,1072,128]{2,1,0:T(8,128)(2,1)S(1)}, u32[]{:S(2)}, u32[]{:S(2)}) collective-permute-start(bf16[4,1072,128]{2,1,0:T(8,128)(2,1)S(1)} %get-tuple-element.135), channel_id=1, source_target_pairs={{0,4},{4,0},{8,12},{12,8},{16,20},{20,16},{24,28},{28,24},{1,5},{5... | collective-permute-start | bytes 3293192 | tf_op jit(solution)/shard_map/ppermute | solution.py:483
  30.5 1.6 %prepare.1 = (bf16[4,768,256]{2,1,0:T(8,128)(2,1)S(1)}, bf16[4,768,256]{2,1,0:T(8,128)(2,1)S(1)}, f32[512,1]{1,0:T(8,128)S(1)}) custom-call(s32[6]{0:T(128)S(1)} %pad_add_fusion.where.place, bf16[512,64]{1,0:T(8,128)(2,1)S(1)} %get-tuple-element.120.q_in.refs_7_, bf16[512,64]{1,0:T(8,128)(2,1)S(1)} %get-tuple-element.121.k_in.refs_8_, ...), custom_call_target="tpu_custom_call" | custom-call | flops 1000 | bytes 1000 | tf_op jit(solution)/shard_map/prepare/pallas_call | solution.py:441
  32.1 2.1 %keeps.1 = (bf16[4,1072,128]{2,1,0:T(8,128)(2,1)S(1)}, bf16[4,992,128]{2,1,0:T(8,128)(2,1)S(1)}) custom-call(s32[6]{0:T(128)S(1)} %pad_add_fusion.where.place, bf16[512,688]{1,0:T(8,128)(2,1)S(1)} %get-tuple-element.124.inner, bf16[512,688]{1,0:T(8,128)(2,1)S(1)} %get-tuple-element.110.gate, bf16[512,688]{1,0:T(8,128)(2,1)S(1)} %get-tuple-element.111.up, ...), custom_call_target="tpu_custom_call" | custom-call | flops 1000 | bytes 1000 | tf_op jit(solution)/shard_map/keeps/pallas_call | solution.py:441
  34.2 5.3 %collective-permute-done.4 = bf16[256,1024]{1,0:T(8,128)(2,1)S(1)} collective-permute-done((bf16[256,1024]{1,0:T(8,128)(2,1)S(1)}, bf16[256,1024]{1,0:T(8,128)(2,1)S(1)}, u32[]{:S(2)}, u32[]{:S(2)}) %collective-permute-start.4) | collective-permute-done | bytes 524320 | tf_op jit(solution)/shard_map/ppermute | solution.py:483
  39.8 1.8 %collective-permute-start.14 = (bf16[256,1024]{1,0:T(8,128)(2,1)S(1)}, bf16[256,1024]{1,0:T(8,128)(2,1)S(1)}, u32[]{:S(2)}, u32[]{:S(2)}) collective-permute-start(bf16[256,1024]{1,0:T(8,128)(2,1)S(1)} %add_convert_fusion.2), channel_id=1, source_target_pairs={{0,2},{1,3},{2,0},{3,1},{4,6},{5,7},{6,4},{7,5},{8,10},{9,11},{10,... | collective-permute-start | bytes 1572872 | tf_op jit(solution)/shard_map/ppermute | solution.py:483
  41.7 4.9 %back.1 = (f32[512,1024]{1,0:T(8,128)S(1)}, bf16[512,1024]{1,0:T(8,128)(2,1)S(1)}, bf16[512,384]{1,0:T(8,128)(2,1)S(1)}, f32[1,1024]{1,0:T(1,128)S(1)}, bf16[4,656,128]{2,1,0:T(8,128)(2,1)S(1)}) custom-call(s32[6]{0:T(128)S(1)} %pad_add_fusion.where.place, bf16[256,1024]{1,0:T(8,128)(2,1)S(1)} %add_convert_fusion.1.refs_0_, ...), custom_call_target="tpu_custom_call" | custom-call | flops 1000 | bytes 1000 | tf_op jit(solution)/shard_map/back/pallas_call | solution.py:441
  46.5 1.8 %collective-permute-start.12 = (bf16[4,656,128]{2,1,0:T(8,128)(2,1)S(1)}, bf16[4,656,128]{2,1,0:T(8,128)(2,1)S(1)}, u32[]{:S(2)}, u32[]{:S(2)}) collective-permute-start(bf16[4,656,128]{2,1,0:T(8,128)(2,1)S(1)} %get-tuple-element.136), channel_id=1, source_target_pairs={{0,4},{4,0},{8,12},{12,8},{16,20},{20,16},{24,28},{28,24},{1,5},{5... | collective-permute-start | bytes 2015240 | tf_op jit(solution)/shard_map/ppermute | solution.py:483
  48.3 1.5 %collective-permute-start.13 = (bf16[512,384]{1,0:T(8,128)(2,1)S(1)}, bf16[512,384]{1,0:T(8,128)(2,1)S(1)}, u32[]{:S(2)}, u32[]{:S(2)}) collective-permute-start(bf16[512,384]{1,0:T(8,128)(2,1)S(1)} %get-tuple-element.133.refs_1_.refs_0_), channel_id=1, source_target_pairs={{0,2},{1,3},{2,0},{3,1},{4,6},{5,7},{6,4},{7,5},{8,10},{9,11},{10,... | collective-permute-start | bytes 1179656 | tf_op jit(solution)/shard_map/ppermute | solution.py:483
  49.8 1.7 %collective-permute-done.9.come = bf16[4,992,128]{2,1,0:T(8,128)(2,1)S(1)} collective-permute-done((bf16[4,992,128]{2,1,0:T(8,128)(2,1)S(1)}, bf16[4,992,128]{2,1,0:T(8,128)(2,1)S(1)}, u32[]{:S(2)}, u32[]{:S(2)}) %collective-permute-start.9) | collective-permute-done | bytes 1015840 | tf_op jit(solution)/shard_map/ppermute | solution.py:483
  51.5 0.8 z_keep.1
  52.3 2.7 %collective-permute-start.11 = (bf16[2,992,128]{2,1,0:T(8,128)(2,1)S(1)}, bf16[2,992,128]{2,1,0:T(8,128)(2,1)S(1)}, u32[]{:S(2)}, u32[]{:S(2)}) collective-permute-start(bf16[2,992,128]{2,1,0:T(8,128)(2,1)S(1)} %get-tuple-element.138), channel_id=1, source_target_pairs={{0,16},{4,20},{8,24},{12,28},{16,0},{20,4},{24,8},{28,12},{1,17},{... | collective-permute-start | bytes 1523720 | tf_op jit(solution)/shard_map/ppermute | solution.py:483
  54.9 1.1 %collective-permute-done.8.come = bf16[4,1072,128]{2,1,0:T(8,128)(2,1)S(1)} collective-permute-done((bf16[4,1072,128]{2,1,0:T(8,128)(2,1)S(1)}, bf16[4,1072,128]{2,1,0:T(8,128)(2,1)S(1)}, u32[]{:S(2)}, u32[]{:S(2)}) %collective-permute-start.8) | collective-permute-done | bytes 1097760 | tf_op jit(solution)/shard_map/ppermute | solution.py:483
  56.0 0.8 x_keep.1
  56.8 0.6 collective-permute-start.10
  57.4 1.1 %late_product.1.held = bf16[4,656,128]{2,1,0:T(8,128)(2,1)S(1)} custom-call(s32[6]{0:T(128)S(1)} %pad_add_fusion.where.place, bf16[512,256]{1,0:T(8,128)(2,1)S(1)} %get-tuple-element.143.ctx.refs_0_.refs_10_, bf16[512,384]{1,0:T(8,128)(2,1)S(1)} %get-tuple-element.133.refs_1_.refs_0_, bf16[512,1024]{1,0:T(8,128)(2,1)S(1)} %get-tuple-element.132.refs_14_.refs_2_, ...), custom_call_target="tpu_custom_call" | custom-call | flops 1000 | bytes 1000 | tf_op jit(solution)/shard_map/late_product/pallas_call | solution.py:441
  58.8 3.7 %collective-permute-done.13.refs_2_ = bf16[512,384]{1,0:T(8,128)(2,1)S(1)} collective-permute-done((bf16[512,384]{1,0:T(8,128)(2,1)S(1)}, bf16[512,384]{1,0:T(8,128)(2,1)S(1)}, u32[]{:S(2)}, u32[]{:S(2)}) %collective-permute-start.13) | collective-permute-done | bytes 393248 | tf_op jit(solution)/shard_map/ppermute | solution.py:483
  62.5 6.4 %collective-permute-done.12.come = bf16[4,656,128]{2,1,0:T(8,128)(2,1)S(1)} collective-permute-done((bf16[4,656,128]{2,1,0:T(8,128)(2,1)S(1)}, bf16[4,656,128]{2,1,0:T(8,128)(2,1)S(1)}, u32[]{:S(2)}, u32[]{:S(2)}) %collective-permute-start.12) | collective-permute-done | bytes 671776 | tf_op jit(solution)/shard_map/ppermute | solution.py:483
  69.0 0.7 late_keep.1
  69.6 2.6 %collective-permute-start.17 = (bf16[656,128]{1,0:T(8,128)(2,1)S(1)}, bf16[656,128]{1,0:T(8,128)(2,1)S(1)}, u32[]{:S(2)}, u32[]{:S(2)}) collective-permute-start(bf16[656,128]{1,0:T(8,128)(2,1)S(1)} %get-tuple-element.158), channel_id=1, source_target_pairs={{0,16},{4,20},{8,24},{12,28},{16,0},{20,4},{24,8},{28,12},{1,17},{... | collective-permute-start | bytes 503816 | tf_op jit(solution)/shard_map/ppermute | solution.py:483
  72.3 0.5 collective-permute-start.18
  72.8 6.3 %collective-permute-done.11.come = bf16[2,992,128]{2,1,0:T(8,128)(2,1)S(1)} collective-permute-done((bf16[2,992,128]{2,1,0:T(8,128)(2,1)S(1)}, bf16[2,992,128]{2,1,0:T(8,128)(2,1)S(1)}, u32[]{:S(2)}, u32[]{:S(2)}) %collective-permute-start.11) | collective-permute-done | bytes 507936 | tf_op jit(solution)/shard_map/ppermute | solution.py:483
  79.1 2.3 %collective-permute-start.19 = (bf16[656,128]{1,0:T(8,128)(2,1)S(1)}, bf16[656,128]{1,0:T(8,128)(2,1)S(1)}, u32[]{:S(2)}, u32[]{:S(2)}) collective-permute-start(bf16[656,128]{1,0:T(8,128)(2,1)S(1)} %get-tuple-element.149), channel_id=1, source_target_pairs={{0,24},{4,28},{8,16},{12,20},{16,8},{20,12},{24,0},{28,4},{1,25},{... | collective-permute-start | bytes 503816 | tf_op jit(solution)/shard_map/ppermute | solution.py:483
  81.4 0.7 z_hop.1
  82.1 1.3 %collective-permute-done.10.come = bf16[2,1072,128]{2,1,0:T(8,128)(2,1)S(1)} collective-permute-done((bf16[2,1072,128]{2,1,0:T(8,128)(2,1)S(1)}, bf16[2,1072,128]{2,1,0:T(8,128)(2,1)S(1)}, u32[]{:S(2)}, u32[]{:S(2)}) %collective-permute-start.10) | collective-permute-done | bytes 548896 | tf_op jit(solution)/shard_map/ppermute | solution.py:483
  83.4 0.7 x_hop.1
  84.1 0.6 collective-permute-start.15
  84.7 1.6 %collective-permute-done.17.refs_0_ = bf16[656,128]{1,0:T(8,128)(2,1)S(1)} collective-permute-done((bf16[656,128]{1,0:T(8,128)(2,1)S(1)}, bf16[656,128]{1,0:T(8,128)(2,1)S(1)}, u32[]{:S(2)}, u32[]{:S(2)}) %collective-permute-start.17) | collective-permute-done | bytes 167968 | tf_op jit(solution)/shard_map/ppermute | solution.py:483
  86.3 3.1 %collective-permute-done.18.refs_1_ = bf16[656,128]{1,0:T(8,128)(2,1)S(1)} collective-permute-done((bf16[656,128]{1,0:T(8,128)(2,1)S(1)}, bf16[656,128]{1,0:T(8,128)(2,1)S(1)}, u32[]{:S(2)}, u32[]{:S(2)}) %collective-permute-start.18) | collective-permute-done | bytes 167968 | tf_op jit(solution)/shard_map/ppermute | solution.py:483
  89.4 1.5 %collective-permute-start.24 = (bf16[1,992,128]{2,1,0:T(8,128)(2,1)S(1)}, bf16[1,992,128]{2,1,0:T(8,128)(2,1)S(1)}, u32[]{:S(2)}, u32[]{:S(2)}) collective-permute-start(bf16[1,992,128]{2,1,0:T(8,128)(2,1)S(1)} %get-tuple-element.151), channel_id=1, source_target_pairs={{0,4},{4,0},{8,12},{12,8},{16,20},{20,16},{24,28},{28,24},{1,5},{5... | collective-permute-start | bytes 761864 | tf_op jit(solution)/shard_map/ppermute | solution.py:483
  91.0 1.3 %late.1 = (f32[256,128]{1,0:T(8,128)}, f32[1,128]{1,0:T(1,128)}, bf16[128,384]{1,0:T(8,128)(2,1)S(1)}) custom-call(s32[6]{0:T(128)S(1)} %pad_add_fusion.where.place, f32[656,128]{1,0:T(8,128)S(1)} %get-tuple-element.157.held, bf16[656,128]{1,0:T(8,128)(2,1)S(1)} %collective-permute-done.17.refs_0_, bf16[656,128]{1,0:T(8,128)(2,1)S(1)} %collective-permute-done.18.refs_1_, ...), custom_call_target="tpu_custom_call" | custom-call | flops 10000000000 | bytes 1000 | tf_op jit(solution)/shard_map/late/pallas_call | solution.py:441
  92.2 0.5 collective-permute-start.21
  92.8 4.6 %grad_input.1 = (bf16[512,1024]{1,0:T(8,128)(2,1)}, bf16[512,1024]{1,0:T(8,128)(2,1)}) custom-call(s32[6]{0:T(128)S(1)} %pad_add_fusion.where.place, bf16[512,384]{1,0:T(8,128)(2,1)S(1)} %get-tuple-element.133.refs_1_.refs_0_, bf16[512,384]{1,0:T(8,128)(2,1)S(1)} %collective-permute-done.7.refs_1_, bf16[512,384]{1,0:T(8,128)(2,1)S(1)} %collective-permute-done.13.refs_2_, ...), custom_call_target="tpu_custom_call" | custom-call | flops 1000 | bytes 1000 | tf_op jit(solution)/shard_map/grad_input/pallas_call | solution.py:441
  97.4 0.5 collective-permute-start.22
  97.9 4.9 %collective-permute-done.23.x_come = bf16[1,1072,128]{2,1,0:T(8,128)(2,1)S(1)} collective-permute-done((bf16[1,1072,128]{2,1,0:T(8,128)(2,1)S(1)}, bf16[1,1072,128]{2,1,0:T(8,128)(2,1)S(1)}, u32[]{:S(2)}, u32[]{:S(2)}) %collective-permute-start.23) | collective-permute-done | bytes 274464 | tf_op jit(solution)/shard_map/ppermute | solution.py:483
  102.8 1.5 %hidden.1 = (f32[688,128]{1,0:T(8,128)}, f32[688,128]{1,0:T(8,128)}, f32[688,128]{1,0:T(8,128)}) custom-call(s32[6]{0:T(128)S(1)} %pad_add_fusion.where.place, bf16[1,1072,128]{2,1,0:T(8,128)(2,1)S(1)} %get-tuple-element.168.x_held, bf16[1,1072,128]{2,1,0:T(8,128)(2,1)S(1)} %collective-permute-done.23.x_come, ...), custom_call_target="tpu_custom_call" | custom-call | flops 10000000000 | bytes 1000 | tf_op jit(solution)/shard_map/hidden/pallas_call | solution.py:441
  104.3 1.6 %finish.1 = (f32[128,256]{1,0:T(8,128)}, f32[128,256]{1,0:T(8,128)}, f32[128,1024]{1,0:T(8,128)}, f32[1,128]{1,0:T(1,128)}) custom-call(s32[6]{0:T(128)S(1)} %pad_add_fusion.where.place, bf16[128,384]{1,0:T(8,128)(2,1)S(1)} %get-tuple-element.173.refs_0_, bf16[128,384]{1,0:T(8,128)(2,1)S(1)} %collective-permute-done.20.refs_1_, ...), custom_call_target="tpu_custom_call" | custom-call | flops 1000 | bytes 1000 | tf_op jit(solution)/shard_map/finish/pallas_call | solution.py:441
  (41 shorter events, 1.2 us)
Async XLA Ops:
  0.6 7.0 %copy-start.7 = (s32[1,4]{1,0:T(1,128)S(1)}, s32[1,4]{1,0:T(1,128)}, u32[]{:S(2)}) copy-start(s32[1,4]{1,0:T(1,128)} %lengths.1) | copy-start | bytes 52
  4.6 9.3 %collective-permute-start.1 = (bf16[512,256]{1,0:T(8,128)(2,1)S(1)}, bf16[512,256]{1,0:T(8,128)(2,1)S(1)}, u32[]{:S(2)}, u32[]{:S(2)}) collective-permute-start(bf16[512,256]{1,0:T(8,128)(2,1)S(1)} %get-tuple-element.143.ctx.refs_0_.refs_10_), channel_id=1, source_target_pairs={{0,2},{1,3},{2,0},{3,1},{4,6},{5,7},{6,4},{7,5},{8,10},{9,11},{10,... | collective-permute-start | bytes 786440 | tf_op jit(solution)/shard_map/ppermute | solution.py:483
  7.6 6.3 %collective-permute-start = (bf16[512,256]{1,0:T(8,128)(2,1)S(1)}, bf16[512,256]{1,0:T(8,128)(2,1)S(1)}, u32[]{:S(2)}, u32[]{:S(2)}) collective-permute-start(bf16[512,256]{1,0:T(8,128)(2,1)S(1)} %get-tuple-element.143.ctx.refs_0_.refs_10_), channel_id=1, source_target_pairs={{0,1},{1,0},{2,3},{3,2},{4,5},{5,4},{6,7},{7,6},{8,9},{9,8},{10,11... | collective-permute-start | bytes 786440 | tf_op jit(solution)/shard_map/ppermute | solution.py:483
  7.7 7.8 %copy-start.4 = (bf16[512,1024]{1,0:T(8,128)(2,1)S(1)}, bf16[512,1024]{1,0:T(8,128)(2,1)}, u32[]{:S(2)}) copy-start(bf16[512,1024]{1,0:T(8,128)(2,1)} %refs_5_.2) | copy-start | bytes 3145732
  7.7 7.8 %copy-start.6 = (f32[1024]{0:T(1024)S(1)}, f32[1024]{0:T(1024)}, u32[]{:S(2)}) copy-start(f32[1024]{0:T(1024)} %param.18) | copy-start | bytes 12292
  13.9 1.5 %collective-permute-start.2 = (bf16[512,256]{1,0:T(8,128)(2,1)S(1)}, bf16[512,256]{1,0:T(8,128)(2,1)S(1)}, u32[]{:S(2)}, u32[]{:S(2)}) collective-permute-start(bf16[512,256]{1,0:T(8,128)(2,1)S(1)} %collective-permute-done.1.refs_2_), channel_id=1, source_target_pairs={{0,1},{1,0},{2,3},{3,2},{4,5},{5,4},{6,7},{7,6},{8,9},{9,8},{10,11... | collective-permute-start | bytes 786440 | tf_op jit(solution)/shard_map/ppermute | solution.py:483
  15.5 5.9 %copy-start.1 = (bf16[512,1024]{1,0:T(8,128)(2,1)S(1)}, bf16[512,1024]{1,0:T(8,128)(2,1)}, u32[]{:S(2)}) copy-start(bf16[512,1024]{1,0:T(8,128)(2,1)} %refs_4_.3) | copy-start | bytes 3145732
  21.2 2.1 %collective-permute-start.3 = (bf16[256,1024]{1,0:T(8,128)(2,1)S(1)}, bf16[256,1024]{1,0:T(8,128)(2,1)S(1)}, u32[]{:S(2)}, u32[]{:S(2)}) collective-permute-start(bf16[256,1024]{1,0:T(8,128)(2,1)S(1)} %get-tuple-element.108), channel_id=1, source_target_pairs={{0,1},{1,0},{2,3},{3,2},{4,5},{5,4},{6,7},{7,6},{8,9},{9,8},{10,11... | collective-permute-start | bytes 1572872 | tf_op jit(solution)/shard_map/ppermute | solution.py:483
  25.1 5.2 %collective-permute-start.5 = (bf16[256,1024]{1,0:T(8,128)(2,1)S(1)}, bf16[256,1024]{1,0:T(8,128)(2,1)S(1)}, u32[]{:S(2)}, u32[]{:S(2)}) collective-permute-start(bf16[256,1024]{1,0:T(8,128)(2,1)S(1)} %get-tuple-element.118), channel_id=1, source_target_pairs={{0,1},{1,0},{2,3},{3,2},{4,5},{5,4},{6,7},{7,6},{8,9},{9,8},{10,11... | collective-permute-start | bytes 1572872 | tf_op jit(solution)/shard_map/ppermute | solution.py:483
  25.6 14.0 %collective-permute-start.4 = (bf16[256,1024]{1,0:T(8,128)(2,1)S(1)}, bf16[256,1024]{1,0:T(8,128)(2,1)S(1)}, u32[]{:S(2)}, u32[]{:S(2)}) collective-permute-start(bf16[256,1024]{1,0:T(8,128)(2,1)S(1)} %add_convert_fusion.3), channel_id=1, source_target_pairs={{0,2},{1,3},{2,0},{3,1},{4,6},{5,7},{6,4},{7,5},{8,10},{9,11},{10,... | collective-permute-start | bytes 1572872 | tf_op jit(solution)/shard_map/ppermute | solution.py:483
  27.3 24.2 %collective-permute-start.9 = (bf16[4,992,128]{2,1,0:T(8,128)(2,1)S(1)}, bf16[4,992,128]{2,1,0:T(8,128)(2,1)S(1)}, u32[]{:S(2)}, u32[]{:S(2)}) collective-permute-start(bf16[4,992,128]{2,1,0:T(8,128)(2,1)S(1)} %get-tuple-element.113), channel_id=1, source_target_pairs={{0,8},{4,12},{8,0},{12,4},{16,24},{20,28},{24,16},{28,20},{1,9},{5... | collective-permute-start | bytes 3047432 | tf_op jit(solution)/shard_map/ppermute | solution.py:483
  28.9 27.1 %collective-permute-start.8 = (bf16[4,1072,128]{2,1,0:T(8,128)(2,1)S(1)}, bf16[4,1072,128]{2,1,0:T(8,128)(2,1)S(1)}, u32[]{:S(2)}, u32[]{:S(2)}) collective-permute-start(bf16[4,1072,128]{2,1,0:T(8,128)(2,1)S(1)} %get-tuple-element.135), channel_id=1, source_target_pairs={{0,4},{4,0},{8,12},{12,8},{16,20},{20,16},{24,28},{28,24},{1,5},{5... | collective-permute-start | bytes 3293192 | tf_op jit(solution)/shard_map/ppermute | solution.py:483
  39.7 2.0 %collective-permute-start.6 = (bf16[256,1024]{1,0:T(8,128)(2,1)S(1)}, bf16[256,1024]{1,0:T(8,128)(2,1)S(1)}, u32[]{:S(2)}, u32[]{:S(2)}) collective-permute-start(bf16[256,1024]{1,0:T(8,128)(2,1)S(1)} %add_convert_fusion.1.refs_0_), channel_id=1, source_target_pairs={{0,1},{1,0},{2,3},{3,2},{4,5},{5,4},{6,7},{7,6},{8,9},{9,8},{10,11... | collective-permute-start | bytes 1572872 | tf_op jit(solution)/shard_map/ppermute | solution.py:483
  39.8 18.7 %collective-permute-start.14 = (bf16[256,1024]{1,0:T(8,128)(2,1)S(1)}, bf16[256,1024]{1,0:T(8,128)(2,1)S(1)}, u32[]{:S(2)}, u32[]{:S(2)}) collective-permute-start(bf16[256,1024]{1,0:T(8,128)(2,1)S(1)} %add_convert_fusion.2), channel_id=1, source_target_pairs={{0,2},{1,3},{2,0},{3,1},{4,6},{5,7},{6,4},{7,5},{8,10},{9,11},{10,... | collective-permute-start | bytes 1572872 | tf_op jit(solution)/shard_map/ppermute | solution.py:483
  46.5 22.4 %collective-permute-start.12 = (bf16[4,656,128]{2,1,0:T(8,128)(2,1)S(1)}, bf16[4,656,128]{2,1,0:T(8,128)(2,1)S(1)}, u32[]{:S(2)}, u32[]{:S(2)}) collective-permute-start(bf16[4,656,128]{2,1,0:T(8,128)(2,1)S(1)} %get-tuple-element.136), channel_id=1, source_target_pairs={{0,4},{4,0},{8,12},{12,8},{16,20},{20,16},{24,28},{28,24},{1,5},{5... | collective-permute-start | bytes 2015240 | tf_op jit(solution)/shard_map/ppermute | solution.py:483
  48.3 14.3 %collective-permute-start.13 = (bf16[512,384]{1,0:T(8,128)(2,1)S(1)}, bf16[512,384]{1,0:T(8,128)(2,1)S(1)}, u32[]{:S(2)}, u32[]{:S(2)}) collective-permute-start(bf16[512,384]{1,0:T(8,128)(2,1)S(1)} %get-tuple-element.133.refs_1_.refs_0_), channel_id=1, source_target_pairs={{0,2},{1,3},{2,0},{3,1},{4,6},{5,7},{6,4},{7,5},{8,10},{9,11},{10,... | collective-permute-start | bytes 1179656 | tf_op jit(solution)/shard_map/ppermute | solution.py:483
  52.3 26.8 %collective-permute-start.11 = (bf16[2,992,128]{2,1,0:T(8,128)(2,1)S(1)}, bf16[2,992,128]{2,1,0:T(8,128)(2,1)S(1)}, u32[]{:S(2)}, u32[]{:S(2)}) collective-permute-start(bf16[2,992,128]{2,1,0:T(8,128)(2,1)S(1)} %get-tuple-element.138), channel_id=1, source_target_pairs={{0,16},{4,20},{8,24},{12,28},{16,0},{20,4},{24,8},{28,12},{1,17},{... | collective-permute-start | bytes 1523720 | tf_op jit(solution)/shard_map/ppermute | solution.py:483
  56.8 26.6 %collective-permute-start.10 = (bf16[2,1072,128]{2,1,0:T(8,128)(2,1)S(1)}, bf16[2,1072,128]{2,1,0:T(8,128)(2,1)S(1)}, u32[]{:S(2)}, u32[]{:S(2)}) collective-permute-start(bf16[2,1072,128]{2,1,0:T(8,128)(2,1)S(1)} %get-tuple-element.141), channel_id=1, source_target_pairs={{0,8},{4,12},{8,0},{12,4},{16,24},{20,28},{24,16},{28,20},{1,9},{5... | collective-permute-start | bytes 1646600 | tf_op jit(solution)/shard_map/ppermute | solution.py:483
  58.5 25.6 %collective-permute-start.7 = (bf16[512,384]{1,0:T(8,128)(2,1)S(1)}, bf16[512,384]{1,0:T(8,128)(2,1)S(1)}, u32[]{:S(2)}, u32[]{:S(2)}) collective-permute-start(bf16[512,384]{1,0:T(8,128)(2,1)S(1)} %get-tuple-element.133.refs_1_.refs_0_), channel_id=1, source_target_pairs={{0,1},{1,0},{2,3},{3,2},{4,5},{5,4},{6,7},{7,6},{8,9},{9,8},{10,11... | collective-permute-start | bytes 1179656 | tf_op jit(solution)/shard_map/ppermute | solution.py:483
  69.6 16.7 %collective-permute-start.17 = (bf16[656,128]{1,0:T(8,128)(2,1)S(1)}, bf16[656,128]{1,0:T(8,128)(2,1)S(1)}, u32[]{:S(2)}, u32[]{:S(2)}) collective-permute-start(bf16[656,128]{1,0:T(8,128)(2,1)S(1)} %get-tuple-element.158), channel_id=1, source_target_pairs={{0,16},{4,20},{8,24},{12,28},{16,0},{20,4},{24,8},{28,12},{1,17},{... | collective-permute-start | bytes 503816 | tf_op jit(solution)/shard_map/ppermute | solution.py:483
  72.3 17.1 %collective-permute-start.18 = (bf16[656,128]{1,0:T(8,128)(2,1)S(1)}, bf16[656,128]{1,0:T(8,128)(2,1)S(1)}, u32[]{:S(2)}, u32[]{:S(2)}) collective-permute-start(bf16[656,128]{1,0:T(8,128)(2,1)S(1)} %get-tuple-element.159), channel_id=1, source_target_pairs={{0,8},{4,12},{8,0},{12,4},{16,24},{20,28},{24,16},{28,20},{1,9},{5... | collective-permute-start | bytes 503816 | tf_op jit(solution)/shard_map/ppermute | solution.py:483
  79.1 11.8 %collective-permute-start.19 = (bf16[656,128]{1,0:T(8,128)(2,1)S(1)}, bf16[656,128]{1,0:T(8,128)(2,1)S(1)}, u32[]{:S(2)}, u32[]{:S(2)}) collective-permute-start(bf16[656,128]{1,0:T(8,128)(2,1)S(1)} %get-tuple-element.149), channel_id=1, source_target_pairs={{0,24},{4,28},{8,16},{12,20},{16,8},{20,12},{24,0},{28,4},{1,25},{... | collective-permute-start | bytes 503816 | tf_op jit(solution)/shard_map/ppermute | solution.py:483
  83.4 9.3 %collective-permute-start.16 = (bf16[256,1024]{1,0:T(8,128)(2,1)S(1)}, bf16[256,1024]{1,0:T(8,128)(2,1)S(1)}, u32[]{:S(2)}, u32[]{:S(2)}) collective-permute-start(bf16[256,1024]{1,0:T(8,128)(2,1)S(1)} %add_convert_fusion.refs_7_), channel_id=1, source_target_pairs={{0,1},{1,0},{2,3},{3,2},{4,5},{5,4},{6,7},{7,6},{8,9},{9,8},{10,11... | collective-permute-start | bytes 1572872 | tf_op jit(solution)/shard_map/ppermute | solution.py:483
  84.1 8.6 %collective-permute-start.15 = (bf16[512,384]{1,0:T(8,128)(2,1)S(1)}, bf16[512,384]{1,0:T(8,128)(2,1)S(1)}, u32[]{:S(2)}, u32[]{:S(2)}) collective-permute-start(bf16[512,384]{1,0:T(8,128)(2,1)S(1)} %collective-permute-done.13.refs_2_), channel_id=1, source_target_pairs={{0,1},{1,0},{2,3},{3,2},{4,5},{5,4},{6,7},{7,6},{8,9},{9,8},{10,11... | collective-permute-start | bytes 1179656 | tf_op jit(solution)/shard_map/ppermute | solution.py:483
  86.3 16.5 %collective-permute-start.23 = (bf16[1,1072,128]{2,1,0:T(8,128)(2,1)S(1)}, bf16[1,1072,128]{2,1,0:T(8,128)(2,1)S(1)}, u32[]{:S(2)}, u32[]{:S(2)}) collective-permute-start(bf16[1,1072,128]{2,1,0:T(8,128)(2,1)S(1)} %get-tuple-element.153), channel_id=1, source_target_pairs={{0,16},{4,20},{8,24},{12,28},{16,0},{20,4},{24,8},{28,12},{1,17},{... | collective-permute-start | bytes 823304 | tf_op jit(solution)/shard_map/ppermute | solution.py:483
  89.4 8.5 %collective-permute-start.24 = (bf16[1,992,128]{2,1,0:T(8,128)(2,1)S(1)}, bf16[1,992,128]{2,1,0:T(8,128)(2,1)S(1)}, u32[]{:S(2)}, u32[]{:S(2)}) collective-permute-start(bf16[1,992,128]{2,1,0:T(8,128)(2,1)S(1)} %get-tuple-element.151), channel_id=1, source_target_pairs={{0,4},{4,0},{8,12},{12,8},{16,20},{20,16},{24,28},{28,24},{1,5},{5... | collective-permute-start | bytes 761864 | tf_op jit(solution)/shard_map/ppermute | solution.py:483
  90.9 1.8 %copy-start = (bf16[1024,1024]{1,0:T(8,128)(2,1)S(1)}, bf16[1024,1024]{1,0:T(8,128)(2,1)}, u32[]{:S(2)}) copy-start(bf16[1024,1024]{1,0:T(8,128)(2,1)} %refs_7_.1) | copy-start | bytes 6291460
  90.9 1.8 %copy-start.2 = (bf16[1024,256]{1,0:T(8,128)(2,1)S(1)}, bf16[1024,256]{1,0:T(8,128)(2,1)}, u32[]{:S(2)}) copy-start(bf16[1024,256]{1,0:T(8,128)(2,1)} %refs_5_.3) | copy-start | bytes 1572868
  90.9 1.9 %copy-start.3 = (bf16[1024,256]{1,0:T(8,128)(2,1)S(1)}, bf16[1024,256]{1,0:T(8,128)(2,1)}, u32[]{:S(2)}) copy-start(bf16[1024,256]{1,0:T(8,128)(2,1)} %refs_6_.1) | copy-start | bytes 1572868
  90.9 1.9 %copy-start.5 = (f32[1024]{0:T(1024)S(1)}, f32[1024]{0:T(1024)}, u32[]{:S(2)}) copy-start(f32[1024]{0:T(1024)} %param.13) | copy-start | bytes 12292
  92.2 5.2 %collective-permute-start.21 = (bf16[128,384]{1,0:T(8,128)(2,1)S(1)}, bf16[128,384]{1,0:T(8,128)(2,1)S(1)}, u32[]{:S(2)}, u32[]{:S(2)}) collective-permute-start(bf16[128,384]{1,0:T(8,128)(2,1)S(1)} %get-tuple-element.173.refs_0_), channel_id=1, source_target_pairs={{0,2},{1,3},{2,0},{3,1},{4,6},{5,7},{6,4},{7,5},{8,10},{9,11},{10,... | collective-permute-start | bytes 294920 | tf_op jit(solution)/shard_map/ppermute | solution.py:483
  92.8 11.6 %collective-permute-start.20 = (bf16[128,384]{1,0:T(8,128)(2,1)S(1)}, bf16[128,384]{1,0:T(8,128)(2,1)S(1)}, u32[]{:S(2)}, u32[]{:S(2)}) collective-permute-start(bf16[128,384]{1,0:T(8,128)(2,1)S(1)} %get-tuple-element.173.refs_0_), channel_id=1, source_target_pairs={{0,1},{1,0},{2,3},{3,2},{4,5},{5,4},{6,7},{7,6},{8,9},{9,8},{10,11... | collective-permute-start | bytes 294920 | tf_op jit(solution)/shard_map/ppermute | solution.py:483
  97.4 6.9 %collective-permute-start.22 = (bf16[128,384]{1,0:T(8,128)(2,1)S(1)}, bf16[128,384]{1,0:T(8,128)(2,1)S(1)}, u32[]{:S(2)}, u32[]{:S(2)}) collective-permute-start(bf16[128,384]{1,0:T(8,128)(2,1)S(1)} %collective-permute-done.21.refs_2_), channel_id=1, source_target_pairs={{0,1},{1,0},{2,3},{3,2},{4,5},{5,4},{6,7},{7,6},{8,9},{9,8},{10,11... | collective-permute-start | bytes 294920 | tf_op jit(solution)/shard_map/ppermute | solution.py:483
